TPU v7x, 32 devices: a whole 2x2x4 slice. The times are simulated.
32 devices in a mesh: groups: 2 (over x), expert: 4 (over y, core), donor: 4 (over z).
Axes of the slice: x: 2, y: 2, z: 4, core: 2. Of those that a mesh axis runs over, the one named last changes fastest.
Arguments:
- hidden_in: bfloat16 [1024, 4096], P(('groups', 'expert')), parts along dimension 0, may hold values from -6 to 6
- queries: bfloat16 [1024, 4096], P(('groups', 'expert'), 'donor'), parts along dimension 0, may hold values from -39 to 39
- suffix_kv: bfloat16 [1024, 2, 256], P(('groups', 'expert')), parts along dimension 0, may hold values from -12 to 12
- kv_pool: bfloat16 [128, 2, 32, 256], P(('groups', 'expert', 'donor')), parts along dimension 0, may hold values from -12 to 12
- page_table: int32 [8, 16], P('groups'), parts along dimension 0, may hold values from 0 to 63, as said below
- prefix_len: int32 [8], P('groups'), parts along dimension 0, may hold values from 1 to 512, as said below
- out_weight: bfloat16 [4096, 4096], P('donor', 'expert'), may hold values from -0.09375 to 0.09375
- norm_gain: bfloat16 [4096], replicated, may hold values from 0.099609375 to 1.8984375
- expert_ids: int32 [1024, 4], P(('groups', 'expert')), parts along dimension 0, may hold values from 0 to 7, all different within a row; in each aligned block of 128 rows (0 to 127, 128 to 255, ...) at most 80 rows name the same one
- route_probs: float32 [1024, 4], P(('groups', 'expert')), parts along dimension 0, may hold values from 0.05 to 1
- w_gate_up: bfloat16 [16, 4096, 2, 768], P(('expert', 'donor')), may hold values from -0.09375 to 0.09375
- w_down: bfloat16 [16, 768, 4096], P(('expert', 'donor')), may hold values from -0.15625 to 0.15625
Outputs:
- layer_out: bfloat16 [1024, 4096], P(('groups', 'expert'), 'donor'), parts along dimension 0
- head_out: bfloat16 [1024, 4096], P(('groups', 'expert'), 'donor'), parts along dimension 0
There are 2 independent parts, one for each index of `groups`. A program takes and returns all parts, laid end to end along the dimension named above; an argument that names none is the same for every part. Nothing has to cross between parts.
Inputs may be any that keep to these rules, and one draw needn't show every extreme that they name: For every sequence s the values page_table[s, j] // 4 over j are 0 to 15, each once; pages b * 4 to b * 4 + 3 hold one page of every sequence. `prefix_len`: in every draw one sequence has the longest prefix, 512 tokens. `expert_ids`: the 4 experts of a token differ. Among the 128 tokens of one sequence no expert is named by more than 80 tokens, and in some sequence of every draw some expert is named by exactly 80.
All inputs are finite; a program needn't handle non-finite values.
Results may differ from a plain program's by a relative error of at most 0.0056.
Values may be sent and summed in bfloat16 or wider, within the bound.
No kernel may reach another device: no remote copies, remote signals or barrier semaphores. Data moves between devices by JAX's collectives and lax.ppermute only.
A program may use at most 128 MiB of HBM per device.

v0:
```python
import jax
import jax.numpy as jnp
from jax import lax
from jax.sharding import PartitionSpec as P


def shards(
    hidden_in,
    queries,
    suffix_kv,
    kv_pool,
    page_table,
    prefix_len,
    out_weight,
    norm_gain,
    expert_ids,
    route_probs,
    w_gate_up,
    w_down,
):
    n_expert = lax.axis_size("expert")
    n_donor = lax.axis_size("donor")
    expert_index = lax.axis_index("expert")
    donor_index = lax.axis_index("donor")
    share_count = n_donor // 2
    seq_count, page_count = page_table.shape
    suffix_len = queries.shape[0]
    kv_heads = suffix_kv.shape[1]
    head_dim = suffix_kv.shape[2] // 2
    page_len = kv_pool.shape[2]
    model_width = hidden_in.shape[1]
    columns = model_width // n_donor
    top_count = expert_ids.shape[1]
    experts_all = 2 * n_expert
    capacity = suffix_len * top_count * 5 // (experts_all * 4)
    ff_local = w_gate_up.shape[3]
    my_group = donor_index * kv_heads // n_donor
    owner_index = expert_index * n_donor + donor_index
    owner_of = page_table // seq_count
    held_slot = jnp.sum(jnp.where(owner_of == owner_index, page_table % seq_count, 0), axis=1)
    dest_group = jnp.arange(n_donor, dtype=jnp.int32) * kv_heads // n_donor
    wanted = (held_slot[:, None] * kv_heads + dest_group[None, :]).reshape(-1)
    outgoing = jnp.take(
        kv_pool.reshape(seq_count * kv_heads, page_len, 2 * head_dim), wanted, axis=0
    )
    arrived = lax.all_to_all(outgoing, ("expert", "donor"), split_axis=0, concat_axis=0, tiled=True)
    my_owners = lax.dynamic_index_in_dim(owner_of, expert_index, 0, keepdims=False)
    ordered = jnp.take(arrived, my_owners, axis=0).reshape(page_count * page_len, 2 * head_dim)
    prefix_keys = ordered[:, :head_dim]
    prefix_vals = ordered[:, head_dim:]
    score_scale = head_dim ** (-0.5)
    query_heads = queries.reshape(suffix_len, -1, head_dim)
    fresh_pair = lax.dynamic_index_in_dim(suffix_kv, my_group, 1, keepdims=False)
    causal = jnp.arange(suffix_len)[:, None] >= jnp.arange(suffix_len)[None, :]
    fresh_scores = (
        jnp.einsum(
            "thc,uc->thu", query_heads, fresh_pair[:, :head_dim], preferred_element_type=jnp.float32
        )
        * score_scale
    )
    fresh_scores = jnp.where(causal[:, None, :], fresh_scores, -jnp.inf)
    prefix_tokens = lax.dynamic_index_in_dim(prefix_len, expert_index, 0, keepdims=False)
    block_keys = min(1024, page_count * page_len)
    live_blocks = (prefix_tokens + block_keys - 1) // block_keys

    def block_scores(block_index):
        keys_block = lax.dynamic_slice_in_dim(prefix_keys, block_index * block_keys, block_keys, 0)
        raw_scores = (
            jnp.einsum("thc,kc->thk", query_heads, keys_block, preferred_element_type=jnp.float32)
            * score_scale
        )
        visible = block_index * block_keys + jnp.arange(block_keys) < prefix_tokens
        return jnp.where(visible[None, None, :], raw_scores, -jnp.inf)

    def raise_max(block_index, running):
        return jnp.maximum(running, jnp.max(block_scores(block_index), axis=2))

    row_max = lax.fori_loop(0, live_blocks, raise_max, jnp.max(fresh_scores, axis=2))

    def add_block(block_index, loop_state):
        row_total, weighted = loop_state
        exp_scores = jnp.exp(block_scores(block_index) - row_max[:, :, None])
        vals_block = lax.dynamic_slice_in_dim(prefix_vals, block_index * block_keys, block_keys, 0)
        weighted = weighted + jnp.einsum(
            "thk,kc->thc",
            exp_scores.astype(jnp.bfloat16),
            vals_block,
            preferred_element_type=jnp.float32,
        )
        return (row_total + jnp.sum(exp_scores, axis=2), weighted)

    fresh_exp = jnp.exp(fresh_scores - row_max[:, :, None])
    start_state = (
        jnp.sum(fresh_exp, axis=2),
        jnp.einsum(
            "thu,uc->thc",
            fresh_exp.astype(jnp.bfloat16),
            fresh_pair[:, head_dim:],
            preferred_element_type=jnp.float32,
        ),
    )
    row_total, weighted = lax.fori_loop(0, live_blocks, add_block, start_state)
    head_out = (weighted / row_total[:, :, None]).astype(jnp.bfloat16).reshape(suffix_len, -1)
    counts = jnp.sum(
        (expert_ids[:, :, None] == jnp.arange(experts_all, dtype=jnp.int32)).astype(jnp.int32),
        axis=1,
    )
    before = jnp.cumsum(counts, axis=0) - counts
    slot_index = jnp.take_along_axis(before, expert_ids, axis=1)
    within = expert_ids * capacity + slot_index
    token_rows = jnp.broadcast_to(
        jnp.arange(1, suffix_len + 1, dtype=jnp.int32)[:, None], within.shape
    )
    source = (
        jnp.zeros((experts_all * capacity,), jnp.int32)
        .at[within.reshape(-1)]
        .set(token_rows.reshape(-1))
    )
    gate_weights = route_probs / jnp.sum(route_probs, axis=1, keepdims=True)
    attn_terms = jnp.dot(
        head_out,
        lax.all_gather(out_weight, "expert", axis=1, tiled=True),
        preferred_element_type=jnp.float32,
    )
    gain_f = norm_gain.astype(jnp.float32)
    shares = lax.psum_scatter(attn_terms, "donor", scatter_dimension=1, tiled=True)
    hidden_cols = lax.dynamic_slice_in_dim(hidden_in, donor_index * columns, columns, 1)
    resid_cols = (hidden_cols.astype(jnp.float32) + shares).astype(jnp.bfloat16)
    padded = jnp.concatenate([jnp.zeros((1, columns), jnp.bfloat16), resid_cols], axis=0)
    picked = jnp.take(padded, source, axis=0).reshape(n_expert, 2, capacity, columns)
    copies = jnp.repeat(picked, share_count, axis=1).reshape(n_expert * n_donor, capacity, columns)
    arrived_cols = lax.all_to_all(
        copies, ("expert", "donor"), split_axis=0, concat_axis=0, tiled=True
    ).reshape(n_expert, n_donor, capacity, columns)
    cols_f = arrived_cols.astype(jnp.float32)
    inverse = lax.rsqrt(jnp.mean(cols_f * cols_f, axis=(1, 3), keepdims=True) + 1e-06)
    normed = (cols_f * inverse * gain_f.reshape(1, n_donor, 1, columns)).astype(jnp.bfloat16)
    gate_up = jnp.einsum(
        "sdcf,dfh->sch",
        normed,
        w_gate_up[0].reshape(n_donor, columns, 2 * ff_local),
        preferred_element_type=jnp.float32,
    )
    activated = (jax.nn.silu(gate_up[:, :, :ff_local]) * gate_up[:, :, ff_local:]).astype(
        jnp.bfloat16
    )
    down_local = w_down[0].reshape(ff_local, n_donor, columns)
    partial_out = jnp.einsum(
        "scf,fdo->sdco", activated, down_local, preferred_element_type=jnp.float32
    )
    received = lax.all_to_all(
        partial_out.astype(jnp.bfloat16), "donor", split_axis=1, concat_axis=1, tiled=True
    ).astype(partial_out.dtype)
    expert_sum = jnp.sum(received.reshape(seq_count, 2, share_count, capacity, columns), axis=2)
    returned = lax.all_to_all(
        expert_sum.astype(jnp.bfloat16), "expert", split_axis=0, concat_axis=0, tiled=True
    )
    flat_back = returned.reshape(experts_all * capacity, columns)
    contrib = jnp.take(flat_back, within, axis=0).astype(jnp.float32)
    expert_mix = jnp.sum(contrib * gate_weights[:, :, None], axis=1)
    layer_out = (resid_cols.astype(jnp.float32) + expert_mix).astype(jnp.bfloat16)
    return (layer_out, head_out)


def solution(mesh):
    in_specs = (
        P(("groups", "expert"), None),
        P(("groups", "expert"), "donor"),
        P(("groups", "expert"), None, None),
        P(("groups", "expert", "donor"), None, None, None),
        P("groups", None),
        P("groups"),
        P("donor", "expert"),
        P(),
        P(("groups", "expert"), None),
        P(("groups", "expert"), None),
        P(("expert", "donor"), None, None, None),
        P(("expert", "donor"), None, None),
    )
    out_specs = (P(("groups", "expert"), "donor"), P(("groups", "expert"), "donor"))
    return jax.shard_map(shards, mesh=mesh, in_specs=in_specs, out_specs=out_specs, check_vma=False)
```

profile of v0, /device:TPU:0, one launch (start us, length us, event | category | flops | bytes accessed | tf_op | source)
XLA Modules:
  0.0 302.7 jit_solution(8824726079238525368)
XLA Ops:
  7.3 0.7 all-gather.2.cloned.1.call-update
  8.0 0.8 fusion.24
  9.6 0.8 broadcast_select_fusion.1
  10.4 7.4 %all-to-all-start = ((bf16[16,32,256]{2,1,0:T(8,128)(2,1)}), bf16[16,32,256]{2,1,0:T(8,128)(2,1)S(1)}, u32[]{:S(2)}, u32[]{:S(2)}) async-start(bf16[16,32,256]{2,1,0:T(8,128)(2,1)} %broadcast_select_fusion.1), calls=%async_computation | async-start | bytes 524288 | tf_op jit(solution)/shard_map/all_to_all | solution.py:46
  20.1 7.8 %all-to-all-done = bf16[16,32,256]{2,1,0:T(8,128)(2,1)S(1)} async-done(((bf16[16,32,256]{2,1,0:T(8,128)(2,1)}), bf16[16,32,256]{2,1,0:T(8,128)(2,1)S(1)}, u32[]{:S(2)}, u32[]{:S(2)}) %all-to-all-start) | async-done | bytes 262176 | tf_op jit(solution)/shard_map/all_to_all | solution.py:46
  28.7 1.1 while.22
  30.2 1.8 while.23
  30.8 0.7 fusion.55
  32.2 39.4 %all-gather.2.cloned.1.call-done = bf16[1024,4096]{1,0:T(8,128)(2,1)} async-done(((bf16[1024,1024]{1,0:T(8,128)(2,1)}), bf16[1024,4096]{1,0:T(8,128)(2,1)}) %all-gather.2.cloned.1.call-update) | async-done | bytes 8388624 | tf_op jit(solution)/shard_map/all_gather | solution.py:122
  71.6 6.0 %fusion.34 = f32[128,4096]{1,0:T(8,128)} fusion(bf16[128,1024]{1,0:T(8,128)(2,1)S(1)} %copy_bitcast_fusion, bf16[1024,4096]{1,0:T(8,128)(2,1)} %all-gather.2.cloned.1.call-done), kind=kOutput, calls=%fused_computation.99 | convolution fusion | flops 1073741824 | bytes 10747904 | tf_op jit(solution)/shard_map/dot_general | solution.py:120
  78.2 3.8 %gather_fusion.4 = s32[512]{0:T(512)S(1)} fusion(s32[128,8]{1,0:T(8,128)S(1)} %sub.46, s32[512]{0:T(512)S(1)} %reshape.269), kind=kCustom, calls=%fused_computation.4 | custom fusion | bytes 8192 | tf_op jit(solution)/shard_map/jit(take_along_axis)/gather | solution.py:109
  82.6 2.4 scatter_custom_fusion
  85.2 36.3 %reduce-scatter.2.cloned.1.call-done = f32[128,1024]{1,0:T(8,128)} async-done(((f32[128,4096]{1,0:T(8,128)}), f32[128,1024]{1,0:T(8,128)}) %reduce-scatter.2.cloned.1.call-update) | async-done | bytes 524304 | tf_op jit(solution)/shard_map/reduce_scatter | solution.py:126
  121.5 1.2 add_convert_fusion.1
  122.7 2.8 gather_fusion.2
  125.8 1.8 broadcast_in_dim.133
  127.6 4.1 %all-to-all-start.1 = ((bf16[16,80,1024]{2,1,0:T(8,128)(2,1)}), bf16[16,80,1024]{2,1,0:T(8,128)(2,1)S(1)}, u32[]{:S(2)}, u32[]{:S(2)}) async-start(bf16[16,80,1024]{2,1,0:T(8,128)(2,1)} %bitcast.94), calls=%async_computation.2 | async-start | bytes 5242880 | tf_op jit(solution)/shard_map/all_to_all | solution.py:132
  131.8 27.4 %reshape.296 = bf16[4,1024,1536,1]{2,1,0,3:T(8,128)(2,1)} reshape(bf16[1,4096,2,768]{3,2,1,0:T(2,128)(2,1)} %param.26) | data formatting | bytes 25165824 | tf_op jit(solution)/shard_map/reshape;squeeze | solution.py:141
  159.1 11.2 %reshape_squeeze.7 = bf16[768,4,1024]{2,1,0:T(4,128)(2,1)} reshape(bf16[1,768,4096]{2,1,0:T(8,128)(2,1)} %param.27) | data formatting | bytes 12582912 | tf_op jit(solution)/shard_map/reshape;squeeze | solution.py:147
  170.4 22.0 %all-to-all-done.1 = bf16[16,80,1024]{2,1,0:T(8,128)(2,1)S(1)} async-done(((bf16[16,80,1024]{2,1,0:T(8,128)(2,1)}), bf16[16,80,1024]{2,1,0:T(8,128)(2,1)S(1)}, u32[]{:S(2)}, u32[]{:S(2)}) %all-to-all-start.1) | async-done | bytes 2621472 | tf_op jit(solution)/shard_map/all_to_all | solution.py:132
  192.4 0.6 fusion.7
  193.1 0.7 fusion.9
  193.7 7.6 %convolution_bitcast_fusion = f32[4,80,1536]{2,1,0:T(8,128)S(1)} fusion(bf16[4,4,80,1024]{3,2,1,0:T(8,128)(2,1)S(1)} %bitcast.98, bf16[4,1024,1536,1]{2,1,0,3:T(8,128)(2,1)} %reshape.296), kind=kOutput, calls=%fused_computation.23 | convolution fusion | flops 4026531840 | bytes 17170432 | tf_op jit(solution)/shard_map/sdcf,dfh->sch/dot_general | solution.py:138
  201.4 4.6 %convert_bitcast_fusion = bf16[4,4,80,1024]{3,2,1,0:T(8,128)(2,1)S(1)} fusion(bf16[768,4,1024]{2,1,0:T(4,128)(2,1)S(1)} %bitcast.96, f32[4,80,1536]{2,1,0:T(8,128)S(1)} %convolution_bitcast_fusion), kind=kOutput, calls=%fused_computation.25 | convolution fusion | flops 2016051200 | bytes 10878976 | tf_op jit(solution)/shard_map/scf,fdo->sdco/dot_general | solution.py:148
  206.3 62.0 %all_to_all.20 = bf16[4,4,80,1024]{3,2,0,1:T(8,128)(2,1)S(1)} all-to-all(bf16[4,4,80,1024]{3,2,0,1:T(8,128)(2,1)S(1)} %copy.127), channel_id=1, replica_groups=mesh['groups'=2,'expert'=4,'donor'=4] {'donor'}, dimensions={1} | all-to-all | bytes 5242880 | tf_op jit(solution)/shard_map/all_to_all | solution.py:151
  268.4 0.6 bitcast_reduce_fusion
  269.0 1.2 copy.128
  270.2 3.8 %all-to-all-start.3 = ((bf16[4,2,80,1024]{3,2,1,0:T(8,128)(2,1)}), bf16[4,2,80,1024]{3,2,1,0:T(8,128)(2,1)S(1)}, u32[]{:S(2)}, u32[]{:S(2)}) async-start(bf16[4,2,80,1024]{3,2,1,0:T(8,128)(2,1)} %copy.128), calls=%async_computation.4 | async-start | bytes 2621440 | tf_op jit(solution)/shard_map/all_to_all | solution.py:155
  274.5 16.5 %all-to-all-done.3 = bf16[4,2,80,1024]{3,2,1,0:T(8,128)(2,1)S(1)} async-done(((bf16[4,2,80,1024]{3,2,1,0:T(8,128)(2,1)}), bf16[4,2,80,1024]{3,2,1,0:T(8,128)(2,1)S(1)}, u32[]{:S(2)}, u32[]{:S(2)}) %all-to-all-start.3) | async-done | bytes 1310752 | tf_op jit(solution)/shard_map/all_to_all | solution.py:155
  290.9 2.0 gather_fusion.3
  293.4 1.6 multiply_reduce_fusion
  295.1 0.8 add_convert_fusion
  (96 shorter events, 8.7 us)
Async XLA Ops:
  7.2 1.9 copy-start
  7.2 10.7 %copy-start.4 = (bf16[128,2,256]{2,1,0:T(2,128)(2,1)S(1)}, bf16[128,2,256]{2,1,0:T(2,128)(2,1)}, u32[]{:S(2)}) copy-start(bf16[128,2,256]{2,1,0:T(2,128)(2,1)} %param.18) | copy-start | bytes 393220
  7.2 10.9 %copy-start.8 = (s32[4]{0:T(128)S(1)}, s32[4]{0:T(128)}, u32[]{:S(2)}) copy-start(s32[4]{0:T(128)} %param.21) | copy-start | bytes 52
  7.2 12.1 %copy-start.3 = (bf16[128,1024]{1,0:T(8,128)(2,1)S(1)}, bf16[128,1024]{1,0:T(8,128)(2,1)}, u32[]{:S(2)}) copy-start(bf16[128,1024]{1,0:T(8,128)(2,1)} %param.17) | copy-start | bytes 786436
  7.2 64.4 %all-gather.2.cloned.1.call-start = ((), (), s32[]{:S(2)}) async-start(), calls=%async_computation.5 | async-start | bytes 10485760 | tf_op jit(solution)/shard_map/all_gather | solution.py:122
  10.4 17.5 %all-to-all-start = ((bf16[16,32,256]{2,1,0:T(8,128)(2,1)}), bf16[16,32,256]{2,1,0:T(8,128)(2,1)S(1)}, u32[]{:S(2)}, u32[]{:S(2)}) async-start(bf16[16,32,256]{2,1,0:T(8,128)(2,1)} %broadcast_select_fusion.1), calls=%async_computation | async-start | bytes 524288 | tf_op jit(solution)/shard_map/all_to_all | solution.py:46
  17.8 103.6 %reduce-scatter.2.cloned.1.call-start = ((), (), s32[]{:S(2)}) async-start(), calls=%async_computation.6 | async-start | bytes 2621440 | tf_op jit(solution)/shard_map/reduce_scatter | solution.py:126
  32.2 45.5 %copy-start.2 = (bf16[128,1024]{1,0:T(8,128)(2,1)}, bf16[128,1024]{1,0:T(8,128)(2,1)S(1)}, u32[]{:S(2)}) copy-start(bf16[128,1024]{1,0:T(8,128)(2,1)S(1)} %copy_bitcast_fusion) | copy-start | bytes 786436
  32.2 45.5 %copy-start.5 = (s32[128,4]{0,1:T(4,128)S(1)}, s32[128,4]{0,1:T(4,128)}, u32[]{:S(2)}) copy-start(s32[128,4]{0,1:T(4,128)} %param.24) | copy-start | bytes 6148
  127.6 4.2 %copy-start.6 = (bf16[4096]{0:T(1024)(128)(2,1)S(1)}, bf16[4096]{0:T(1024)(128)(2,1)}, u32[]{:S(2)}) copy-start(bf16[4096]{0:T(1024)(128)(2,1)} %param.23) | copy-start | bytes 24580
  127.6 64.8 %all-to-all-start.1 = ((bf16[16,80,1024]{2,1,0:T(8,128)(2,1)}), bf16[16,80,1024]{2,1,0:T(8,128)(2,1)S(1)}, u32[]{:S(2)}, u32[]{:S(2)}) async-start(bf16[16,80,1024]{2,1,0:T(8,128)(2,1)} %bitcast.94), calls=%async_computation.2 | async-start | bytes 5242880 | tf_op jit(solution)/shard_map/all_to_all | solution.py:132
  193.0 8.4 %slice-start = ((s8[6291456]{0:T(1024)(128)(4,1)}), s8[4194304]{0:T(1024)(128)(4,1)S(1)}, s32[]{:S(2)}) async-start(s8[6291456]{0:T(1024)(128)(4,1)} %bitcast.95), calls=%async_computation.7 | async-start | bytes 8388608
  193.7 7.7 %slice-start.1 = ((s8[6291456]{0:T(1024)(128)(4,1)}), s8[2097152]{0:T(1024)(128)(4,1)S(1)}, s32[]{:S(2)}) async-start(s8[6291456]{0:T(1024)(128)(4,1)} %bitcast.95), calls=%async_computation.8 | async-start | bytes 4194304
  269.0 5.3 %copy-start.7 = (f32[128,4]{0,1:T(4,128)S(1)}, f32[128,4]{0,1:T(4,128)}, u32[]{:S(2)}) copy-start(f32[128,4]{0,1:T(4,128)} %param.25) | copy-start | bytes 6148
  270.2 20.8 %all-to-all-start.3 = ((bf16[4,2,80,1024]{3,2,1,0:T(8,128)(2,1)}), bf16[4,2,80,1024]{3,2,1,0:T(8,128)(2,1)S(1)}, u32[]{:S(2)}, u32[]{:S(2)}) async-start(bf16[4,2,80,1024]{3,2,1,0:T(8,128)(2,1)} %copy.128), calls=%async_computation.4 | async-start | bytes 2621440 | tf_op jit(solution)/shard_map/all_to_all | solution.py:155
  290.9 4.9 %copy-start.1 = (bf16[4,2,32,256]{3,2,1,0:T(8,128)(2,1)S(1)}, bf16[4,2,32,256]{3,2,1,0:T(8,128)(2,1)}, u32[]{:S(2)}) copy-start(bf16[4,2,32,256]{3,2,1,0:T(8,128)(2,1)} %param.19) | copy-start | bytes 393220
Sparse Core Ops, SparseCore 0:
  9.6 61.9 all-gather.1
  77.8 43.6 reduce-scatter.1
where the time goes:
time: 304 us; the launch traced here: 303 us
  waiting for transfers between devices  123 us (40%)
  blocking collectives  62 us (20%)
  local copies, waits for them, and re-layouts  57.5 us (19%)
  matrix products  20.5 us (7%)
  starting transfers between devices  15.4 us (5%)
  between operations  15.2 us (5%)
  other arithmetic  9.3 us (3%)
    all_to_all x1, blocking collectives, shards(): lax.all_to_all(partial_out.astype(jnp.bfloat16), 'donor', split_axis=1, c...  62 us
    all_gather x1, waiting for transfers between devices, shards(): lax.all_gather(out_weight, 'expert', axis=1, tiled=True)  39.4 us
    reduce_scatter x1, waiting for transfers between devices, shards(): lax.psum_scatter(attn_terms, 'donor', scatter_dimension=1, tiled=True)  36.3 us
    another operation x1, local copies, waits for them, and re-layouts, shards(): w_gate_up[0].reshape(n_donor, columns, 2 * ff_local)  27.4 us
    all_to_all x1, waiting for transfers between devices, shards(): lax.all_to_all(copies, ('expert', 'donor'), split_axis=0, concat_axis=0,...  22 us
    all_to_all x1, waiting for transfers between devices, shards(): lax.all_to_all(expert_sum.astype(jnp.bfloat16), 'expert', split_axis=0, c...  16.5 us
    another operation x1, local copies, waits for them, and re-layouts, shards(): down_local = w_down[0].reshape(ff_local, n_donor, columns)  11.2 us
    all_to_all x1, waiting for transfers between devices, shards(): lax.all_to_all(outgoing, ('expert', 'donor'), split_axis=0, concat_axis=0...  7.81 us
  transfers between devices with their start and end apart: 5, of which 5 were waited for; matrix products, arithmetic and copies ran while one was open for 18% of the time, Pallas kernels for 0%

commit v1 on v0

v1 whole, which is shorter than its diff:
```python
import jax
import jax.numpy as jnp
from jax import lax
from jax.sharding import PartitionSpec as P


def attention(queries, suffix_kv, kv_pool, page_table, prefix_len):
    n_expert = lax.axis_size("expert")
    n_donor = lax.axis_size("donor")
    expert_index = lax.axis_index("expert")
    donor_index = lax.axis_index("donor")
    seq_count, page_count = page_table.shape
    suffix_len = queries.shape[0]
    kv_heads = suffix_kv.shape[1]
    head_dim = suffix_kv.shape[2] // 2
    page_len = kv_pool.shape[2]
    my_group = donor_index * kv_heads // n_donor
    owner_index = expert_index * n_donor + donor_index
    owner_of = page_table // seq_count
    held_slot = jnp.sum(jnp.where(owner_of == owner_index, page_table % seq_count, 0), axis=1)
    dest_group = jnp.arange(n_donor, dtype=jnp.int32) * kv_heads // n_donor
    wanted = (held_slot[:, None] * kv_heads + dest_group[None, :]).reshape(-1)
    outgoing = jnp.take(
        kv_pool.reshape(seq_count * kv_heads, page_len, 2 * head_dim), wanted, axis=0
    )
    arrived = lax.all_to_all(outgoing, ("expert", "donor"), split_axis=0, concat_axis=0, tiled=True)
    my_owners = lax.dynamic_index_in_dim(owner_of, expert_index, 0, keepdims=False)
    ordered = jnp.take(arrived, my_owners, axis=0).reshape(page_count * page_len, 2 * head_dim)
    prefix_keys = ordered[:, :head_dim]
    prefix_vals = ordered[:, head_dim:]
    score_scale = head_dim ** (-0.5)
    query_heads = queries.reshape(suffix_len, -1, head_dim)
    fresh_pair = lax.dynamic_index_in_dim(suffix_kv, my_group, 1, keepdims=False)
    causal = jnp.arange(suffix_len)[:, None] >= jnp.arange(suffix_len)[None, :]
    fresh_scores = (
        jnp.einsum(
            "thc,uc->thu", query_heads, fresh_pair[:, :head_dim], preferred_element_type=jnp.float32
        )
        * score_scale
    )
    fresh_scores = jnp.where(causal[:, None, :], fresh_scores, -jnp.inf)
    prefix_tokens = lax.dynamic_index_in_dim(prefix_len, expert_index, 0, keepdims=False)
    block_keys = min(1024, page_count * page_len)
    live_blocks = (prefix_tokens + block_keys - 1) // block_keys

    def block_scores(block_index):
        keys_block = lax.dynamic_slice_in_dim(prefix_keys, block_index * block_keys, block_keys, 0)
        raw_scores = (
            jnp.einsum("thc,kc->thk", query_heads, keys_block, preferred_element_type=jnp.float32)
            * score_scale
        )
        visible = block_index * block_keys + jnp.arange(block_keys) < prefix_tokens
        return jnp.where(visible[None, None, :], raw_scores, -jnp.inf)

    def raise_max(block_index, running):
        return jnp.maximum(running, jnp.max(block_scores(block_index), axis=2))

    row_max = lax.fori_loop(0, live_blocks, raise_max, jnp.max(fresh_scores, axis=2))

    def add_block(block_index, loop_state):
        row_total, weighted = loop_state
        exp_scores = jnp.exp(block_scores(block_index) - row_max[:, :, None])
        vals_block = lax.dynamic_slice_in_dim(prefix_vals, block_index * block_keys, block_keys, 0)
        weighted = weighted + jnp.einsum(
            "thk,kc->thc",
            exp_scores.astype(jnp.bfloat16),
            vals_block,
            preferred_element_type=jnp.float32,
        )
        return (row_total + jnp.sum(exp_scores, axis=2), weighted)

    fresh_exp = jnp.exp(fresh_scores - row_max[:, :, None])
    start_state = (
        jnp.sum(fresh_exp, axis=2),
        jnp.einsum(
            "thu,uc->thc",
            fresh_exp.astype(jnp.bfloat16),
            fresh_pair[:, head_dim:],
            preferred_element_type=jnp.float32,
        ),
    )
    row_total, weighted = lax.fori_loop(0, live_blocks, add_block, start_state)
    return (weighted / row_total[:, :, None]).astype(jnp.bfloat16).reshape(suffix_len, -1)


def shards(
    hidden_in,
    queries,
    suffix_kv,
    kv_pool,
    page_table,
    prefix_len,
    out_weight,
    norm_gain,
    expert_ids,
    route_probs,
    w_gate_up,
    w_down,
):
    f32, bf16 = jnp.float32, jnp.bfloat16
    n_expert = lax.axis_size("expert")
    n_donor = lax.axis_size("donor")
    expert_index = lax.axis_index("expert")
    z = lax.axis_index("donor")
    n_rows = n_expert // 2
    y = expert_index // 2
    core = expert_index % 2
    swap = [(i, i ^ 1) for i in range(n_expert)]
    ring = [(i, (i + 1) % n_donor) for i in range(n_donor)]

    def turn(step):
        return [(i, (i + 2 * step) % n_expert) for i in range(n_expert)]

    suffix_len, model_width = hidden_in.shape
    experts_all = 2 * n_expert
    ff_local = w_gate_up.shape[3]
    share_count = n_donor // 2
    my_expert = 2 * expert_index + z // share_count
    pair_cols = model_width // n_rows
    part_rows = n_rows * suffix_len // n_donor
    columns = model_width // n_donor

    gates = route_probs / jnp.sum(route_probs, axis=1, keepdims=True)
    hits = expert_ids[:, :, None] == jnp.arange(experts_all, dtype=jnp.int32)
    gate_table = jnp.sum(jnp.where(hits, gates[:, :, None], 0.0), axis=1)
    all_gates = lax.all_gather(gate_table.T, "expert", axis=0)
    my_gates = lax.dynamic_index_in_dim(all_gates, my_expert, 1, keepdims=False)
    my_gates = my_gates.reshape(n_rows, 2, suffix_len)

    def core_gates(which):
        rows = lax.dynamic_index_in_dim(my_gates, which, 1, keepdims=False)
        return rows.reshape(n_donor, part_rows)

    own_gates, other_gates = core_gates(core), core_gates(1 - core)

    other_weight = lax.ppermute(out_weight, "expert", swap)
    first_weight = jnp.where(core == 0, out_weight, other_weight)
    second_weight = jnp.where(core == 0, other_weight, out_weight)

    part_owner = z * part_rows // suffix_len
    hidden_rows = lax.dynamic_slice_in_dim(
        hidden_in, z * part_rows % suffix_len, part_rows, 0
    )

    def hidden_block(row):
        return lax.dynamic_slice_in_dim(hidden_rows, row * pair_cols, pair_cols, 1)

    hidden_part = hidden_block(y)
    for step in range(1, n_rows):
        got = lax.ppermute(hidden_block((y + step) % n_rows), "expert", turn(step))
        hidden_part = jnp.where((y - step) % n_rows == part_owner, got, hidden_part)

    head_out = attention(queries, suffix_kv, kv_pool, page_table, prefix_len)

    heads = jnp.zeros((n_rows, suffix_len, head_out.shape[1]), bf16)
    heads = lax.dynamic_update_index_in_dim(heads, head_out, y, 0)
    for step in range(1, n_rows):
        got = lax.ppermute(head_out, "expert", turn(step))
        heads = lax.dynamic_update_index_in_dim(heads, got, (y - step) % n_rows, 0)
    heads = heads.reshape(n_rows * suffix_len, -1)
    terms = jnp.concatenate(
        [
            jnp.dot(heads, first_weight, preferred_element_type=f32),
            jnp.dot(heads, second_weight, preferred_element_type=f32),
        ],
        axis=1,
    ).reshape(n_donor, part_rows, pair_cols)

    def term_part(index):
        return lax.dynamic_index_in_dim(terms, index % n_donor, 0, keepdims=False)

    total = term_part(z - 1)
    for step in range(1, n_donor):
        got = lax.ppermute(total.astype(bf16), "donor", ring)
        total = got.astype(f32) + term_part(z - 1 - step)
    current = (total + hidden_part.astype(f32)).astype(bf16)

    gain_f = norm_gain.astype(f32)
    gate_up_weight = w_gate_up[0].reshape(model_width, 2 * ff_local)
    resid_parts, own_act, other_act = [], [], []
    pending = []
    for step in range(n_donor):
        following = lax.ppermute(current, "donor", ring) if step < n_donor - 1 else None
        block = jnp.zeros((part_rows, n_rows, pair_cols), bf16)
        if n_rows == 2:
            got = lax.ppermute(current, "expert", turn(1))
            block = jnp.concatenate(
                [jnp.where(y == 0, current, got), jnp.where(y == 0, got, current)], axis=1
            )
        else:
            block = lax.dynamic_update_index_in_dim(block, current, y, 1)
            for hop in range(1, n_rows):
                got = lax.ppermute(current, "expert", turn(hop))
                block = lax.dynamic_update_index_in_dim(block, got, (y - hop) % n_rows, 1)
            block = block.reshape(part_rows, model_width)
        resid_parts.append(lax.dynamic_slice_in_dim(block, z * columns, columns, 1))
        block_f = block.astype(f32)
        inverse = lax.rsqrt(jnp.mean(block_f * block_f, axis=1, keepdims=True) + 1e-06)
        normed = (block_f * inverse * gain_f[None, :]).astype(bf16)
        other = lax.ppermute(normed, "expert", swap)
        pending.append((step, normed, other))
        if len(pending) == max(1, n_donor // 2):
            rows_in = jnp.concatenate([p[1] for p in pending] + [p[2] for p in pending], axis=0)
            row_gates = jnp.concatenate(
                [
                    lax.dynamic_index_in_dim(table, (z - p[0]) % n_donor, 0, keepdims=False)
                    for table in (own_gates, other_gates)
                    for p in pending
                ]
            )
            gate_up = jnp.dot(rows_in, gate_up_weight, preferred_element_type=f32)
            act = jax.nn.silu(gate_up[:, :ff_local]) * gate_up[:, ff_local:]
            act = (act * row_gates[:, None]).astype(bf16)
            act = act.reshape(2, len(pending), part_rows, ff_local)
            own_act.append(act[0])
            other_act.append(act[1])
            pending = []
        current = following

    def absolute(parts):
        stacked = jnp.concatenate(parts, axis=0)
        return jnp.concatenate(
            [
                lax.dynamic_index_in_dim(stacked, (z - part) % n_donor, 0, keepdims=False)
                for part in range(n_donor)
            ],
            axis=0,
        )

    act_rows = jnp.concatenate([absolute(other_act), absolute(own_act)], axis=0)
    half_rows = n_rows * suffix_len
    resid_all = absolute([p[None] for p in resid_parts])
    resid = lax.dynamic_slice_in_dim(resid_all, y * suffix_len, suffix_len, 0)

    total = None
    for step in range(1, n_donor + 1):
        down = lax.dynamic_slice_in_dim(
            w_down[0], (z - step) % n_donor * columns, columns, 1
        )
        mixed = jnp.dot(act_rows, down, preferred_element_type=f32)
        got = lax.ppermute(mixed[:half_rows].astype(bf16), "expert", swap)
        pair_sum = (mixed[half_rows:] + got.astype(f32)).reshape(n_rows, suffix_len, columns)
        part_sum = lax.dynamic_index_in_dim(pair_sum, y, 0, keepdims=False)
        for hop in range(1, n_rows):
            sent = lax.dynamic_index_in_dim(pair_sum, (y + hop) % n_rows, 0, keepdims=False)
            part_sum = part_sum + lax.ppermute(sent.astype(bf16), "expert", turn(hop)).astype(f32)
        if total is not None:
            part_sum = part_sum + lax.ppermute(total.astype(bf16), "donor", ring).astype(f32)
        total = part_sum
    layer_out = (total + resid.astype(f32)).astype(bf16)
    return (layer_out, head_out)


def solution(mesh):
    in_specs = (
        P(("groups", "expert"), None),
        P(("groups", "expert"), "donor"),
        P(("groups", "expert"), None, None),
        P(("groups", "expert", "donor"), None, None, None),
        P("groups", None),
        P("groups"),
        P("donor", "expert"),
        P(),
        P(("groups", "expert"), None),
        P(("groups", "expert"), None),
        P(("expert", "donor"), None, None, None),
        P(("expert", "donor"), None, None),
    )
    out_specs = (P(("groups", "expert"), "donor"), P(("groups", "expert"), "donor"))
    return jax.shard_map(shards, mesh=mesh, in_specs=in_specs, out_specs=out_specs, check_vma=False)
```

time: 304 us -> 173 us (0.57)
  blocking collectives: 62 us -> 5.17 us
  local copies, waits for them, and re-layouts: 57.5 us -> 18.9 us
  waiting for transfers between devices: 123 us -> 93.6 us
  between operations: 15.2 us -> 2.19 us
  other arithmetic: 9.3 us -> 13.4 us
  starting transfers between devices: 15.4 us -> 19.5 us
    ppermute x0 -> x28, waiting for transfers between devices: none -> 87.8 us  [the longest x3 22.9 us: shards(): got = lax.ppermute(total.astype(bf16), 'donor', ring)]
    all_to_all x1 -> x0, blocking collectives: 62 us -> none  [shards(): lax.all_to_all(partial_out.astype(jnp.bfloat16), 'donor', split_axis=1, c...]
    all_to_all x3 -> x1, waiting for transfers between devices: 46.3 us -> 5.84 us  [attention(): lax.all_to_all(outgoing, ('expert', 'donor'), split_axis=0, concat_axis=0...]
    all_gather x1 -> x0, waiting for transfers between devices: 39.4 us -> none  [shards(): lax.all_gather(out_weight, 'expert', axis=1, tiled=True)]
    another operation x2 -> x0, local copies, waits for them, and re-layouts: 38.6 us -> none  [the longest x1 27.4 us: shards(): w_gate_up[0].reshape(n_donor, columns, 2 * ff_local)]
    reduce_scatter x1 -> x0, waiting for transfers between devices: 36.3 us -> none  [shards(): lax.psum_scatter(attn_terms, 'donor', scatter_dimension=1, tiled=True)]
    unnamed x24 -> x31, local copies, waits for them, and re-layouts: 0.24 us -> 13.4 us
    ppermute x0 -> x28, starting transfers between devices: none -> 12.1 us  [the longest x4 2.86 us: shards(): lax.ppermute(sent.astype(bf16), 'expert', turn(hop)).astype(f32)]
  transfers between devices with their start and end apart: 5 -> 29, of which waited for: 5 -> 16; matrix products, arithmetic and copies ran while one was open for 18% -> 21% of each run, Pallas kernels for 0% -> 0%
where the time goes in v1:
time: 173 us; the launch traced here: 172 us
  waiting for transfers between devices  93.6 us (54%)
  starting transfers between devices  19.5 us (11%)
  matrix products  19.3 us (11%)
  local copies, waits for them, and re-layouts  18.9 us (11%)
  other arithmetic  13.4 us (8%)
  blocking collectives  5.17 us (3%)
  between operations  2.19 us (1%)
    ppermute x3, waiting for transfers between devices, shards(): got = lax.ppermute(total.astype(bf16), 'donor', ring)  22.9 us
    ppermute x3, waiting for transfers between devices, shards(): lax.ppermute(current, 'donor', ring)  19.6 us
    ppermute x3, waiting for transfers between devices, shards(): lax.ppermute(total.astype(bf16), 'donor', ring).astype(f32)  16.6 us
    ppermute x4, waiting for transfers between devices, shards(): lax.ppermute(sent.astype(bf16), 'expert', turn(hop)).astype(f32)  13.6 us
    unnamed x31, local copies, waits for them, and re-layouts  13.4 us
    dot_general x2, matrix products, shards(): gate_up = jnp.dot(rows_in, gate_up_weight, preferred_element_type=f32)  10 us
    all_to_all x1, starting transfers between devices, attention(): lax.all_to_all(outgoing, ('expert', 'donor'), split_axis=0, concat_axis=0...  7.39 us
    ppermute x1, waiting for transfers between devices, shards(): got = lax.ppermute(head_out, 'expert', turn(step))  7.11 us
  transfers between devices with their start and end apart: 29, of which 16 were waited for; matrix products, arithmetic and copies ran while one was open for 21% of the time, Pallas kernels for 0%

profile of v1, /device:TPU:0, one launch (start us, length us, event | category | flops | bytes accessed | tf_op | source)
XLA Modules:
  0.0 172.2 jit_solution(6420195562300894088)
XLA Ops:
  3.2 7.4 %all-to-all-start = ((bf16[16,32,256]{2,1,0:T(8,128)(2,1)}), bf16[16,32,256]{2,1,0:T(8,128)(2,1)S(1)}, u32[]{:S(2)}, u32[]{:S(2)}) async-start(bf16[16,32,256]{2,1,0:T(8,128)(2,1)} %broadcast_select_fusion), calls=%async_computation | async-start | bytes 524288 | tf_op jit(solution)/shard_map/all_to_all | solution.py:26
  11.0 1.0 constant_dynamic-slice_fusion.12
  12.1 1.3 dynamic_slice.170
  14.8 5.8 %all-to-all-done = bf16[16,32,256]{2,1,0:T(8,128)(2,1)S(1)} async-done(((bf16[16,32,256]{2,1,0:T(8,128)(2,1)}), bf16[16,32,256]{2,1,0:T(8,128)(2,1)S(1)}, u32[]{:S(2)}, u32[]{:S(2)}) %all-to-all-start) | async-done | bytes 262176 | tf_op jit(solution)/shard_map/all_to_all | solution.py:26
  21.4 1.2 while.22
  23.0 1.8 %while.23 = (s32[]{:T(128)}, f32[128,8]{0,1:T(8,128)S(1)}, f32[128,8,128]{2,0,1:T(8,128)S(1)}, s32[]{:T(128)}, s32[]{:T(128)}, /*index=5*/bf16[128,8,128]{2,0,1:...) while((s32[]{:T(128)}, f32[128,8]{0,1:T(8,128)S(1)}, ...), condition=%wide.region_8.9_spmd, body=%wide.region_6.8_spmd.sunk | while | flops 271188992 | bytes 3691649 | solution.py:82
  26.1 7.1 %collective-permute-done = bf16[128,1024]{1,0:T(8,128)(2,1)S(1)} collective-permute-done((bf16[128,1024]{1,0:T(8,128)(2,1)S(1)}, bf16[128,1024]{1,0:T(8,128)(2,1)S(1)}, u32[]{:S(2)}, u32[]{:S(2)}) %collective-permute-start) | collective-permute-done | bytes 262176 | tf_op jit(solution)/shard_map/ppermute | solution.py:158
  34.0 2.4 %fusion.20 = f32[256,1024]{1,0:T(8,128)S(1)} fusion(bf16[256,1024]{1,0:T(8,128)(2,1)S(1)} %bitcast.246, bf16[1024,1024]{1,0:T(8,128)(2,1)} %collective-permute-done.1, bf16[1024,1024]{1,0:T(8,128)(2,1)S(1)} %copy-done.8, pred[]{:T(512)S(6)} %eq.79), kind=kOutput, calls=%fused_computation.28 | convolution fusion | flops 537919488 | bytes 5767169 | tf_op jit(solution)/shard_map/dot_general | solution.py:164
  37.5 8.1 %collective-permute-done.2 = bf16[64,2048]{1,0:T(8,128)(2,1)} collective-permute-done((bf16[64,2048]{1,0:T(8,128)(2,1)S(1)}, bf16[64,2048]{1,0:T(8,128)(2,1)}, u32[]{:S(2)}, u32[]{:S(2)}) %collective-permute-start.2) | collective-permute-done | bytes 262176 | tf_op jit(solution)/shard_map/ppermute | solution.py:174
  45.6 1.7 fusion.67
  47.4 1.9 %collective-permute-start.5 = (bf16[64,2048]{1,0:T(8,128)(2,1)S(1)}, bf16[64,2048]{1,0:T(8,128)(2,1)}, u32[]{:S(2)}, u32[]{:S(2)}) collective-permute-start(bf16[64,2048]{1,0:T(8,128)(2,1)S(1)} %dynamic_slice.176), channel_id=1, source_target_pairs={{0,8},{4,12},{8,0},{12,4},{1,9},{5,13},{9,1},{13,5},{2,10},{6,14},... | collective-permute-start | bytes 786440 | tf_op jit(solution)/shard_map/ppermute | solution.py:150
  49.3 6.4 %collective-permute-done.3 = bf16[64,2048]{1,0:T(8,128)(2,1)} collective-permute-done((bf16[64,2048]{1,0:T(8,128)(2,1)}, bf16[64,2048]{1,0:T(8,128)(2,1)}, u32[]{:S(2)}, u32[]{:S(2)}) %collective-permute-start.3) | collective-permute-done | bytes 262176 | tf_op jit(solution)/shard_map/ppermute | solution.py:174
  55.7 1.7 fusion.66
  57.5 8.4 %collective-permute-done.4 = bf16[64,2048]{1,0:T(8,128)(2,1)} collective-permute-done((bf16[64,2048]{1,0:T(8,128)(2,1)}, bf16[64,2048]{1,0:T(8,128)(2,1)}, u32[]{:S(2)}, u32[]{:S(2)}) %collective-permute-start.4) | collective-permute-done | bytes 262176 | tf_op jit(solution)/shard_map/ppermute | solution.py:174
  65.9 1.1 fusion.65
  67.1 2.4 %collective-permute-start.6 = (bf16[64,2048]{1,0:T(8,128)(2,1)S(1)}, bf16[64,2048]{1,0:T(8,128)(2,1)S(1)}, u32[]{:S(2)}, u32[]{:S(2)}) collective-permute-start(bf16[64,2048]{1,0:T(8,128)(2,1)S(1)} %fusion.65), channel_id=1, source_target_pairs={{0,8},{4,12},{8,0},{12,4},{1,9},{5,13},{9,1},{13,5},{2,10},{6,14},... | collective-permute-start | bytes 786440 | tf_op jit(solution)/shard_map/ppermute | solution.py:186
  69.6 13.1 %copy.53 = bf16[512,8,2,768]{3,1,2,0:T(8,128)(2,1)} copy(bf16[512,8,2,768]{3,2,1,0:T(2,128)(2,1)} %bitcast.208) | data formatting | bytes 25165824
  82.7 5.2 %all-gather = f32[32,128]{1,0:T(8,128)S(1)} all-gather(f32[8,128]{1,0:T(8,128)S(1)} %bitcast.250), channel_id=2, replica_groups=mesh['groups'=2,'expert'=4,'donor'=4] {'expert'}, dimensions={0}, use_global_device_ids=true | all-gather | bytes 20480 | tf_op jit(solution)/shard_map/all_gather | solution.py:126
  88.6 10.2 %collective-permute-done.11 = bf16[64,2048]{1,0:T(8,128)(2,1)S(1)} collective-permute-done((bf16[64,2048]{1,0:T(8,128)(2,1)S(1)}, bf16[64,2048]{1,0:T(8,128)(2,1)S(1)}, u32[]{:S(2)}, u32[]{:S(2)}) %collective-permute-start.11) | collective-permute-done | bytes 262176 | tf_op jit(solution)/shard_map/ppermute | solution.py:183
  99.1 9.5 %collective-permute-done.13 = bf16[64,2048]{1,0:T(8,128)(2,1)S(1)} collective-permute-done((bf16[64,2048]{1,0:T(8,128)(2,1)S(1)}, bf16[64,2048]{1,0:T(8,128)(2,1)S(1)}, u32[]{:S(2)}, u32[]{:S(2)}) %collective-permute-start.13) | collective-permute-done | bytes 262176 | tf_op jit(solution)/shard_map/ppermute | solution.py:183
  108.9 6.8 %collective-permute-done.14 = bf16[64,2048]{1,0:T(8,128)(2,1)S(1)} collective-permute-done((bf16[64,2048]{1,0:T(8,128)(2,1)S(1)}, bf16[64,2048]{1,0:T(8,128)(2,1)S(1)}, u32[]{:S(2)}, u32[]{:S(2)}) %collective-permute-start.14) | collective-permute-done | bytes 262176 | tf_op jit(solution)/shard_map/ppermute | solution.py:186
  119.3 6.6 %fusion.12 = f32[256,1536]{1,0:T(8,128)S(1)} fusion(bf16[4096,1536]{1,0:T(8,128)(2,1)} %bitcast.209, bf16[64,4096]{1,0:T(8,128)(2,1)S(1)} %collective-permute-done.16, bf16[64,4096]{1,0:T(8,128)(2,1)S(1)} %collective-permute-done.15, bf16[64,4096]{1,0:T(8,128)(2,1)S(1)} %get-tuple-element.194, bf16[64,4096]{1,0:T(8,128)(2,1)S(1)} %get-tuple-element.192), kind=kOutput, calls=%fused_computation.20 | convolution fusion | flops 3229614080 | bytes 16252928 | tf_op jit(solution)/shard_map/dot_general | solution.py:211
  126.4 3.4 %fusion.4 = f32[256,1536]{1,0:T(8,128)S(1)} fusion(bf16[4096,1536]{1,0:T(8,128)(2,1)S(1)} %bitcast.212, bf16[64,4096]{1,0:T(8,128)(2,1)S(1)} %collective-permute-done.10, bf16[64,4096]{1,0:T(8,128)(2,1)S(1)} %collective-permute-done.9, bf16[64,4096]{1,0:T(8,128)(2,1)S(1)} %get-tuple-element.193, bf16[64,4096]{1,0:T(8,128)(2,1)S(1)} %get-tuple-element.195), kind=kOutput, calls=%fused_computation.12 | convolution fusion | flops 3229614080 | bytes 16252928 | tf_op jit(solution)/shard_map/dot_general | solution.py:211
  130.6 1.0 fusion.32
  137.0 1.8 %collective-permute-start.22 = (bf16[128,1024]{1,0:T(8,128)(2,1)S(1)}, bf16[128,1024]{1,0:T(8,128)(2,1)S(1)}, u32[]{:S(2)}, u32[]{:S(2)}) collective-permute-start(bf16[128,1024]{1,0:T(8,128)(2,1)S(1)} %fusion.75), channel_id=1, source_target_pairs={{0,8},{4,12},{8,0},{12,4},{1,9},{5,13},{9,1},{13,5},{2,10},{6,14},... | collective-permute-start | bytes 786440 | tf_op jit(solution)/shard_map/ppermute | solution.py:246
  138.8 6.8 %collective-permute-done.24 = bf16[128,1024]{1,0:T(8,128)(2,1)S(1)} collective-permute-done((bf16[128,1024]{1,0:T(8,128)(2,1)S(1)}, bf16[128,1024]{1,0:T(8,128)(2,1)S(1)}, u32[]{:S(2)}, u32[]{:S(2)}) %collective-permute-start.24) | collective-permute-done | bytes 262176 | tf_op jit(solution)/shard_map/ppermute | solution.py:246
  146.4 4.9 %collective-permute-done.22 = bf16[128,1024]{1,0:T(8,128)(2,1)S(1)} collective-permute-done((bf16[128,1024]{1,0:T(8,128)(2,1)S(1)}, bf16[128,1024]{1,0:T(8,128)(2,1)S(1)}, u32[]{:S(2)}, u32[]{:S(2)}) %collective-permute-start.22) | collective-permute-done | bytes 262176 | tf_op jit(solution)/shard_map/ppermute | solution.py:246
  151.3 3.0 %collective-permute-done.25 = bf16[128,1024]{1,0:T(8,128)(2,1)S(1)} collective-permute-done((bf16[128,1024]{1,0:T(8,128)(2,1)S(1)}, bf16[128,1024]{1,0:T(8,128)(2,1)S(1)}, u32[]{:S(2)}, u32[]{:S(2)}) %collective-permute-start.25) | collective-permute-done | bytes 262176 | tf_op jit(solution)/shard_map/ppermute | solution.py:248
  155.0 1.9 %collective-permute-done.20 = bf16[128,1024]{1,0:T(8,128)(2,1)S(1)} collective-permute-done((bf16[128,1024]{1,0:T(8,128)(2,1)S(1)}, bf16[128,1024]{1,0:T(8,128)(2,1)S(1)}, u32[]{:S(2)}, u32[]{:S(2)}) %collective-permute-start.20) | collective-permute-done | bytes 262176 | tf_op jit(solution)/shard_map/ppermute | solution.py:246
  156.9 5.7 %collective-permute-done.26 = bf16[128,1024]{1,0:T(8,128)(2,1)S(1)} collective-permute-done((bf16[128,1024]{1,0:T(8,128)(2,1)S(1)}, bf16[128,1024]{1,0:T(8,128)(2,1)S(1)}, u32[]{:S(2)}, u32[]{:S(2)}) %collective-permute-start.26) | collective-permute-done | bytes 262176 | tf_op jit(solution)/shard_map/ppermute | solution.py:248
  163.0 7.9 %collective-permute-done.27 = bf16[128,1024]{1,0:T(8,128)(2,1)S(1)} collective-permute-done((bf16[128,1024]{1,0:T(8,128)(2,1)S(1)}, bf16[128,1024]{1,0:T(8,128)(2,1)S(1)}, u32[]{:S(2)}, u32[]{:S(2)}) %collective-permute-start.27) | collective-permute-done | bytes 262176 | tf_op jit(solution)/shard_map/ppermute | solution.py:248
  170.9 1.2 fusion.63
  (173 shorter events, 24.2 us)
Async XLA Ops:
  3.2 17.5 %all-to-all-start = ((bf16[16,32,256]{2,1,0:T(8,128)(2,1)}), bf16[16,32,256]{2,1,0:T(8,128)(2,1)S(1)}, u32[]{:S(2)}, u32[]{:S(2)}) async-start(bf16[16,32,256]{2,1,0:T(8,128)(2,1)} %broadcast_select_fusion), calls=%async_computation | async-start | bytes 524288 | tf_op jit(solution)/shard_map/all_to_all | solution.py:26
  10.6 22.6 %collective-permute-start.1 = (bf16[1024,1024]{1,0:T(8,128)(2,1)}, bf16[1024,1024]{1,0:T(8,128)(2,1)}, u32[]{:S(2)}, u32[]{:S(2)}) collective-permute-start(bf16[1024,1024]{1,0:T(8,128)(2,1)} %param.22), channel_id=1, source_target_pairs={{0,4},{4,0},{8,12},{12,8},{1,5},{5,1},{9,13},{13,9},{2,6},{6,2},{1... | collective-permute-start | bytes 6291464 | tf_op jit(solution)/shard_map/ppermute | solution.py:136
  25.2 8.0 %collective-permute-start = (bf16[128,1024]{1,0:T(8,128)(2,1)S(1)}, bf16[128,1024]{1,0:T(8,128)(2,1)S(1)}, u32[]{:S(2)}, u32[]{:S(2)}) collective-permute-start(bf16[128,1024]{1,0:T(8,128)(2,1)S(1)} %copy.48), channel_id=1, source_target_pairs={{0,8},{4,12},{8,0},{12,4},{1,9},{5,13},{9,1},{13,5},{2,10},{6,14},... | collective-permute-start | bytes 786440 | tf_op jit(solution)/shard_map/ppermute | solution.py:158
  36.5 20.9 %copy-start.6 = (f32[128,4]{0,1:T(4,128)S(1)}, f32[128,4]{0,1:T(4,128)}, u32[]{:S(2)}) copy-start(f32[128,4]{0,1:T(4,128)} %param.25) | copy-start | bytes 6148
  36.6 9.0 %collective-permute-start.2 = (bf16[64,2048]{1,0:T(8,128)(2,1)S(1)}, bf16[64,2048]{1,0:T(8,128)(2,1)}, u32[]{:S(2)}, u32[]{:S(2)}) collective-permute-start(bf16[64,2048]{1,0:T(8,128)(2,1)S(1)} %fusion.72), channel_id=1, source_target_pairs={{0,1},{1,2},{2,3},{3,0},{4,5},{5,6},{6,7},{7,4},{8,9},{9,10},{10,1... | collective-permute-start | bytes 786440 | tf_op jit(solution)/shard_map/ppermute | solution.py:174
  37.5 32.0 %copy-start.7 = (s32[128,4]{0,1:T(4,128)S(1)}, s32[128,4]{0,1:T(4,128)}, u32[]{:S(2)}) copy-start(s32[128,4]{0,1:T(4,128)} %param.24) | copy-start | bytes 6148
  37.5 32.1 %copy-start.5 = (bf16[4096]{0:T(1024)(128)(2,1)S(1)}, bf16[4096]{0:T(1024)(128)(2,1)}, u32[]{:S(2)}) copy-start(bf16[4096]{0:T(1024)(128)(2,1)} %param.23) | copy-start | bytes 24580
  47.3 8.5 %collective-permute-start.3 = (bf16[64,2048]{1,0:T(8,128)(2,1)}, bf16[64,2048]{1,0:T(8,128)(2,1)}, u32[]{:S(2)}, u32[]{:S(2)}) collective-permute-start(bf16[64,2048]{1,0:T(8,128)(2,1)} %fusion.67), channel_id=1, source_target_pairs={{0,1},{1,2},{2,3},{3,0},{4,5},{5,6},{6,7},{7,4},{8,9},{9,10},{10,1... | collective-permute-start | bytes 786440 | tf_op jit(solution)/shard_map/ppermute | solution.py:174
  47.4 10.1 %collective-permute-start.5 = (bf16[64,2048]{1,0:T(8,128)(2,1)S(1)}, bf16[64,2048]{1,0:T(8,128)(2,1)}, u32[]{:S(2)}, u32[]{:S(2)}) collective-permute-start(bf16[64,2048]{1,0:T(8,128)(2,1)S(1)} %dynamic_slice.176), channel_id=1, source_target_pairs={{0,8},{4,12},{8,0},{12,4},{1,9},{5,13},{9,1},{13,5},{2,10},{6,14},... | collective-permute-start | bytes 786440 | tf_op jit(solution)/shard_map/ppermute | solution.py:150
  57.4 8.5 %collective-permute-start.4 = (bf16[64,2048]{1,0:T(8,128)(2,1)}, bf16[64,2048]{1,0:T(8,128)(2,1)}, u32[]{:S(2)}, u32[]{:S(2)}) collective-permute-start(bf16[64,2048]{1,0:T(8,128)(2,1)} %fusion.66), channel_id=1, source_target_pairs={{0,1},{1,2},{2,3},{3,0},{4,5},{5,6},{6,7},{7,4},{8,9},{9,10},{10,1... | collective-permute-start | bytes 786440 | tf_op jit(solution)/shard_map/ppermute | solution.py:174
  67.1 21.2 %collective-permute-start.6 = (bf16[64,2048]{1,0:T(8,128)(2,1)S(1)}, bf16[64,2048]{1,0:T(8,128)(2,1)S(1)}, u32[]{:S(2)}, u32[]{:S(2)}) collective-permute-start(bf16[64,2048]{1,0:T(8,128)(2,1)S(1)} %fusion.65), channel_id=1, source_target_pairs={{0,8},{4,12},{8,0},{12,4},{1,9},{5,13},{9,1},{13,5},{2,10},{6,14},... | collective-permute-start | bytes 786440 | tf_op jit(solution)/shard_map/ppermute | solution.py:186
  69.5 18.6 %collective-permute-start.7 = (bf16[64,2048]{1,0:T(8,128)(2,1)S(1)}, bf16[64,2048]{1,0:T(8,128)(2,1)S(1)}, u32[]{:S(2)}, u32[]{:S(2)}) collective-permute-start(bf16[64,2048]{1,0:T(8,128)(2,1)S(1)} %fusion.65), channel_id=1, source_target_pairs={{0,1},{1,2},{2,3},{3,0},{4,5},{5,6},{6,7},{7,4},{8,9},{9,10},{10,1... | collective-permute-start | bytes 786440 | tf_op jit(solution)/shard_map/ppermute | solution.py:183
  88.1 10.6 %collective-permute-start.11 = (bf16[64,2048]{1,0:T(8,128)(2,1)S(1)}, bf16[64,2048]{1,0:T(8,128)(2,1)S(1)}, u32[]{:S(2)}, u32[]{:S(2)}) collective-permute-start(bf16[64,2048]{1,0:T(8,128)(2,1)S(1)} %collective-permute-done.7), channel_id=1, source_target_pairs={{0,1},{1,2},{2,3},{3,0},{4,5},{5,6},{6,7},{7,4},{8,9},{9,10},{10,1... | collective-permute-start | bytes 786440 | tf_op jit(solution)/shard_map/ppermute | solution.py:183
  88.1 10.7 %collective-permute-start.8 = (bf16[64,2048]{1,0:T(8,128)(2,1)S(1)}, bf16[64,2048]{1,0:T(8,128)(2,1)S(1)}, u32[]{:S(2)}, u32[]{:S(2)}) collective-permute-start(bf16[64,2048]{1,0:T(8,128)(2,1)S(1)} %collective-permute-done.7), channel_id=1, source_target_pairs={{0,8},{4,12},{8,0},{12,4},{1,9},{5,13},{9,1},{13,5},{2,10},{6,14},... | collective-permute-start | bytes 786440 | tf_op jit(solution)/shard_map/ppermute | solution.py:186
  98.7 9.8 %collective-permute-start.13 = (bf16[64,2048]{1,0:T(8,128)(2,1)S(1)}, bf16[64,2048]{1,0:T(8,128)(2,1)S(1)}, u32[]{:S(2)}, u32[]{:S(2)}) collective-permute-start(bf16[64,2048]{1,0:T(8,128)(2,1)S(1)} %collective-permute-done.11), channel_id=1, source_target_pairs={{0,1},{1,2},{2,3},{3,0},{4,5},{5,6},{6,7},{7,4},{8,9},{9,10},{10,1... | collective-permute-start | bytes 786440 | tf_op jit(solution)/shard_map/ppermute | solution.py:183
  98.7 9.9 %collective-permute-start.12 = (bf16[64,2048]{1,0:T(8,128)(2,1)S(1)}, bf16[64,2048]{1,0:T(8,128)(2,1)S(1)}, u32[]{:S(2)}, u32[]{:S(2)}) collective-permute-start(bf16[64,2048]{1,0:T(8,128)(2,1)S(1)} %collective-permute-done.11), channel_id=1, source_target_pairs={{0,8},{4,12},{8,0},{12,4},{1,9},{5,13},{9,1},{13,5},{2,10},{6,14},... | collective-permute-start | bytes 786440 | tf_op jit(solution)/shard_map/ppermute | solution.py:186
  108.5 7.1 %collective-permute-start.14 = (bf16[64,2048]{1,0:T(8,128)(2,1)S(1)}, bf16[64,2048]{1,0:T(8,128)(2,1)S(1)}, u32[]{:S(2)}, u32[]{:S(2)}) collective-permute-start(bf16[64,2048]{1,0:T(8,128)(2,1)S(1)} %collective-permute-done.13), channel_id=1, source_target_pairs={{0,8},{4,12},{8,0},{12,4},{1,9},{5,13},{9,1},{13,5},{2,10},{6,14},... | collective-permute-start | bytes 786440 | tf_op jit(solution)/shard_map/ppermute | solution.py:186
  116.6 2.0 %collective-permute-start.15 = (bf16[64,4096]{1,0:T(8,128)(2,1)S(1)}, bf16[64,4096]{1,0:T(8,128)(2,1)S(1)}, u32[]{:S(2)}, u32[]{:S(2)}) collective-permute-start(bf16[64,4096]{1,0:T(8,128)(2,1)S(1)} %get-tuple-element.192), channel_id=1, source_target_pairs={{0,4},{4,0},{8,12},{12,8},{1,5},{5,1},{9,13},{13,9},{2,6},{6,2},{1... | collective-permute-start | bytes 1572872 | tf_op jit(solution)/shard_map/ppermute | solution.py:200
  116.7 2.6 %collective-permute-start.16 = (bf16[64,4096]{1,0:T(8,128)(2,1)S(1)}, bf16[64,4096]{1,0:T(8,128)(2,1)S(1)}, u32[]{:S(2)}, u32[]{:S(2)}) collective-permute-start(bf16[64,4096]{1,0:T(8,128)(2,1)S(1)} %get-tuple-element.194), channel_id=1, source_target_pairs={{0,4},{4,0},{8,12},{12,8},{1,5},{5,1},{9,13},{13,9},{2,6},{6,2},{1... | collective-permute-start | bytes 1572872 | tf_op jit(solution)/shard_map/ppermute | solution.py:200
  117.6 8.7 %collective-permute-start.10 = (bf16[64,4096]{1,0:T(8,128)(2,1)S(1)}, bf16[64,4096]{1,0:T(8,128)(2,1)S(1)}, u32[]{:S(2)}, u32[]{:S(2)}) collective-permute-start(bf16[64,4096]{1,0:T(8,128)(2,1)S(1)} %get-tuple-element.193), channel_id=1, source_target_pairs={{0,4},{4,0},{8,12},{12,8},{1,5},{5,1},{9,13},{13,9},{2,6},{6,2},{1... | collective-permute-start | bytes 1572872 | tf_op jit(solution)/shard_map/ppermute | solution.py:200
  117.7 8.6 %collective-permute-start.9 = (bf16[64,4096]{1,0:T(8,128)(2,1)S(1)}, bf16[64,4096]{1,0:T(8,128)(2,1)S(1)}, u32[]{:S(2)}, u32[]{:S(2)}) collective-permute-start(bf16[64,4096]{1,0:T(8,128)(2,1)S(1)} %get-tuple-element.195), channel_id=1, source_target_pairs={{0,4},{4,0},{8,12},{12,8},{1,5},{5,1},{9,13},{13,9},{2,6},{6,2},{1... | collective-permute-start | bytes 1572872 | tf_op jit(solution)/shard_map/ppermute | solution.py:200
  131.7 22.8 %collective-permute-start.17 = (bf16[256,1024]{1,0:T(8,128)(2,1)S(1)}, bf16[256,1024]{1,0:T(8,128)(2,1)S(1)}, u32[]{:S(2)}, u32[]{:S(2)}) collective-permute-start(bf16[256,1024]{1,0:T(8,128)(2,1)S(1)} %slice.139), channel_id=1, source_target_pairs={{0,4},{4,0},{8,12},{12,8},{1,5},{5,1},{9,13},{13,9},{2,6},{6,2},{1... | collective-permute-start | bytes 1572872 | tf_op jit(solution)/shard_map/ppermute | solution.py:241
  133.0 3.3 %collective-permute-start.23 = (bf16[256,1024]{1,0:T(8,128)(2,1)S(1)}, bf16[256,1024]{1,0:T(8,128)(2,1)S(1)}, u32[]{:S(2)}, u32[]{:S(2)}) collective-permute-start(bf16[256,1024]{1,0:T(8,128)(2,1)S(1)} %slice.136), channel_id=1, source_target_pairs={{0,4},{4,0},{8,12},{12,8},{1,5},{5,1},{9,13},{13,9},{2,6},{6,2},{1... | collective-permute-start | bytes 1572872 | tf_op jit(solution)/shard_map/ppermute | solution.py:241
  134.5 2.3 %collective-permute-start.21 = (bf16[256,1024]{1,0:T(8,128)(2,1)S(1)}, bf16[256,1024]{1,0:T(8,128)(2,1)S(1)}, u32[]{:S(2)}, u32[]{:S(2)}) collective-permute-start(bf16[256,1024]{1,0:T(8,128)(2,1)S(1)} %slice.137), channel_id=1, source_target_pairs={{0,4},{4,0},{8,12},{12,8},{1,5},{5,1},{9,13},{13,9},{2,6},{6,2},{1... | collective-permute-start | bytes 1572872 | tf_op jit(solution)/shard_map/ppermute | solution.py:241
  135.8 10.0 %collective-permute-start.19 = (bf16[256,1024]{1,0:T(8,128)(2,1)S(1)}, bf16[256,1024]{1,0:T(8,128)(2,1)S(1)}, u32[]{:S(2)}, u32[]{:S(2)}) collective-permute-start(bf16[256,1024]{1,0:T(8,128)(2,1)S(1)} %slice.138), channel_id=1, source_target_pairs={{0,4},{4,0},{8,12},{12,8},{1,5},{5,1},{9,13},{13,9},{2,6},{6,2},{1... | collective-permute-start | bytes 1572872 | tf_op jit(solution)/shard_map/ppermute | solution.py:241
  136.5 9.2 %collective-permute-start.24 = (bf16[128,1024]{1,0:T(8,128)(2,1)S(1)}, bf16[128,1024]{1,0:T(8,128)(2,1)S(1)}, u32[]{:S(2)}, u32[]{:S(2)}) collective-permute-start(bf16[128,1024]{1,0:T(8,128)(2,1)S(1)} %fusion.76), channel_id=1, source_target_pairs={{0,8},{4,12},{8,0},{12,4},{1,9},{5,13},{9,1},{13,5},{2,10},{6,14},... | collective-permute-start | bytes 786440 | tf_op jit(solution)/shard_map/ppermute | solution.py:246
  137.0 14.3 %collective-permute-start.22 = (bf16[128,1024]{1,0:T(8,128)(2,1)S(1)}, bf16[128,1024]{1,0:T(8,128)(2,1)S(1)}, u32[]{:S(2)}, u32[]{:S(2)}) collective-permute-start(bf16[128,1024]{1,0:T(8,128)(2,1)S(1)} %fusion.75), channel_id=1, source_target_pairs={{0,8},{4,12},{8,0},{12,4},{1,9},{5,13},{9,1},{13,5},{2,10},{6,14},... | collective-permute-start | bytes 786440 | tf_op jit(solution)/shard_map/ppermute | solution.py:246
  145.7 8.5 %collective-permute-start.25 = (bf16[128,1024]{1,0:T(8,128)(2,1)S(1)}, bf16[128,1024]{1,0:T(8,128)(2,1)S(1)}, u32[]{:S(2)}, u32[]{:S(2)}) collective-permute-start(bf16[128,1024]{1,0:T(8,128)(2,1)S(1)} %fusion.56), channel_id=1, source_target_pairs={{0,1},{1,2},{2,3},{3,0},{4,5},{5,6},{6,7},{7,4},{8,9},{9,10},{10,1... | collective-permute-start | bytes 786440 | tf_op jit(solution)/shard_map/ppermute | solution.py:248
  146.1 10.9 %collective-permute-start.20 = (bf16[128,1024]{1,0:T(8,128)(2,1)S(1)}, bf16[128,1024]{1,0:T(8,128)(2,1)S(1)}, u32[]{:S(2)}, u32[]{:S(2)}) collective-permute-start(bf16[128,1024]{1,0:T(8,128)(2,1)S(1)} %fusion.74), channel_id=1, source_target_pairs={{0,8},{4,12},{8,0},{12,4},{1,9},{5,13},{9,1},{13,5},{2,10},{6,14},... | collective-permute-start | bytes 786440 | tf_op jit(solution)/shard_map/ppermute | solution.py:246
  154.4 8.2 %collective-permute-start.26 = (bf16[128,1024]{1,0:T(8,128)(2,1)S(1)}, bf16[128,1024]{1,0:T(8,128)(2,1)S(1)}, u32[]{:S(2)}, u32[]{:S(2)}) collective-permute-start(bf16[128,1024]{1,0:T(8,128)(2,1)S(1)} %fusion.58), channel_id=1, source_target_pairs={{0,1},{1,2},{2,3},{3,0},{4,5},{5,6},{6,7},{7,4},{8,9},{9,10},{10,1... | collective-permute-start | bytes 786440 | tf_op jit(solution)/shard_map/ppermute | solution.py:248
  154.7 8.3 %collective-permute-start.18 = (bf16[128,1024]{1,0:T(8,128)(2,1)S(1)}, bf16[128,1024]{1,0:T(8,128)(2,1)S(1)}, u32[]{:S(2)}, u32[]{:S(2)}) collective-permute-start(bf16[128,1024]{1,0:T(8,128)(2,1)S(1)} %fusion.73), channel_id=1, source_target_pairs={{0,8},{4,12},{8,0},{12,4},{1,9},{5,13},{9,1},{13,5},{2,10},{6,14},... | collective-permute-start | bytes 786440 | tf_op jit(solution)/shard_map/ppermute | solution.py:246
  162.7 8.2 %collective-permute-start.27 = (bf16[128,1024]{1,0:T(8,128)(2,1)S(1)}, bf16[128,1024]{1,0:T(8,128)(2,1)S(1)}, u32[]{:S(2)}, u32[]{:S(2)}) collective-permute-start(bf16[128,1024]{1,0:T(8,128)(2,1)S(1)} %fusion.60), channel_id=1, source_target_pairs={{0,1},{1,2},{2,3},{3,0},{4,5},{5,6},{6,7},{7,4},{8,9},{9,10},{10,1... | collective-permute-start | bytes 786440 | tf_op jit(solution)/shard_map/ppermute | solution.py:248
  (11 other events, 83.6 us)

commit v2 on v1

v2 whole, which is shorter than its diff:
```python
import jax
import jax.numpy as jnp
from jax import lax
from jax.sharding import PartitionSpec as P


def rotation(count, step):
    return [(i, (i + step) % count) for i in range(count)]


def pick(array, index, axis=0):
    return lax.dynamic_index_in_dim(array, index, axis, keepdims=False)


def fetch_pages(kv_pool, page_table, expert_index, z):
    n_expert = lax.axis_size("expert")
    n_donor = lax.axis_size("donor")
    seq_count = page_table.shape[0]
    kv_heads = kv_pool.shape[1]
    owner_of = page_table // seq_count
    mine = expert_index * n_donor + z
    held_slot = jnp.sum(jnp.where(owner_of == mine, page_table % seq_count, 0), axis=1)
    pages = []
    for step in range(n_expert):
        page = pick(kv_pool, pick(held_slot, (expert_index + step) % n_expert))
        pages.append(lax.ppermute(page, "expert", rotation(n_expert, step)) if step else page)
    column = jnp.stack(pages, axis=0)
    arrived = []
    for step in range(n_donor):
        group = (z + step) % n_donor * kv_heads // n_donor
        block = pick(column, group, 1)
        arrived.append(lax.ppermute(block, "donor", rotation(n_donor, step)) if step else block)
    owners = (
        (z - jnp.arange(n_donor))[:, None] % n_donor
        + (expert_index - jnp.arange(n_expert))[None, :] % n_expert * n_donor
    ).reshape(-1)
    my_owner_of = pick(owner_of, expert_index)
    places = jnp.sum(
        jnp.where(owners[:, None] == my_owner_of[None, :], jnp.arange(my_owner_of.shape[0]), 0),
        axis=1,
    )
    return jnp.concatenate(arrived, axis=0), places


def attention(queries, suffix_kv, pages, places, prefix_tokens, my_group):
    suffix_len = queries.shape[0]
    head_dim = suffix_kv.shape[2] // 2
    page_len = pages.shape[1]
    score_scale = head_dim ** (-0.5)
    query_rows = queries.reshape(suffix_len, -1, head_dim)
    fresh_pair = pick(suffix_kv, my_group, 1)
    flat = pages.reshape(-1, 2 * head_dim)
    visible = (places[:, None] * page_len + jnp.arange(page_len) < prefix_tokens).reshape(-1)
    causal = jnp.arange(suffix_len)[:, None] >= jnp.arange(suffix_len)[None, :]

    def scores(keys, seen):
        raw = jnp.einsum("thc,kc->thk", query_rows, keys, preferred_element_type=jnp.float32)
        return jnp.where(seen, raw * score_scale, -jnp.inf)

    fresh_scores = scores(fresh_pair[:, :head_dim], causal[:, None, :])
    page_scores = scores(flat[:, :head_dim], visible[None, None, :])
    row_top = jnp.maximum(
        jnp.max(fresh_scores, axis=2, keepdims=True), jnp.max(page_scores, axis=2, keepdims=True)
    )
    fresh_exp = jnp.exp(fresh_scores - row_top)
    page_exp = jnp.exp(page_scores - row_top)
    row_total = jnp.sum(fresh_exp, axis=2) + jnp.sum(page_exp, axis=2)

    def mix(exps, vals):
        return jnp.einsum(
            "thk,kc->thc", exps.astype(jnp.bfloat16), vals, preferred_element_type=jnp.float32
        )

    weighted = mix(fresh_exp, fresh_pair[:, head_dim:]) + mix(page_exp, flat[:, head_dim:])
    return (weighted / row_total[:, :, None]).astype(jnp.bfloat16).reshape(suffix_len, -1)


def shards(
    hidden_in,
    queries,
    suffix_kv,
    kv_pool,
    page_table,
    prefix_len,
    out_weight,
    norm_gain,
    expert_ids,
    route_probs,
    w_gate_up,
    w_down,
):
    f32, bf16 = jnp.float32, jnp.bfloat16
    n_expert = lax.axis_size("expert")
    n_donor = lax.axis_size("donor")
    expert_index = lax.axis_index("expert")
    z = lax.axis_index("donor")
    n_rows = n_expert // 2
    y = expert_index // 2
    core = expert_index % 2
    swap = [(i, i ^ 1) for i in range(n_expert)]
    ring = rotation(n_donor, 1)

    def turn(step):
        return rotation(n_expert, 2 * step)

    suffix_len, model_width = hidden_in.shape
    experts_all = 2 * n_expert
    ff_local = w_gate_up.shape[3]
    share_count = n_donor // 2
    my_expert = 2 * expert_index + z // share_count
    pair_cols = model_width // n_rows
    part_rows = n_rows * suffix_len // n_donor
    parts_per_seq = suffix_len // part_rows
    columns = model_width // n_donor
    streams = 2 if n_rows <= 2 else 1
    sub_rows = part_rows // streams
    sub_cols = columns // streams
    pieces = 4
    depth = model_width // pieces

    def weight_piece(index):
        piece = w_gate_up[0, index * depth : (index + 1) * depth]
        return piece.reshape(depth, 2 * ff_local)

    pages, places = fetch_pages(kv_pool, page_table, expert_index, z)

    gates = route_probs / jnp.sum(route_probs, axis=1, keepdims=True)
    hits = expert_ids[:, :, None] == jnp.arange(experts_all, dtype=jnp.int32)
    gate_table = jnp.sum(jnp.where(hits, gates[:, :, None], 0.0), axis=1).T
    tables = [gate_table] + [
        lax.ppermute(gate_table, "expert", rotation(n_expert, step)) for step in range(1, n_expert)
    ]
    all_gates = jnp.stack([pick(table, my_expert) for table in tables], axis=0)

    def core_gates(which):
        rows = [pick(all_gates, (expert_index - 2 * r - which) % n_expert) for r in range(n_rows)]
        return jnp.concatenate(rows).reshape(n_donor, part_rows)

    own_gates, other_gates = core_gates(core), core_gates(1 - core)

    other_weight = lax.ppermute(out_weight, "expert", swap)
    pair_weight = jnp.where(
        core == 0,
        jnp.concatenate([out_weight, other_weight], axis=1),
        jnp.concatenate([other_weight, out_weight], axis=1),
    )

    part_owner = z * part_rows // suffix_len
    hidden_rows = lax.dynamic_slice_in_dim(hidden_in, z * part_rows % suffix_len, part_rows, 0)

    def hidden_block(row):
        return lax.dynamic_slice_in_dim(hidden_rows, row * pair_cols, pair_cols, 1)

    hidden_part = hidden_block(y)
    for step in range(1, n_rows):
        got = lax.ppermute(hidden_block((y + step) % n_rows), "expert", turn(step))
        hidden_part = jnp.where((y - step) % n_rows == part_owner, got, hidden_part)

    weights = [weight_piece(index) for index in range(pieces)]
    pages, pair_weight, hidden_part, weights[0], weights[1] = lax.optimization_barrier(
        (pages, pair_weight, hidden_part, weights[0], weights[1])
    )
    head_out = attention(
        queries,
        suffix_kv,
        pages,
        places,
        pick(prefix_len, expert_index),
        z * suffix_kv.shape[1] // n_donor,
    )

    heads = jnp.zeros((n_rows, suffix_len, head_out.shape[1]), bf16)
    heads = lax.dynamic_update_index_in_dim(heads, head_out, y, 0)
    for step in range(1, n_rows):
        got = lax.ppermute(head_out, "expert", turn(step))
        if step == 1:
            got, weights[2] = lax.optimization_barrier((got, weights[2]))
        heads = lax.dynamic_update_index_in_dim(heads, got, (y - step) % n_rows, 0)
    heads = heads.reshape(n_donor, part_rows, -1)
    heads = jnp.concatenate([pick(heads, (z - 1 - step) % n_donor) for step in range(n_donor)])
    terms = jnp.dot(heads, pair_weight, preferred_element_type=f32)
    terms = terms.reshape(n_donor, streams, sub_rows, pair_cols)

    totals = [terms[0, stream] for stream in range(streams)]
    for step in range(1, n_donor):
        for stream in range(streams):
            got = lax.ppermute(totals[stream].astype(bf16), "donor", ring)
            if step == 1 and stream == 0:
                got, weights[3] = lax.optimization_barrier((got, weights[3]))
            totals[stream] = got.astype(f32) + terms[step, stream]
    hidden_part = hidden_part.reshape(streams, sub_rows, pair_cols)
    current = [
        (totals[stream] + hidden_part[stream].astype(f32)).astype(bf16)
        for stream in range(streams)
    ]

    gain_f = norm_gain.astype(f32)
    resid_parts, own_act, other_act = [], [], []
    batch = max(1, n_donor // 2)
    own_rows, other_rows, row_gates = [], [], []
    for step in range(n_donor):
        following = []
        part = (z - step) % n_donor
        for stream in range(streams):
            if step < n_donor - 1:
                following.append(lax.ppermute(current[stream], "donor", ring))
        for stream in range(streams):
            chunk = current[stream]
            gots = [lax.ppermute(chunk, "expert", turn(hop)) for hop in range(1, n_rows)]
            if step == n_donor - 1 and stream == 0 and own_act:
                gots[0], own_act[0], other_act[0] = lax.optimization_barrier(
                    (gots[0], own_act[0], other_act[0])
                )
            if n_rows == 2:
                block = jnp.concatenate(
                    [jnp.where(y == 0, chunk, gots[0]), jnp.where(y == 0, gots[0], chunk)], axis=1
                )
            else:
                block = jnp.zeros((sub_rows, n_rows, pair_cols), bf16)
                block = lax.dynamic_update_index_in_dim(block, chunk, y, 1)
                for hop, got in enumerate(gots, 1):
                    block = lax.dynamic_update_index_in_dim(block, got, (y - hop) % n_rows, 1)
                block = block.reshape(sub_rows, model_width)
            resid_parts.append(lax.dynamic_slice_in_dim(block, z * columns, columns, 1))
            block_f = block.astype(f32)
            inverse = lax.rsqrt(jnp.mean(block_f * block_f, axis=1, keepdims=True) + 1e-06)
            normed = (block_f * inverse * gain_f[None, :]).astype(bf16)
            own_rows.append(normed)
            other_rows.append(lax.ppermute(normed, "expert", swap))
        row_gates.append((pick(own_gates, part), pick(other_gates, part)))
        if len(row_gates) == batch:
            rows_in = jnp.concatenate(own_rows + other_rows, axis=0)
            scale = jnp.concatenate([g[0] for g in row_gates] + [g[1] for g in row_gates])
            gate_up = jnp.dot(rows_in[:, :depth], weights[0], preferred_element_type=f32)
            for index in range(1, pieces):
                gate_up = gate_up + jnp.dot(
                    rows_in[:, index * depth : (index + 1) * depth],
                    weights[index],
                    preferred_element_type=f32,
                )
            act = jax.nn.silu(gate_up[:, :ff_local]) * gate_up[:, ff_local:]
            act = (act * scale[:, None]).astype(bf16).reshape(2, batch, part_rows, ff_local)
            own_act.append(act[0])
            other_act.append(act[1])
            own_rows, other_rows, row_gates = [], [], []
        current = following

    def by_sequence(stacked, rows):
        return jnp.concatenate(
            [
                pick(stacked, (z - (y + r) % n_rows * parts_per_seq - i) % n_donor)
                for r in range(rows)
                for i in range(parts_per_seq)
            ],
            axis=0,
        )

    act_rows = jnp.concatenate(
        [
            by_sequence(jnp.concatenate(other_act, axis=0), n_rows),
            by_sequence(jnp.concatenate(own_act, axis=0), n_rows),
        ],
        axis=0,
    )
    half_rows = n_rows * suffix_len
    resid = by_sequence(
        jnp.concatenate(resid_parts, axis=0).reshape(n_donor, part_rows, columns), 1
    ).astype(f32)

    totals = [None] * streams
    swapped = []
    for step in range(1, n_donor + 1):
        if step >= 3:
            act_rows, swapped[step - 3] = lax.optimization_barrier((act_rows, swapped[step - 3]))
        down = lax.dynamic_slice_in_dim(w_down[0], (z - step) % n_donor * columns, columns, 1)
        mixed = jnp.dot(act_rows, down, preferred_element_type=f32)
        swapped.append(
            [
                lax.ppermute(
                    mixed[:half_rows, stream * sub_cols : (stream + 1) * sub_cols].astype(bf16),
                    "expert",
                    swap,
                )
                for stream in range(streams)
            ]
        )
        swapped[step - 1].append(mixed[half_rows:])
    for step in range(1, n_donor + 1):
        kept = swapped[step - 1][streams]
        for stream in range(streams):
            pair_sum = kept[:, stream * sub_cols : (stream + 1) * sub_cols] + swapped[step - 1][
                stream
            ].astype(f32)
            pair_sum = pair_sum.reshape(n_rows, suffix_len, sub_cols)
            part_sum = pair_sum[0]
            for hop in range(1, n_rows):
                sent = pair_sum[hop].astype(bf16)
                part_sum = part_sum + lax.ppermute(sent, "expert", turn(hop)).astype(f32)
            if totals[stream] is not None:
                last = lax.ppermute(totals[stream].astype(bf16), "donor", ring)
                part_sum = part_sum + last.astype(f32)
            totals[stream] = part_sum
    layer_out = (jnp.concatenate(totals, axis=1) + resid).astype(bf16)
    return (layer_out, head_out)


def solution(mesh):
    in_specs = (
        P(("groups", "expert"), None),
        P(("groups", "expert"), "donor"),
        P(("groups", "expert"), None, None),
        P(("groups", "expert", "donor"), None, None, None),
        P("groups", None),
        P("groups"),
        P("donor", "expert"),
        P(),
        P(("groups", "expert"), None),
        P(("groups", "expert"), None),
        P(("expert", "donor"), None, None, None),
        P(("expert", "donor"), None, None),
    )
    out_specs = (P(("groups", "expert"), "donor"), P(("groups", "expert"), "donor"))
    return jax.shard_map(shards, mesh=mesh, in_specs=in_specs, out_specs=out_specs, check_vma=False)
```

time: 173 us -> 211 us (1.22)
  local copies, waits for them, and re-layouts: 18.9 us -> 46.8 us
  waiting for transfers between devices: 93.6 us -> 75.3 us
  starting transfers between devices: 19.5 us -> 37.7 us
  other arithmetic: 13.4 us -> 23.1 us
  between operations: 2.19 us -> 9.37 us
  blocking collectives: 5.17 us -> 0 us
    ppermute x25 -> x59, starting transfers between devices: 9.13 us -> 32.3 us  [the longest x8 9.39 us: shards(): lax.ppermute(chunk, 'expert', turn(hop))]
    slice x5 -> x16, local copies, waits for them, and re-layouts: 0.3 us -> 13.7 us  [the longest x1 13.2 us: weight_piece(): piece = w_gate_up[0, index * depth:(index + 1) * depth]]
    all_to_all x1 -> x0, starting transfers between devices: 7.39 us -> none  [attention(): lax.all_to_all(outgoing, ('expert', 'donor'), split_axis=0, concat_axis=0...]
    ppermute x1, waiting for transfers between devices: 7.11 us -> 0.01 us  [shards(): got = lax.ppermute(head_out, 'expert', turn(step))]
    select_n x9 -> x11, other arithmetic: 1.12 us -> 7.39 us  [the longest x1 5.32 us: shards(): jnp.where(core == 0, jnp.concatenate([out_weight, other_weight], axis=1),...]
    all_to_all x1 -> x0, waiting for transfers between devices: 5.84 us -> none  [attention(): lax.all_to_all(outgoing, ('expert', 'donor'), split_axis=0, concat_axis=0...]
    ppermute x25 -> x59, waiting for transfers between devices: 80.7 us -> 75.3 us  [the longest x6 19.7 us: shards(): got = lax.ppermute(totals[stream].astype(bf16), 'donor', ring)]
    concatenate x0 -> x6, local copies, waits for them, and re-layouts: none -> 5.32 us  [the longest x4 5.29 us: core_gates(): return jnp.concatenate(rows).reshape(n_donor, part_rows)]
  transfers between devices with their start and end apart: 29 -> 62, of which waited for: 16 -> 31; matrix products, arithmetic and copies ran while one was open for 21% -> 35% of each run, Pallas kernels for 0% -> 0%
where the time goes in v2:
time: 211 us; the launch traced here: 210 us
  waiting for transfers between devices  75.3 us (36%)
  local copies, waits for them, and re-layouts  46.8 us (22%)
  starting transfers between devices  37.7 us (18%)
  other arithmetic  23.1 us (11%)
  matrix products  18 us (9%)
  between operations  9.37 us (4%)
    ppermute x6, waiting for transfers between devices, shards(): got = lax.ppermute(totals[stream].astype(bf16), 'donor', ring)  19.7 us
    ppermute x6, waiting for transfers between devices, shards(): last = lax.ppermute(totals[stream].astype(bf16), 'donor', ring)  18.9 us
    unnamed x43, local copies, waits for them, and re-layouts  16.4 us
    ppermute x8, waiting for transfers between devices, shards(): lax.ppermute(chunk, 'expert', turn(hop))  15.6 us
    slice x1, local copies, waits for them, and re-layouts, weight_piece(): piece = w_gate_up[0, index * depth:(index + 1) * depth]  13.2 us
    ppermute x8, starting transfers between devices, shards(): lax.ppermute(chunk, 'expert', turn(hop))  9.39 us
    ppermute x6, waiting for transfers between devices, shards(): following.append(lax.ppermute(current[stream], 'donor', ring))  9.06 us
    ppermute x8, starting transfers between devices, shards(): part_sum = part_sum + lax.ppermute(sent, 'expert', turn(hop)).astype(f32)  7.91 us
  transfers between devices with their start and end apart: 62, of which 31 were waited for; matrix products, arithmetic and copies ran while one was open for 35% of the time, Pallas kernels for 0%

profile of v2, /device:TPU:0, one launch (start us, length us, event | category | flops | bytes accessed | tf_op | source)
XLA Modules:
  0.0 210.3 jit_solution(23914002055517838)
XLA Ops:
  0.7 1.8 dynamic_slice.211
  2.5 3.0 %collective-permute-start.7 = (bf16[64,2048]{1,0:T(8,128)(2,1)}, bf16[64,2048]{1,0:T(8,128)(2,1)}, u32[]{:S(2)}, u32[]{:S(2)}) collective-permute-start(bf16[64,2048]{1,0:T(8,128)(2,1)} %dynamic_slice.211), channel_id=1, source_target_pairs={{0,8},{4,12},{8,0},{12,4},{1,9},{5,13},{9,1},{13,5},{2,10},{6,14},... | collective-permute-start | bytes 786440 | tf_op jit(solution)/shard_map/ppermute | solution.py:156
  23.2 13.2 %fusion.182 = (bf16[1,1024,2,768]{3,2,1,0:T(2,128)(2,1)}, bf16[1,1024,2,768]{3,2,1,0:T(2,128)(2,1)}, bf16[1,1024,2,768]{3,2,1,0:T(2,128)(2,1)}, bf16[1,1024,2,768]{3,2,1,0:T(2,128)(2,1)}) fusion(bf16[1,4096,2,768]{3,2,1,0:T(2,128)(2,1)} %param.22), kind=kLoop, calls=%fused_computation.388 | loop fusion | bytes 25165824 | tf_op jit(solution)/shard_map/slice | solution.py:122
  37.2 2.6 %copy.53 = bf16[128,8,2,768]{3,1,2,0:T(8,128)(2,1)S(1)} copy(bf16[128,8,2,768]{3,2,1,0:T(2,128)(2,1)} %bitcast.250) | data formatting | bytes 6291456
  40.0 2.2 %copy.54 = bf16[128,8,2,768]{3,1,2,0:T(8,128)(2,1)} copy(bf16[128,8,2,768]{3,2,1,0:T(2,128)(2,1)S(1)} %bitcast.249) | data formatting | bytes 6291456
  43.4 1.6 collective-permute-start.3
  45.0 2.6 %collective-permute-start.4 = (bf16[4,32,256]{2,1,0:T(8,128)(2,1)S(1)}, bf16[4,32,256]{2,1,0:T(8,128)(2,1)S(1)}, u32[]{:S(2)}, u32[]{:S(2)}) collective-permute-start(bf16[4,32,256]{2,1,0:T(8,128)(2,1)S(1)} %get-tuple-element.126), channel_id=1, source_target_pairs={{0,2},{1,3},{2,0},{3,1},{4,6},{5,7},{6,4},{7,5},{8,10},{9,11},{10,... | collective-permute-start | bytes 196616 | tf_op jit(solution)/shard_map/ppermute | solution.py:32
  49.8 2.5 %collective-permute-done.4 = bf16[4,32,256]{2,1,0:T(8,128)(2,1)S(1)} collective-permute-done((bf16[4,32,256]{2,1,0:T(8,128)(2,1)S(1)}, bf16[4,32,256]{2,1,0:T(8,128)(2,1)S(1)}, u32[]{:S(2)}, u32[]{:S(2)}) %collective-permute-start.4) | collective-permute-done | bytes 65568 | tf_op jit(solution)/shard_map/ppermute | solution.py:32
  53.3 1.9 dynamic-slice_select_fusion
  55.1 5.3 %maximum_select_fusion = bf16[1024,2048]{1,0:T(8,128)(2,1)} fusion(bf16[1024,1024]{1,0:T(8,128)(2,1)} %collective-permute-done.6, bf16[1024,1024]{1,0:T(8,128)(2,1)S(1)} %copy-done.8, pred[]{:T(512)S(6)} %eq.120), kind=kLoop, calls=%fused_computation | loop fusion | flops 18874368 | bytes 8388609 | tf_op jit(solution)/shard_map/jit(_where)/select_n | solution.py:142
  65.7 4.2 %copy.55 = bf16[128,8,2,768]{3,1,2,0:T(8,128)(2,1)} copy(bf16[128,8,2,768]{3,2,1,0:T(2,128)(2,1)} %bitcast.248) | data formatting | bytes 6291456
  69.9 4.2 %copy.56 = bf16[128,8,2,768]{3,1,2,0:T(8,128)(2,1)} copy(bf16[128,8,2,768]{3,2,1,0:T(2,128)(2,1)} %bitcast.247) | data formatting | bytes 6291456
  77.0 3.4 %fusion.70 = f32[256,2048]{1,0:T(8,128)S(1)} fusion(bf16[1024,2048]{1,0:T(8,128)(2,1)} %maximum_select_fusion, bf16[64,1024]{1,0:T(8,128)(2,1)S(1)} %get-tuple-element.101, bf16[64,1024]{1,0:T(8,128)(2,1)S(1)} %get-tuple-element.102, bf16[64,1024]{1,0:T(8,128)(2,1)S(1)} %get-tuple-element.103, bf16[64,1024]{1,0:T(8,128)(2,1)S(1)} %get-tuple-element.100), kind=kOutput, calls=%fused_computation.115 | convolution fusion | flops 1075838976 | bytes 6815744 | tf_op jit(solution)/shard_map/dot_general | solution.py:181
  82.2 6.7 %collective-permute-done.9 = bf16[32,2048]{1,0:T(8,128)(2,1)S(1)} collective-permute-done((bf16[32,2048]{1,0:T(8,128)(2,1)S(1)}, bf16[32,2048]{1,0:T(8,128)(2,1)S(1)}, u32[]{:S(2)}, u32[]{:S(2)}) %collective-permute-start.9) | collective-permute-done | bytes 131104 | tf_op jit(solution)/shard_map/ppermute | solution.py:187
  88.9 2.6 %collective-permute-done.17 = bf16[32,2048]{1,0:T(8,128)(2,1)S(1)} collective-permute-done((bf16[32,2048]{1,0:T(8,128)(2,1)S(1)}, bf16[32,2048]{1,0:T(8,128)(2,1)S(1)}, u32[]{:S(2)}, u32[]{:S(2)}) %collective-permute-start.17) | collective-permute-done | bytes 131104 | tf_op jit(solution)/shard_map/ppermute | solution.py:187
  98.9 1.7 collective-permute-done.10
  100.6 1.8 collective-permute-done.18
  105.7 5.5 %collective-permute-done.11 = bf16[32,2048]{1,0:T(8,128)(2,1)S(1)} collective-permute-done((bf16[32,2048]{1,0:T(8,128)(2,1)S(1)}, bf16[32,2048]{1,0:T(8,128)(2,1)S(1)}, u32[]{:S(2)}, u32[]{:S(2)}) %collective-permute-start.11) | collective-permute-done | bytes 131104 | tf_op jit(solution)/shard_map/ppermute | solution.py:187
  116.0 3.0 %collective-permute-done.20 = bf16[32,2048]{1,0:T(8,128)(2,1)S(1)} collective-permute-done((bf16[32,2048]{1,0:T(8,128)(2,1)S(1)}, bf16[32,2048]{1,0:T(8,128)(2,1)S(1)}, u32[]{:S(2)}, u32[]{:S(2)}) %collective-permute-start.20) | collective-permute-done | bytes 131104 | tf_op jit(solution)/shard_map/ppermute | solution.py:209
  120.7 3.5 %collective-permute-done.22 = bf16[32,2048]{1,0:T(8,128)(2,1)S(1)} collective-permute-done((bf16[32,2048]{1,0:T(8,128)(2,1)S(1)}, bf16[32,2048]{1,0:T(8,128)(2,1)S(1)}, u32[]{:S(2)}, u32[]{:S(2)}) %collective-permute-start.22) | collective-permute-done | bytes 131104 | tf_op jit(solution)/shard_map/ppermute | solution.py:206
  126.4 2.7 %collective-permute-done.23 = bf16[32,2048]{1,0:T(8,128)(2,1)S(1)} collective-permute-done((bf16[32,2048]{1,0:T(8,128)(2,1)S(1)}, bf16[32,2048]{1,0:T(8,128)(2,1)S(1)}, u32[]{:S(2)}, u32[]{:S(2)}) %collective-permute-start.23) | collective-permute-done | bytes 131104 | tf_op jit(solution)/shard_map/ppermute | solution.py:209
  131.0 3.5 %collective-permute-done.32 = bf16[32,2048]{1,0:T(8,128)(2,1)S(1)} collective-permute-done((bf16[32,2048]{1,0:T(8,128)(2,1)S(1)}, bf16[32,2048]{1,0:T(8,128)(2,1)S(1)}, u32[]{:S(2)}, u32[]{:S(2)}) %collective-permute-start.32) | collective-permute-done | bytes 131104 | tf_op jit(solution)/shard_map/ppermute | solution.py:206
  137.1 2.4 %collective-permute-done.33 = bf16[32,2048]{1,0:T(8,128)(2,1)S(1)} collective-permute-done((bf16[32,2048]{1,0:T(8,128)(2,1)S(1)}, bf16[32,2048]{1,0:T(8,128)(2,1)S(1)}, u32[]{:S(2)}, u32[]{:S(2)}) %collective-permute-start.33) | collective-permute-done | bytes 131104 | tf_op jit(solution)/shard_map/ppermute | solution.py:209
  142.8 2.1 collective-permute-done.34
  146.5 3.3 %collective-permute-done.35 = bf16[32,2048]{1,0:T(8,128)(2,1)S(1)} collective-permute-done((bf16[32,2048]{1,0:T(8,128)(2,1)S(1)}, bf16[32,2048]{1,0:T(8,128)(2,1)S(1)}, u32[]{:S(2)}, u32[]{:S(2)}) %collective-permute-start.35) | collective-permute-done | bytes 131104 | tf_op jit(solution)/shard_map/ppermute | solution.py:209
  176.5 4.5 %collective-permute-done.58 = bf16[128,512]{1,0:T(8,128)(2,1)S(1)} collective-permute-done((bf16[128,512]{1,0:T(8,128)(2,1)S(1)}, bf16[128,512]{1,0:T(8,128)(2,1)S(1)}, u32[]{:S(2)}, u32[]{:S(2)}) %collective-permute-start.58) | collective-permute-done | bytes 131104 | tf_op jit(solution)/shard_map/ppermute | solution.py:298
  181.1 6.6 %collective-permute-done.50 = bf16[128,512]{1,0:T(8,128)(2,1)S(1)} collective-permute-done((bf16[128,512]{1,0:T(8,128)(2,1)S(1)}, bf16[128,512]{1,0:T(8,128)(2,1)S(1)}, u32[]{:S(2)}, u32[]{:S(2)}) %collective-permute-start.50) | collective-permute-done | bytes 131104 | tf_op jit(solution)/shard_map/ppermute | solution.py:300
  191.6 2.4 %collective-permute-done.57 = bf16[128,512]{1,0:T(8,128)(2,1)S(1)} collective-permute-done((bf16[128,512]{1,0:T(8,128)(2,1)S(1)}, bf16[128,512]{1,0:T(8,128)(2,1)S(1)}, u32[]{:S(2)}, u32[]{:S(2)}) %collective-permute-start.57) | collective-permute-done | bytes 131104 | tf_op jit(solution)/shard_map/ppermute | solution.py:298
  194.0 1.7 collective-permute-done.59
  198.9 3.6 %collective-permute-done.60 = bf16[128,512]{1,0:T(8,128)(2,1)S(1)} collective-permute-done((bf16[128,512]{1,0:T(8,128)(2,1)S(1)}, bf16[128,512]{1,0:T(8,128)(2,1)S(1)}, u32[]{:S(2)}, u32[]{:S(2)}) %collective-permute-start.60) | collective-permute-done | bytes 131104 | tf_op jit(solution)/shard_map/ppermute | solution.py:300
  202.7 3.0 %collective-permute-done.52 = bf16[128,512]{1,0:T(8,128)(2,1)S(1)} collective-permute-done((bf16[128,512]{1,0:T(8,128)(2,1)S(1)}, bf16[128,512]{1,0:T(8,128)(2,1)S(1)}, u32[]{:S(2)}, u32[]{:S(2)}) %collective-permute-start.52) | collective-permute-done | bytes 131104 | tf_op jit(solution)/shard_map/ppermute | solution.py:300
  205.7 3.7 %collective-permute-done.61 = bf16[128,512]{1,0:T(8,128)(2,1)S(1)} collective-permute-done((bf16[128,512]{1,0:T(8,128)(2,1)S(1)}, bf16[128,512]{1,0:T(8,128)(2,1)S(1)}, u32[]{:S(2)}, u32[]{:S(2)}) %collective-permute-start.61) | collective-permute-done | bytes 131104 | tf_op jit(solution)/shard_map/ppermute | solution.py:300
  (288 shorter events, 88.0 us)
Async XLA Ops:
  2.5 50.7 %collective-permute-start.7 = (bf16[64,2048]{1,0:T(8,128)(2,1)}, bf16[64,2048]{1,0:T(8,128)(2,1)}, u32[]{:S(2)}, u32[]{:S(2)}) collective-permute-start(bf16[64,2048]{1,0:T(8,128)(2,1)} %dynamic_slice.211), channel_id=1, source_target_pairs={{0,8},{4,12},{8,0},{12,4},{1,9},{5,13},{9,1},{13,5},{2,10},{6,14},... | collective-permute-start | bytes 786440 | tf_op jit(solution)/shard_map/ppermute | solution.py:156
  15.8 26.5 %collective-permute-start.1 = (bf16[2,32,256]{2,1,0:T(8,128)(2,1)}, bf16[2,32,256]{2,1,0:T(8,128)(2,1)}, u32[]{:S(2)}, u32[]{:S(2)}) collective-permute-start(bf16[2,32,256]{2,1,0:T(8,128)(2,1)} %get-tuple-element.131), channel_id=1, source_target_pairs={{0,8},{4,12},{8,0},{12,4},{1,9},{5,13},{9,1},{13,5},{2,10},{6,14},... | collective-permute-start | bytes 98312 | tf_op jit(solution)/shard_map/ppermute | solution.py:26
  15.8 26.5 %collective-permute-start.2 = (bf16[2,32,256]{2,1,0:T(8,128)(2,1)}, bf16[2,32,256]{2,1,0:T(8,128)(2,1)}, u32[]{:S(2)}, u32[]{:S(2)}) collective-permute-start(bf16[2,32,256]{2,1,0:T(8,128)(2,1)} %get-tuple-element.130), channel_id=1, source_target_pairs={{0,12},{4,0},{8,4},{12,8},{1,13},{5,1},{9,5},{13,9},{2,14},{6,2},{... | collective-permute-start | bytes 98312 | tf_op jit(solution)/shard_map/ppermute | solution.py:26
  16.7 25.6 %collective-permute-start = (bf16[2,32,256]{2,1,0:T(8,128)(2,1)S(1)}, bf16[2,32,256]{2,1,0:T(8,128)(2,1)}, u32[]{:S(2)}, u32[]{:S(2)}) collective-permute-start(bf16[2,32,256]{2,1,0:T(8,128)(2,1)S(1)} %get-tuple-element.129), channel_id=1, source_target_pairs={{0,4},{4,8},{8,12},{12,0},{1,5},{5,9},{9,13},{13,1},{2,6},{6,10},{... | collective-permute-start | bytes 98312 | tf_op jit(solution)/shard_map/ppermute | solution.py:26
  16.7 38.4 %collective-permute-start.6 = (bf16[1024,1024]{1,0:T(8,128)(2,1)}, bf16[1024,1024]{1,0:T(8,128)(2,1)}, u32[]{:S(2)}, u32[]{:S(2)}) collective-permute-start(bf16[1024,1024]{1,0:T(8,128)(2,1)} %param.18), channel_id=1, source_target_pairs={{0,4},{4,0},{8,12},{12,8},{1,5},{5,1},{9,13},{13,9},{2,6},{6,2},{1... | collective-permute-start | bytes 6291464 | tf_op jit(solution)/shard_map/ppermute | solution.py:141
  49.8 24.3 %collective-permute-start.30 = (f32[8,128]{1,0:T(8,128)S(1)}, f32[8,128]{1,0:T(8,128)S(1)}, u32[]{:S(2)}, u32[]{:S(2)}) collective-permute-start(f32[8,128]{1,0:T(8,128)S(1)} %bitcast.281), channel_id=1, source_target_pairs={{0,12},{4,0},{8,4},{12,8},{1,13},{5,1},{9,5},{13,9},{2,14},{6,2},{... | collective-permute-start | bytes 12296 | tf_op jit(solution)/shard_map/ppermute | solution.py:131
  52.3 29.9 %collective-permute-start.29 = (f32[8,128]{1,0:T(8,128)S(1)}, f32[8,128]{1,0:T(8,128)S(1)}, u32[]{:S(2)}, u32[]{:S(2)}) collective-permute-start(f32[8,128]{1,0:T(8,128)S(1)} %bitcast.282), channel_id=1, source_target_pairs={{0,8},{4,12},{8,0},{12,4},{1,9},{5,13},{9,1},{13,5},{2,10},{6,14},... | collective-permute-start | bytes 12296 | tf_op jit(solution)/shard_map/ppermute | solution.py:131
  53.2 29.0 %collective-permute-start.28 = (f32[8,128]{1,0:T(8,128)S(1)}, f32[8,128]{1,0:T(8,128)S(1)}, u32[]{:S(2)}, u32[]{:S(2)}) collective-permute-start(f32[8,128]{1,0:T(8,128)S(1)} %bitcast.283), channel_id=1, source_target_pairs={{0,4},{4,8},{8,12},{12,0},{1,5},{5,9},{9,13},{13,1},{2,6},{6,10},{... | collective-permute-start | bytes 12296 | tf_op jit(solution)/shard_map/ppermute | solution.py:131
  63.9 12.0 %collective-permute-start.8 = (bf16[128,1024]{1,0:T(8,128)(2,1)}, bf16[128,1024]{1,0:T(8,128)(2,1)}, u32[]{:S(2)}, u32[]{:S(2)}) collective-permute-start(bf16[128,1024]{1,0:T(8,128)(2,1)} %copy.43), channel_id=1, source_target_pairs={{0,8},{4,12},{8,0},{12,4},{1,9},{5,13},{9,1},{13,5},{2,10},{6,14},... | collective-permute-start | bytes 786440 | tf_op jit(solution)/shard_map/ppermute | solution.py:175
  80.7 8.2 %collective-permute-start.9 = (bf16[32,2048]{1,0:T(8,128)(2,1)S(1)}, bf16[32,2048]{1,0:T(8,128)(2,1)S(1)}, u32[]{:S(2)}, u32[]{:S(2)}) collective-permute-start(bf16[32,2048]{1,0:T(8,128)(2,1)S(1)} %get-tuple-element.97), channel_id=1, source_target_pairs={{0,1},{1,2},{2,3},{3,0},{4,5},{5,6},{6,7},{7,4},{8,9},{9,10},{10,1... | collective-permute-start | bytes 393224 | tf_op jit(solution)/shard_map/ppermute | solution.py:187
  81.3 10.1 %collective-permute-start.17 = (bf16[32,2048]{1,0:T(8,128)(2,1)S(1)}, bf16[32,2048]{1,0:T(8,128)(2,1)S(1)}, u32[]{:S(2)}, u32[]{:S(2)}) collective-permute-start(bf16[32,2048]{1,0:T(8,128)(2,1)S(1)} %get-tuple-element.96), channel_id=1, source_target_pairs={{0,1},{1,2},{2,3},{3,0},{4,5},{5,6},{6,7},{7,4},{8,9},{9,10},{10,1... | collective-permute-start | bytes 393224 | tf_op jit(solution)/shard_map/ppermute | solution.py:187
  92.2 8.4 %collective-permute-start.10 = (bf16[32,2048]{1,0:T(8,128)(2,1)}, bf16[32,2048]{1,0:T(8,128)(2,1)S(1)}, u32[]{:S(2)}, u32[]{:S(2)}) collective-permute-start(bf16[32,2048]{1,0:T(8,128)(2,1)} %get-tuple-element.83), channel_id=1, source_target_pairs={{0,1},{1,2},{2,3},{3,0},{4,5},{5,6},{6,7},{7,4},{8,9},{9,10},{10,1... | collective-permute-start | bytes 393224 | tf_op jit(solution)/shard_map/ppermute | solution.py:187
  92.2 10.2 %collective-permute-start.18 = (bf16[32,2048]{1,0:T(8,128)(2,1)}, bf16[32,2048]{1,0:T(8,128)(2,1)}, u32[]{:S(2)}, u32[]{:S(2)}) collective-permute-start(bf16[32,2048]{1,0:T(8,128)(2,1)} %get-tuple-element.82), channel_id=1, source_target_pairs={{0,1},{1,2},{2,3},{3,0},{4,5},{5,6},{6,7},{7,4},{8,9},{9,10},{10,1... | collective-permute-start | bytes 393224 | tf_op jit(solution)/shard_map/ppermute | solution.py:187
  103.6 9.0 %collective-permute-start.19 = (bf16[32,2048]{1,0:T(8,128)(2,1)S(1)}, bf16[32,2048]{1,0:T(8,128)(2,1)S(1)}, u32[]{:S(2)}, u32[]{:S(2)}) collective-permute-start(bf16[32,2048]{1,0:T(8,128)(2,1)S(1)} %get-tuple-element.80), channel_id=1, source_target_pairs={{0,1},{1,2},{2,3},{3,0},{4,5},{5,6},{6,7},{7,4},{8,9},{9,10},{10,1... | collective-permute-start | bytes 393224 | tf_op jit(solution)/shard_map/ppermute | solution.py:187
  116.0 9.8 %collective-permute-start.12 = (bf16[32,2048]{1,0:T(8,128)(2,1)S(1)}, bf16[32,2048]{1,0:T(8,128)(2,1)S(1)}, u32[]{:S(2)}, u32[]{:S(2)}) collective-permute-start(bf16[32,2048]{1,0:T(8,128)(2,1)S(1)} %get-tuple-element.75), channel_id=1, source_target_pairs={{0,1},{1,2},{2,3},{3,0},{4,5},{5,6},{6,7},{7,4},{8,9},{9,10},{10,1... | collective-permute-start | bytes 393224 | tf_op jit(solution)/shard_map/ppermute | solution.py:206
  126.3 9.8 %collective-permute-start.13 = (bf16[32,2048]{1,0:T(8,128)(2,1)S(1)}, bf16[32,2048]{1,0:T(8,128)(2,1)S(1)}, u32[]{:S(2)}, u32[]{:S(2)}) collective-permute-start(bf16[32,2048]{1,0:T(8,128)(2,1)S(1)} %collective-permute-done.12), channel_id=1, source_target_pairs={{0,1},{1,2},{2,3},{3,0},{4,5},{5,6},{6,7},{7,4},{8,9},{9,10},{10,1... | collective-permute-start | bytes 393224 | tf_op jit(solution)/shard_map/ppermute | solution.py:206
  126.3 8.2 %collective-permute-start.32 = (bf16[32,2048]{1,0:T(8,128)(2,1)S(1)}, bf16[32,2048]{1,0:T(8,128)(2,1)S(1)}, u32[]{:S(2)}, u32[]{:S(2)}) collective-permute-start(bf16[32,2048]{1,0:T(8,128)(2,1)S(1)} %collective-permute-done.22), channel_id=1, source_target_pairs={{0,1},{1,2},{2,3},{3,0},{4,5},{5,6},{6,7},{7,4},{8,9},{9,10},{10,1... | collective-permute-start | bytes 393224 | tf_op jit(solution)/shard_map/ppermute | solution.py:206
  136.7 14.0 %collective-permute-start.14 = (bf16[32,2048]{1,0:T(8,128)(2,1)S(1)}, bf16[32,2048]{1,0:T(8,128)(2,1)S(1)}, u32[]{:S(2)}, u32[]{:S(2)}) collective-permute-start(bf16[32,2048]{1,0:T(8,128)(2,1)S(1)} %collective-permute-done.13), channel_id=1, source_target_pairs={{0,1},{1,2},{2,3},{3,0},{4,5},{5,6},{6,7},{7,4},{8,9},{9,10},{10,1... | collective-permute-start | bytes 393224 | tf_op jit(solution)/shard_map/ppermute | solution.py:206
  141.6 8.5 %collective-permute-start.24 = (bf16[32,4096]{1,0:T(8,128)(2,1)S(1)}, bf16[32,4096]{1,0:T(8,128)(2,1)S(1)}, u32[]{:S(2)}, u32[]{:S(2)}) collective-permute-start(bf16[32,4096]{1,0:T(8,128)(2,1)S(1)} %get-tuple-element.135), channel_id=1, source_target_pairs={{0,4},{4,0},{8,12},{12,8},{1,5},{5,1},{9,13},{13,9},{2,6},{6,2},{1... | collective-permute-start | bytes 786440 | tf_op jit(solution)/shard_map/ppermute | solution.py:229
  141.9 8.9 %collective-permute-start.25 = (bf16[32,4096]{1,0:T(8,128)(2,1)S(1)}, bf16[32,4096]{1,0:T(8,128)(2,1)S(1)}, u32[]{:S(2)}, u32[]{:S(2)}) collective-permute-start(bf16[32,4096]{1,0:T(8,128)(2,1)S(1)} %get-tuple-element.133), channel_id=1, source_target_pairs={{0,4},{4,0},{8,12},{12,8},{1,5},{5,1},{9,13},{13,9},{2,6},{6,2},{1... | collective-permute-start | bytes 786440 | tf_op jit(solution)/shard_map/ppermute | solution.py:229
  142.6 9.8 %collective-permute-start.26 = (bf16[32,4096]{1,0:T(8,128)(2,1)S(1)}, bf16[32,4096]{1,0:T(8,128)(2,1)S(1)}, u32[]{:S(2)}, u32[]{:S(2)}) collective-permute-start(bf16[32,4096]{1,0:T(8,128)(2,1)S(1)} %get-tuple-element.63), channel_id=1, source_target_pairs={{0,4},{4,0},{8,12},{12,8},{1,5},{5,1},{9,13},{13,9},{2,6},{6,2},{1... | collective-permute-start | bytes 786440 | tf_op jit(solution)/shard_map/ppermute | solution.py:229
  150.0 9.6 %collective-permute-start.36 = (bf16[32,4096]{1,0:T(8,128)(2,1)S(1)}, bf16[32,4096]{1,0:T(8,128)(2,1)S(1)}, u32[]{:S(2)}, u32[]{:S(2)}) collective-permute-start(bf16[32,4096]{1,0:T(8,128)(2,1)S(1)} %get-tuple-element.59), channel_id=1, source_target_pairs={{0,4},{4,0},{8,12},{12,8},{1,5},{5,1},{9,13},{13,9},{2,6},{6,2},{1... | collective-permute-start | bytes 786440 | tf_op jit(solution)/shard_map/ppermute | solution.py:229
  150.6 9.0 %collective-permute-start.37 = (bf16[32,4096]{1,0:T(8,128)(2,1)S(1)}, bf16[32,4096]{1,0:T(8,128)(2,1)S(1)}, u32[]{:S(2)}, u32[]{:S(2)}) collective-permute-start(bf16[32,4096]{1,0:T(8,128)(2,1)S(1)} %get-tuple-element.57), channel_id=1, source_target_pairs={{0,4},{4,0},{8,12},{12,8},{1,5},{5,1},{9,13},{13,9},{2,6},{6,2},{1... | collective-permute-start | bytes 786440 | tf_op jit(solution)/shard_map/ppermute | solution.py:229
  170.9 10.1 %collective-permute-start.48 = (bf16[128,512]{1,0:T(8,128)(2,1)S(1)}, bf16[128,512]{1,0:T(8,128)(2,1)S(1)}, u32[]{:S(2)}, u32[]{:S(2)}) collective-permute-start(bf16[128,512]{1,0:T(8,128)(2,1)S(1)} %slice.503), channel_id=1, source_target_pairs={{0,8},{4,12},{8,0},{12,4},{1,9},{5,13},{9,1},{13,5},{2,10},{6,14},... | collective-permute-start | bytes 393224 | tf_op jit(solution)/shard_map/ppermute | solution.py:298
  173.0 15.9 %collective-permute-start.46 = (bf16[256,512]{1,0:T(8,128)(2,1)S(1)}, bf16[256,512]{1,0:T(8,128)(2,1)S(1)}, u32[]{:S(2)}, u32[]{:S(2)}) collective-permute-start(bf16[256,512]{1,0:T(8,128)(2,1)S(1)} %get-tuple-element.88), channel_id=1, source_target_pairs={{0,4},{4,0},{8,12},{12,8},{1,5},{5,1},{9,13},{13,9},{2,6},{6,2},{1... | collective-permute-start | bytes 786440 | tf_op jit(solution)/shard_map/ppermute | solution.py:279
  173.1 15.9 %collective-permute-start.55 = (bf16[256,512]{1,0:T(8,128)(2,1)S(1)}, bf16[256,512]{1,0:T(8,128)(2,1)S(1)}, u32[]{:S(2)}, u32[]{:S(2)}) collective-permute-start(bf16[256,512]{1,0:T(8,128)(2,1)S(1)} %get-tuple-element.89), channel_id=1, source_target_pairs={{0,4},{4,0},{8,12},{12,8},{1,5},{5,1},{9,13},{13,9},{2,6},{6,2},{1... | collective-permute-start | bytes 786440 | tf_op jit(solution)/shard_map/ppermute | solution.py:279
  174.8 14.4 %collective-permute-start.44 = (bf16[256,512]{1,0:T(8,128)(2,1)S(1)}, bf16[256,512]{1,0:T(8,128)(2,1)S(1)}, u32[]{:S(2)}, u32[]{:S(2)}) collective-permute-start(bf16[256,512]{1,0:T(8,128)(2,1)S(1)} %get-tuple-element.90), channel_id=1, source_target_pairs={{0,4},{4,0},{8,12},{12,8},{1,5},{5,1},{9,13},{13,9},{2,6},{6,2},{1... | collective-permute-start | bytes 786440 | tf_op jit(solution)/shard_map/ppermute | solution.py:279
  181.1 9.3 %collective-permute-start.53 = (bf16[256,512]{1,0:T(8,128)(2,1)S(1)}, bf16[256,512]{1,0:T(8,128)(2,1)S(1)}, u32[]{:S(2)}, u32[]{:S(2)}) collective-permute-start(bf16[256,512]{1,0:T(8,128)(2,1)S(1)} %get-tuple-element.91), channel_id=1, source_target_pairs={{0,4},{4,0},{8,12},{12,8},{1,5},{5,1},{9,13},{13,9},{2,6},{6,2},{1... | collective-permute-start | bytes 786440 | tf_op jit(solution)/shard_map/ppermute | solution.py:279
  188.9 8.2 %collective-permute-start.51 = (bf16[128,512]{1,0:T(8,128)(2,1)S(1)}, bf16[128,512]{1,0:T(8,128)(2,1)S(1)}, u32[]{:S(2)}, u32[]{:S(2)}) collective-permute-start(bf16[128,512]{1,0:T(8,128)(2,1)S(1)} %fusion.94), channel_id=1, source_target_pairs={{0,1},{1,2},{2,3},{3,0},{4,5},{5,6},{6,7},{7,4},{8,9},{9,10},{10,1... | collective-permute-start | bytes 393224 | tf_op jit(solution)/shard_map/ppermute | solution.py:300
  189.2 9.5 %collective-permute-start.47 = (bf16[128,512]{1,0:T(8,128)(2,1)S(1)}, bf16[128,512]{1,0:T(8,128)(2,1)S(1)}, u32[]{:S(2)}, u32[]{:S(2)}) collective-permute-start(bf16[128,512]{1,0:T(8,128)(2,1)S(1)} %slice.504), channel_id=1, source_target_pairs={{0,8},{4,12},{8,0},{12,4},{1,9},{5,13},{9,1},{13,5},{2,10},{6,14},... | collective-permute-start | bytes 393224 | tf_op jit(solution)/shard_map/ppermute | solution.py:298
  190.5 12.2 %collective-permute-start.45 = (bf16[128,512]{1,0:T(8,128)(2,1)S(1)}, bf16[128,512]{1,0:T(8,128)(2,1)S(1)}, u32[]{:S(2)}, u32[]{:S(2)}) collective-permute-start(bf16[128,512]{1,0:T(8,128)(2,1)S(1)} %slice.505), channel_id=1, source_target_pairs={{0,8},{4,12},{8,0},{12,4},{1,9},{5,13},{9,1},{13,5},{2,10},{6,14},... | collective-permute-start | bytes 393224 | tf_op jit(solution)/shard_map/ppermute | solution.py:298
  197.2 8.5 %collective-permute-start.54 = (bf16[128,512]{1,0:T(8,128)(2,1)S(1)}, bf16[128,512]{1,0:T(8,128)(2,1)S(1)}, u32[]{:S(2)}, u32[]{:S(2)}) collective-permute-start(bf16[128,512]{1,0:T(8,128)(2,1)S(1)} %slice.501), channel_id=1, source_target_pairs={{0,8},{4,12},{8,0},{12,4},{1,9},{5,13},{9,1},{13,5},{2,10},{6,14},... | collective-permute-start | bytes 393224 | tf_op jit(solution)/shard_map/ppermute | solution.py:298
  (46 other events, 306.4 us)

commit v3 on v1

v3 whole, which is shorter than its diff:
```python
import jax
import jax.numpy as jnp
from jax import lax
from jax.sharding import PartitionSpec as P


def rotation(count, step):
    return [(i, (i + step) % count) for i in range(count)]


def pick(array, index, axis=0):
    return lax.dynamic_index_in_dim(array, index, axis, keepdims=False)


def attention(queries, suffix_kv, kv_pool, page_table, prefix_len, early):
    n_expert = lax.axis_size("expert")
    n_donor = lax.axis_size("donor")
    expert_index = lax.axis_index("expert")
    donor_index = lax.axis_index("donor")
    seq_count, page_count = page_table.shape
    suffix_len = queries.shape[0]
    kv_heads = suffix_kv.shape[1]
    head_dim = suffix_kv.shape[2] // 2
    page_len = kv_pool.shape[2]
    my_group = donor_index * kv_heads // n_donor
    owner_index = expert_index * n_donor + donor_index
    owner_of = page_table // seq_count
    held_slot = jnp.sum(jnp.where(owner_of == owner_index, page_table % seq_count, 0), axis=1)
    dest_group = jnp.arange(n_donor, dtype=jnp.int32) * kv_heads // n_donor
    wanted = (held_slot[:, None] * kv_heads + dest_group[None, :]).reshape(-1)
    outgoing = jnp.take(
        kv_pool.reshape(seq_count * kv_heads, page_len, 2 * head_dim), wanted, axis=0
    )
    arrived = lax.all_to_all(outgoing, ("expert", "donor"), split_axis=0, concat_axis=0, tiled=True)
    arrived, early = lax.optimization_barrier((arrived, early))
    my_owners = lax.dynamic_index_in_dim(owner_of, expert_index, 0, keepdims=False)
    ordered = jnp.take(arrived, my_owners, axis=0).reshape(page_count * page_len, 2 * head_dim)
    prefix_keys = ordered[:, :head_dim]
    prefix_vals = ordered[:, head_dim:]
    score_scale = head_dim ** (-0.5)
    query_heads = queries.reshape(suffix_len, -1, head_dim)
    fresh_pair = lax.dynamic_index_in_dim(suffix_kv, my_group, 1, keepdims=False)
    causal = jnp.arange(suffix_len)[:, None] >= jnp.arange(suffix_len)[None, :]
    fresh_scores = (
        jnp.einsum(
            "thc,uc->thu", query_heads, fresh_pair[:, :head_dim], preferred_element_type=jnp.float32
        )
        * score_scale
    )
    fresh_scores = jnp.where(causal[:, None, :], fresh_scores, -jnp.inf)
    prefix_tokens = lax.dynamic_index_in_dim(prefix_len, expert_index, 0, keepdims=False)
    block_keys = min(1024, page_count * page_len)
    live_blocks = (prefix_tokens + block_keys - 1) // block_keys

    def block_scores(block_index):
        keys_block = lax.dynamic_slice_in_dim(prefix_keys, block_index * block_keys, block_keys, 0)
        raw_scores = (
            jnp.einsum("thc,kc->thk", query_heads, keys_block, preferred_element_type=jnp.float32)
            * score_scale
        )
        visible = block_index * block_keys + jnp.arange(block_keys) < prefix_tokens
        return jnp.where(visible[None, None, :], raw_scores, -jnp.inf)

    def raise_max(block_index, running):
        return jnp.maximum(running, jnp.max(block_scores(block_index), axis=2))

    row_max = lax.fori_loop(0, live_blocks, raise_max, jnp.max(fresh_scores, axis=2))

    def add_block(block_index, loop_state):
        row_total, weighted = loop_state
        exp_scores = jnp.exp(block_scores(block_index) - row_max[:, :, None])
        vals_block = lax.dynamic_slice_in_dim(prefix_vals, block_index * block_keys, block_keys, 0)
        weighted = weighted + jnp.einsum(
            "thk,kc->thc",
            exp_scores.astype(jnp.bfloat16),
            vals_block,
            preferred_element_type=jnp.float32,
        )
        return (row_total + jnp.sum(exp_scores, axis=2), weighted)

    fresh_exp = jnp.exp(fresh_scores - row_max[:, :, None])
    start_state = (
        jnp.sum(fresh_exp, axis=2),
        jnp.einsum(
            "thu,uc->thc",
            fresh_exp.astype(jnp.bfloat16),
            fresh_pair[:, head_dim:],
            preferred_element_type=jnp.float32,
        ),
    )
    row_total, weighted = lax.fori_loop(0, live_blocks, add_block, start_state)
    return (weighted / row_total[:, :, None]).astype(jnp.bfloat16).reshape(suffix_len, -1), early


def shards(
    hidden_in,
    queries,
    suffix_kv,
    kv_pool,
    page_table,
    prefix_len,
    out_weight,
    norm_gain,
    expert_ids,
    route_probs,
    w_gate_up,
    w_down,
):
    f32, bf16 = jnp.float32, jnp.bfloat16
    n_expert = lax.axis_size("expert")
    n_donor = lax.axis_size("donor")
    expert_index = lax.axis_index("expert")
    z = lax.axis_index("donor")
    n_rows = n_expert // 2
    y = expert_index // 2
    core = expert_index % 2
    swap = [(i, i ^ 1) for i in range(n_expert)]

    def turn(step):
        return rotation(n_expert, 2 * step)

    suffix_len, model_width = hidden_in.shape
    experts_all = 2 * n_expert
    ff_local = w_gate_up.shape[3]
    share_count = n_donor // 2
    my_expert = 2 * expert_index + z // share_count
    pair_cols = model_width // n_rows
    part_rows = n_rows * suffix_len // n_donor
    parts_per_seq = suffix_len // part_rows
    columns = model_width // n_donor
    steps = sorted(range(1, n_donor), key=lambda step: min(step, n_donor - step))

    gates = route_probs / jnp.sum(route_probs, axis=1, keepdims=True)
    hits = expert_ids[:, :, None] == jnp.arange(experts_all, dtype=jnp.int32)
    gate_table = jnp.sum(jnp.where(hits, gates[:, :, None], 0.0), axis=1).T
    tables = [gate_table] + [
        lax.ppermute(gate_table, "expert", rotation(n_expert, step)) for step in range(1, n_expert)
    ]

    other_weight = lax.ppermute(out_weight, "expert", swap)

    part_owner = z * part_rows // suffix_len
    hidden_rows = lax.dynamic_slice_in_dim(hidden_in, z * part_rows % suffix_len, part_rows, 0)

    def hidden_block(row):
        return lax.dynamic_slice_in_dim(hidden_rows, row * pair_cols, pair_cols, 1)

    hidden_part = hidden_block(y)
    for step in range(1, n_rows):
        got = lax.ppermute(hidden_block((y + step) % n_rows), "expert", turn(step))
        hidden_part = jnp.where((y - step) % n_rows == part_owner, got, hidden_part)

    head_out, (tables, other_weight, hidden_part) = attention(
        queries,
        suffix_kv,
        kv_pool,
        page_table,
        prefix_len,
        (tables, other_weight, hidden_part),
    )

    heads = jnp.zeros((n_rows, suffix_len, head_out.shape[1]), bf16)
    heads = lax.dynamic_update_index_in_dim(heads, head_out, y, 0)
    for step in range(1, n_rows):
        got = lax.ppermute(head_out, "expert", turn(step))
        heads = lax.dynamic_update_index_in_dim(heads, got, (y - step) % n_rows, 0)
    heads = heads.reshape(n_donor, part_rows, -1)
    heads = jnp.concatenate([pick(heads, (z + step) % n_donor) for step in range(n_donor)])
    own_terms = jnp.dot(heads, out_weight, preferred_element_type=f32)
    other_terms = jnp.dot(heads, other_weight, preferred_element_type=f32)

    def term(step):
        rows = slice(step * part_rows, (step + 1) * part_rows)
        own, other = own_terms[rows], other_terms[rows]
        return jnp.concatenate(
            [jnp.where(core == 0, own, other), jnp.where(core == 0, other, own)], axis=1
        )

    gate_up_weight = w_gate_up[0].reshape(model_width, 2 * ff_local)
    gots = [
        lax.ppermute(term(step).astype(bf16), "donor", rotation(n_donor, step)) for step in steps
    ]
    gots, gate_up_weight = lax.optimization_barrier((gots, gate_up_weight))
    total = term(0) + hidden_part.astype(f32)
    for got in gots:
        total = total + got.astype(f32)
    chunk = total.astype(bf16)

    all_gates = jnp.stack([pick(table, my_expert) for table in tables], axis=0)

    def core_gates(which):
        rows = [pick(all_gates, (expert_index - 2 * r - which) % n_expert) for r in range(n_rows)]
        return jnp.concatenate(rows).reshape(n_donor, part_rows)

    own_gates, other_gates = core_gates(core), core_gates(1 - core)

    gain_f = norm_gain.astype(f32)
    chunks = [chunk] + [lax.ppermute(chunk, "donor", rotation(n_donor, step)) for step in steps]
    slots = [0] + steps
    resid_parts = [None] * n_donor
    own_act, other_act = [None] * n_donor, [None] * n_donor
    batch = max(1, n_donor // 2)
    own_rows, other_rows, row_gates = [], [], []
    for place, (slot, chunk) in enumerate(zip(slots, chunks)):
        part = (z - slot) % n_donor
        gots = [lax.ppermute(chunk, "expert", turn(hop)) for hop in range(1, n_rows)]
        if place == n_donor - 1 and place >= batch and gots:
            early = [slots[i] for i in range(batch)]
            gots, acts = lax.optimization_barrier(
                (gots, [(own_act[i], other_act[i]) for i in early])
            )
            for i, pair in zip(early, acts):
                own_act[i], other_act[i] = pair
        if n_rows == 2:
            block = jnp.concatenate(
                [jnp.where(y == 0, chunk, gots[0]), jnp.where(y == 0, gots[0], chunk)], axis=1
            )
        else:
            block = jnp.zeros((part_rows, n_rows, pair_cols), bf16)
            block = lax.dynamic_update_index_in_dim(block, chunk, y, 1)
            for hop, got in enumerate(gots, 1):
                block = lax.dynamic_update_index_in_dim(block, got, (y - hop) % n_rows, 1)
            block = block.reshape(part_rows, model_width)
        resid_parts[slot] = lax.dynamic_slice_in_dim(block, z * columns, columns, 1)
        block_f = block.astype(f32)
        inverse = lax.rsqrt(jnp.mean(block_f * block_f, axis=1, keepdims=True) + 1e-06)
        normed = (block_f * inverse * gain_f[None, :]).astype(bf16)
        own_rows.append(normed)
        other_rows.append(lax.ppermute(normed, "expert", swap))
        row_gates.append((pick(own_gates, part), pick(other_gates, part)))
        if len(row_gates) == batch:
            rows_in = jnp.concatenate(own_rows + other_rows, axis=0)
            scale = jnp.concatenate([g[0] for g in row_gates] + [g[1] for g in row_gates])
            gate_up = jnp.dot(rows_in, gate_up_weight, preferred_element_type=f32)
            act = jax.nn.silu(gate_up[:, :ff_local]) * gate_up[:, ff_local:]
            act = (act * scale[:, None]).astype(bf16).reshape(2, batch, part_rows, ff_local)
            for i in range(batch):
                own_act[slots[place - batch + 1 + i]] = act[0, i]
                other_act[slots[place - batch + 1 + i]] = act[1, i]
            own_rows, other_rows, row_gates = [], [], []

    def by_sequence(parts, rows):
        stacked = jnp.stack(parts, axis=0)
        return jnp.concatenate(
            [
                pick(stacked, (z - (y + r) % n_rows * parts_per_seq - i) % n_donor)
                for r in range(rows)
                for i in range(parts_per_seq)
            ],
            axis=0,
        )

    act_rows = jnp.concatenate(
        [by_sequence(other_act, n_rows), by_sequence(own_act, n_rows)], axis=0
    )
    half_rows = n_rows * suffix_len
    resid = by_sequence(resid_parts, 1).astype(f32)

    swapped, kept = [], []
    order = steps[::-1] + [0]
    for place, step in enumerate(order):
        if place >= 2:
            act_rows, swapped[place - 2] = lax.optimization_barrier((act_rows, swapped[place - 2]))
        down = lax.dynamic_slice_in_dim(w_down[0], (z + step) % n_donor * columns, columns, 1)
        mixed = jnp.dot(act_rows, down, preferred_element_type=f32)
        swapped.append(lax.ppermute(mixed[:half_rows].astype(bf16), "expert", swap))
        kept.append(mixed[half_rows:])
    total = resid
    for place, step in enumerate(order):
        pair_sum = (kept[place] + swapped[place].astype(f32)).reshape(n_rows, suffix_len, columns)
        part_sum = pair_sum[0]
        for hop in range(1, n_rows):
            sent = pair_sum[hop].astype(bf16)
            part_sum = part_sum + lax.ppermute(sent, "expert", turn(hop)).astype(f32)
        if step:
            part_sum = lax.ppermute(part_sum.astype(bf16), "donor", rotation(n_donor, step))
        total = total + part_sum.astype(f32)
    return (total.astype(bf16), head_out)


def solution(mesh):
    in_specs = (
        P(("groups", "expert"), None),
        P(("groups", "expert"), "donor"),
        P(("groups", "expert"), None, None),
        P(("groups", "expert", "donor"), None, None, None),
        P("groups", None),
        P("groups"),
        P("donor", "expert"),
        P(),
        P(("groups", "expert"), None),
        P(("groups", "expert"), None),
        P(("expert", "donor"), None, None, None),
        P(("expert", "donor"), None, None),
    )
    out_specs = (P(("groups", "expert"), "donor"), P(("groups", "expert"), "donor"))
    return jax.shard_map(shards, mesh=mesh, in_specs=in_specs, out_specs=out_specs, check_vma=False)
```

time: 173 us -> 176 us (1.017)
  starting transfers between devices: 19.5 us -> 37.4 us
  waiting for transfers between devices: 93.6 us -> 80.5 us
  blocking collectives: 5.17 us -> 0 us
  matrix products: 19.3 us -> 22.6 us
  local copies, waits for them, and re-layouts: 18.9 us -> 21.1 us
  other arithmetic: 13.4 us -> 11.6 us
    ppermute x25 -> x28, starting transfers between devices: 9.13 us -> 27.8 us  [the longest x3 6.33 us: shards(): lax.ppermute(chunk, 'donor', rotation(n_donor, step))]
    ppermute x1, waiting for transfers between devices: 7.11 us -> 0.01 us  [shards(): got = lax.ppermute(head_out, 'expert', turn(step))]
    ppermute x25 -> x28, waiting for transfers between devices: 80.7 us -> 74.2 us  [the longest x3 21.2 us: shards(): lax.ppermute(term(step).astype(bf16), 'donor', rotation(n_donor, step))]
    ppermute x1, waiting for transfers between devices: 0.01 us -> 6.29 us  [shards(): got = lax.ppermute(hidden_block((y + step) % n_rows), 'expert', turn(step))]
    all_to_all x1, waiting for transfers between devices: 5.84 us -> 0.01 us  [attention(): lax.all_to_all(outgoing, ('expert', 'donor'), split_axis=0, concat_axis=0...]
    all_gather x1 -> x0, blocking collectives: 5.17 us -> none  [shards(): all_gates = lax.all_gather(gate_table.T, 'expert', axis=0)]
    convert_element_type x9 -> x7, other arithmetic: 6.52 us -> 1.75 us  [the longest x1 0.94 us: shards(): return (total.astype(bf16), head_out)]
    dot_general x2, matrix products: 10 us -> 13.4 us  [shards(): gate_up = jnp.dot(rows_in, gate_up_weight, preferred_element_type=f32)]
  transfers between devices with their start and end apart: 29 -> 32, of which waited for: 16 -> 17; matrix products, arithmetic and copies ran while one was open for 21% -> 19% of each run, Pallas kernels for 0% -> 0%
where the time goes in v3:
time: 176 us
  waiting for transfers between devices  80.5 us (46%)
  starting transfers between devices  37.4 us (21%)
  matrix products  22.6 us (13%)
  local copies, waits for them, and re-layouts  21.1 us (12%)
  other arithmetic  11.6 us (7%)
  between operations  2.25 us (1%)
    ppermute x3, waiting for transfers between devices, shards(): lax.ppermute(term(step).astype(bf16), 'donor', rotation(n_donor, step))  21.2 us
    ppermute x4, waiting for transfers between devices, shards(): part_sum = part_sum + lax.ppermute(sent, 'expert', turn(hop)).astype(f32)  19 us
    ppermute x3, waiting for transfers between devices, shards(): lax.ppermute(chunk, 'donor', rotation(n_donor, step))  18.6 us
    unnamed x32, local copies, waits for them, and re-layouts  15.3 us
    dot_general x2, matrix products, shards(): gate_up = jnp.dot(rows_in, gate_up_weight, preferred_element_type=f32)  13.4 us
    ppermute x4, waiting for transfers between devices, shards(): lax.ppermute(chunk, 'expert', turn(hop))  7.69 us
    ppermute x3, starting transfers between devices, shards(): lax.ppermute(chunk, 'donor', rotation(n_donor, step))  6.33 us
    ppermute x1, waiting for transfers between devices, shards(): got = lax.ppermute(hidden_block((y + step) % n_rows), 'expert', turn(step))  6.29 us
  transfers between devices with their start and end apart: 32, of which 17 were waited for; matrix products, arithmetic and copies ran while one was open for 19% of the time, Pallas kernels for 0%

profile of v3, /device:TPU:0, one launch (start us, length us, event | category | flops | bytes accessed | tf_op | source)
XLA Modules:
  0.0 175.5 jit_solution(16562670679835997167)
XLA Ops:
  2.8 2.4 %collective-permute-start.2 = (f32[8,128]{1,0:T(8,128)S(1)}, f32[8,128]{1,0:T(8,128)S(1)}, u32[]{:S(2)}, u32[]{:S(2)}) collective-permute-start(f32[8,128]{1,0:T(8,128)S(1)} %bitcast.175), channel_id=1, source_target_pairs={{0,12},{4,0},{8,4},{12,8},{1,13},{5,1},{9,5},{13,9},{2,14},{6,2},{... | collective-permute-start | bytes 12296 | tf_op jit(solution)/shard_map/ppermute | solution.py:137
  6.0 1.4 collective-permute-start.3
  9.8 5.0 %all-to-all-start = ((bf16[16,32,256]{2,1,0:T(8,128)(2,1)}), bf16[16,32,256]{2,1,0:T(8,128)(2,1)S(1)}, u32[]{:S(2)}, u32[]{:S(2)}) async-start(bf16[16,32,256]{2,1,0:T(8,128)(2,1)} %broadcast_select_fusion), calls=%async_computation | async-start | bytes 524288 | tf_op jit(solution)/shard_map/all_to_all | solution.py:34
  16.1 1.9 %collective-permute-start.4 = (bf16[64,2048]{1,0:T(8,128)(2,1)S(1)}, bf16[64,2048]{1,0:T(8,128)(2,1)S(1)}, u32[]{:S(2)}, u32[]{:S(2)}) collective-permute-start(bf16[64,2048]{1,0:T(8,128)(2,1)S(1)} %dynamic_slice.152), channel_id=1, source_target_pairs={{0,8},{4,12},{8,0},{12,4},{1,9},{5,13},{9,1},{13,5},{2,10},{6,14},... | collective-permute-start | bytes 786440 | tf_op jit(solution)/shard_map/ppermute | solution.py:150
  20.4 6.3 %collective-permute-done.4 = bf16[64,2048]{1,0:T(8,128)(2,1)S(1)} collective-permute-done((bf16[64,2048]{1,0:T(8,128)(2,1)S(1)}, bf16[64,2048]{1,0:T(8,128)(2,1)S(1)}, u32[]{:S(2)}, u32[]{:S(2)}) %collective-permute-start.4) | collective-permute-done | bytes 262176 | tf_op jit(solution)/shard_map/ppermute | solution.py:150
  28.6 1.2 while.22
  30.1 1.8 %while.23 = (s32[]{:T(128)}, f32[128,8]{0,1:T(8,128)S(1)}, f32[128,8,128]{2,0,1:T(8,128)S(1)}, s32[]{:T(128)}, s32[]{:T(128)}, /*index=5*/bf16[128,8,128]{2,0,1:...) while((s32[]{:T(128)}, f32[128,8]{0,1:T(8,128)S(1)}, ...), condition=%wide.region_10.11_spmd, body=%wide.region_8.10_spmd.sunk | while | flops 271188992 | bytes 3691649 | solution.py:91
  32.4 1.2 collective-permute-start.5
  33.7 13.2 %copy.53 = bf16[512,8,2,768]{3,1,2,0:T(8,128)(2,1)} copy(bf16[512,8,2,768]{3,2,1,0:T(2,128)(2,1)} %bitcast.159) | data formatting | bytes 25165824
  47.2 1.2 copy-done.7
  49.1 2.3 %fusion.72 = f32[256,1024]{1,0:T(8,128)S(1)} fusion(bf16[1024,1024]{1,0:T(8,128)(2,1)} %collective-permute-done.3, bf16[64,1024]{1,0:T(8,128)(2,1)S(1)} %get-tuple-element.235, bf16[64,1024]{1,0:T(8,128)(2,1)S(1)} %get-tuple-element.236, bf16[64,1024]{1,0:T(8,128)(2,1)S(1)} %get-tuple-element.237, bf16[64,1024]{1,0:T(8,128)(2,1)S(1)} %get-tuple-element.234), kind=kOutput, calls=%fused_computation.169 | convolution fusion | flops 538968064 | bytes 3670016 | tf_op jit(solution)/shard_map/dot_general | solution.py:170
  51.6 2.9 %collective-permute-start.7 = (bf16[64,2048]{1,0:T(8,128)(2,1)S(1)}, bf16[64,2048]{1,0:T(8,128)(2,1)S(1)}, u32[]{:S(2)}, u32[]{:S(2)}) collective-permute-start(bf16[64,2048]{1,0:T(8,128)(2,1)S(1)} %pad_maximum_fusion.9), channel_id=1, source_target_pairs={{0,3},{1,0},{2,1},{3,2},{4,7},{5,4},{6,5},{7,6},{8,11},{9,8},{10,9... | collective-permute-start | bytes 786440 | tf_op jit(solution)/shard_map/ppermute | solution.py:181
  54.6 1.3 collective-permute-start.8
  56.0 5.2 %collective-permute-done.7 = bf16[64,2048]{1,0:T(8,128)(2,1)S(1)} collective-permute-done((bf16[64,2048]{1,0:T(8,128)(2,1)S(1)}, bf16[64,2048]{1,0:T(8,128)(2,1)S(1)}, u32[]{:S(2)}, u32[]{:S(2)}) %collective-permute-start.7) | collective-permute-done | bytes 262176 | tf_op jit(solution)/shard_map/ppermute | solution.py:181
  61.3 6.9 %collective-permute-done.6 = bf16[64,2048]{1,0:T(8,128)(2,1)S(1)} collective-permute-done((bf16[64,2048]{1,0:T(8,128)(2,1)S(1)}, bf16[64,2048]{1,0:T(8,128)(2,1)S(1)}, u32[]{:S(2)}, u32[]{:S(2)}) %collective-permute-start.6) | collective-permute-done | bytes 262176 | tf_op jit(solution)/shard_map/ppermute | solution.py:181
  68.2 9.0 %collective-permute-done.8 = bf16[64,2048]{1,0:T(8,128)(2,1)S(1)} collective-permute-done((bf16[64,2048]{1,0:T(8,128)(2,1)S(1)}, bf16[64,2048]{1,0:T(8,128)(2,1)S(1)}, u32[]{:S(2)}, u32[]{:S(2)}) %collective-permute-start.8) | collective-permute-done | bytes 262176 | tf_op jit(solution)/shard_map/ppermute | solution.py:181
  77.7 3.6 %collective-permute-start.16 = (bf16[64,2048]{1,0:T(8,128)(2,1)S(1)}, bf16[64,2048]{1,0:T(8,128)(2,1)S(1)}, u32[]{:S(2)}, u32[]{:S(2)}) collective-permute-start(bf16[64,2048]{1,0:T(8,128)(2,1)S(1)} %fusion.58), channel_id=1, source_target_pairs={{0,3},{1,0},{2,1},{3,2},{4,7},{5,4},{6,5},{7,6},{8,11},{9,8},{10,9... | collective-permute-start | bytes 786440 | tf_op jit(solution)/shard_map/ppermute | solution.py:198
  82.8 5.7 %collective-permute-done.10 = bf16[64,2048]{1,0:T(8,128)(2,1)S(1)} collective-permute-done((bf16[64,2048]{1,0:T(8,128)(2,1)S(1)}, bf16[64,2048]{1,0:T(8,128)(2,1)S(1)}, u32[]{:S(2)}, u32[]{:S(2)}) %collective-permute-start.10) | collective-permute-done | bytes 262176 | tf_op jit(solution)/shard_map/ppermute | solution.py:198
  91.6 5.1 %collective-permute-done.11 = bf16[64,2048]{1,0:T(8,128)(2,1)S(1)} collective-permute-done((bf16[64,2048]{1,0:T(8,128)(2,1)S(1)}, bf16[64,2048]{1,0:T(8,128)(2,1)S(1)}, u32[]{:S(2)}, u32[]{:S(2)}) %collective-permute-start.11) | collective-permute-done | bytes 262176 | tf_op jit(solution)/shard_map/ppermute | solution.py:206
  97.0 2.5 %collective-permute-done.17 = bf16[64,2048]{1,0:T(8,128)(2,1)S(1)} collective-permute-done((bf16[64,2048]{1,0:T(8,128)(2,1)S(1)}, bf16[64,2048]{1,0:T(8,128)(2,1)S(1)}, u32[]{:S(2)}, u32[]{:S(2)}) %collective-permute-start.17) | collective-permute-done | bytes 262176 | tf_op jit(solution)/shard_map/ppermute | solution.py:206
  100.8 2.5 %collective-permute-start.12 = (bf16[64,2048]{1,0:T(8,128)(2,1)S(1)}, bf16[64,2048]{1,0:T(8,128)(2,1)S(1)}, u32[]{:S(2)}, u32[]{:S(2)}) collective-permute-start(bf16[64,2048]{1,0:T(8,128)(2,1)S(1)} %fusion.58), channel_id=1, source_target_pairs={{0,2},{1,3},{2,0},{3,1},{4,6},{5,7},{6,4},{7,5},{8,10},{9,11},{10,... | collective-permute-start | bytes 786440 | tf_op jit(solution)/shard_map/ppermute | solution.py:198
  103.4 12.3 %collective-permute-done.12 = bf16[64,2048]{1,0:T(8,128)(2,1)S(1)} collective-permute-done((bf16[64,2048]{1,0:T(8,128)(2,1)S(1)}, bf16[64,2048]{1,0:T(8,128)(2,1)S(1)}, u32[]{:S(2)}, u32[]{:S(2)}) %collective-permute-start.12) | collective-permute-done | bytes 262176 | tf_op jit(solution)/shard_map/ppermute | solution.py:198
  116.8 6.4 %fusion.4 = f32[256,1536]{1,0:T(8,128)S(1)} fusion(bf16[4096,1536]{1,0:T(8,128)(2,1)} %bitcast.160, bf16[64,4096]{1,0:T(8,128)(2,1)S(1)} %collective-permute-done.15, bf16[64,4096]{1,0:T(8,128)(2,1)S(1)} %collective-permute-done.14, bf16[64,4096]{1,0:T(8,128)(2,1)S(1)} %get-tuple-element.249, bf16[64,4096]{1,0:T(8,128)(2,1)S(1)} %get-tuple-element.250), kind=kOutput, calls=%fused_computation.11 | convolution fusion | flops 3229614080 | bytes 16252928 | tf_op jit(solution)/shard_map/dot_general | solution.py:234
  125.3 1.6 collective-permute-done.19
  126.8 6.9 %fusion.12 = f32[256,1536]{1,0:T(8,128)S(1)} fusion(bf16[4096,1536]{1,0:T(8,128)(2,1)} %bitcast.161, bf16[64,4096]{1,0:T(8,128)(2,1)} %collective-permute-done.19, bf16[64,4096]{1,0:T(8,128)(2,1)} %collective-permute-done.18, bf16[64,4096]{1,0:T(8,128)(2,1)S(1)} %fusion.45, bf16[64,4096]{1,0:T(8,128)(2,1)S(1)} %get-tuple-element.248), kind=kOutput, calls=%fused_computation.19 | convolution fusion | flops 3229614080 | bytes 16252928 | tf_op jit(solution)/shard_map/dot_general | solution.py:234
  144.6 4.3 %collective-permute-done.21 = bf16[128,1024]{1,0:T(8,128)(2,1)S(1)} collective-permute-done((bf16[128,1024]{1,0:T(8,128)(2,1)S(1)}, bf16[128,1024]{1,0:T(8,128)(2,1)S(1)}, u32[]{:S(2)}, u32[]{:S(2)}) %collective-permute-start.21) | collective-permute-done | bytes 262176 | tf_op jit(solution)/shard_map/ppermute | solution.py:274
  149.0 4.9 %collective-permute-done.24 = bf16[128,1024]{1,0:T(8,128)(2,1)S(1)} collective-permute-done((bf16[128,1024]{1,0:T(8,128)(2,1)S(1)}, bf16[128,1024]{1,0:T(8,128)(2,1)S(1)}, u32[]{:S(2)}, u32[]{:S(2)}) %collective-permute-start.24) | collective-permute-done | bytes 262176 | tf_op jit(solution)/shard_map/ppermute | solution.py:274
  154.0 2.8 %collective-permute-start.25 = (bf16[128,1024]{1,0:T(8,128)(2,1)S(1)}, bf16[128,1024]{1,0:T(8,128)(2,1)S(1)}, u32[]{:S(2)}, u32[]{:S(2)}) collective-permute-start(bf16[128,1024]{1,0:T(8,128)(2,1)S(1)} %fusion.53), channel_id=1, source_target_pairs={{0,3},{1,0},{2,1},{3,2},{4,7},{5,4},{6,5},{7,6},{8,11},{9,8},{10,9... | collective-permute-start | bytes 786440 | tf_op jit(solution)/shard_map/ppermute | solution.py:276
  158.2 1.2 collective-permute-start.30
  159.4 6.9 %collective-permute-done.27 = bf16[128,1024]{1,0:T(8,128)(2,1)S(1)} collective-permute-done((bf16[128,1024]{1,0:T(8,128)(2,1)S(1)}, bf16[128,1024]{1,0:T(8,128)(2,1)S(1)}, u32[]{:S(2)}, u32[]{:S(2)}) %collective-permute-start.27) | collective-permute-done | bytes 262176 | tf_op jit(solution)/shard_map/ppermute | solution.py:274
  167.2 2.9 %collective-permute-done.30 = bf16[128,1024]{1,0:T(8,128)(2,1)S(1)} collective-permute-done((bf16[128,1024]{1,0:T(8,128)(2,1)S(1)}, bf16[128,1024]{1,0:T(8,128)(2,1)S(1)}, u32[]{:S(2)}, u32[]{:S(2)}) %collective-permute-start.30) | collective-permute-done | bytes 262176 | tf_op jit(solution)/shard_map/ppermute | solution.py:274
  170.1 4.5 %collective-permute-done.28 = bf16[128,1024]{1,0:T(8,128)(2,1)S(1)} collective-permute-done((bf16[128,1024]{1,0:T(8,128)(2,1)S(1)}, bf16[128,1024]{1,0:T(8,128)(2,1)S(1)}, u32[]{:S(2)}, u32[]{:S(2)}) %collective-permute-start.28) | collective-permute-done | bytes 262176 | tf_op jit(solution)/shard_map/ppermute | solution.py:276
  (186 shorter events, 38.6 us)
Async XLA Ops:
  2.8 25.0 %collective-permute-start.2 = (f32[8,128]{1,0:T(8,128)S(1)}, f32[8,128]{1,0:T(8,128)S(1)}, u32[]{:S(2)}, u32[]{:S(2)}) collective-permute-start(f32[8,128]{1,0:T(8,128)S(1)} %bitcast.175), channel_id=1, source_target_pairs={{0,12},{4,0},{8,4},{12,8},{1,13},{5,1},{9,5},{13,9},{2,14},{6,2},{... | collective-permute-start | bytes 12296 | tf_op jit(solution)/shard_map/ppermute | solution.py:137
  5.2 22.6 %collective-permute-start.1 = (f32[8,128]{1,0:T(8,128)S(1)}, f32[8,128]{1,0:T(8,128)S(1)}, u32[]{:S(2)}, u32[]{:S(2)}) collective-permute-start(f32[8,128]{1,0:T(8,128)S(1)} %bitcast.176), channel_id=1, source_target_pairs={{0,8},{4,12},{8,0},{12,4},{1,9},{5,13},{9,1},{13,5},{2,10},{6,14},... | collective-permute-start | bytes 12296 | tf_op jit(solution)/shard_map/ppermute | solution.py:137
  5.9 22.0 %collective-permute-start = (f32[8,128]{1,0:T(8,128)S(1)}, f32[8,128]{1,0:T(8,128)S(1)}, u32[]{:S(2)}, u32[]{:S(2)}) collective-permute-start(f32[8,128]{1,0:T(8,128)S(1)} %bitcast.177), channel_id=1, source_target_pairs={{0,4},{4,8},{8,12},{12,0},{1,5},{5,9},{9,13},{13,1},{2,6},{6,10},{... | collective-permute-start | bytes 12296 | tf_op jit(solution)/shard_map/ppermute | solution.py:137
  6.0 21.8 %collective-permute-start.3 = (bf16[1024,1024]{1,0:T(8,128)(2,1)}, bf16[1024,1024]{1,0:T(8,128)(2,1)}, u32[]{:S(2)}, u32[]{:S(2)}) collective-permute-start(bf16[1024,1024]{1,0:T(8,128)(2,1)} %param.22), channel_id=1, source_target_pairs={{0,4},{4,0},{8,12},{12,8},{1,5},{5,1},{9,13},{13,9},{2,6},{6,2},{1... | collective-permute-start | bytes 6291464 | tf_op jit(solution)/shard_map/ppermute | solution.py:140
  9.8 18.0 %all-to-all-start = ((bf16[16,32,256]{2,1,0:T(8,128)(2,1)}), bf16[16,32,256]{2,1,0:T(8,128)(2,1)S(1)}, u32[]{:S(2)}, u32[]{:S(2)}) async-start(bf16[16,32,256]{2,1,0:T(8,128)(2,1)} %broadcast_select_fusion), calls=%async_computation | async-start | bytes 524288 | tf_op jit(solution)/shard_map/all_to_all | solution.py:34
  16.1 10.6 %collective-permute-start.4 = (bf16[64,2048]{1,0:T(8,128)(2,1)S(1)}, bf16[64,2048]{1,0:T(8,128)(2,1)S(1)}, u32[]{:S(2)}, u32[]{:S(2)}) collective-permute-start(bf16[64,2048]{1,0:T(8,128)(2,1)S(1)} %dynamic_slice.152), channel_id=1, source_target_pairs={{0,8},{4,12},{8,0},{12,4},{1,9},{5,13},{9,1},{13,5},{2,10},{6,14},... | collective-permute-start | bytes 786440 | tf_op jit(solution)/shard_map/ppermute | solution.py:150
  32.4 14.7 %collective-permute-start.5 = (bf16[128,1024]{1,0:T(8,128)(2,1)S(1)}, bf16[128,1024]{1,0:T(8,128)(2,1)S(1)}, u32[]{:S(2)}, u32[]{:S(2)}) collective-permute-start(bf16[128,1024]{1,0:T(8,128)(2,1)S(1)} %copy.48), channel_id=1, source_target_pairs={{0,8},{4,12},{8,0},{12,4},{1,9},{5,13},{9,1},{13,5},{2,10},{6,14},... | collective-permute-start | bytes 786440 | tf_op jit(solution)/shard_map/ppermute | solution.py:165
  51.6 9.7 %collective-permute-start.7 = (bf16[64,2048]{1,0:T(8,128)(2,1)S(1)}, bf16[64,2048]{1,0:T(8,128)(2,1)S(1)}, u32[]{:S(2)}, u32[]{:S(2)}) collective-permute-start(bf16[64,2048]{1,0:T(8,128)(2,1)S(1)} %pad_maximum_fusion.9), channel_id=1, source_target_pairs={{0,3},{1,0},{2,1},{3,2},{4,7},{5,4},{6,5},{7,6},{8,11},{9,8},{10,9... | collective-permute-start | bytes 786440 | tf_op jit(solution)/shard_map/ppermute | solution.py:181
  54.5 13.6 %collective-permute-start.6 = (bf16[64,2048]{1,0:T(8,128)(2,1)S(1)}, bf16[64,2048]{1,0:T(8,128)(2,1)S(1)}, u32[]{:S(2)}, u32[]{:S(2)}) collective-permute-start(bf16[64,2048]{1,0:T(8,128)(2,1)S(1)} %pad_maximum_fusion.8), channel_id=1, source_target_pairs={{0,1},{1,2},{2,3},{3,0},{4,5},{5,6},{6,7},{7,4},{8,9},{9,10},{10,1... | collective-permute-start | bytes 786440 | tf_op jit(solution)/shard_map/ppermute | solution.py:181
  54.6 22.6 %collective-permute-start.8 = (bf16[64,2048]{1,0:T(8,128)(2,1)S(1)}, bf16[64,2048]{1,0:T(8,128)(2,1)S(1)}, u32[]{:S(2)}, u32[]{:S(2)}) collective-permute-start(bf16[64,2048]{1,0:T(8,128)(2,1)S(1)} %pad_maximum_fusion.10), channel_id=1, source_target_pairs={{0,2},{1,3},{2,0},{3,1},{4,6},{5,7},{6,4},{7,5},{8,10},{9,11},{10,... | collective-permute-start | bytes 786440 | tf_op jit(solution)/shard_map/ppermute | solution.py:181
  77.4 11.1 %collective-permute-start.10 = (bf16[64,2048]{1,0:T(8,128)(2,1)S(1)}, bf16[64,2048]{1,0:T(8,128)(2,1)S(1)}, u32[]{:S(2)}, u32[]{:S(2)}) collective-permute-start(bf16[64,2048]{1,0:T(8,128)(2,1)S(1)} %fusion.58), channel_id=1, source_target_pairs={{0,1},{1,2},{2,3},{3,0},{4,5},{5,6},{6,7},{7,4},{8,9},{9,10},{10,1... | collective-permute-start | bytes 786440 | tf_op jit(solution)/shard_map/ppermute | solution.py:198
  77.7 12.5 %collective-permute-start.16 = (bf16[64,2048]{1,0:T(8,128)(2,1)S(1)}, bf16[64,2048]{1,0:T(8,128)(2,1)S(1)}, u32[]{:S(2)}, u32[]{:S(2)}) collective-permute-start(bf16[64,2048]{1,0:T(8,128)(2,1)S(1)} %fusion.58), channel_id=1, source_target_pairs={{0,3},{1,0},{2,1},{3,2},{4,7},{5,4},{6,5},{7,6},{8,11},{9,8},{10,9... | collective-permute-start | bytes 786440 | tf_op jit(solution)/shard_map/ppermute | solution.py:198
  81.3 10.0 %collective-permute-start.9 = (bf16[64,2048]{1,0:T(8,128)(2,1)S(1)}, bf16[64,2048]{1,0:T(8,128)(2,1)S(1)}, u32[]{:S(2)}, u32[]{:S(2)}) collective-permute-start(bf16[64,2048]{1,0:T(8,128)(2,1)S(1)} %fusion.58), channel_id=1, source_target_pairs={{0,8},{4,12},{8,0},{12,4},{1,9},{5,13},{9,1},{13,5},{2,10},{6,14},... | collective-permute-start | bytes 786440 | tf_op jit(solution)/shard_map/ppermute | solution.py:206
  88.5 8.2 %collective-permute-start.11 = (bf16[64,2048]{1,0:T(8,128)(2,1)S(1)}, bf16[64,2048]{1,0:T(8,128)(2,1)S(1)}, u32[]{:S(2)}, u32[]{:S(2)}) collective-permute-start(bf16[64,2048]{1,0:T(8,128)(2,1)S(1)} %collective-permute-done.10), channel_id=1, source_target_pairs={{0,8},{4,12},{8,0},{12,4},{1,9},{5,13},{9,1},{13,5},{2,10},{6,14},... | collective-permute-start | bytes 786440 | tf_op jit(solution)/shard_map/ppermute | solution.py:206
  90.2 9.3 %collective-permute-start.17 = (bf16[64,2048]{1,0:T(8,128)(2,1)S(1)}, bf16[64,2048]{1,0:T(8,128)(2,1)S(1)}, u32[]{:S(2)}, u32[]{:S(2)}) collective-permute-start(bf16[64,2048]{1,0:T(8,128)(2,1)S(1)} %collective-permute-done.16), channel_id=1, source_target_pairs={{0,8},{4,12},{8,0},{12,4},{1,9},{5,13},{9,1},{13,5},{2,10},{6,14},... | collective-permute-start | bytes 786440 | tf_op jit(solution)/shard_map/ppermute | solution.py:206
  100.2 16.5 %collective-permute-start.15 = (bf16[64,4096]{1,0:T(8,128)(2,1)S(1)}, bf16[64,4096]{1,0:T(8,128)(2,1)S(1)}, u32[]{:S(2)}, u32[]{:S(2)}) collective-permute-start(bf16[64,4096]{1,0:T(8,128)(2,1)S(1)} %get-tuple-element.249), channel_id=1, source_target_pairs={{0,4},{4,0},{8,12},{12,8},{1,5},{5,1},{9,13},{13,9},{2,6},{6,2},{1... | collective-permute-start | bytes 1572872 | tf_op jit(solution)/shard_map/ppermute | solution.py:229
  100.3 16.5 %collective-permute-start.14 = (bf16[64,4096]{1,0:T(8,128)(2,1)S(1)}, bf16[64,4096]{1,0:T(8,128)(2,1)S(1)}, u32[]{:S(2)}, u32[]{:S(2)}) collective-permute-start(bf16[64,4096]{1,0:T(8,128)(2,1)S(1)} %get-tuple-element.250), channel_id=1, source_target_pairs={{0,4},{4,0},{8,12},{12,8},{1,5},{5,1},{9,13},{13,9},{2,6},{6,2},{1... | collective-permute-start | bytes 1572872 | tf_op jit(solution)/shard_map/ppermute | solution.py:229
  100.8 14.9 %collective-permute-start.12 = (bf16[64,2048]{1,0:T(8,128)(2,1)S(1)}, bf16[64,2048]{1,0:T(8,128)(2,1)S(1)}, u32[]{:S(2)}, u32[]{:S(2)}) collective-permute-start(bf16[64,2048]{1,0:T(8,128)(2,1)S(1)} %fusion.58), channel_id=1, source_target_pairs={{0,2},{1,3},{2,0},{3,1},{4,6},{5,7},{6,4},{7,5},{8,10},{9,11},{10,... | collective-permute-start | bytes 786440 | tf_op jit(solution)/shard_map/ppermute | solution.py:198
  115.7 8.4 %collective-permute-start.13 = (bf16[64,2048]{1,0:T(8,128)(2,1)S(1)}, bf16[64,2048]{1,0:T(8,128)(2,1)S(1)}, u32[]{:S(2)}, u32[]{:S(2)}) collective-permute-start(bf16[64,2048]{1,0:T(8,128)(2,1)S(1)} %collective-permute-done.12), channel_id=1, source_target_pairs={{0,8},{4,12},{8,0},{12,4},{1,9},{5,13},{9,1},{13,5},{2,10},{6,14},... | collective-permute-start | bytes 786440 | tf_op jit(solution)/shard_map/ppermute | solution.py:206
  116.7 8.5 %collective-permute-start.18 = (bf16[64,4096]{1,0:T(8,128)(2,1)S(1)}, bf16[64,4096]{1,0:T(8,128)(2,1)}, u32[]{:S(2)}, u32[]{:S(2)}) collective-permute-start(bf16[64,4096]{1,0:T(8,128)(2,1)S(1)} %get-tuple-element.248), channel_id=1, source_target_pairs={{0,4},{4,0},{8,12},{12,8},{1,5},{5,1},{9,13},{13,9},{2,6},{6,2},{1... | collective-permute-start | bytes 1572872 | tf_op jit(solution)/shard_map/ppermute | solution.py:229
  124.6 2.2 %collective-permute-start.19 = (bf16[64,4096]{1,0:T(8,128)(2,1)S(1)}, bf16[64,4096]{1,0:T(8,128)(2,1)}, u32[]{:S(2)}, u32[]{:S(2)}) collective-permute-start(bf16[64,4096]{1,0:T(8,128)(2,1)S(1)} %fusion.45), channel_id=1, source_target_pairs={{0,4},{4,0},{8,12},{12,8},{1,5},{5,1},{9,13},{13,9},{2,6},{6,2},{1... | collective-permute-start | bytes 1572872 | tf_op jit(solution)/shard_map/ppermute | solution.py:229
  136.1 2.0 %collective-permute-start.20 = (bf16[256,1024]{1,0:T(8,128)(2,1)S(1)}, bf16[256,1024]{1,0:T(8,128)(2,1)S(1)}, u32[]{:S(2)}, u32[]{:S(2)}) collective-permute-start(bf16[256,1024]{1,0:T(8,128)(2,1)S(1)} %slice.289), channel_id=1, source_target_pairs={{0,4},{4,0},{8,12},{12,8},{1,5},{5,1},{9,13},{13,9},{2,6},{6,2},{1... | collective-permute-start | bytes 1572872 | tf_op jit(solution)/shard_map/ppermute | solution.py:266
  137.4 2.0 %collective-permute-start.23 = (bf16[256,1024]{1,0:T(8,128)(2,1)S(1)}, bf16[256,1024]{1,0:T(8,128)(2,1)S(1)}, u32[]{:S(2)}, u32[]{:S(2)}) collective-permute-start(bf16[256,1024]{1,0:T(8,128)(2,1)S(1)} %slice.288), channel_id=1, source_target_pairs={{0,4},{4,0},{8,12},{12,8},{1,5},{5,1},{9,13},{13,9},{2,6},{6,2},{1... | collective-permute-start | bytes 1572872 | tf_op jit(solution)/shard_map/ppermute | solution.py:266
  139.7 9.2 %collective-permute-start.21 = (bf16[128,1024]{1,0:T(8,128)(2,1)S(1)}, bf16[128,1024]{1,0:T(8,128)(2,1)S(1)}, u32[]{:S(2)}, u32[]{:S(2)}) collective-permute-start(bf16[128,1024]{1,0:T(8,128)(2,1)S(1)} %slice.293), channel_id=1, source_target_pairs={{0,8},{4,12},{8,0},{12,4},{1,9},{5,13},{9,1},{13,5},{2,10},{6,14},... | collective-permute-start | bytes 786440 | tf_op jit(solution)/shard_map/ppermute | solution.py:274
  140.7 13.2 %collective-permute-start.24 = (bf16[128,1024]{1,0:T(8,128)(2,1)S(1)}, bf16[128,1024]{1,0:T(8,128)(2,1)S(1)}, u32[]{:S(2)}, u32[]{:S(2)}) collective-permute-start(bf16[128,1024]{1,0:T(8,128)(2,1)S(1)} %slice.292), channel_id=1, source_target_pairs={{0,8},{4,12},{8,0},{12,4},{1,9},{5,13},{9,1},{13,5},{2,10},{6,14},... | collective-permute-start | bytes 786440 | tf_op jit(solution)/shard_map/ppermute | solution.py:274
  142.8 13.9 %collective-permute-start.26 = (bf16[256,1024]{1,0:T(8,128)(2,1)S(1)}, bf16[256,1024]{1,0:T(8,128)(2,1)S(1)}, u32[]{:S(2)}, u32[]{:S(2)}) collective-permute-start(bf16[256,1024]{1,0:T(8,128)(2,1)S(1)} %slice.287), channel_id=1, source_target_pairs={{0,4},{4,0},{8,12},{12,8},{1,5},{5,1},{9,13},{13,9},{2,6},{6,2},{1... | collective-permute-start | bytes 1572872 | tf_op jit(solution)/shard_map/ppermute | solution.py:266
  144.0 13.9 %collective-permute-start.29 = (bf16[256,1024]{1,0:T(8,128)(2,1)S(1)}, bf16[256,1024]{1,0:T(8,128)(2,1)S(1)}, u32[]{:S(2)}, u32[]{:S(2)}) collective-permute-start(bf16[256,1024]{1,0:T(8,128)(2,1)S(1)} %slice.286), channel_id=1, source_target_pairs={{0,4},{4,0},{8,12},{12,8},{1,5},{5,1},{9,13},{13,9},{2,6},{6,2},{1... | collective-permute-start | bytes 1572872 | tf_op jit(solution)/shard_map/ppermute | solution.py:266
  148.9 17.7 %collective-permute-start.22 = (bf16[128,1024]{1,0:T(8,128)(2,1)S(1)}, bf16[128,1024]{1,0:T(8,128)(2,1)S(1)}, u32[]{:S(2)}, u32[]{:S(2)}) collective-permute-start(bf16[128,1024]{1,0:T(8,128)(2,1)S(1)} %fusion.54), channel_id=1, source_target_pairs={{0,2},{1,3},{2,0},{3,1},{4,6},{5,7},{6,4},{7,5},{8,10},{9,11},{10,... | collective-permute-start | bytes 786440 | tf_op jit(solution)/shard_map/ppermute | solution.py:276
  154.0 13.2 %collective-permute-start.25 = (bf16[128,1024]{1,0:T(8,128)(2,1)S(1)}, bf16[128,1024]{1,0:T(8,128)(2,1)S(1)}, u32[]{:S(2)}, u32[]{:S(2)}) collective-permute-start(bf16[128,1024]{1,0:T(8,128)(2,1)S(1)} %fusion.53), channel_id=1, source_target_pairs={{0,3},{1,0},{2,1},{3,2},{4,7},{5,4},{6,5},{7,6},{8,11},{9,8},{10,9... | collective-permute-start | bytes 786440 | tf_op jit(solution)/shard_map/ppermute | solution.py:276
  157.0 9.3 %collective-permute-start.27 = (bf16[128,1024]{1,0:T(8,128)(2,1)S(1)}, bf16[128,1024]{1,0:T(8,128)(2,1)S(1)}, u32[]{:S(2)}, u32[]{:S(2)}) collective-permute-start(bf16[128,1024]{1,0:T(8,128)(2,1)S(1)} %slice.291), channel_id=1, source_target_pairs={{0,8},{4,12},{8,0},{12,4},{1,9},{5,13},{9,1},{13,5},{2,10},{6,14},... | collective-permute-start | bytes 786440 | tf_op jit(solution)/shard_map/ppermute | solution.py:274
  158.2 11.9 %collective-permute-start.30 = (bf16[128,1024]{1,0:T(8,128)(2,1)S(1)}, bf16[128,1024]{1,0:T(8,128)(2,1)S(1)}, u32[]{:S(2)}, u32[]{:S(2)}) collective-permute-start(bf16[128,1024]{1,0:T(8,128)(2,1)S(1)} %slice.290), channel_id=1, source_target_pairs={{0,8},{4,12},{8,0},{12,4},{1,9},{5,13},{9,1},{13,5},{2,10},{6,14},... | collective-permute-start | bytes 786440 | tf_op jit(solution)/shard_map/ppermute | solution.py:274
  166.3 8.2 %collective-permute-start.28 = (bf16[128,1024]{1,0:T(8,128)(2,1)S(1)}, bf16[128,1024]{1,0:T(8,128)(2,1)S(1)}, u32[]{:S(2)}, u32[]{:S(2)}) collective-permute-start(bf16[128,1024]{1,0:T(8,128)(2,1)S(1)} %fusion.52), channel_id=1, source_target_pairs={{0,1},{1,2},{2,3},{3,0},{4,5},{5,6},{6,7},{7,4},{8,9},{9,10},{10,1... | collective-permute-start | bytes 786440 | tf_op jit(solution)/shard_map/ppermute | solution.py:276
  (11 other events, 108.1 us)

commit v4 on v3

--- a/solution.py
+++ b/solution.py
@@ -12,7 +12,7 @@
     return lax.dynamic_index_in_dim(array, index, axis, keepdims=False)
 
 
-def attention(queries, suffix_kv, kv_pool, page_table, prefix_len, early):
+def attention(queries, suffix_kv, kv_pool, page_table, prefix_len):
     n_expert = lax.axis_size("expert")
     n_donor = lax.axis_size("donor")
     expert_index = lax.axis_index("expert")
@@ -32,7 +32,6 @@
         kv_pool.reshape(seq_count * kv_heads, page_len, 2 * head_dim), wanted, axis=0
     )
     arrived = lax.all_to_all(outgoing, ("expert", "donor"), split_axis=0, concat_axis=0, tiled=True)
-    arrived, early = lax.optimization_barrier((arrived, early))
     my_owners = lax.dynamic_index_in_dim(owner_of, expert_index, 0, keepdims=False)
     ordered = jnp.take(arrived, my_owners, axis=0).reshape(page_count * page_len, 2 * head_dim)
     prefix_keys = ordered[:, :head_dim]
@@ -89,7 +88,7 @@
         ),
     )
     row_total, weighted = lax.fori_loop(0, live_blocks, add_block, start_state)
-    return (weighted / row_total[:, :, None]).astype(jnp.bfloat16).reshape(suffix_len, -1), early
+    return (weighted / row_total[:, :, None]).astype(jnp.bfloat16).reshape(suffix_len, -1)
 
 
 def shards(
@@ -150,19 +149,13 @@
         got = lax.ppermute(hidden_block((y + step) % n_rows), "expert", turn(step))
         hidden_part = jnp.where((y - step) % n_rows == part_owner, got, hidden_part)
 
-    head_out, (tables, other_weight, hidden_part) = attention(
-        queries,
-        suffix_kv,
-        kv_pool,
-        page_table,
-        prefix_len,
-        (tables, other_weight, hidden_part),
-    )
+    head_out = attention(queries, suffix_kv, kv_pool, page_table, prefix_len)
 
     heads = jnp.zeros((n_rows, suffix_len, head_out.shape[1]), bf16)
     heads = lax.dynamic_update_index_in_dim(heads, head_out, y, 0)
     for step in range(1, n_rows):
         got = lax.ppermute(head_out, "expert", turn(step))
+        got, tables = lax.optimization_barrier((got, tables))
         heads = lax.dynamic_update_index_in_dim(heads, got, (y - step) % n_rows, 0)
     heads = heads.reshape(n_donor, part_rows, -1)
     heads = jnp.concatenate([pick(heads, (z + step) % n_donor) for step in range(n_donor)])
@@ -176,6 +169,9 @@
             [jnp.where(core == 0, own, other), jnp.where(core == 0, other, own)], axis=1
         )
 
+    own_terms, other_terms, w_gate_up = lax.optimization_barrier(
+        (own_terms, other_terms, w_gate_up)
+    )
     gate_up_weight = w_gate_up[0].reshape(model_width, 2 * ff_local)
     gots = [
         lax.ppermute(term(step).astype(bf16), "donor", rotation(n_donor, step)) for step in steps
@@ -195,29 +191,28 @@
     own_gates, other_gates = core_gates(core), core_gates(1 - core)
 
     gain_f = norm_gain.astype(f32)
-    chunks = [chunk] + [lax.ppermute(chunk, "donor", rotation(n_donor, step)) for step in steps]
-    slots = [0] + steps
     resid_parts = [None] * n_donor
     own_act, other_act = [None] * n_donor, [None] * n_donor
     batch = max(1, n_donor // 2)
     own_rows, other_rows, row_gates = [], [], []
-    for place, (slot, chunk) in enumerate(zip(slots, chunks)):
+    for slot in range(n_donor):
         part = (z - slot) % n_donor
         gots = [lax.ppermute(chunk, "expert", turn(hop)) for hop in range(1, n_rows)]
-        if place == n_donor - 1 and place >= batch and gots:
-            early = [slots[i] for i in range(batch)]
-            gots, acts = lax.optimization_barrier(
-                (gots, [(own_act[i], other_act[i]) for i in early])
+        here = chunk
+        if slot < n_donor - 1:
+            chunk = lax.ppermute(chunk, "donor", rotation(n_donor, 1))
+            chunk, gots = lax.optimization_barrier((chunk, gots))
+        if slot == n_donor - 1 and slot >= batch:
+            gots, own_act[:batch], other_act[:batch] = lax.optimization_barrier(
+                (gots, own_act[:batch], other_act[:batch])
             )
-            for i, pair in zip(early, acts):
-                own_act[i], other_act[i] = pair
         if n_rows == 2:
             block = jnp.concatenate(
-                [jnp.where(y == 0, chunk, gots[0]), jnp.where(y == 0, gots[0], chunk)], axis=1
+                [jnp.where(y == 0, here, gots[0]), jnp.where(y == 0, gots[0], here)], axis=1
             )
         else:
             block = jnp.zeros((part_rows, n_rows, pair_cols), bf16)
-            block = lax.dynamic_update_index_in_dim(block, chunk, y, 1)
+            block = lax.dynamic_update_index_in_dim(block, here, y, 1)
             for hop, got in enumerate(gots, 1):
                 block = lax.dynamic_update_index_in_dim(block, got, (y - hop) % n_rows, 1)
             block = block.reshape(part_rows, model_width)
@@ -235,8 +230,8 @@
             act = jax.nn.silu(gate_up[:, :ff_local]) * gate_up[:, ff_local:]
             act = (act * scale[:, None]).astype(bf16).reshape(2, batch, part_rows, ff_local)
             for i in range(batch):
-                own_act[slots[place - batch + 1 + i]] = act[0, i]
-                other_act[slots[place - batch + 1 + i]] = act[1, i]
+                own_act[slot - batch + 1 + i] = act[0, i]
+                other_act[slot - batch + 1 + i] = act[1, i]
             own_rows, other_rows, row_gates = [], [], []
 
     def by_sequence(parts, rows):
@@ -265,13 +260,22 @@
         mixed = jnp.dot(act_rows, down, preferred_element_type=f32)
         swapped.append(lax.ppermute(mixed[:half_rows].astype(bf16), "expert", swap))
         kept.append(mixed[half_rows:])
+    pending = []
+    for place in range(n_donor):
+        pair_sum = (kept[place] + swapped[place].astype(f32)).reshape(n_rows, suffix_len, columns)
+        arriving = [
+            lax.ppermute(pair_sum[hop].astype(bf16), "expert", turn(hop)) for hop in range(1, n_rows)
+        ]
+        pending.append((pair_sum[0], arriving))
+    first = pending[0][0]
+    first, swapped[-1] = lax.optimization_barrier((first, swapped[-1]))
     total = resid
     for place, step in enumerate(order):
-        pair_sum = (kept[place] + swapped[place].astype(f32)).reshape(n_rows, suffix_len, columns)
-        part_sum = pair_sum[0]
-        for hop in range(1, n_rows):
-            sent = pair_sum[hop].astype(bf16)
-            part_sum = part_sum + lax.ppermute(sent, "expert", turn(hop)).astype(f32)
+        part_sum, arriving = pending[place]
+        if place == 0:
+            part_sum = first
+        for got in arriving:
+            part_sum = part_sum + got.astype(f32)
         if step:
             part_sum = lax.ppermute(part_sum.astype(bf16), "donor", rotation(n_donor, step))
         total = total + part_sum.astype(f32)

time: 176 us -> 156 us (0.89)
  starting transfers between devices: 37.4 us -> 26.6 us
  waiting for transfers between devices: 80.5 us -> 75.7 us
  other arithmetic: 11.6 us -> 8.53 us
    ppermute x3, waiting for transfers between devices: 21.2 us -> 9.41 us  [shards(): lax.ppermute(term(step).astype(bf16), 'donor', rotation(n_donor, step))]
    ppermute x7, waiting for transfers between devices: 37.6 us -> 26 us  [the longest x4 17.6 us: shards(): lax.ppermute(pair_sum[hop].astype(bf16), 'expert', turn(hop))]
    ppermute x4, waiting for transfers between devices: 7.69 us -> 16.8 us  [shards(): lax.ppermute(chunk, 'expert', turn(hop))]
    ppermute x1, waiting for transfers between devices: 6.29 us -> 0.01 us  [shards(): got = lax.ppermute(hidden_block((y + step) % n_rows), 'expert', turn(step))]
    ppermute x7, starting transfers between devices: 10.6 us -> 4.66 us  [the longest x4 4.25 us: shards(): lax.ppermute(pair_sum[hop].astype(bf16), 'expert', turn(hop))]
    all_to_all x1, waiting for transfers between devices: 0.01 us -> 5.8 us  [attention(): lax.all_to_all(outgoing, ('expert', 'donor'), split_axis=0, concat_axis=0...]
    ppermute x3, waiting for transfers between devices: 0.01 us -> 4.41 us  [shards(): lax.ppermute(gate_table, 'expert', rotation(n_expert, step))]
    ppermute x3, waiting for transfers between devices: 4.99 us -> 8.55 us  [shards(): lax.ppermute(part_sum.astype(bf16), 'donor', rotation(n_donor, step))]
  transfers between devices with their start and end apart: 32 -> 32, of which waited for: 17 -> 18; matrix products, arithmetic and copies ran while one was open for 19% -> 24% of each run, Pallas kernels for 0% -> 0%
where the time goes in v4:
time: 156 us
  waiting for transfers between devices  75.7 us (49%)
  starting transfers between devices  26.6 us (17%)
  matrix products  22.3 us (14%)
  local copies, waits for them, and re-layouts  20.4 us (13%)
  other arithmetic  8.53 us (5%)
  between operations  2.25 us (1%)
    ppermute x4, waiting for transfers between devices, shards(): lax.ppermute(pair_sum[hop].astype(bf16), 'expert', turn(hop))  17.6 us
    ppermute x4, waiting for transfers between devices, shards(): lax.ppermute(chunk, 'expert', turn(hop))  16.8 us
    unnamed x36, local copies, waits for them, and re-layouts  14 us
    dot_general x2, matrix products, shards(): gate_up = jnp.dot(rows_in, gate_up_weight, preferred_element_type=f32)  13.1 us
    ppermute x3, waiting for transfers between devices, shards(): lax.ppermute(term(step).astype(bf16), 'donor', rotation(n_donor, step))  9.41 us
    ppermute x3, waiting for transfers between devices, shards(): lax.ppermute(part_sum.astype(bf16), 'donor', rotation(n_donor, step))  8.55 us
    ppermute x3, waiting for transfers between devices, shards(): chunk = lax.ppermute(chunk, 'donor', rotation(n_donor, 1))  8.42 us
    all_to_all x1, starting transfers between devices, attention(): lax.all_to_all(outgoing, ('expert', 'donor'), split_axis=0, concat_axis=0...  7.39 us
  transfers between devices with their start and end apart: 32, of which 18 were waited for; matrix products, arithmetic and copies ran while one was open for 24% of the time, Pallas kernels for 0%

profile of v4, /device:TPU:0, one launch (start us, length us, event | category | flops | bytes accessed | tf_op | source)
XLA Modules:
  0.0 155.8 jit_solution(1126274014951173638)
XLA Ops:
  3.2 7.4 %all-to-all-start = ((bf16[16,32,256]{2,1,0:T(8,128)(2,1)}), bf16[16,32,256]{2,1,0:T(8,128)(2,1)S(1)}, u32[]{:S(2)}, u32[]{:S(2)}) async-start(bf16[16,32,256]{2,1,0:T(8,128)(2,1)} %broadcast_select_fusion), calls=%async_computation | async-start | bytes 524288 | tf_op jit(solution)/shard_map/all_to_all | solution.py:34
  11.0 1.0 constant_dynamic-slice_fusion.17
  12.1 1.3 dynamic_slice.150
  14.9 5.8 %all-to-all-done = bf16[16,32,256]{2,1,0:T(8,128)(2,1)S(1)} async-done(((bf16[16,32,256]{2,1,0:T(8,128)(2,1)}), bf16[16,32,256]{2,1,0:T(8,128)(2,1)S(1)}, u32[]{:S(2)}, u32[]{:S(2)}) %all-to-all-start) | async-done | bytes 262176 | tf_op jit(solution)/shard_map/all_to_all | solution.py:34
  21.4 1.2 while.22
  23.0 1.9 %while.23 = (s32[]{:T(128)}, f32[128,8]{0,1:T(8,128)S(1)}, f32[128,8,128]{2,0,1:T(8,128)S(1)}, s32[]{:T(128)}, s32[]{:T(128)}, /*index=5*/bf16[128,8,128]{2,0,1:...) while((s32[]{:T(128)}, f32[128,8]{0,1:T(8,128)S(1)}, ...), condition=%wide.region_8.9_spmd, body=%wide.region_6.8_spmd.sunk | while | flops 271188992 | bytes 3691649 | solution.py:90
  26.5 1.2 collective-permute-start.2
  28.2 3.9 %collective-permute-done.3 = f32[8,128]{1,0:T(8,128)S(1)} collective-permute-done((f32[8,128]{1,0:T(8,128)S(1)}, f32[8,128]{1,0:T(8,128)S(1)}, u32[]{:S(2)}, u32[]{:S(2)}) %collective-permute-start.3) | collective-permute-done | bytes 4128 | tf_op jit(solution)/shard_map/ppermute | solution.py:136
  34.3 2.3 %fusion.71 = f32[256,1024]{1,0:T(8,128)S(1)} fusion(bf16[1024,1024]{1,0:T(8,128)(2,1)} %collective-permute-done.4, bf16[64,1024]{1,0:T(8,128)(2,1)S(1)} %get-tuple-element.251, bf16[64,1024]{1,0:T(8,128)(2,1)S(1)} %get-tuple-element.252, bf16[64,1024]{1,0:T(8,128)(2,1)S(1)} %get-tuple-element.253, bf16[64,1024]{1,0:T(8,128)(2,1)S(1)} %get-tuple-element.250), kind=kOutput, calls=%fused_computation.167 | convolution fusion | flops 538968064 | bytes 3670016 | tf_op jit(solution)/shard_map/dot_general | solution.py:163
  36.7 1.3 collective-permute-start.7
  39.9 13.1 %copy.53 = bf16[512,8,2,768]{3,1,2,0:T(8,128)(2,1)} copy(bf16[512,8,2,768]{3,2,1,0:T(2,128)(2,1)} %bitcast.159) | data formatting | bytes 25165824
  53.0 9.4 %collective-permute-done.8 = bf16[64,2048]{1,0:T(8,128)(2,1)S(1)} collective-permute-done((bf16[64,2048]{1,0:T(8,128)(2,1)S(1)}, bf16[64,2048]{1,0:T(8,128)(2,1)S(1)}, u32[]{:S(2)}, u32[]{:S(2)}) %collective-permute-start.8) | collective-permute-done | bytes 262176 | tf_op jit(solution)/shard_map/ppermute | solution.py:177
  62.7 1.0 collective-permute-start.10
  64.6 6.0 %collective-permute-done.10 = bf16[64,2048]{1,0:T(8,128)(2,1)S(1)} collective-permute-done((bf16[64,2048]{1,0:T(8,128)(2,1)S(1)}, bf16[64,2048]{1,0:T(8,128)(2,1)S(1)}, u32[]{:S(2)}, u32[]{:S(2)}) %collective-permute-start.10) | collective-permute-done | bytes 262176 | tf_op jit(solution)/shard_map/ppermute | solution.py:200
  70.5 3.1 %collective-permute-done.9 = bf16[64,2048]{1,0:T(8,128)(2,1)S(1)} collective-permute-done((bf16[64,2048]{1,0:T(8,128)(2,1)S(1)}, bf16[64,2048]{1,0:T(8,128)(2,1)S(1)}, u32[]{:S(2)}, u32[]{:S(2)}) %collective-permute-start.9) | collective-permute-done | bytes 262176 | tf_op jit(solution)/shard_map/ppermute | solution.py:203
  74.3 6.4 %collective-permute-done.12 = bf16[64,2048]{1,0:T(8,128)(2,1)S(1)} collective-permute-done((bf16[64,2048]{1,0:T(8,128)(2,1)S(1)}, bf16[64,2048]{1,0:T(8,128)(2,1)S(1)}, u32[]{:S(2)}, u32[]{:S(2)}) %collective-permute-start.12) | collective-permute-done | bytes 262176 | tf_op jit(solution)/shard_map/ppermute | solution.py:200
  80.8 1.8 %collective-permute-done.11 = bf16[64,2048]{1,0:T(8,128)(2,1)S(1)} collective-permute-done((bf16[64,2048]{1,0:T(8,128)(2,1)S(1)}, bf16[64,2048]{1,0:T(8,128)(2,1)S(1)}, u32[]{:S(2)}, u32[]{:S(2)}) %collective-permute-start.11) | collective-permute-done | bytes 262176 | tf_op jit(solution)/shard_map/ppermute | solution.py:203
  82.6 1.7 %collective-permute-start.14 = (bf16[64,2048]{1,0:T(8,128)(2,1)S(1)}, bf16[64,2048]{1,0:T(8,128)(2,1)S(1)}, u32[]{:S(2)}, u32[]{:S(2)}) collective-permute-start(bf16[64,2048]{1,0:T(8,128)(2,1)S(1)} %collective-permute-done.11), channel_id=1, source_target_pairs={{0,8},{4,12},{8,0},{12,4},{1,9},{5,13},{9,1},{13,5},{2,10},{6,14},... | collective-permute-start | bytes 786440 | tf_op jit(solution)/shard_map/ppermute | solution.py:200
  84.6 4.4 %collective-permute-done.14 = bf16[64,2048]{1,0:T(8,128)(2,1)S(1)} collective-permute-done((bf16[64,2048]{1,0:T(8,128)(2,1)S(1)}, bf16[64,2048]{1,0:T(8,128)(2,1)S(1)}, u32[]{:S(2)}, u32[]{:S(2)}) %collective-permute-start.14) | collective-permute-done | bytes 262176 | tf_op jit(solution)/shard_map/ppermute | solution.py:200
  89.0 3.5 %collective-permute-done.13 = bf16[64,2048]{1,0:T(8,128)(2,1)S(1)} collective-permute-done((bf16[64,2048]{1,0:T(8,128)(2,1)S(1)}, bf16[64,2048]{1,0:T(8,128)(2,1)S(1)}, u32[]{:S(2)}, u32[]{:S(2)}) %collective-permute-start.13) | collective-permute-done | bytes 262176 | tf_op jit(solution)/shard_map/ppermute | solution.py:203
  95.9 6.4 %fusion.4 = f32[256,1536]{1,0:T(8,128)S(1)} fusion(bf16[4096,1536]{1,0:T(8,128)(2,1)} %bitcast.160, bf16[64,4096]{1,0:T(8,128)(2,1)S(1)} %collective-permute-done.17, bf16[64,4096]{1,0:T(8,128)(2,1)S(1)} %collective-permute-done.16, bf16[64,4096]{1,0:T(8,128)(2,1)S(1)} %get-tuple-element.265, bf16[64,4096]{1,0:T(8,128)(2,1)S(1)} %get-tuple-element.266), kind=kOutput, calls=%fused_computation.11 | convolution fusion | flops 3229614080 | bytes 16252928 | tf_op jit(solution)/shard_map/dot_general | solution.py:229
  104.1 1.8 %collective-permute-done.19 = bf16[64,4096]{1,0:T(8,128)(2,1)} collective-permute-done((bf16[64,4096]{1,0:T(8,128)(2,1)S(1)}, bf16[64,4096]{1,0:T(8,128)(2,1)}, u32[]{:S(2)}, u32[]{:S(2)}) %collective-permute-start.19) | collective-permute-done | bytes 524320 | tf_op jit(solution)/shard_map/ppermute | solution.py:224
  105.9 6.7 %fusion.12 = f32[256,1536]{1,0:T(8,128)S(1)} fusion(bf16[4096,1536]{1,0:T(8,128)(2,1)} %bitcast.161, bf16[64,4096]{1,0:T(8,128)(2,1)} %collective-permute-done.19, bf16[64,4096]{1,0:T(8,128)(2,1)} %collective-permute-done.18, bf16[64,4096]{1,0:T(8,128)(2,1)S(1)} %fusion.45, bf16[64,4096]{1,0:T(8,128)(2,1)S(1)} %get-tuple-element.264), kind=kOutput, calls=%fused_computation.19 | convolution fusion | flops 3229614080 | bytes 16252928 | tf_op jit(solution)/shard_map/dot_general | solution.py:229
  113.8 1.0 fusion.26
  117.2 1.2 collective-permute-done.21
  119.0 1.7 %collective-permute-start.25 = (bf16[128,1024]{1,0:T(8,128)(2,1)S(1)}, bf16[128,1024]{1,0:T(8,128)(2,1)S(1)}, u32[]{:S(2)}, u32[]{:S(2)}) collective-permute-start(bf16[128,1024]{1,0:T(8,128)(2,1)S(1)} %slice.281), channel_id=1, source_target_pairs={{0,8},{4,12},{8,0},{12,4},{1,9},{5,13},{9,1},{13,5},{2,10},{6,14},... | collective-permute-start | bytes 786440 | tf_op jit(solution)/shard_map/ppermute | solution.py:267
  123.5 9.2 %collective-permute-done.25 = bf16[128,1024]{1,0:T(8,128)(2,1)S(1)} collective-permute-done((bf16[128,1024]{1,0:T(8,128)(2,1)S(1)}, bf16[128,1024]{1,0:T(8,128)(2,1)S(1)}, u32[]{:S(2)}, u32[]{:S(2)}) %collective-permute-start.25) | collective-permute-done | bytes 262176 | tf_op jit(solution)/shard_map/ppermute | solution.py:267
  133.7 1.7 %collective-permute-start.30 = (bf16[128,1024]{1,0:T(8,128)(2,1)S(1)}, bf16[128,1024]{1,0:T(8,128)(2,1)S(1)}, u32[]{:S(2)}, u32[]{:S(2)}) collective-permute-start(bf16[128,1024]{1,0:T(8,128)(2,1)S(1)} %slice.279), channel_id=1, source_target_pairs={{0,8},{4,12},{8,0},{12,4},{1,9},{5,13},{9,1},{13,5},{2,10},{6,14},... | collective-permute-start | bytes 786440 | tf_op jit(solution)/shard_map/ppermute | solution.py:267
  135.6 6.8 %collective-permute-done.28 = bf16[128,1024]{1,0:T(8,128)(2,1)S(1)} collective-permute-done((bf16[128,1024]{1,0:T(8,128)(2,1)S(1)}, bf16[128,1024]{1,0:T(8,128)(2,1)S(1)}, u32[]{:S(2)}, u32[]{:S(2)}) %collective-permute-start.28) | collective-permute-done | bytes 262176 | tf_op jit(solution)/shard_map/ppermute | solution.py:267
  142.4 2.1 %collective-permute-start.29 = (bf16[128,1024]{1,0:T(8,128)(2,1)S(1)}, bf16[128,1024]{1,0:T(8,128)(2,1)S(1)}, u32[]{:S(2)}, u32[]{:S(2)}) collective-permute-start(bf16[128,1024]{1,0:T(8,128)(2,1)S(1)} %fusion.52), channel_id=1, source_target_pairs={{0,1},{1,2},{2,3},{3,0},{4,5},{5,6},{6,7},{7,4},{8,9},{9,10},{10,1... | collective-permute-start | bytes 786440 | tf_op jit(solution)/shard_map/ppermute | solution.py:280
  144.7 1.6 %collective-permute-done.30 = bf16[128,1024]{1,0:T(8,128)(2,1)S(1)} collective-permute-done((bf16[128,1024]{1,0:T(8,128)(2,1)S(1)}, bf16[128,1024]{1,0:T(8,128)(2,1)S(1)}, u32[]{:S(2)}, u32[]{:S(2)}) %collective-permute-start.30) | collective-permute-done | bytes 262176 | tf_op jit(solution)/shard_map/ppermute | solution.py:267
  146.3 8.5 %collective-permute-done.24 = bf16[128,1024]{1,0:T(8,128)(2,1)S(1)} collective-permute-done((bf16[128,1024]{1,0:T(8,128)(2,1)S(1)}, bf16[128,1024]{1,0:T(8,128)(2,1)S(1)}, u32[]{:S(2)}, u32[]{:S(2)}) %collective-permute-start.24) | collective-permute-done | bytes 262176 | tf_op jit(solution)/shard_map/ppermute | solution.py:280
  (191 shorter events, 30.0 us)
Async XLA Ops:
  3.2 17.5 %all-to-all-start = ((bf16[16,32,256]{2,1,0:T(8,128)(2,1)}), bf16[16,32,256]{2,1,0:T(8,128)(2,1)S(1)}, u32[]{:S(2)}, u32[]{:S(2)}) async-start(bf16[16,32,256]{2,1,0:T(8,128)(2,1)} %broadcast_select_fusion), calls=%async_computation | async-start | bytes 524288 | tf_op jit(solution)/shard_map/all_to_all | solution.py:34
  10.6 23.7 %collective-permute-start.4 = (bf16[1024,1024]{1,0:T(8,128)(2,1)}, bf16[1024,1024]{1,0:T(8,128)(2,1)}, u32[]{:S(2)}, u32[]{:S(2)}) collective-permute-start(bf16[1024,1024]{1,0:T(8,128)(2,1)} %param.22), channel_id=1, source_target_pairs={{0,4},{4,0},{8,12},{12,8},{1,5},{5,1},{9,13},{13,9},{2,6},{6,2},{1... | collective-permute-start | bytes 6291464 | tf_op jit(solution)/shard_map/ppermute | solution.py:139
  25.3 8.1 %collective-permute-start = (bf16[128,1024]{1,0:T(8,128)(2,1)S(1)}, bf16[128,1024]{1,0:T(8,128)(2,1)S(1)}, u32[]{:S(2)}, u32[]{:S(2)}) collective-permute-start(bf16[128,1024]{1,0:T(8,128)(2,1)S(1)} %copy.48), channel_id=1, source_target_pairs={{0,8},{4,12},{8,0},{12,4},{1,9},{5,13},{9,1},{13,5},{2,10},{6,14},... | collective-permute-start | bytes 786440 | tf_op jit(solution)/shard_map/ppermute | solution.py:157
  25.9 6.2 %collective-permute-start.3 = (f32[8,128]{1,0:T(8,128)S(1)}, f32[8,128]{1,0:T(8,128)S(1)}, u32[]{:S(2)}, u32[]{:S(2)}) collective-permute-start(f32[8,128]{1,0:T(8,128)S(1)} %bitcast.175), channel_id=1, source_target_pairs={{0,12},{4,0},{8,4},{12,8},{1,13},{5,1},{9,5},{13,9},{2,14},{6,2},{... | collective-permute-start | bytes 12296 | tf_op jit(solution)/shard_map/ppermute | solution.py:136
  26.5 7.0 %collective-permute-start.2 = (f32[8,128]{1,0:T(8,128)S(1)}, f32[8,128]{1,0:T(8,128)S(1)}, u32[]{:S(2)}, u32[]{:S(2)}) collective-permute-start(f32[8,128]{1,0:T(8,128)S(1)} %bitcast.176), channel_id=1, source_target_pairs={{0,8},{4,12},{8,0},{12,4},{1,9},{5,13},{9,1},{13,5},{2,10},{6,14},... | collective-permute-start | bytes 12296 | tf_op jit(solution)/shard_map/ppermute | solution.py:136
  27.7 5.8 %collective-permute-start.1 = (f32[8,128]{1,0:T(8,128)S(1)}, f32[8,128]{1,0:T(8,128)S(1)}, u32[]{:S(2)}, u32[]{:S(2)}) collective-permute-start(f32[8,128]{1,0:T(8,128)S(1)} %bitcast.177), channel_id=1, source_target_pairs={{0,4},{4,8},{8,12},{12,0},{1,5},{5,9},{9,13},{13,1},{2,6},{6,10},{... | collective-permute-start | bytes 12296 | tf_op jit(solution)/shard_map/ppermute | solution.py:136
  32.1 30.3 %collective-permute-start.5 = (bf16[64,2048]{1,0:T(8,128)(2,1)S(1)}, bf16[64,2048]{1,0:T(8,128)(2,1)S(1)}, u32[]{:S(2)}, u32[]{:S(2)}) collective-permute-start(bf16[64,2048]{1,0:T(8,128)(2,1)S(1)} %dynamic_slice.156), channel_id=1, source_target_pairs={{0,8},{4,12},{8,0},{12,4},{1,9},{5,13},{9,1},{13,5},{2,10},{6,14},... | collective-permute-start | bytes 786440 | tf_op jit(solution)/shard_map/ppermute | solution.py:149
  36.7 16.3 %collective-permute-start.7 = (bf16[64,2048]{1,0:T(8,128)(2,1)S(1)}, bf16[64,2048]{1,0:T(8,128)(2,1)S(1)}, u32[]{:S(2)}, u32[]{:S(2)}) collective-permute-start(bf16[64,2048]{1,0:T(8,128)(2,1)S(1)} %pad_maximum_fusion.9), channel_id=1, source_target_pairs={{0,3},{1,0},{2,1},{3,2},{4,7},{5,4},{6,5},{7,6},{8,11},{9,8},{10,9... | collective-permute-start | bytes 786440 | tf_op jit(solution)/shard_map/ppermute | solution.py:177
  38.1 15.0 %collective-permute-start.6 = (bf16[64,2048]{1,0:T(8,128)(2,1)S(1)}, bf16[64,2048]{1,0:T(8,128)(2,1)S(1)}, u32[]{:S(2)}, u32[]{:S(2)}) collective-permute-start(bf16[64,2048]{1,0:T(8,128)(2,1)S(1)} %pad_maximum_fusion.8), channel_id=1, source_target_pairs={{0,1},{1,2},{2,3},{3,0},{4,5},{5,6},{6,7},{7,4},{8,9},{9,10},{10,1... | collective-permute-start | bytes 786440 | tf_op jit(solution)/shard_map/ppermute | solution.py:177
  38.9 23.5 %collective-permute-start.8 = (bf16[64,2048]{1,0:T(8,128)(2,1)S(1)}, bf16[64,2048]{1,0:T(8,128)(2,1)S(1)}, u32[]{:S(2)}, u32[]{:S(2)}) collective-permute-start(bf16[64,2048]{1,0:T(8,128)(2,1)S(1)} %pad_maximum_fusion.10), channel_id=1, source_target_pairs={{0,2},{1,3},{2,0},{3,1},{4,6},{5,7},{6,4},{7,5},{8,10},{9,11},{10,... | collective-permute-start | bytes 786440 | tf_op jit(solution)/shard_map/ppermute | solution.py:177
  62.7 7.8 %collective-permute-start.10 = (bf16[64,2048]{1,0:T(8,128)(2,1)S(1)}, bf16[64,2048]{1,0:T(8,128)(2,1)S(1)}, u32[]{:S(2)}, u32[]{:S(2)}) collective-permute-start(bf16[64,2048]{1,0:T(8,128)(2,1)S(1)} %fusion.57), channel_id=1, source_target_pairs={{0,8},{4,12},{8,0},{12,4},{1,9},{5,13},{9,1},{13,5},{2,10},{6,14},... | collective-permute-start | bytes 786440 | tf_op jit(solution)/shard_map/ppermute | solution.py:200
  63.8 9.8 %collective-permute-start.9 = (bf16[64,2048]{1,0:T(8,128)(2,1)S(1)}, bf16[64,2048]{1,0:T(8,128)(2,1)S(1)}, u32[]{:S(2)}, u32[]{:S(2)}) collective-permute-start(bf16[64,2048]{1,0:T(8,128)(2,1)S(1)} %fusion.57), channel_id=1, source_target_pairs={{0,1},{1,2},{2,3},{3,0},{4,5},{5,6},{6,7},{7,4},{8,9},{9,10},{10,1... | collective-permute-start | bytes 786440 | tf_op jit(solution)/shard_map/ppermute | solution.py:203
  73.6 7.2 %collective-permute-start.12 = (bf16[64,2048]{1,0:T(8,128)(2,1)S(1)}, bf16[64,2048]{1,0:T(8,128)(2,1)S(1)}, u32[]{:S(2)}, u32[]{:S(2)}) collective-permute-start(bf16[64,2048]{1,0:T(8,128)(2,1)S(1)} %collective-permute-done.9), channel_id=1, source_target_pairs={{0,8},{4,12},{8,0},{12,4},{1,9},{5,13},{9,1},{13,5},{2,10},{6,14},... | collective-permute-start | bytes 786440 | tf_op jit(solution)/shard_map/ppermute | solution.py:200
  74.1 8.5 %collective-permute-start.11 = (bf16[64,2048]{1,0:T(8,128)(2,1)S(1)}, bf16[64,2048]{1,0:T(8,128)(2,1)S(1)}, u32[]{:S(2)}, u32[]{:S(2)}) collective-permute-start(bf16[64,2048]{1,0:T(8,128)(2,1)S(1)} %collective-permute-done.9), channel_id=1, source_target_pairs={{0,1},{1,2},{2,3},{3,0},{4,5},{5,6},{6,7},{7,4},{8,9},{9,10},{10,1... | collective-permute-start | bytes 786440 | tf_op jit(solution)/shard_map/ppermute | solution.py:203
  82.6 6.4 %collective-permute-start.14 = (bf16[64,2048]{1,0:T(8,128)(2,1)S(1)}, bf16[64,2048]{1,0:T(8,128)(2,1)S(1)}, u32[]{:S(2)}, u32[]{:S(2)}) collective-permute-start(bf16[64,2048]{1,0:T(8,128)(2,1)S(1)} %collective-permute-done.11), channel_id=1, source_target_pairs={{0,8},{4,12},{8,0},{12,4},{1,9},{5,13},{9,1},{13,5},{2,10},{6,14},... | collective-permute-start | bytes 786440 | tf_op jit(solution)/shard_map/ppermute | solution.py:200
  84.3 8.2 %collective-permute-start.13 = (bf16[64,2048]{1,0:T(8,128)(2,1)S(1)}, bf16[64,2048]{1,0:T(8,128)(2,1)S(1)}, u32[]{:S(2)}, u32[]{:S(2)}) collective-permute-start(bf16[64,2048]{1,0:T(8,128)(2,1)S(1)} %collective-permute-done.11), channel_id=1, source_target_pairs={{0,1},{1,2},{2,3},{3,0},{4,5},{5,6},{6,7},{7,4},{8,9},{9,10},{10,1... | collective-permute-start | bytes 786440 | tf_op jit(solution)/shard_map/ppermute | solution.py:203
  93.2 2.0 %collective-permute-start.17 = (bf16[64,4096]{1,0:T(8,128)(2,1)S(1)}, bf16[64,4096]{1,0:T(8,128)(2,1)S(1)}, u32[]{:S(2)}, u32[]{:S(2)}) collective-permute-start(bf16[64,4096]{1,0:T(8,128)(2,1)S(1)} %get-tuple-element.265), channel_id=1, source_target_pairs={{0,4},{4,0},{8,12},{12,8},{1,5},{5,1},{9,13},{13,9},{2,6},{6,2},{1... | collective-permute-start | bytes 1572872 | tf_op jit(solution)/shard_map/ppermute | solution.py:224
  93.3 2.6 %collective-permute-start.16 = (bf16[64,4096]{1,0:T(8,128)(2,1)S(1)}, bf16[64,4096]{1,0:T(8,128)(2,1)S(1)}, u32[]{:S(2)}, u32[]{:S(2)}) collective-permute-start(bf16[64,4096]{1,0:T(8,128)(2,1)S(1)} %get-tuple-element.266), channel_id=1, source_target_pairs={{0,4},{4,0},{8,12},{12,8},{1,5},{5,1},{9,13},{13,9},{2,6},{6,2},{1... | collective-permute-start | bytes 1572872 | tf_op jit(solution)/shard_map/ppermute | solution.py:224
  93.9 9.4 %collective-permute-start.15 = (bf16[64,2048]{1,0:T(8,128)(2,1)S(1)}, bf16[64,2048]{1,0:T(8,128)(2,1)S(1)}, u32[]{:S(2)}, u32[]{:S(2)}) collective-permute-start(bf16[64,2048]{1,0:T(8,128)(2,1)S(1)} %collective-permute-done.13), channel_id=1, source_target_pairs={{0,8},{4,12},{8,0},{12,4},{1,9},{5,13},{9,1},{13,5},{2,10},{6,14},... | collective-permute-start | bytes 786440 | tf_op jit(solution)/shard_map/ppermute | solution.py:200
  94.2 9.9 %collective-permute-start.18 = (bf16[64,4096]{1,0:T(8,128)(2,1)S(1)}, bf16[64,4096]{1,0:T(8,128)(2,1)}, u32[]{:S(2)}, u32[]{:S(2)}) collective-permute-start(bf16[64,4096]{1,0:T(8,128)(2,1)S(1)} %get-tuple-element.264), channel_id=1, source_target_pairs={{0,4},{4,0},{8,12},{12,8},{1,5},{5,1},{9,13},{13,9},{2,6},{6,2},{1... | collective-permute-start | bytes 1572872 | tf_op jit(solution)/shard_map/ppermute | solution.py:224
  103.8 2.1 %collective-permute-start.19 = (bf16[64,4096]{1,0:T(8,128)(2,1)S(1)}, bf16[64,4096]{1,0:T(8,128)(2,1)}, u32[]{:S(2)}, u32[]{:S(2)}) collective-permute-start(bf16[64,4096]{1,0:T(8,128)(2,1)S(1)} %fusion.45), channel_id=1, source_target_pairs={{0,4},{4,0},{8,12},{12,8},{1,5},{5,1},{9,13},{13,9},{2,6},{6,2},{1... | collective-permute-start | bytes 1572872 | tf_op jit(solution)/shard_map/ppermute | solution.py:224
  114.9 2.0 %collective-permute-start.20 = (bf16[256,1024]{1,0:T(8,128)(2,1)S(1)}, bf16[256,1024]{1,0:T(8,128)(2,1)S(1)}, u32[]{:S(2)}, u32[]{:S(2)}) collective-permute-start(bf16[256,1024]{1,0:T(8,128)(2,1)S(1)} %slice.278), channel_id=1, source_target_pairs={{0,4},{4,0},{8,12},{12,8},{1,5},{5,1},{9,13},{13,9},{2,6},{6,2},{1... | collective-permute-start | bytes 1572872 | tf_op jit(solution)/shard_map/ppermute | solution.py:261
  116.4 2.0 %collective-permute-start.21 = (bf16[256,1024]{1,0:T(8,128)(2,1)S(1)}, bf16[256,1024]{1,0:T(8,128)(2,1)S(1)}, u32[]{:S(2)}, u32[]{:S(2)}) collective-permute-start(bf16[256,1024]{1,0:T(8,128)(2,1)S(1)} %slice.277), channel_id=1, source_target_pairs={{0,4},{4,0},{8,12},{12,8},{1,5},{5,1},{9,13},{13,9},{2,6},{6,2},{1... | collective-permute-start | bytes 1572872 | tf_op jit(solution)/shard_map/ppermute | solution.py:261
  118.6 16.8 %collective-permute-start.23 = (bf16[128,1024]{1,0:T(8,128)(2,1)S(1)}, bf16[128,1024]{1,0:T(8,128)(2,1)S(1)}, u32[]{:S(2)}, u32[]{:S(2)}) collective-permute-start(bf16[128,1024]{1,0:T(8,128)(2,1)S(1)} %slice.282), channel_id=1, source_target_pairs={{0,8},{4,12},{8,0},{12,4},{1,9},{5,13},{9,1},{13,5},{2,10},{6,14},... | collective-permute-start | bytes 786440 | tf_op jit(solution)/shard_map/ppermute | solution.py:267
  119.0 13.7 %collective-permute-start.25 = (bf16[128,1024]{1,0:T(8,128)(2,1)S(1)}, bf16[128,1024]{1,0:T(8,128)(2,1)S(1)}, u32[]{:S(2)}, u32[]{:S(2)}) collective-permute-start(bf16[128,1024]{1,0:T(8,128)(2,1)S(1)} %slice.281), channel_id=1, source_target_pairs={{0,8},{4,12},{8,0},{12,4},{1,9},{5,13},{9,1},{13,5},{2,10},{6,14},... | collective-permute-start | bytes 786440 | tf_op jit(solution)/shard_map/ppermute | solution.py:267
  121.8 11.0 %collective-permute-start.27 = (bf16[256,1024]{1,0:T(8,128)(2,1)S(1)}, bf16[256,1024]{1,0:T(8,128)(2,1)S(1)}, u32[]{:S(2)}, u32[]{:S(2)}) collective-permute-start(bf16[256,1024]{1,0:T(8,128)(2,1)S(1)} %slice.275), channel_id=1, source_target_pairs={{0,4},{4,0},{8,12},{12,8},{1,5},{5,1},{9,13},{13,9},{2,6},{6,2},{1... | collective-permute-start | bytes 1572872 | tf_op jit(solution)/shard_map/ppermute | solution.py:261
  123.0 10.5 %collective-permute-start.22 = (bf16[256,1024]{1,0:T(8,128)(2,1)S(1)}, bf16[256,1024]{1,0:T(8,128)(2,1)S(1)}, u32[]{:S(2)}, u32[]{:S(2)}) collective-permute-start(bf16[256,1024]{1,0:T(8,128)(2,1)S(1)} %slice.276), channel_id=1, source_target_pairs={{0,4},{4,0},{8,12},{12,8},{1,5},{5,1},{9,13},{13,9},{2,6},{6,2},{1... | collective-permute-start | bytes 1572872 | tf_op jit(solution)/shard_map/ppermute | solution.py:261
  132.7 11.9 %collective-permute-start.26 = (bf16[128,1024]{1,0:T(8,128)(2,1)S(1)}, bf16[128,1024]{1,0:T(8,128)(2,1)S(1)}, u32[]{:S(2)}, u32[]{:S(2)}) collective-permute-start(bf16[128,1024]{1,0:T(8,128)(2,1)S(1)} %fusion.53), channel_id=1, source_target_pairs={{0,3},{1,0},{2,1},{3,2},{4,7},{5,4},{6,5},{7,6},{8,11},{9,8},{10,9... | collective-permute-start | bytes 786440 | tf_op jit(solution)/shard_map/ppermute | solution.py:280
  133.1 9.3 %collective-permute-start.28 = (bf16[128,1024]{1,0:T(8,128)(2,1)S(1)}, bf16[128,1024]{1,0:T(8,128)(2,1)S(1)}, u32[]{:S(2)}, u32[]{:S(2)}) collective-permute-start(bf16[128,1024]{1,0:T(8,128)(2,1)S(1)} %slice.280), channel_id=1, source_target_pairs={{0,8},{4,12},{8,0},{12,4},{1,9},{5,13},{9,1},{13,5},{2,10},{6,14},... | collective-permute-start | bytes 786440 | tf_op jit(solution)/shard_map/ppermute | solution.py:267
  133.7 12.6 %collective-permute-start.30 = (bf16[128,1024]{1,0:T(8,128)(2,1)S(1)}, bf16[128,1024]{1,0:T(8,128)(2,1)S(1)}, u32[]{:S(2)}, u32[]{:S(2)}) collective-permute-start(bf16[128,1024]{1,0:T(8,128)(2,1)S(1)} %slice.279), channel_id=1, source_target_pairs={{0,8},{4,12},{8,0},{12,4},{1,9},{5,13},{9,1},{13,5},{2,10},{6,14},... | collective-permute-start | bytes 786440 | tf_op jit(solution)/shard_map/ppermute | solution.py:267
  135.5 19.4 %collective-permute-start.24 = (bf16[128,1024]{1,0:T(8,128)(2,1)S(1)}, bf16[128,1024]{1,0:T(8,128)(2,1)S(1)}, u32[]{:S(2)}, u32[]{:S(2)}) collective-permute-start(bf16[128,1024]{1,0:T(8,128)(2,1)S(1)} %add_convert_fusion), channel_id=1, source_target_pairs={{0,2},{1,3},{2,0},{3,1},{4,6},{5,7},{6,4},{7,5},{8,10},{9,11},{10,... | collective-permute-start | bytes 786440 | tf_op jit(solution)/shard_map/ppermute | solution.py:280
  142.4 12.4 %collective-permute-start.29 = (bf16[128,1024]{1,0:T(8,128)(2,1)S(1)}, bf16[128,1024]{1,0:T(8,128)(2,1)S(1)}, u32[]{:S(2)}, u32[]{:S(2)}) collective-permute-start(bf16[128,1024]{1,0:T(8,128)(2,1)S(1)} %fusion.52), channel_id=1, source_target_pairs={{0,1},{1,2},{2,3},{3,0},{4,5},{5,6},{6,7},{7,4},{8,9},{9,10},{10,1... | collective-permute-start | bytes 786440 | tf_op jit(solution)/shard_map/ppermute | solution.py:280
  (14 other events, 87.0 us)

commit v5 on v4

--- a/solution.py
+++ b/solution.py
@@ -1,6 +1,8 @@
 import jax
 import jax.numpy as jnp
 from jax import lax
+from jax.experimental import pallas as pl
+from jax.experimental.pallas import tpu as pltpu
 from jax.sharding import PartitionSpec as P
 
 
@@ -10,6 +12,52 @@
 
 def pick(array, index, axis=0):
     return lax.dynamic_index_in_dim(array, index, axis, keepdims=False)
+
+
+def after(array, *others):
+    return lax.optimization_barrier((array, *others))[0]
+
+
+def hidden_units_kernel(count, *refs):
+    rows, (scale_ref, weight_ref, out_ref, total) = refs[:count], refs[count:]
+    step = pl.program_id(0)
+    block = jnp.concatenate([ref[...] for ref in rows], axis=0)
+    part = jnp.dot(block, weight_ref[...], preferred_element_type=jnp.float32)
+
+    @pl.when(step == 0)
+    def _():
+        total[...] = part
+
+    @pl.when(step > 0)
+    def _():
+        total[...] += part
+
+    @pl.when(step == pl.num_programs(0) - 1)
+    def _():
+        units = out_ref.shape[1]
+        gate, up = total[:, :units], total[:, units:]
+        act = gate / (1.0 + jnp.exp(-gate)) * up
+        out_ref[...] = (act * scale_ref[...]).astype(out_ref.dtype)
+
+
+def hidden_units(rows, scale, weight):
+    model_width, units = weight.shape
+    height = sum(part.shape[0] for part in rows)
+    depth = min(512, model_width)
+    row_specs = [pl.BlockSpec((part.shape[0], depth), lambda k: (0, k)) for part in rows]
+    return pl.pallas_call(
+        lambda *refs: hidden_units_kernel(len(rows), *refs),
+        grid=(model_width // depth,),
+        in_specs=row_specs
+        + [
+            pl.BlockSpec((height, 1), lambda k: (0, 0)),
+            pl.BlockSpec((depth, units), lambda k: (k, 0)),
+        ],
+        out_specs=pl.BlockSpec((height, units // 2), lambda k: (0, 0)),
+        out_shape=jax.ShapeDtypeStruct((height, units // 2), jnp.bfloat16),
+        scratch_shapes=[pltpu.VMEM((height, units), jnp.float32)],
+        compiler_params=pltpu.CompilerParams(vmem_limit_bytes=24 * 1024 * 1024),
+    )(*rows, scale, weight)
 
 
 def attention(queries, suffix_kv, kv_pool, page_table, prefix_len):
@@ -224,11 +272,9 @@
         other_rows.append(lax.ppermute(normed, "expert", swap))
         row_gates.append((pick(own_gates, part), pick(other_gates, part)))
         if len(row_gates) == batch:
-            rows_in = jnp.concatenate(own_rows + other_rows, axis=0)
             scale = jnp.concatenate([g[0] for g in row_gates] + [g[1] for g in row_gates])
-            gate_up = jnp.dot(rows_in, gate_up_weight, preferred_element_type=f32)
-            act = jax.nn.silu(gate_up[:, :ff_local]) * gate_up[:, ff_local:]
-            act = (act * scale[:, None]).astype(bf16).reshape(2, batch, part_rows, ff_local)
+            act = hidden_units(own_rows + other_rows, scale[:, None], gate_up_weight)
+            act = act.reshape(2, batch, part_rows, ff_local)
             for i in range(batch):
                 own_act[slot - batch + 1 + i] = act[0, i]
                 other_act[slot - batch + 1 + i] = act[1, i]
@@ -267,15 +313,13 @@
             lax.ppermute(pair_sum[hop].astype(bf16), "expert", turn(hop)) for hop in range(1, n_rows)
         ]
         pending.append((pair_sum[0], arriving))
-    first = pending[0][0]
-    first, swapped[-1] = lax.optimization_barrier((first, swapped[-1]))
-    total = resid
+    total, before = resid, swapped[-2:]
     for place, step in enumerate(order):
         part_sum, arriving = pending[place]
-        if place == 0:
-            part_sum = first
+        part_sum = after(part_sum, *before)
         for got in arriving:
             part_sum = part_sum + got.astype(f32)
+        before = [part_sum]
         if step:
             part_sum = lax.ppermute(part_sum.astype(bf16), "donor", rotation(n_donor, step))
         total = total + part_sum.astype(f32)

time: 156 us -> 176 us (1.13)
  local copies, waits for them, and re-layouts: 20.4 us -> 33.6 us
  Pallas kernels: 0 us -> 12.6 us
  matrix products: 22.3 us -> 17.1 us
  starting transfers between devices: 26.6 us -> 24.7 us
    dot_general x2 -> x0, matrix products: 13.1 us -> none  [shards(): gate_up = jnp.dot(rows_in, gate_up_weight, preferred_element_type=f32)]
    pallas_call x0 -> x2, Pallas kernels: none -> 12.6 us  [hidden_units(): pl.pallas_call(lambda *refs: hidden_units_kernel(len(rows), *refs), grid=...]
    unnamed x36 -> x72, local copies, waits for them, and re-layouts: 14 us -> 24 us
    dot_general x4, matrix products: 4.02 us -> 10.4 us  [shards(): mixed = jnp.dot(act_rows, down, preferred_element_type=f32)]
    ppermute x4, waiting for transfers between devices: 17.6 us -> 20.6 us  [shards(): lax.ppermute(pair_sum[hop].astype(bf16), 'expert', turn(hop))]
    ppermute x3, starting transfers between devices: 2.19 us -> 0.19 us  [shards(): lax.ppermute(part_sum.astype(bf16), 'donor', rotation(n_donor, step))]
    ppermute x4, waiting for transfers between devices: 16.8 us -> 14.8 us  [shards(): lax.ppermute(chunk, 'expert', turn(hop))]
  transfers between devices with their start and end apart: 32 -> 32, of which waited for: 18 -> 18; matrix products, arithmetic and copies ran while one was open for 24% -> 21% of each run, Pallas kernels for 0% -> 4%
where the time goes in v5:
time: 176 us
  waiting for transfers between devices  76.2 us (43%)
  local copies, waits for them, and re-layouts  33.6 us (19%)
  starting transfers between devices  24.7 us (14%)
  matrix products  17.1 us (10%)
  Pallas kernels  12.6 us (7%)
  other arithmetic  9.07 us (5%)
  between operations  2.37 us (1%)
    unnamed x72, local copies, waits for them, and re-layouts  24 us
    ppermute x4, waiting for transfers between devices, shards(): lax.ppermute(pair_sum[hop].astype(bf16), 'expert', turn(hop))  20.6 us
    ppermute x4, waiting for transfers between devices, shards(): lax.ppermute(chunk, 'expert', turn(hop))  14.8 us
    pallas_call x2, Pallas kernels, hidden_units(): pl.pallas_call(lambda *refs: hidden_units_kernel(len(rows), *refs), grid=...  12.6 us
    dot_general x4, matrix products, shards(): mixed = jnp.dot(act_rows, down, preferred_element_type=f32)  10.4 us
    ppermute x3, waiting for transfers between devices, shards(): lax.ppermute(part_sum.astype(bf16), 'donor', rotation(n_donor, step))  9.37 us
    ppermute x3, waiting for transfers between devices, shards(): lax.ppermute(term(step).astype(bf16), 'donor', rotation(n_donor, step))  9.35 us
    ppermute x3, waiting for transfers between devices, shards(): chunk = lax.ppermute(chunk, 'donor', rotation(n_donor, 1))  8.41 us
  transfers between devices with their start and end apart: 32, of which 18 were waited for; matrix products, arithmetic and copies ran while one was open for 21% of the time, Pallas kernels for 4%

profile of v5, /device:TPU:0, one launch (start us, length us, event | category | flops | bytes accessed | tf_op | source)
XLA Modules:
  0.0 175.7 jit_solution(8393009846001333629)
XLA Ops:
  3.2 7.4 %all-to-all-start = ((bf16[16,32,256]{2,1,0:T(8,128)(2,1)}), bf16[16,32,256]{2,1,0:T(8,128)(2,1)S(1)}, u32[]{:S(2)}, u32[]{:S(2)}) async-start(bf16[16,32,256]{2,1,0:T(8,128)(2,1)} %broadcast_select_fusion), calls=%async_computation | async-start | bytes 524288 | tf_op jit(solution)/shard_map/all_to_all | solution.py:82
  14.7 5.9 %all-to-all-done = bf16[16,32,256]{2,1,0:T(8,128)(2,1)S(1)} async-done(((bf16[16,32,256]{2,1,0:T(8,128)(2,1)}), bf16[16,32,256]{2,1,0:T(8,128)(2,1)S(1)}, u32[]{:S(2)}, u32[]{:S(2)}) %all-to-all-start) | async-done | bytes 262176 | tf_op jit(solution)/shard_map/all_to_all | solution.py:82
  22.9 1.7 while.23
  28.0 3.9 %collective-permute-done.3 = f32[8,128]{1,0:T(8,128)S(1)} collective-permute-done((f32[8,128]{1,0:T(8,128)S(1)}, f32[8,128]{1,0:T(8,128)S(1)}, u32[]{:S(2)}, u32[]{:S(2)}) %collective-permute-start.3) | collective-permute-done | bytes 4128 | tf_op jit(solution)/shard_map/ppermute | solution.py:184
  33.8 2.3 %fusion.48 = f32[256,1024]{1,0:T(8,128)S(1)} fusion(bf16[1024,1024]{1,0:T(8,128)(2,1)} %param.22, bf16[64,1024]{1,0:T(8,128)(2,1)S(1)} %get-tuple-element.257, bf16[64,1024]{1,0:T(8,128)(2,1)S(1)} %get-tuple-element.258, bf16[64,1024]{1,0:T(8,128)(2,1)S(1)} %get-tuple-element.259, bf16[64,1024]{1,0:T(8,128)(2,1)S(1)} %get-tuple-element.256), kind=kOutput, calls=%fused_computation.142 | convolution fusion | flops 538968064 | bytes 3670016 | tf_op jit(solution)/shard_map/dot_general | solution.py:210
  36.1 2.3 %fusion.47 = f32[256,1024]{1,0:T(8,128)S(1)} fusion(bf16[1024,1024]{1,0:T(8,128)(2,1)} %collective-permute-done.4, bf16[64,1024]{1,0:T(8,128)(2,1)S(1)} %get-tuple-element.257, bf16[64,1024]{1,0:T(8,128)(2,1)S(1)} %get-tuple-element.258, bf16[64,1024]{1,0:T(8,128)(2,1)S(1)} %get-tuple-element.259, bf16[64,1024]{1,0:T(8,128)(2,1)S(1)} %get-tuple-element.256), kind=kOutput, calls=%fused_computation.141 | convolution fusion | flops 538968064 | bytes 3670016 | tf_op jit(solution)/shard_map/dot_general | solution.py:211
  38.6 1.3 collective-permute-start.7
  41.7 13.1 %copy.59 = bf16[512,8,2,768]{3,1,2,0:T(8,128)(2,1)} copy(bf16[512,8,2,768]{3,2,1,0:T(2,128)(2,1)} %bitcast.163) | data formatting | bytes 25165824
  54.9 9.3 %collective-permute-done.8 = bf16[64,2048]{1,0:T(8,128)(2,1)S(1)} collective-permute-done((bf16[64,2048]{1,0:T(8,128)(2,1)S(1)}, bf16[64,2048]{1,0:T(8,128)(2,1)S(1)}, u32[]{:S(2)}, u32[]{:S(2)}) %collective-permute-start.8) | collective-permute-done | bytes 262176 | tf_op jit(solution)/shard_map/ppermute | solution.py:225
  67.4 4.9 %collective-permute-done.10 = bf16[64,2048]{1,0:T(8,128)(2,1)S(1)} collective-permute-done((bf16[64,2048]{1,0:T(8,128)(2,1)S(1)}, bf16[64,2048]{1,0:T(8,128)(2,1)S(1)}, u32[]{:S(2)}, u32[]{:S(2)}) %collective-permute-start.10) | collective-permute-done | bytes 262176 | tf_op jit(solution)/shard_map/ppermute | solution.py:248
  72.3 3.1 %collective-permute-done.9 = bf16[64,2048]{1,0:T(8,128)(2,1)S(1)} collective-permute-done((bf16[64,2048]{1,0:T(8,128)(2,1)S(1)}, bf16[64,2048]{1,0:T(8,128)(2,1)S(1)}, u32[]{:S(2)}, u32[]{:S(2)}) %collective-permute-start.9) | collective-permute-done | bytes 262176 | tf_op jit(solution)/shard_map/ppermute | solution.py:251
  76.1 6.4 %collective-permute-done.12 = bf16[64,2048]{1,0:T(8,128)(2,1)S(1)} collective-permute-done((bf16[64,2048]{1,0:T(8,128)(2,1)S(1)}, bf16[64,2048]{1,0:T(8,128)(2,1)S(1)}, u32[]{:S(2)}, u32[]{:S(2)}) %collective-permute-start.12) | collective-permute-done | bytes 262176 | tf_op jit(solution)/shard_map/ppermute | solution.py:248
  82.5 1.8 %collective-permute-done.11 = bf16[64,2048]{1,0:T(8,128)(2,1)S(1)} collective-permute-done((bf16[64,2048]{1,0:T(8,128)(2,1)S(1)}, bf16[64,2048]{1,0:T(8,128)(2,1)S(1)}, u32[]{:S(2)}, u32[]{:S(2)}) %collective-permute-start.11) | collective-permute-done | bytes 262176 | tf_op jit(solution)/shard_map/ppermute | solution.py:251
  84.4 1.7 collective-permute-start.14
  87.3 3.4 %collective-permute-done.14 = bf16[64,2048]{1,0:T(8,128)(2,1)S(1)} collective-permute-done((bf16[64,2048]{1,0:T(8,128)(2,1)S(1)}, bf16[64,2048]{1,0:T(8,128)(2,1)S(1)}, u32[]{:S(2)}, u32[]{:S(2)}) %collective-permute-start.14) | collective-permute-done | bytes 262176 | tf_op jit(solution)/shard_map/ppermute | solution.py:248
  90.7 3.5 %collective-permute-done.13 = bf16[64,2048]{1,0:T(8,128)(2,1)S(1)} collective-permute-done((bf16[64,2048]{1,0:T(8,128)(2,1)S(1)}, bf16[64,2048]{1,0:T(8,128)(2,1)S(1)}, u32[]{:S(2)}, u32[]{:S(2)}) %collective-permute-start.13) | collective-permute-done | bytes 262176 | tf_op jit(solution)/shard_map/ppermute | solution.py:251
  94.9 4.6 %copy-done.2 = bf16[512,8,2,768]{3,1,2,0:T(8,128)(2,1)S(1)} copy-done((bf16[512,8,2,768]{3,1,2,0:T(8,128)(2,1)S(1)}, bf16[512,8,2,768]{3,1,2,0:T(8,128)(2,1)}, u32[]{:S(2)}) %copy-start.2) | copy-done | bytes 12582936
  99.4 6.3 %shard_map.131 = bf16[256,768]{1,0:T(8,128)(2,1)S(1)} custom-call(bf16[64,4096]{1,0:T(8,128)(2,1)S(1)} %get-tuple-element.273.refs_0_, bf16[64,4096]{1,0:T(8,128)(2,1)S(1)} %get-tuple-element.272.refs_1_, bf16[64,4096]{1,0:T(8,128)(2,1)S(1)} %collective-permute-done.16.refs_2_, bf16[64,4096]{1,0:T(8,128)(2,1)S(1)} %collective-permute-done.17.refs_3_, ...), custom_call_target="tpu_custom_call" | custom-call | tf_op jit(solution)/shard_map/pallas_call | solution.py:48
  109.8 4.6 %copy-done.3 = bf16[512,8,2,768]{3,1,2,0:T(8,128)(2,1)S(1)} copy-done((bf16[512,8,2,768]{3,1,2,0:T(8,128)(2,1)S(1)}, bf16[512,8,2,768]{3,1,2,0:T(8,128)(2,1)}, u32[]{:S(2)}) %copy-start.3) | copy-done | bytes 12582936
  114.4 6.3 %shard_map.132 = bf16[256,768]{1,0:T(8,128)(2,1)S(1)} custom-call(bf16[64,4096]{1,0:T(8,128)(2,1)S(1)} %get-tuple-element.271.refs_0_, bf16[64,4096]{1,0:T(8,128)(2,1)S(1)} %get-tuple-element.270.refs_1_, bf16[64,4096]{1,0:T(8,128)(2,1)S(1)} %collective-permute-done.18.refs_2_, bf16[64,4096]{1,0:T(8,128)(2,1)S(1)} %collective-permute-done.19.refs_3_, ...), custom_call_target="tpu_custom_call" | custom-call | tf_op jit(solution)/shard_map/pallas_call | solution.py:48
  121.8 2.7 %fusion.10 = f32[512,1024]{1,0:T(8,128)S(1)} fusion(bf16[512,768]{1,0:T(8,128)(2,1)S(1)} %bitcast_dynamic-update-slice_fusion.1, bf16[1,768,4096]{2,1,0:T(8,128)(2,1)} %param.27, s32[]{:T(128)S(6)} %select_n.502), kind=kOutput, calls=%fused_computation.17 | convolution fusion | flops 805306368 | bytes 4456452 | tf_op jit(solution)/shard_map/dot_general | solution.py:306
  125.6 2.4 %fusion.6 = f32[512,1024]{1,0:T(8,128)S(1)} fusion(bf16[512,768]{1,0:T(8,128)(2,1)S(1)} %bitcast_dynamic-update-slice_fusion.1, bf16[1,768,4096]{2,1,0:T(8,128)(2,1)} %param.27, s32[]{:T(128)S(6)} %select_n.504), kind=kOutput, calls=%fused_computation.13 | convolution fusion | flops 805306368 | bytes 4456452 | tf_op jit(solution)/shard_map/dot_general | solution.py:306
  130.2 1.4 collective-permute-done.22
  131.7 1.4 slice_add_fusion.2
  133.1 2.7 %fusion.4 = f32[512,1024]{1,0:T(8,128)S(1)} fusion(bf16[512,768]{1,0:T(8,128)(2,1)S(1)} %copy-done.23, bf16[1,768,4096]{2,1,0:T(8,128)(2,1)} %param.27, s32[]{:T(128)S(6)} %select_n.505), kind=kOutput, calls=%fused_computation.11 | convolution fusion | flops 805306368 | bytes 4456452 | tf_op jit(solution)/shard_map/dot_general | solution.py:306
  136.4 2.6 %fusion.8 = f32[512,1024]{1,0:T(8,128)S(1)} fusion(bf16[512,768]{1,0:T(8,128)(2,1)S(1)} %copy-done.23, bf16[1,768,4096]{2,1,0:T(8,128)(2,1)} %param.27, s32[]{:T(128)S(6)} %select_n.503), kind=kOutput, calls=%fused_computation.15 | convolution fusion | flops 805306368 | bytes 4456452 | tf_op jit(solution)/shard_map/dot_general | solution.py:306
  139.4 1.8 %collective-permute-start.24 = (bf16[128,1024]{1,0:T(8,128)(2,1)S(1)}, bf16[128,1024]{1,0:T(8,128)(2,1)S(1)}, u32[]{:S(2)}, u32[]{:S(2)}) collective-permute-start(bf16[128,1024]{1,0:T(8,128)(2,1)S(1)} %slice.239), channel_id=1, source_target_pairs={{0,8},{4,12},{8,0},{12,4},{1,9},{5,13},{9,1},{13,5},{2,10},{6,14},... | collective-permute-start | bytes 786440 | tf_op jit(solution)/shard_map/ppermute | solution.py:313
  142.0 1.8 %collective-permute-start.30 = (bf16[128,1024]{1,0:T(8,128)(2,1)S(1)}, bf16[128,1024]{1,0:T(8,128)(2,1)S(1)}, u32[]{:S(2)}, u32[]{:S(2)}) collective-permute-start(bf16[128,1024]{1,0:T(8,128)(2,1)S(1)} %slice.236), channel_id=1, source_target_pairs={{0,8},{4,12},{8,0},{12,4},{1,9},{5,13},{9,1},{13,5},{2,10},{6,14},... | collective-permute-start | bytes 786440 | tf_op jit(solution)/shard_map/ppermute | solution.py:313
  144.1 4.5 %collective-permute-done.24 = bf16[128,1024]{1,0:T(8,128)(2,1)S(1)} collective-permute-done((bf16[128,1024]{1,0:T(8,128)(2,1)S(1)}, bf16[128,1024]{1,0:T(8,128)(2,1)S(1)}, u32[]{:S(2)}, u32[]{:S(2)}) %collective-permute-start.24) | collective-permute-done | bytes 262176 | tf_op jit(solution)/shard_map/ppermute | solution.py:313
  148.7 5.5 %collective-permute-done.26 = bf16[128,1024]{1,0:T(8,128)(2,1)S(1)} collective-permute-done((bf16[128,1024]{1,0:T(8,128)(2,1)S(1)}, bf16[128,1024]{1,0:T(8,128)(2,1)S(1)}, u32[]{:S(2)}, u32[]{:S(2)}) %collective-permute-start.26) | collective-permute-done | bytes 262176 | tf_op jit(solution)/shard_map/ppermute | solution.py:313
  154.3 10.6 %collective-permute-done.28 = bf16[128,1024]{1,0:T(8,128)(2,1)S(1)} collective-permute-done((bf16[128,1024]{1,0:T(8,128)(2,1)S(1)}, bf16[128,1024]{1,0:T(8,128)(2,1)S(1)}, u32[]{:S(2)}, u32[]{:S(2)}) %collective-permute-start.28) | collective-permute-done | bytes 262176 | tf_op jit(solution)/shard_map/ppermute | solution.py:313
  165.9 8.9 %collective-permute-done.29 = bf16[128,1024]{1,0:T(8,128)(2,1)S(1)} collective-permute-done((bf16[128,1024]{1,0:T(8,128)(2,1)S(1)}, bf16[128,1024]{1,0:T(8,128)(2,1)S(1)}, u32[]{:S(2)}, u32[]{:S(2)}) %collective-permute-start.29) | collective-permute-done | bytes 262176 | tf_op jit(solution)/shard_map/ppermute | solution.py:324
  (230 shorter events, 35.9 us)
Async XLA Ops:
  3.2 17.5 %all-to-all-start = ((bf16[16,32,256]{2,1,0:T(8,128)(2,1)}), bf16[16,32,256]{2,1,0:T(8,128)(2,1)S(1)}, u32[]{:S(2)}, u32[]{:S(2)}) async-start(bf16[16,32,256]{2,1,0:T(8,128)(2,1)} %broadcast_select_fusion), calls=%async_computation | async-start | bytes 524288 | tf_op jit(solution)/shard_map/all_to_all | solution.py:82
  10.6 25.5 %collective-permute-start.4 = (bf16[1024,1024]{1,0:T(8,128)(2,1)}, bf16[1024,1024]{1,0:T(8,128)(2,1)}, u32[]{:S(2)}, u32[]{:S(2)}) collective-permute-start(bf16[1024,1024]{1,0:T(8,128)(2,1)} %param.22), channel_id=1, source_target_pairs={{0,4},{4,0},{8,12},{12,8},{1,5},{5,1},{9,13},{13,9},{2,6},{6,2},{1... | collective-permute-start | bytes 6291464 | tf_op jit(solution)/shard_map/ppermute | solution.py:187
  25.1 8.2 %collective-permute-start = (bf16[128,1024]{1,0:T(8,128)(2,1)S(1)}, bf16[128,1024]{1,0:T(8,128)(2,1)S(1)}, u32[]{:S(2)}, u32[]{:S(2)}) collective-permute-start(bf16[128,1024]{1,0:T(8,128)(2,1)S(1)} %copy.52), channel_id=1, source_target_pairs={{0,8},{4,12},{8,0},{12,4},{1,9},{5,13},{9,1},{13,5},{2,10},{6,14},... | collective-permute-start | bytes 786440 | tf_op jit(solution)/shard_map/ppermute | solution.py:205
  25.8 6.1 %collective-permute-start.3 = (f32[8,128]{1,0:T(8,128)S(1)}, f32[8,128]{1,0:T(8,128)S(1)}, u32[]{:S(2)}, u32[]{:S(2)}) collective-permute-start(f32[8,128]{1,0:T(8,128)S(1)} %bitcast.177), channel_id=1, source_target_pairs={{0,12},{4,0},{8,4},{12,8},{1,13},{5,1},{9,5},{13,9},{2,14},{6,2},{... | collective-permute-start | bytes 12296 | tf_op jit(solution)/shard_map/ppermute | solution.py:184
  26.3 7.0 %collective-permute-start.2 = (f32[8,128]{1,0:T(8,128)S(1)}, f32[8,128]{1,0:T(8,128)S(1)}, u32[]{:S(2)}, u32[]{:S(2)}) collective-permute-start(f32[8,128]{1,0:T(8,128)S(1)} %bitcast.178), channel_id=1, source_target_pairs={{0,8},{4,12},{8,0},{12,4},{1,9},{5,13},{9,1},{13,5},{2,10},{6,14},... | collective-permute-start | bytes 12296 | tf_op jit(solution)/shard_map/ppermute | solution.py:184
  27.5 5.8 %collective-permute-start.1 = (f32[8,128]{1,0:T(8,128)S(1)}, f32[8,128]{1,0:T(8,128)S(1)}, u32[]{:S(2)}, u32[]{:S(2)}) collective-permute-start(f32[8,128]{1,0:T(8,128)S(1)} %bitcast.179), channel_id=1, source_target_pairs={{0,4},{4,8},{8,12},{12,0},{1,5},{5,9},{9,13},{13,1},{2,6},{6,10},{... | collective-permute-start | bytes 12296 | tf_op jit(solution)/shard_map/ppermute | solution.py:184
  31.9 32.3 %collective-permute-start.5 = (bf16[64,2048]{1,0:T(8,128)(2,1)S(1)}, bf16[64,2048]{1,0:T(8,128)(2,1)S(1)}, u32[]{:S(2)}, u32[]{:S(2)}) collective-permute-start(bf16[64,2048]{1,0:T(8,128)(2,1)S(1)} %dynamic_slice.156), channel_id=1, source_target_pairs={{0,8},{4,12},{8,0},{12,4},{1,9},{5,13},{9,1},{13,5},{2,10},{6,14},... | collective-permute-start | bytes 786440 | tf_op jit(solution)/shard_map/ppermute | solution.py:197
  38.6 16.3 %collective-permute-start.7 = (bf16[64,2048]{1,0:T(8,128)(2,1)S(1)}, bf16[64,2048]{1,0:T(8,128)(2,1)S(1)}, u32[]{:S(2)}, u32[]{:S(2)}) collective-permute-start(bf16[64,2048]{1,0:T(8,128)(2,1)S(1)} %pad_maximum_fusion.9), channel_id=1, source_target_pairs={{0,3},{1,0},{2,1},{3,2},{4,7},{5,4},{6,5},{7,6},{8,11},{9,8},{10,9... | collective-permute-start | bytes 786440 | tf_op jit(solution)/shard_map/ppermute | solution.py:225
  39.9 15.0 %collective-permute-start.6 = (bf16[64,2048]{1,0:T(8,128)(2,1)S(1)}, bf16[64,2048]{1,0:T(8,128)(2,1)S(1)}, u32[]{:S(2)}, u32[]{:S(2)}) collective-permute-start(bf16[64,2048]{1,0:T(8,128)(2,1)S(1)} %pad_maximum_fusion.8), channel_id=1, source_target_pairs={{0,1},{1,2},{2,3},{3,0},{4,5},{5,6},{6,7},{7,4},{8,9},{9,10},{10,1... | collective-permute-start | bytes 786440 | tf_op jit(solution)/shard_map/ppermute | solution.py:225
  40.7 23.5 %collective-permute-start.8 = (bf16[64,2048]{1,0:T(8,128)(2,1)S(1)}, bf16[64,2048]{1,0:T(8,128)(2,1)S(1)}, u32[]{:S(2)}, u32[]{:S(2)}) collective-permute-start(bf16[64,2048]{1,0:T(8,128)(2,1)S(1)} %pad_maximum_fusion.10), channel_id=1, source_target_pairs={{0,2},{1,3},{2,0},{3,1},{4,6},{5,7},{6,4},{7,5},{8,10},{9,11},{10,... | collective-permute-start | bytes 786440 | tf_op jit(solution)/shard_map/ppermute | solution.py:225
  64.5 7.8 %collective-permute-start.10 = (bf16[64,2048]{1,0:T(8,128)(2,1)S(1)}, bf16[64,2048]{1,0:T(8,128)(2,1)S(1)}, u32[]{:S(2)}, u32[]{:S(2)}) collective-permute-start(bf16[64,2048]{1,0:T(8,128)(2,1)S(1)} %fusion.33), channel_id=1, source_target_pairs={{0,8},{4,12},{8,0},{12,4},{1,9},{5,13},{9,1},{13,5},{2,10},{6,14},... | collective-permute-start | bytes 786440 | tf_op jit(solution)/shard_map/ppermute | solution.py:248
  65.5 9.8 %collective-permute-start.9 = (bf16[64,2048]{1,0:T(8,128)(2,1)S(1)}, bf16[64,2048]{1,0:T(8,128)(2,1)S(1)}, u32[]{:S(2)}, u32[]{:S(2)}) collective-permute-start(bf16[64,2048]{1,0:T(8,128)(2,1)S(1)} %fusion.33), channel_id=1, source_target_pairs={{0,1},{1,2},{2,3},{3,0},{4,5},{5,6},{6,7},{7,4},{8,9},{9,10},{10,1... | collective-permute-start | bytes 786440 | tf_op jit(solution)/shard_map/ppermute | solution.py:251
  75.4 7.2 %collective-permute-start.12 = (bf16[64,2048]{1,0:T(8,128)(2,1)S(1)}, bf16[64,2048]{1,0:T(8,128)(2,1)S(1)}, u32[]{:S(2)}, u32[]{:S(2)}) collective-permute-start(bf16[64,2048]{1,0:T(8,128)(2,1)S(1)} %collective-permute-done.9), channel_id=1, source_target_pairs={{0,8},{4,12},{8,0},{12,4},{1,9},{5,13},{9,1},{13,5},{2,10},{6,14},... | collective-permute-start | bytes 786440 | tf_op jit(solution)/shard_map/ppermute | solution.py:248
  75.9 8.5 %collective-permute-start.11 = (bf16[64,2048]{1,0:T(8,128)(2,1)S(1)}, bf16[64,2048]{1,0:T(8,128)(2,1)S(1)}, u32[]{:S(2)}, u32[]{:S(2)}) collective-permute-start(bf16[64,2048]{1,0:T(8,128)(2,1)S(1)} %collective-permute-done.9), channel_id=1, source_target_pairs={{0,1},{1,2},{2,3},{3,0},{4,5},{5,6},{6,7},{7,4},{8,9},{9,10},{10,1... | collective-permute-start | bytes 786440 | tf_op jit(solution)/shard_map/ppermute | solution.py:251
  84.4 6.4 %collective-permute-start.14 = (bf16[64,2048]{1,0:T(8,128)(2,1)S(1)}, bf16[64,2048]{1,0:T(8,128)(2,1)S(1)}, u32[]{:S(2)}, u32[]{:S(2)}) collective-permute-start(bf16[64,2048]{1,0:T(8,128)(2,1)S(1)} %collective-permute-done.11), channel_id=1, source_target_pairs={{0,8},{4,12},{8,0},{12,4},{1,9},{5,13},{9,1},{13,5},{2,10},{6,14},... | collective-permute-start | bytes 786440 | tf_op jit(solution)/shard_map/ppermute | solution.py:248
  86.1 8.2 %collective-permute-start.13 = (bf16[64,2048]{1,0:T(8,128)(2,1)S(1)}, bf16[64,2048]{1,0:T(8,128)(2,1)S(1)}, u32[]{:S(2)}, u32[]{:S(2)}) collective-permute-start(bf16[64,2048]{1,0:T(8,128)(2,1)S(1)} %collective-permute-done.11), channel_id=1, source_target_pairs={{0,1},{1,2},{2,3},{3,0},{4,5},{5,6},{6,7},{7,4},{8,9},{9,10},{10,1... | collective-permute-start | bytes 786440 | tf_op jit(solution)/shard_map/ppermute | solution.py:251
  86.7 8.1 %collective-permute-start.17 = (bf16[64,4096]{1,0:T(8,128)(2,1)S(1)}, bf16[64,4096]{1,0:T(8,128)(2,1)S(1)}, u32[]{:S(2)}, u32[]{:S(2)}) collective-permute-start(bf16[64,4096]{1,0:T(8,128)(2,1)S(1)} %get-tuple-element.272.refs_1_), channel_id=1, source_target_pairs={{0,4},{4,0},{8,12},{12,8},{1,5},{5,1},{9,13},{13,9},{2,6},{6,2},{1... | collective-permute-start | bytes 1572872 | tf_op jit(solution)/shard_map/ppermute | solution.py:272
  86.8 8.1 %collective-permute-start.16 = (bf16[64,4096]{1,0:T(8,128)(2,1)S(1)}, bf16[64,4096]{1,0:T(8,128)(2,1)S(1)}, u32[]{:S(2)}, u32[]{:S(2)}) collective-permute-start(bf16[64,4096]{1,0:T(8,128)(2,1)S(1)} %get-tuple-element.273.refs_0_), channel_id=1, source_target_pairs={{0,4},{4,0},{8,12},{12,8},{1,5},{5,1},{9,13},{13,9},{2,6},{6,2},{1... | collective-permute-start | bytes 1572872 | tf_op jit(solution)/shard_map/ppermute | solution.py:272
  94.3 12.2 %collective-permute-start.15 = (bf16[64,2048]{1,0:T(8,128)(2,1)S(1)}, bf16[64,2048]{1,0:T(8,128)(2,1)S(1)}, u32[]{:S(2)}, u32[]{:S(2)}) collective-permute-start(bf16[64,2048]{1,0:T(8,128)(2,1)S(1)} %collective-permute-done.13), channel_id=1, source_target_pairs={{0,8},{4,12},{8,0},{12,4},{1,9},{5,13},{9,1},{13,5},{2,10},{6,14},... | collective-permute-start | bytes 786440 | tf_op jit(solution)/shard_map/ppermute | solution.py:248
  107.1 2.0 %collective-permute-start.19 = (bf16[64,4096]{1,0:T(8,128)(2,1)S(1)}, bf16[64,4096]{1,0:T(8,128)(2,1)S(1)}, u32[]{:S(2)}, u32[]{:S(2)}) collective-permute-start(bf16[64,4096]{1,0:T(8,128)(2,1)S(1)} %get-tuple-element.270.refs_1_), channel_id=1, source_target_pairs={{0,4},{4,0},{8,12},{12,8},{1,5},{5,1},{9,13},{13,9},{2,6},{6,2},{1... | collective-permute-start | bytes 1572872 | tf_op jit(solution)/shard_map/ppermute | solution.py:272
  107.2 2.6 %collective-permute-start.18 = (bf16[64,4096]{1,0:T(8,128)(2,1)S(1)}, bf16[64,4096]{1,0:T(8,128)(2,1)S(1)}, u32[]{:S(2)}, u32[]{:S(2)}) collective-permute-start(bf16[64,4096]{1,0:T(8,128)(2,1)S(1)} %get-tuple-element.271.refs_0_), channel_id=1, source_target_pairs={{0,4},{4,0},{8,12},{12,8},{1,5},{5,1},{9,13},{13,9},{2,6},{6,2},{1... | collective-permute-start | bytes 1572872 | tf_op jit(solution)/shard_map/ppermute | solution.py:272
  125.5 4.7 %collective-permute-start.20 = (bf16[256,1024]{1,0:T(8,128)(2,1)}, bf16[256,1024]{1,0:T(8,128)(2,1)S(1)}, u32[]{:S(2)}, u32[]{:S(2)}) collective-permute-start(bf16[256,1024]{1,0:T(8,128)(2,1)} %slice.235), channel_id=1, source_target_pairs={{0,4},{4,0},{8,12},{12,8},{1,5},{5,1},{9,13},{13,9},{2,6},{6,2},{1... | collective-permute-start | bytes 1572872 | tf_op jit(solution)/shard_map/ppermute | solution.py:307
  129.5 2.1 %collective-permute-start.22 = (bf16[256,1024]{1,0:T(8,128)(2,1)}, bf16[256,1024]{1,0:T(8,128)(2,1)S(1)}, u32[]{:S(2)}, u32[]{:S(2)}) collective-permute-start(bf16[256,1024]{1,0:T(8,128)(2,1)} %slice.233), channel_id=1, source_target_pairs={{0,4},{4,0},{8,12},{12,8},{1,5},{5,1},{9,13},{13,9},{2,6},{6,2},{1... | collective-permute-start | bytes 1572872 | tf_op jit(solution)/shard_map/ppermute | solution.py:307
  135.9 5.5 %collective-permute-start.23 = (bf16[256,1024]{1,0:T(8,128)(2,1)S(1)}, bf16[256,1024]{1,0:T(8,128)(2,1)S(1)}, u32[]{:S(2)}, u32[]{:S(2)}) collective-permute-start(bf16[256,1024]{1,0:T(8,128)(2,1)S(1)} %slice.232), channel_id=1, source_target_pairs={{0,4},{4,0},{8,12},{12,8},{1,5},{5,1},{9,13},{13,9},{2,6},{6,2},{1... | collective-permute-start | bytes 1572872 | tf_op jit(solution)/shard_map/ppermute | solution.py:307
  139.0 2.7 %collective-permute-start.21 = (bf16[256,1024]{1,0:T(8,128)(2,1)S(1)}, bf16[256,1024]{1,0:T(8,128)(2,1)S(1)}, u32[]{:S(2)}, u32[]{:S(2)}) collective-permute-start(bf16[256,1024]{1,0:T(8,128)(2,1)S(1)} %slice.234), channel_id=1, source_target_pairs={{0,4},{4,0},{8,12},{12,8},{1,5},{5,1},{9,13},{13,9},{2,6},{6,2},{1... | collective-permute-start | bytes 1572872 | tf_op jit(solution)/shard_map/ppermute | solution.py:307
  139.4 9.2 %collective-permute-start.24 = (bf16[128,1024]{1,0:T(8,128)(2,1)S(1)}, bf16[128,1024]{1,0:T(8,128)(2,1)S(1)}, u32[]{:S(2)}, u32[]{:S(2)}) collective-permute-start(bf16[128,1024]{1,0:T(8,128)(2,1)S(1)} %slice.239), channel_id=1, source_target_pairs={{0,8},{4,12},{8,0},{12,4},{1,9},{5,13},{9,1},{13,5},{2,10},{6,14},... | collective-permute-start | bytes 786440 | tf_op jit(solution)/shard_map/ppermute | solution.py:313
  141.2 13.0 %collective-permute-start.26 = (bf16[128,1024]{1,0:T(8,128)(2,1)S(1)}, bf16[128,1024]{1,0:T(8,128)(2,1)S(1)}, u32[]{:S(2)}, u32[]{:S(2)}) collective-permute-start(bf16[128,1024]{1,0:T(8,128)(2,1)S(1)} %slice.238), channel_id=1, source_target_pairs={{0,8},{4,12},{8,0},{12,4},{1,9},{5,13},{9,1},{13,5},{2,10},{6,14},... | collective-permute-start | bytes 786440 | tf_op jit(solution)/shard_map/ppermute | solution.py:313
  142.0 23.4 %collective-permute-start.30 = (bf16[128,1024]{1,0:T(8,128)(2,1)S(1)}, bf16[128,1024]{1,0:T(8,128)(2,1)S(1)}, u32[]{:S(2)}, u32[]{:S(2)}) collective-permute-start(bf16[128,1024]{1,0:T(8,128)(2,1)S(1)} %slice.236), channel_id=1, source_target_pairs={{0,8},{4,12},{8,0},{12,4},{1,9},{5,13},{9,1},{13,5},{2,10},{6,14},... | collective-permute-start | bytes 786440 | tf_op jit(solution)/shard_map/ppermute | solution.py:313
  143.8 21.1 %collective-permute-start.28 = (bf16[128,1024]{1,0:T(8,128)(2,1)S(1)}, bf16[128,1024]{1,0:T(8,128)(2,1)S(1)}, u32[]{:S(2)}, u32[]{:S(2)}) collective-permute-start(bf16[128,1024]{1,0:T(8,128)(2,1)S(1)} %slice.237), channel_id=1, source_target_pairs={{0,8},{4,12},{8,0},{12,4},{1,9},{5,13},{9,1},{13,5},{2,10},{6,14},... | collective-permute-start | bytes 786440 | tf_op jit(solution)/shard_map/ppermute | solution.py:313
  148.6 17.3 %collective-permute-start.25 = (bf16[128,1024]{1,0:T(8,128)(2,1)S(1)}, bf16[128,1024]{1,0:T(8,128)(2,1)S(1)}, u32[]{:S(2)}, u32[]{:S(2)}) collective-permute-start(bf16[128,1024]{1,0:T(8,128)(2,1)S(1)} %convert_add_fusion.2), channel_id=1, source_target_pairs={{0,2},{1,3},{2,0},{3,1},{4,6},{5,7},{6,4},{7,5},{8,10},{9,11},{10,... | collective-permute-start | bytes 786440 | tf_op jit(solution)/shard_map/ppermute | solution.py:324
  154.2 11.6 %collective-permute-start.27 = (bf16[128,1024]{1,0:T(8,128)(2,1)S(1)}, bf16[128,1024]{1,0:T(8,128)(2,1)S(1)}, u32[]{:S(2)}, u32[]{:S(2)}) collective-permute-start(bf16[128,1024]{1,0:T(8,128)(2,1)S(1)} %convert_add_fusion.1), channel_id=1, source_target_pairs={{0,3},{1,0},{2,1},{3,2},{4,7},{5,4},{6,5},{7,6},{8,11},{9,8},{10,9... | collective-permute-start | bytes 786440 | tf_op jit(solution)/shard_map/ppermute | solution.py:324
  165.0 9.7 %collective-permute-start.29 = (bf16[128,1024]{1,0:T(8,128)(2,1)S(1)}, bf16[128,1024]{1,0:T(8,128)(2,1)S(1)}, u32[]{:S(2)}, u32[]{:S(2)}) collective-permute-start(bf16[128,1024]{1,0:T(8,128)(2,1)S(1)} %convert_add_fusion), channel_id=1, source_target_pairs={{0,1},{1,2},{2,3},{3,0},{4,5},{5,6},{6,7},{7,4},{8,9},{9,10},{10,1... | collective-permute-start | bytes 786440 | tf_op jit(solution)/shard_map/ppermute | solution.py:324
  (33 other events, 163.9 us)

commit v6 on v4

--- a/solution.py
+++ b/solution.py
@@ -1,6 +1,8 @@
 import jax
 import jax.numpy as jnp
 from jax import lax
+from jax.experimental import pallas as pl
+from jax.experimental.pallas import tpu as pltpu
 from jax.sharding import PartitionSpec as P
 
 
@@ -10,6 +12,27 @@
 
 def pick(array, index, axis=0):
     return lax.dynamic_index_in_dim(array, index, axis, keepdims=False)
+
+
+def after(array, *others):
+    return lax.optimization_barrier((array, *others))[0]
+
+
+def bring_kernel(source, target, sem):
+    copy = pltpu.make_async_copy(source, target, sem)
+    copy.start()
+    copy.wait()
+
+
+def bring(array):
+    return pl.pallas_call(
+        bring_kernel,
+        in_specs=[pl.BlockSpec(memory_space=pl.ANY)],
+        out_specs=pl.BlockSpec(memory_space=pltpu.VMEM),
+        out_shape=pltpu.VMEM(array.shape, array.dtype),
+        scratch_shapes=[pltpu.SemaphoreType.DMA],
+        compiler_params=pltpu.CompilerParams(vmem_limit_bytes=1024 * 1024),
+    )(array)
 
 
 def attention(queries, suffix_kv, kv_pool, page_table, prefix_len):
@@ -172,7 +195,7 @@
     own_terms, other_terms, w_gate_up = lax.optimization_barrier(
         (own_terms, other_terms, w_gate_up)
     )
-    gate_up_weight = w_gate_up[0].reshape(model_width, 2 * ff_local)
+    gate_up_weight = bring(w_gate_up[0].reshape(model_width, 2 * ff_local))
     gots = [
         lax.ppermute(term(step).astype(bf16), "donor", rotation(n_donor, step)) for step in steps
     ]
@@ -260,22 +283,22 @@
         mixed = jnp.dot(act_rows, down, preferred_element_type=f32)
         swapped.append(lax.ppermute(mixed[:half_rows].astype(bf16), "expert", swap))
         kept.append(mixed[half_rows:])
-    pending = []
+    pending, before = [], []
     for place in range(n_donor):
-        pair_sum = (kept[place] + swapped[place].astype(f32)).reshape(n_rows, suffix_len, columns)
+        block = kept[place] + after(swapped[place], *before).astype(f32)
+        before = [block]
+        block = block.reshape(n_rows, suffix_len, columns)
         arriving = [
-            lax.ppermute(pair_sum[hop].astype(bf16), "expert", turn(hop)) for hop in range(1, n_rows)
+            lax.ppermute(block[hop].astype(bf16), "expert", turn(hop)) for hop in range(1, n_rows)
         ]
-        pending.append((pair_sum[0], arriving))
-    first = pending[0][0]
-    first, swapped[-1] = lax.optimization_barrier((first, swapped[-1]))
+        pending.append((block[0], arriving))
     total = resid
     for place, step in enumerate(order):
         part_sum, arriving = pending[place]
-        if place == 0:
-            part_sum = first
+        part_sum = after(part_sum, *before)
         for got in arriving:
             part_sum = part_sum + got.astype(f32)
+        before = [part_sum]
         if step:
             part_sum = lax.ppermute(part_sum.astype(bf16), "donor", rotation(n_donor, step))
         total = total + part_sum.astype(f32)

time: 156 us -> 155 us (level)
  starting transfers between devices: 26.6 us -> 23.2 us
    ppermute x4, waiting for transfers between devices: 17.6 us -> 21.3 us  [shards(): lax.ppermute(block[hop].astype(bf16), 'expert', turn(hop))]
    ppermute x3, waiting for transfers between devices: 8.55 us -> 6.43 us  [shards(): lax.ppermute(part_sum.astype(bf16), 'donor', rotation(n_donor, step))]
    ppermute x3, starting transfers between devices: 2.19 us -> 0.19 us  [shards(): lax.ppermute(part_sum.astype(bf16), 'donor', rotation(n_donor, step))]
    unnamed x36 -> x40, local copies, waits for them, and re-layouts: 14 us -> 14.5 us
  transfers between devices with their start and end apart: 32 -> 32, of which waited for: 18 -> 19; matrix products, arithmetic and copies ran while one was open for 24% -> 21% of each run, Pallas kernels for 0% -> 1%
where the time goes in v6:
time: 155 us; the launch traced here: 154 us
  waiting for transfers between devices  75.7 us (49%)
  starting transfers between devices  23.2 us (15%)
  matrix products  22.5 us (15%)
  local copies, waits for them, and re-layouts  21 us (14%)
  other arithmetic  8.67 us (6%)
  between operations  2.37 us (2%)
    ppermute x4, waiting for transfers between devices, shards(): lax.ppermute(block[hop].astype(bf16), 'expert', turn(hop))  21.3 us
    ppermute x4, waiting for transfers between devices, shards(): lax.ppermute(chunk, 'expert', turn(hop))  16.7 us
    unnamed x40, local copies, waits for them, and re-layouts  14.5 us
    dot_general x2, matrix products, shards(): gate_up = jnp.dot(rows_in, gate_up_weight, preferred_element_type=f32)  13.3 us
    ppermute x3, waiting for transfers between devices, shards(): chunk = lax.ppermute(chunk, 'donor', rotation(n_donor, 1))  8.42 us
    ppermute x3, waiting for transfers between devices, shards(): lax.ppermute(term(step).astype(bf16), 'donor', rotation(n_donor, step))  8.05 us
    all_to_all x1, starting transfers between devices, attention(): lax.all_to_all(outgoing, ('expert', 'donor'), split_axis=0, concat_axis=0...  7.39 us
    ppermute x3, waiting for transfers between devices, shards(): lax.ppermute(part_sum.astype(bf16), 'donor', rotation(n_donor, step))  6.43 us
  transfers between devices with their start and end apart: 32, of which 19 were waited for; matrix products, arithmetic and copies ran while one was open for 21% of the time, Pallas kernels for 1%

profile of v6, /device:TPU:0, one launch (start us, length us, event | category | flops | bytes accessed | tf_op | source)
XLA Modules:
  0.0 154.3 jit_solution(6502209920170010848)
XLA Ops:
  3.2 7.4 %all-to-all-start = ((bf16[16,32,256]{2,1,0:T(8,128)(2,1)}), bf16[16,32,256]{2,1,0:T(8,128)(2,1)S(1)}, u32[]{:S(2)}, u32[]{:S(2)}) async-start(bf16[16,32,256]{2,1,0:T(8,128)(2,1)} %broadcast_select_fusion), calls=%async_computation | async-start | bytes 524288 | tf_op jit(solution)/shard_map/all_to_all | solution.py:57
  11.0 1.0 constant_dynamic-slice_fusion.17
  12.1 1.3 dynamic_slice.150
  15.0 5.7 %all-to-all-done = bf16[16,32,256]{2,1,0:T(8,128)(2,1)S(1)} async-done(((bf16[16,32,256]{2,1,0:T(8,128)(2,1)}), bf16[16,32,256]{2,1,0:T(8,128)(2,1)S(1)}, u32[]{:S(2)}, u32[]{:S(2)}) %all-to-all-start) | async-done | bytes 262176 | tf_op jit(solution)/shard_map/all_to_all | solution.py:57
  21.4 1.2 while.22
  23.1 1.9 %while.23 = (s32[]{:T(128)}, f32[128,8]{0,1:T(8,128)S(1)}, f32[128,8,128]{2,0,1:T(8,128)S(1)}, s32[]{:T(128)}, s32[]{:T(128)}, /*index=5*/bf16[128,8,128]{2,0,1:...) while((s32[]{:T(128)}, f32[128,8]{0,1:T(8,128)S(1)}, ...), condition=%wide.region_8.9_spmd, body=%wide.region_6.8_spmd.sunk | while | flops 271188992 | bytes 3691649 | solution.py:113
  26.6 1.2 collective-permute-start.2
  28.3 3.9 %collective-permute-done.3 = f32[8,128]{1,0:T(8,128)S(1)} collective-permute-done((f32[8,128]{1,0:T(8,128)S(1)}, f32[8,128]{1,0:T(8,128)S(1)}, u32[]{:S(2)}, u32[]{:S(2)}) %collective-permute-start.3) | collective-permute-done | bytes 4128 | tf_op jit(solution)/shard_map/ppermute | solution.py:159
  34.4 2.3 %fusion.67 = f32[256,1024]{1,0:T(8,128)S(1)} fusion(bf16[1024,1024]{1,0:T(8,128)(2,1)} %collective-permute-done.4, bf16[64,1024]{1,0:T(8,128)(2,1)S(1)} %get-tuple-element.263, bf16[64,1024]{1,0:T(8,128)(2,1)S(1)} %get-tuple-element.264, bf16[64,1024]{1,0:T(8,128)(2,1)S(1)} %get-tuple-element.265, bf16[64,1024]{1,0:T(8,128)(2,1)S(1)} %get-tuple-element.262), kind=kOutput, calls=%fused_computation.163 | convolution fusion | flops 538968064 | bytes 3670016 | tf_op jit(solution)/shard_map/dot_general | solution.py:186
  36.8 1.3 collective-permute-start.7
  40.0 9.1 %copy.53 = bf16[512,8,2,768]{3,1,2,0:T(8,128)(2,1)S(1)} copy(bf16[512,8,2,768]{3,2,1,0:T(2,128)(2,1)} %bitcast.160) | data formatting | bytes 25165824
  49.9 4.5 %copy-done.2 = bf16[4096,1536]{1,0:T(8,128)(2,1)} copy-done((bf16[4096,1536]{1,0:T(8,128)(2,1)}, bf16[4096,1536]{1,0:T(8,128)(2,1)S(1)}, u32[]{:S(2)}) %copy-start.2) | copy-done | bytes 12582936
  54.5 8.0 %collective-permute-done.8 = bf16[64,2048]{1,0:T(8,128)(2,1)S(1)} collective-permute-done((bf16[64,2048]{1,0:T(8,128)(2,1)S(1)}, bf16[64,2048]{1,0:T(8,128)(2,1)S(1)}, u32[]{:S(2)}, u32[]{:S(2)}) %collective-permute-start.8) | collective-permute-done | bytes 262176 | tf_op jit(solution)/shard_map/ppermute | solution.py:200
  62.8 1.0 collective-permute-start.10
  64.7 5.9 %collective-permute-done.10 = bf16[64,2048]{1,0:T(8,128)(2,1)S(1)} collective-permute-done((bf16[64,2048]{1,0:T(8,128)(2,1)S(1)}, bf16[64,2048]{1,0:T(8,128)(2,1)S(1)}, u32[]{:S(2)}, u32[]{:S(2)}) %collective-permute-start.10) | collective-permute-done | bytes 262176 | tf_op jit(solution)/shard_map/ppermute | solution.py:223
  70.6 3.1 %collective-permute-done.9 = bf16[64,2048]{1,0:T(8,128)(2,1)S(1)} collective-permute-done((bf16[64,2048]{1,0:T(8,128)(2,1)S(1)}, bf16[64,2048]{1,0:T(8,128)(2,1)S(1)}, u32[]{:S(2)}, u32[]{:S(2)}) %collective-permute-start.9) | collective-permute-done | bytes 262176 | tf_op jit(solution)/shard_map/ppermute | solution.py:226
  74.4 6.4 %collective-permute-done.12 = bf16[64,2048]{1,0:T(8,128)(2,1)S(1)} collective-permute-done((bf16[64,2048]{1,0:T(8,128)(2,1)S(1)}, bf16[64,2048]{1,0:T(8,128)(2,1)S(1)}, u32[]{:S(2)}, u32[]{:S(2)}) %collective-permute-start.12) | collective-permute-done | bytes 262176 | tf_op jit(solution)/shard_map/ppermute | solution.py:223
  80.9 1.8 %collective-permute-done.11 = bf16[64,2048]{1,0:T(8,128)(2,1)S(1)} collective-permute-done((bf16[64,2048]{1,0:T(8,128)(2,1)S(1)}, bf16[64,2048]{1,0:T(8,128)(2,1)S(1)}, u32[]{:S(2)}, u32[]{:S(2)}) %collective-permute-start.11) | collective-permute-done | bytes 262176 | tf_op jit(solution)/shard_map/ppermute | solution.py:226
  82.7 1.7 %collective-permute-start.14 = (bf16[64,2048]{1,0:T(8,128)(2,1)S(1)}, bf16[64,2048]{1,0:T(8,128)(2,1)S(1)}, u32[]{:S(2)}, u32[]{:S(2)}) collective-permute-start(bf16[64,2048]{1,0:T(8,128)(2,1)S(1)} %collective-permute-done.11), channel_id=1, source_target_pairs={{0,8},{4,12},{8,0},{12,4},{1,9},{5,13},{9,1},{13,5},{2,10},{6,14},... | collective-permute-start | bytes 786440 | tf_op jit(solution)/shard_map/ppermute | solution.py:223
  84.7 4.4 %collective-permute-done.14 = bf16[64,2048]{1,0:T(8,128)(2,1)S(1)} collective-permute-done((bf16[64,2048]{1,0:T(8,128)(2,1)S(1)}, bf16[64,2048]{1,0:T(8,128)(2,1)S(1)}, u32[]{:S(2)}, u32[]{:S(2)}) %collective-permute-start.14) | collective-permute-done | bytes 262176 | tf_op jit(solution)/shard_map/ppermute | solution.py:223
  89.0 3.5 %collective-permute-done.13 = bf16[64,2048]{1,0:T(8,128)(2,1)S(1)} collective-permute-done((bf16[64,2048]{1,0:T(8,128)(2,1)S(1)}, bf16[64,2048]{1,0:T(8,128)(2,1)S(1)}, u32[]{:S(2)}, u32[]{:S(2)}) %collective-permute-start.13) | collective-permute-done | bytes 262176 | tf_op jit(solution)/shard_map/ppermute | solution.py:226
  96.0 6.5 %fusion.4 = f32[256,1536]{1,0:T(8,128)S(1)} fusion(bf16[4096,1536]{1,0:T(8,128)(2,1)} %copy-done.2, bf16[64,4096]{1,0:T(8,128)(2,1)S(1)} %collective-permute-done.17, bf16[64,4096]{1,0:T(8,128)(2,1)S(1)} %collective-permute-done.16, bf16[64,4096]{1,0:T(8,128)(2,1)S(1)} %get-tuple-element.277, bf16[64,4096]{1,0:T(8,128)(2,1)S(1)} %get-tuple-element.278), kind=kOutput, calls=%fused_computation.11 | convolution fusion | flops 3229614080 | bytes 16252928 | tf_op jit(solution)/shard_map/dot_general | solution.py:252
  104.2 1.8 %collective-permute-done.19 = bf16[64,4096]{1,0:T(8,128)(2,1)} collective-permute-done((bf16[64,4096]{1,0:T(8,128)(2,1)S(1)}, bf16[64,4096]{1,0:T(8,128)(2,1)}, u32[]{:S(2)}, u32[]{:S(2)}) %collective-permute-start.19) | collective-permute-done | bytes 524320 | tf_op jit(solution)/shard_map/ppermute | solution.py:247
  106.0 6.8 %fusion.12 = f32[256,1536]{1,0:T(8,128)S(1)} fusion(bf16[4096,1536]{1,0:T(8,128)(2,1)} %copy-done.2, bf16[64,4096]{1,0:T(8,128)(2,1)} %collective-permute-done.19, bf16[64,4096]{1,0:T(8,128)(2,1)} %collective-permute-done.18, bf16[64,4096]{1,0:T(8,128)(2,1)S(1)} %fusion.45, bf16[64,4096]{1,0:T(8,128)(2,1)S(1)} %get-tuple-element.276), kind=kOutput, calls=%fused_computation.19 | convolution fusion | flops 3229614080 | bytes 16252928 | tf_op jit(solution)/shard_map/dot_general | solution.py:252
  114.0 1.0 fusion.26
  117.4 1.1 collective-permute-done.21
  121.9 1.7 %collective-permute-start.26 = (bf16[128,1024]{1,0:T(8,128)(2,1)S(1)}, bf16[128,1024]{1,0:T(8,128)(2,1)S(1)}, u32[]{:S(2)}, u32[]{:S(2)}) collective-permute-start(bf16[128,1024]{1,0:T(8,128)(2,1)S(1)} %slice.270), channel_id=1, source_target_pairs={{0,8},{4,12},{8,0},{12,4},{1,9},{5,13},{9,1},{13,5},{2,10},{6,14},... | collective-permute-start | bytes 786440 | tf_op jit(solution)/shard_map/ppermute | solution.py:292
  124.5 6.3 %collective-permute-done.24 = bf16[128,1024]{1,0:T(8,128)(2,1)S(1)} collective-permute-done((bf16[128,1024]{1,0:T(8,128)(2,1)S(1)}, bf16[128,1024]{1,0:T(8,128)(2,1)S(1)}, u32[]{:S(2)}, u32[]{:S(2)}) %collective-permute-start.24) | collective-permute-done | bytes 262176 | tf_op jit(solution)/shard_map/ppermute | solution.py:292
  131.0 5.4 %collective-permute-done.26 = bf16[128,1024]{1,0:T(8,128)(2,1)S(1)} collective-permute-done((bf16[128,1024]{1,0:T(8,128)(2,1)S(1)}, bf16[128,1024]{1,0:T(8,128)(2,1)S(1)}, u32[]{:S(2)}, u32[]{:S(2)}) %collective-permute-start.26) | collective-permute-done | bytes 262176 | tf_op jit(solution)/shard_map/ppermute | solution.py:292
  136.9 5.1 %collective-permute-done.28 = bf16[128,1024]{1,0:T(8,128)(2,1)S(1)} collective-permute-done((bf16[128,1024]{1,0:T(8,128)(2,1)S(1)}, bf16[128,1024]{1,0:T(8,128)(2,1)S(1)}, u32[]{:S(2)}, u32[]{:S(2)}) %collective-permute-start.28) | collective-permute-done | bytes 262176 | tf_op jit(solution)/shard_map/ppermute | solution.py:292
  142.4 4.6 %collective-permute-done.30 = bf16[128,1024]{1,0:T(8,128)(2,1)S(1)} collective-permute-done((bf16[128,1024]{1,0:T(8,128)(2,1)S(1)}, bf16[128,1024]{1,0:T(8,128)(2,1)S(1)}, u32[]{:S(2)}, u32[]{:S(2)}) %collective-permute-start.30) | collective-permute-done | bytes 262176 | tf_op jit(solution)/shard_map/ppermute | solution.py:292
  146.9 6.4 %collective-permute-done.27 = bf16[128,1024]{1,0:T(8,128)(2,1)S(1)} collective-permute-done((bf16[128,1024]{1,0:T(8,128)(2,1)S(1)}, bf16[128,1024]{1,0:T(8,128)(2,1)S(1)}, u32[]{:S(2)}, u32[]{:S(2)}) %collective-permute-start.27) | collective-permute-done | bytes 262176 | tf_op jit(solution)/shard_map/ppermute | solution.py:303
  (200 shorter events, 31.5 us)
Async XLA Ops:
  3.2 17.5 %all-to-all-start = ((bf16[16,32,256]{2,1,0:T(8,128)(2,1)}), bf16[16,32,256]{2,1,0:T(8,128)(2,1)S(1)}, u32[]{:S(2)}, u32[]{:S(2)}) async-start(bf16[16,32,256]{2,1,0:T(8,128)(2,1)} %broadcast_select_fusion), calls=%async_computation | async-start | bytes 524288 | tf_op jit(solution)/shard_map/all_to_all | solution.py:57
  10.6 23.8 %collective-permute-start.4 = (bf16[1024,1024]{1,0:T(8,128)(2,1)}, bf16[1024,1024]{1,0:T(8,128)(2,1)}, u32[]{:S(2)}, u32[]{:S(2)}) collective-permute-start(bf16[1024,1024]{1,0:T(8,128)(2,1)} %param.22), channel_id=1, source_target_pairs={{0,4},{4,0},{8,12},{12,8},{1,5},{5,1},{9,13},{13,9},{2,6},{6,2},{1... | collective-permute-start | bytes 6291464 | tf_op jit(solution)/shard_map/ppermute | solution.py:162
  25.4 8.1 %collective-permute-start = (bf16[128,1024]{1,0:T(8,128)(2,1)S(1)}, bf16[128,1024]{1,0:T(8,128)(2,1)S(1)}, u32[]{:S(2)}, u32[]{:S(2)}) collective-permute-start(bf16[128,1024]{1,0:T(8,128)(2,1)S(1)} %copy.48), channel_id=1, source_target_pairs={{0,8},{4,12},{8,0},{12,4},{1,9},{5,13},{9,1},{13,5},{2,10},{6,14},... | collective-permute-start | bytes 786440 | tf_op jit(solution)/shard_map/ppermute | solution.py:180
  26.1 6.1 %collective-permute-start.3 = (f32[8,128]{1,0:T(8,128)S(1)}, f32[8,128]{1,0:T(8,128)S(1)}, u32[]{:S(2)}, u32[]{:S(2)}) collective-permute-start(f32[8,128]{1,0:T(8,128)S(1)} %bitcast.174), channel_id=1, source_target_pairs={{0,12},{4,0},{8,4},{12,8},{1,13},{5,1},{9,5},{13,9},{2,14},{6,2},{... | collective-permute-start | bytes 12296 | tf_op jit(solution)/shard_map/ppermute | solution.py:159
  26.6 7.0 %collective-permute-start.2 = (f32[8,128]{1,0:T(8,128)S(1)}, f32[8,128]{1,0:T(8,128)S(1)}, u32[]{:S(2)}, u32[]{:S(2)}) collective-permute-start(f32[8,128]{1,0:T(8,128)S(1)} %bitcast.175), channel_id=1, source_target_pairs={{0,8},{4,12},{8,0},{12,4},{1,9},{5,13},{9,1},{13,5},{2,10},{6,14},... | collective-permute-start | bytes 12296 | tf_op jit(solution)/shard_map/ppermute | solution.py:159
  27.8 5.8 %collective-permute-start.1 = (f32[8,128]{1,0:T(8,128)S(1)}, f32[8,128]{1,0:T(8,128)S(1)}, u32[]{:S(2)}, u32[]{:S(2)}) collective-permute-start(f32[8,128]{1,0:T(8,128)S(1)} %bitcast.176), channel_id=1, source_target_pairs={{0,4},{4,8},{8,12},{12,0},{1,5},{5,9},{9,13},{13,1},{2,6},{6,10},{... | collective-permute-start | bytes 12296 | tf_op jit(solution)/shard_map/ppermute | solution.py:159
  32.2 30.3 %collective-permute-start.5 = (bf16[64,2048]{1,0:T(8,128)(2,1)S(1)}, bf16[64,2048]{1,0:T(8,128)(2,1)S(1)}, u32[]{:S(2)}, u32[]{:S(2)}) collective-permute-start(bf16[64,2048]{1,0:T(8,128)(2,1)S(1)} %dynamic_slice.156), channel_id=1, source_target_pairs={{0,8},{4,12},{8,0},{12,4},{1,9},{5,13},{9,1},{13,5},{2,10},{6,14},... | collective-permute-start | bytes 786440 | tf_op jit(solution)/shard_map/ppermute | solution.py:172
  36.8 17.6 %collective-permute-start.7 = (bf16[64,2048]{1,0:T(8,128)(2,1)S(1)}, bf16[64,2048]{1,0:T(8,128)(2,1)S(1)}, u32[]{:S(2)}, u32[]{:S(2)}) collective-permute-start(bf16[64,2048]{1,0:T(8,128)(2,1)S(1)} %pad_maximum_fusion.9), channel_id=1, source_target_pairs={{0,3},{1,0},{2,1},{3,2},{4,7},{5,4},{6,5},{7,6},{8,11},{9,8},{10,9... | collective-permute-start | bytes 786440 | tf_op jit(solution)/shard_map/ppermute | solution.py:200
  38.2 16.3 %collective-permute-start.6 = (bf16[64,2048]{1,0:T(8,128)(2,1)S(1)}, bf16[64,2048]{1,0:T(8,128)(2,1)S(1)}, u32[]{:S(2)}, u32[]{:S(2)}) collective-permute-start(bf16[64,2048]{1,0:T(8,128)(2,1)S(1)} %pad_maximum_fusion.8), channel_id=1, source_target_pairs={{0,1},{1,2},{2,3},{3,0},{4,5},{5,6},{6,7},{7,4},{8,9},{9,10},{10,1... | collective-permute-start | bytes 786440 | tf_op jit(solution)/shard_map/ppermute | solution.py:200
  39.0 23.5 %collective-permute-start.8 = (bf16[64,2048]{1,0:T(8,128)(2,1)S(1)}, bf16[64,2048]{1,0:T(8,128)(2,1)S(1)}, u32[]{:S(2)}, u32[]{:S(2)}) collective-permute-start(bf16[64,2048]{1,0:T(8,128)(2,1)S(1)} %pad_maximum_fusion.10), channel_id=1, source_target_pairs={{0,2},{1,3},{2,0},{3,1},{4,6},{5,7},{6,4},{7,5},{8,10},{9,11},{10,... | collective-permute-start | bytes 786440 | tf_op jit(solution)/shard_map/ppermute | solution.py:200
  62.8 7.8 %collective-permute-start.10 = (bf16[64,2048]{1,0:T(8,128)(2,1)S(1)}, bf16[64,2048]{1,0:T(8,128)(2,1)S(1)}, u32[]{:S(2)}, u32[]{:S(2)}) collective-permute-start(bf16[64,2048]{1,0:T(8,128)(2,1)S(1)} %fusion.53), channel_id=1, source_target_pairs={{0,8},{4,12},{8,0},{12,4},{1,9},{5,13},{9,1},{13,5},{2,10},{6,14},... | collective-permute-start | bytes 786440 | tf_op jit(solution)/shard_map/ppermute | solution.py:223
  63.8 9.8 %collective-permute-start.9 = (bf16[64,2048]{1,0:T(8,128)(2,1)S(1)}, bf16[64,2048]{1,0:T(8,128)(2,1)S(1)}, u32[]{:S(2)}, u32[]{:S(2)}) collective-permute-start(bf16[64,2048]{1,0:T(8,128)(2,1)S(1)} %fusion.53), channel_id=1, source_target_pairs={{0,1},{1,2},{2,3},{3,0},{4,5},{5,6},{6,7},{7,4},{8,9},{9,10},{10,1... | collective-permute-start | bytes 786440 | tf_op jit(solution)/shard_map/ppermute | solution.py:226
  73.7 7.2 %collective-permute-start.12 = (bf16[64,2048]{1,0:T(8,128)(2,1)S(1)}, bf16[64,2048]{1,0:T(8,128)(2,1)S(1)}, u32[]{:S(2)}, u32[]{:S(2)}) collective-permute-start(bf16[64,2048]{1,0:T(8,128)(2,1)S(1)} %collective-permute-done.9), channel_id=1, source_target_pairs={{0,8},{4,12},{8,0},{12,4},{1,9},{5,13},{9,1},{13,5},{2,10},{6,14},... | collective-permute-start | bytes 786440 | tf_op jit(solution)/shard_map/ppermute | solution.py:223
  74.2 8.5 %collective-permute-start.11 = (bf16[64,2048]{1,0:T(8,128)(2,1)S(1)}, bf16[64,2048]{1,0:T(8,128)(2,1)S(1)}, u32[]{:S(2)}, u32[]{:S(2)}) collective-permute-start(bf16[64,2048]{1,0:T(8,128)(2,1)S(1)} %collective-permute-done.9), channel_id=1, source_target_pairs={{0,1},{1,2},{2,3},{3,0},{4,5},{5,6},{6,7},{7,4},{8,9},{9,10},{10,1... | collective-permute-start | bytes 786440 | tf_op jit(solution)/shard_map/ppermute | solution.py:226
  82.7 6.4 %collective-permute-start.14 = (bf16[64,2048]{1,0:T(8,128)(2,1)S(1)}, bf16[64,2048]{1,0:T(8,128)(2,1)S(1)}, u32[]{:S(2)}, u32[]{:S(2)}) collective-permute-start(bf16[64,2048]{1,0:T(8,128)(2,1)S(1)} %collective-permute-done.11), channel_id=1, source_target_pairs={{0,8},{4,12},{8,0},{12,4},{1,9},{5,13},{9,1},{13,5},{2,10},{6,14},... | collective-permute-start | bytes 786440 | tf_op jit(solution)/shard_map/ppermute | solution.py:223
  84.4 8.2 %collective-permute-start.13 = (bf16[64,2048]{1,0:T(8,128)(2,1)S(1)}, bf16[64,2048]{1,0:T(8,128)(2,1)S(1)}, u32[]{:S(2)}, u32[]{:S(2)}) collective-permute-start(bf16[64,2048]{1,0:T(8,128)(2,1)S(1)} %collective-permute-done.11), channel_id=1, source_target_pairs={{0,1},{1,2},{2,3},{3,0},{4,5},{5,6},{6,7},{7,4},{8,9},{9,10},{10,1... | collective-permute-start | bytes 786440 | tf_op jit(solution)/shard_map/ppermute | solution.py:226
  93.3 2.0 %collective-permute-start.17 = (bf16[64,4096]{1,0:T(8,128)(2,1)S(1)}, bf16[64,4096]{1,0:T(8,128)(2,1)S(1)}, u32[]{:S(2)}, u32[]{:S(2)}) collective-permute-start(bf16[64,4096]{1,0:T(8,128)(2,1)S(1)} %get-tuple-element.277), channel_id=1, source_target_pairs={{0,4},{4,0},{8,12},{12,8},{1,5},{5,1},{9,13},{13,9},{2,6},{6,2},{1... | collective-permute-start | bytes 1572872 | tf_op jit(solution)/shard_map/ppermute | solution.py:247
  93.4 2.6 %collective-permute-start.16 = (bf16[64,4096]{1,0:T(8,128)(2,1)S(1)}, bf16[64,4096]{1,0:T(8,128)(2,1)S(1)}, u32[]{:S(2)}, u32[]{:S(2)}) collective-permute-start(bf16[64,4096]{1,0:T(8,128)(2,1)S(1)} %get-tuple-element.278), channel_id=1, source_target_pairs={{0,4},{4,0},{8,12},{12,8},{1,5},{5,1},{9,13},{13,9},{2,6},{6,2},{1... | collective-permute-start | bytes 1572872 | tf_op jit(solution)/shard_map/ppermute | solution.py:247
  94.0 9.4 %collective-permute-start.15 = (bf16[64,2048]{1,0:T(8,128)(2,1)S(1)}, bf16[64,2048]{1,0:T(8,128)(2,1)S(1)}, u32[]{:S(2)}, u32[]{:S(2)}) collective-permute-start(bf16[64,2048]{1,0:T(8,128)(2,1)S(1)} %collective-permute-done.13), channel_id=1, source_target_pairs={{0,8},{4,12},{8,0},{12,4},{1,9},{5,13},{9,1},{13,5},{2,10},{6,14},... | collective-permute-start | bytes 786440 | tf_op jit(solution)/shard_map/ppermute | solution.py:223
  94.3 9.9 %collective-permute-start.18 = (bf16[64,4096]{1,0:T(8,128)(2,1)S(1)}, bf16[64,4096]{1,0:T(8,128)(2,1)}, u32[]{:S(2)}, u32[]{:S(2)}) collective-permute-start(bf16[64,4096]{1,0:T(8,128)(2,1)S(1)} %get-tuple-element.276), channel_id=1, source_target_pairs={{0,4},{4,0},{8,12},{12,8},{1,5},{5,1},{9,13},{13,9},{2,6},{6,2},{1... | collective-permute-start | bytes 1572872 | tf_op jit(solution)/shard_map/ppermute | solution.py:247
  103.9 2.1 %collective-permute-start.19 = (bf16[64,4096]{1,0:T(8,128)(2,1)S(1)}, bf16[64,4096]{1,0:T(8,128)(2,1)}, u32[]{:S(2)}, u32[]{:S(2)}) collective-permute-start(bf16[64,4096]{1,0:T(8,128)(2,1)S(1)} %fusion.45), channel_id=1, source_target_pairs={{0,4},{4,0},{8,12},{12,8},{1,5},{5,1},{9,13},{13,9},{2,6},{6,2},{1... | collective-permute-start | bytes 1572872 | tf_op jit(solution)/shard_map/ppermute | solution.py:247
  115.1 2.0 %collective-permute-start.20 = (bf16[256,1024]{1,0:T(8,128)(2,1)S(1)}, bf16[256,1024]{1,0:T(8,128)(2,1)S(1)}, u32[]{:S(2)}, u32[]{:S(2)}) collective-permute-start(bf16[256,1024]{1,0:T(8,128)(2,1)S(1)} %slice.267), channel_id=1, source_target_pairs={{0,4},{4,0},{8,12},{12,8},{1,5},{5,1},{9,13},{13,9},{2,6},{6,2},{1... | collective-permute-start | bytes 1572872 | tf_op jit(solution)/shard_map/ppermute | solution.py:284
  116.5 2.0 %collective-permute-start.21 = (bf16[256,1024]{1,0:T(8,128)(2,1)S(1)}, bf16[256,1024]{1,0:T(8,128)(2,1)S(1)}, u32[]{:S(2)}, u32[]{:S(2)}) collective-permute-start(bf16[256,1024]{1,0:T(8,128)(2,1)S(1)} %slice.266), channel_id=1, source_target_pairs={{0,4},{4,0},{8,12},{12,8},{1,5},{5,1},{9,13},{13,9},{2,6},{6,2},{1... | collective-permute-start | bytes 1572872 | tf_op jit(solution)/shard_map/ppermute | solution.py:284
  119.6 4.1 %collective-permute-start.23 = (bf16[256,1024]{1,0:T(8,128)(2,1)S(1)}, bf16[256,1024]{1,0:T(8,128)(2,1)S(1)}, u32[]{:S(2)}, u32[]{:S(2)}) collective-permute-start(bf16[256,1024]{1,0:T(8,128)(2,1)S(1)} %slice.264), channel_id=1, source_target_pairs={{0,4},{4,0},{8,12},{12,8},{1,5},{5,1},{9,13},{13,9},{2,6},{6,2},{1... | collective-permute-start | bytes 1572872 | tf_op jit(solution)/shard_map/ppermute | solution.py:284
  121.0 2.8 %collective-permute-start.22 = (bf16[256,1024]{1,0:T(8,128)(2,1)S(1)}, bf16[256,1024]{1,0:T(8,128)(2,1)S(1)}, u32[]{:S(2)}, u32[]{:S(2)}) collective-permute-start(bf16[256,1024]{1,0:T(8,128)(2,1)S(1)} %slice.265), channel_id=1, source_target_pairs={{0,4},{4,0},{8,12},{12,8},{1,5},{5,1},{9,13},{13,9},{2,6},{6,2},{1... | collective-permute-start | bytes 1572872 | tf_op jit(solution)/shard_map/ppermute | solution.py:284
  121.5 9.2 %collective-permute-start.24 = (bf16[128,1024]{1,0:T(8,128)(2,1)S(1)}, bf16[128,1024]{1,0:T(8,128)(2,1)S(1)}, u32[]{:S(2)}, u32[]{:S(2)}) collective-permute-start(bf16[128,1024]{1,0:T(8,128)(2,1)S(1)} %slice.271), channel_id=1, source_target_pairs={{0,8},{4,12},{8,0},{12,4},{1,9},{5,13},{9,1},{13,5},{2,10},{6,14},... | collective-permute-start | bytes 786440 | tf_op jit(solution)/shard_map/ppermute | solution.py:292
  121.9 14.4 %collective-permute-start.26 = (bf16[128,1024]{1,0:T(8,128)(2,1)S(1)}, bf16[128,1024]{1,0:T(8,128)(2,1)S(1)}, u32[]{:S(2)}, u32[]{:S(2)}) collective-permute-start(bf16[128,1024]{1,0:T(8,128)(2,1)S(1)} %slice.270), channel_id=1, source_target_pairs={{0,8},{4,12},{8,0},{12,4},{1,9},{5,13},{9,1},{13,5},{2,10},{6,14},... | collective-permute-start | bytes 786440 | tf_op jit(solution)/shard_map/ppermute | solution.py:292
  124.1 17.9 %collective-permute-start.28 = (bf16[128,1024]{1,0:T(8,128)(2,1)S(1)}, bf16[128,1024]{1,0:T(8,128)(2,1)S(1)}, u32[]{:S(2)}, u32[]{:S(2)}) collective-permute-start(bf16[128,1024]{1,0:T(8,128)(2,1)S(1)} %slice.269), channel_id=1, source_target_pairs={{0,8},{4,12},{8,0},{12,4},{1,9},{5,13},{9,1},{13,5},{2,10},{6,14},... | collective-permute-start | bytes 786440 | tf_op jit(solution)/shard_map/ppermute | solution.py:292
  130.9 22.5 %collective-permute-start.25 = (bf16[128,1024]{1,0:T(8,128)(2,1)S(1)}, bf16[128,1024]{1,0:T(8,128)(2,1)S(1)}, u32[]{:S(2)}, u32[]{:S(2)}) collective-permute-start(bf16[128,1024]{1,0:T(8,128)(2,1)S(1)} %convert_add_fusion.2), channel_id=1, source_target_pairs={{0,2},{1,3},{2,0},{3,1},{4,6},{5,7},{6,4},{7,5},{8,10},{9,11},{10,... | collective-permute-start | bytes 786440 | tf_op jit(solution)/shard_map/ppermute | solution.py:303
  136.4 16.9 %collective-permute-start.27 = (bf16[128,1024]{1,0:T(8,128)(2,1)S(1)}, bf16[128,1024]{1,0:T(8,128)(2,1)S(1)}, u32[]{:S(2)}, u32[]{:S(2)}) collective-permute-start(bf16[128,1024]{1,0:T(8,128)(2,1)S(1)} %convert_add_fusion.1), channel_id=1, source_target_pairs={{0,3},{1,0},{2,1},{3,2},{4,7},{5,4},{6,5},{7,6},{8,11},{9,8},{10,9... | collective-permute-start | bytes 786440 | tf_op jit(solution)/shard_map/ppermute | solution.py:303
  136.5 10.4 %collective-permute-start.30 = (bf16[128,1024]{1,0:T(8,128)(2,1)S(1)}, bf16[128,1024]{1,0:T(8,128)(2,1)S(1)}, u32[]{:S(2)}, u32[]{:S(2)}) collective-permute-start(bf16[128,1024]{1,0:T(8,128)(2,1)S(1)} %slice.268), channel_id=1, source_target_pairs={{0,8},{4,12},{8,0},{12,4},{1,9},{5,13},{9,1},{13,5},{2,10},{6,14},... | collective-permute-start | bytes 786440 | tf_op jit(solution)/shard_map/ppermute | solution.py:292
  142.0 11.3 %collective-permute-start.29 = (bf16[128,1024]{1,0:T(8,128)(2,1)S(1)}, bf16[128,1024]{1,0:T(8,128)(2,1)S(1)}, u32[]{:S(2)}, u32[]{:S(2)}) collective-permute-start(bf16[128,1024]{1,0:T(8,128)(2,1)S(1)} %convert_add_fusion), channel_id=1, source_target_pairs={{0,1},{1,2},{2,3},{3,0},{4,5},{5,6},{6,7},{7,4},{8,9},{9,10},{10,1... | collective-permute-start | bytes 786440 | tf_op jit(solution)/shard_map/ppermute | solution.py:303
  (17 other events, 110.4 us)

commit v7 on v4

--- a/solution.py
+++ b/solution.py
@@ -10,6 +10,10 @@
 
 def pick(array, index, axis=0):
     return lax.dynamic_index_in_dim(array, index, axis, keepdims=False)
+
+
+def after(array, *others):
+    return lax.optimization_barrier((array, *others))[0]
 
 
 def attention(queries, suffix_kv, kv_pool, page_table, prefix_len):
@@ -193,7 +197,7 @@
     gain_f = norm_gain.astype(f32)
     resid_parts = [None] * n_donor
     own_act, other_act = [None] * n_donor, [None] * n_donor
-    batch = max(1, n_donor // 2)
+    batches = [max(1, n_donor - 1), 1]
     own_rows, other_rows, row_gates = [], [], []
     for slot in range(n_donor):
         part = (z - slot) % n_donor
@@ -201,10 +205,10 @@
         here = chunk
         if slot < n_donor - 1:
             chunk = lax.ppermute(chunk, "donor", rotation(n_donor, 1))
-            chunk, gots = lax.optimization_barrier((chunk, gots))
-        if slot == n_donor - 1 and slot >= batch:
-            gots, own_act[:batch], other_act[:batch] = lax.optimization_barrier(
-                (gots, own_act[:batch], other_act[:batch])
+            chunk, gots, other_rows[:-1] = lax.optimization_barrier((chunk, gots, other_rows[:-1]))
+        if slot == n_donor - 1 and slot > 0:
+            gots, own_act[:slot], other_act[:slot] = lax.optimization_barrier(
+                (gots, own_act[:slot], other_act[:slot])
             )
         if n_rows == 2:
             block = jnp.concatenate(
@@ -223,7 +227,8 @@
         own_rows.append(normed)
         other_rows.append(lax.ppermute(normed, "expert", swap))
         row_gates.append((pick(own_gates, part), pick(other_gates, part)))
-        if len(row_gates) == batch:
+        if len(row_gates) == batches[0]:
+            batch = batches.pop(0)
             rows_in = jnp.concatenate(own_rows + other_rows, axis=0)
             scale = jnp.concatenate([g[0] for g in row_gates] + [g[1] for g in row_gates])
             gate_up = jnp.dot(rows_in, gate_up_weight, preferred_element_type=f32)
@@ -251,34 +256,39 @@
     half_rows = n_rows * suffix_len
     resid = by_sequence(resid_parts, 1).astype(f32)
 
-    swapped, kept = [], []
     order = steps[::-1] + [0]
+    pending, before = [], []
     for place, step in enumerate(order):
-        if place >= 2:
-            act_rows, swapped[place - 2] = lax.optimization_barrier((act_rows, swapped[place - 2]))
+        if place == 2:
+            act_rows = after(act_rows, *pending[0][1])
         down = lax.dynamic_slice_in_dim(w_down[0], (z + step) % n_donor * columns, columns, 1)
         mixed = jnp.dot(act_rows, down, preferred_element_type=f32)
-        swapped.append(lax.ppermute(mixed[:half_rows].astype(bf16), "expert", swap))
-        kept.append(mixed[half_rows:])
-    pending = []
-    for place in range(n_donor):
-        pair_sum = (kept[place] + swapped[place].astype(f32)).reshape(n_rows, suffix_len, columns)
+        got = lax.ppermute(mixed[:half_rows].astype(bf16), "expert", swap)
+        block = mixed[half_rows:] + after(got, *before).astype(f32)
+        before = [block]
+        block = block.reshape(n_rows, suffix_len, columns)
         arriving = [
-            lax.ppermute(pair_sum[hop].astype(bf16), "expert", turn(hop)) for hop in range(1, n_rows)
+            lax.ppermute(block[hop].astype(bf16), "expert", turn(hop)) for hop in range(1, n_rows)
         ]
-        pending.append((pair_sum[0], arriving))
-    first = pending[0][0]
-    first, swapped[-1] = lax.optimization_barrier((first, swapped[-1]))
+        pending.append((block[0], arriving))
     total = resid
+    carry = {1: [], -1: []}
+    before = []
     for place, step in enumerate(order):
         part_sum, arriving = pending[place]
-        if place == 0:
-            part_sum = first
+        part_sum = after(part_sum, *before)
         for got in arriving:
             part_sum = part_sum + got.astype(f32)
+        before = [part_sum]
         if step:
-            part_sum = lax.ppermute(part_sum.astype(bf16), "donor", rotation(n_donor, step))
-        total = total + part_sum.astype(f32)
+            way = 1 if step <= n_donor // 2 else -1
+            for got in carry[way]:
+                part_sum = part_sum + got.astype(f32)
+            carry[way] = [lax.ppermute(part_sum.astype(bf16), "donor", rotation(n_donor, way))]
+        else:
+            total = total + part_sum
+    for got in carry[1] + carry[-1]:
+        total = total + got.astype(f32)
     return (total.astype(bf16), head_out)
 
 

time: 156 us -> 157 us (level)
  waiting for transfers between devices: 75.7 us -> 68.8 us
  local copies, waits for them, and re-layouts: 20.4 us -> 24.1 us
  other arithmetic: 8.53 us -> 11.6 us
    ppermute x11, waiting for transfers between devices: 27.4 us -> 24.6 us  [the longest x4 19.3 us: shards(): lax.ppermute(block[hop].astype(bf16), 'expert', turn(hop))]
    ppermute x3, waiting for transfers between devices: 9.41 us -> 6.79 us  [shards(): lax.ppermute(term(step).astype(bf16), 'donor', rotation(n_donor, step))]
    concatenate x4, local copies, waits for them, and re-layouts: 0.32 us -> 2.73 us  [core_gates(): return jnp.concatenate(rows).reshape(n_donor, part_rows)]
    concatenate x3, other arithmetic: 0.06 us -> 2.18 us  [term(): jnp.concatenate([jnp.where(core == 0, own, other), jnp.where(core == 0, o...]
    dot_general x1, matrix products: 0.71 us -> 2.3 us  [shards(): own_terms = jnp.dot(heads, out_weight, preferred_element_type=f32)]
    unnamed x36 -> x44, local copies, waits for them, and re-layouts: 14 us -> 13.6 us
  transfers between devices with their start and end apart: 32 -> 32, of which waited for: 18 -> 19; matrix products, arithmetic and copies ran while one was open for 24% -> 29% of each run, Pallas kernels for 0% -> 0%
where the time goes in v7:
time: 157 us; the launch traced here: 156 us
  waiting for transfers between devices  68.8 us (44%)
  starting transfers between devices  26.7 us (17%)
  local copies, waits for them, and re-layouts  24.1 us (15%)
  matrix products  22.5 us (14%)
  other arithmetic  11.6 us (7%)
  between operations  2.33 us (1%)
    ppermute x4, waiting for transfers between devices, shards(): lax.ppermute(block[hop].astype(bf16), 'expert', turn(hop))  19.3 us
    ppermute x4, waiting for transfers between devices, shards(): lax.ppermute(chunk, 'expert', turn(hop))  16.3 us
    unnamed x44, local copies, waits for them, and re-layouts  13.6 us
    dot_general x2, matrix products, shards(): gate_up = jnp.dot(rows_in, gate_up_weight, preferred_element_type=f32)  11.7 us
    ppermute x3, waiting for transfers between devices, shards(): chunk = lax.ppermute(chunk, 'donor', rotation(n_donor, 1))  8.41 us
    all_to_all x1, starting transfers between devices, attention(): lax.all_to_all(outgoing, ('expert', 'donor'), split_axis=0, concat_axis=0...  7.39 us
    ppermute x3, waiting for transfers between devices, shards(): lax.ppermute(term(step).astype(bf16), 'donor', rotation(n_donor, step))  6.79 us
    all_to_all x1, waiting for transfers between devices, attention(): lax.all_to_all(outgoing, ('expert', 'donor'), split_axis=0, concat_axis=0...  5.83 us
  transfers between devices with their start and end apart: 32, of which 19 were waited for; matrix products, arithmetic and copies ran while one was open for 29% of the time, Pallas kernels for 0%

profile of v7, /device:TPU:0, one launch (start us, length us, event | category | flops | bytes accessed | tf_op | source)
XLA Modules:
  0.0 156.2 jit_solution(4947756854947115060)
XLA Ops:
  3.2 7.4 %all-to-all-start = ((bf16[16,32,256]{2,1,0:T(8,128)(2,1)}), bf16[16,32,256]{2,1,0:T(8,128)(2,1)S(1)}, u32[]{:S(2)}, u32[]{:S(2)}) async-start(bf16[16,32,256]{2,1,0:T(8,128)(2,1)} %broadcast_select_fusion), calls=%async_computation | async-start | bytes 524288 | tf_op jit(solution)/shard_map/all_to_all | solution.py:38
  12.1 1.3 dynamic_slice.150
  14.8 5.8 %all-to-all-done = bf16[16,32,256]{2,1,0:T(8,128)(2,1)S(1)} async-done(((bf16[16,32,256]{2,1,0:T(8,128)(2,1)}), bf16[16,32,256]{2,1,0:T(8,128)(2,1)S(1)}, u32[]{:S(2)}, u32[]{:S(2)}) %all-to-all-start) | async-done | bytes 262176 | tf_op jit(solution)/shard_map/all_to_all | solution.py:38
  23.0 1.8 %while.23 = (s32[]{:T(128)}, f32[128,8]{0,1:T(8,128)S(1)}, f32[128,8,128]{2,0,1:T(8,128)S(1)}, s32[]{:T(128)}, s32[]{:T(128)}, /*index=5*/bf16[128,8,128]{2,0,1:...) while((s32[]{:T(128)}, f32[128,8]{0,1:T(8,128)S(1)}, ...), condition=%wide.region_8.9_spmd, body=%wide.region_6.8_spmd.sunk | while | flops 271188992 | bytes 3691649 | solution.py:94
  26.4 1.2 collective-permute-start.2
  29.1 3.0 %collective-permute-done.3 = f32[8,128]{1,0:T(8,128)S(1)} collective-permute-done((f32[8,128]{1,0:T(8,128)S(1)}, f32[8,128]{1,0:T(8,128)S(1)}, u32[]{:S(2)}, u32[]{:S(2)}) %collective-permute-start.3) | collective-permute-done | bytes 4128 | tf_op jit(solution)/shard_map/ppermute | solution.py:140
  35.5 2.3 %fusion.56 = f32[256,1024]{1,0:T(8,128)S(1)} fusion(bf16[1024,1024]{1,0:T(8,128)(2,1)} %param.22, bf16[64,1024]{1,0:T(8,128)(2,1)S(1)} %get-tuple-element.275, bf16[64,1024]{1,0:T(8,128)(2,1)S(1)} %get-tuple-element.276, bf16[64,1024]{1,0:T(8,128)(2,1)S(1)} %get-tuple-element.277, bf16[64,1024]{1,0:T(8,128)(2,1)S(1)} %get-tuple-element.274), kind=kOutput, calls=%fused_computation.153 | convolution fusion | flops 538968064 | bytes 3670016 | tf_op jit(solution)/shard_map/dot_general | solution.py:166
  37.8 2.3 %fusion.55 = f32[256,1024]{1,0:T(8,128)S(1)} fusion(bf16[1024,1024]{1,0:T(8,128)(2,1)} %collective-permute-done.4, bf16[64,1024]{1,0:T(8,128)(2,1)S(1)} %get-tuple-element.275, bf16[64,1024]{1,0:T(8,128)(2,1)S(1)} %get-tuple-element.276, bf16[64,1024]{1,0:T(8,128)(2,1)S(1)} %get-tuple-element.277, bf16[64,1024]{1,0:T(8,128)(2,1)S(1)} %get-tuple-element.274), kind=kOutput, calls=%fused_computation.152 | convolution fusion | flops 538968064 | bytes 3670016 | tf_op jit(solution)/shard_map/dot_general | solution.py:167
  41.0 1.3 collective-permute-start.7
  46.8 13.2 %copy.53 = bf16[512,8,2,768]{3,1,2,0:T(8,128)(2,1)} copy(bf16[512,8,2,768]{3,2,1,0:T(2,128)(2,1)} %bitcast.163) | data formatting | bytes 25165824
  60.0 6.8 %collective-permute-done.8 = bf16[64,2048]{1,0:T(8,128)(2,1)S(1)} collective-permute-done((bf16[64,2048]{1,0:T(8,128)(2,1)}, bf16[64,2048]{1,0:T(8,128)(2,1)S(1)}, u32[]{:S(2)}, u32[]{:S(2)}) %collective-permute-start.8) | collective-permute-done | bytes 262176 | tf_op jit(solution)/shard_map/ppermute | solution.py:181
  66.8 1.2 fusion.39
  69.8 6.1 %collective-permute-done.10 = bf16[64,2048]{1,0:T(8,128)(2,1)S(1)} collective-permute-done((bf16[64,2048]{1,0:T(8,128)(2,1)S(1)}, bf16[64,2048]{1,0:T(8,128)(2,1)S(1)}, u32[]{:S(2)}, u32[]{:S(2)}) %collective-permute-start.10) | collective-permute-done | bytes 262176 | tf_op jit(solution)/shard_map/ppermute | solution.py:204
  75.9 3.1 %collective-permute-done.9 = bf16[64,2048]{1,0:T(8,128)(2,1)S(1)} collective-permute-done((bf16[64,2048]{1,0:T(8,128)(2,1)S(1)}, bf16[64,2048]{1,0:T(8,128)(2,1)S(1)}, u32[]{:S(2)}, u32[]{:S(2)}) %collective-permute-start.9) | collective-permute-done | bytes 262176 | tf_op jit(solution)/shard_map/ppermute | solution.py:207
  80.4 5.7 %collective-permute-done.12 = bf16[64,2048]{1,0:T(8,128)(2,1)S(1)} collective-permute-done((bf16[64,2048]{1,0:T(8,128)(2,1)S(1)}, bf16[64,2048]{1,0:T(8,128)(2,1)S(1)}, u32[]{:S(2)}, u32[]{:S(2)}) %collective-permute-start.12) | collective-permute-done | bytes 262176 | tf_op jit(solution)/shard_map/ppermute | solution.py:204
  86.1 2.2 %collective-permute-done.11 = bf16[64,2048]{1,0:T(8,128)(2,1)S(1)} collective-permute-done((bf16[64,2048]{1,0:T(8,128)(2,1)S(1)}, bf16[64,2048]{1,0:T(8,128)(2,1)S(1)}, u32[]{:S(2)}, u32[]{:S(2)}) %collective-permute-start.11) | collective-permute-done | bytes 262176 | tf_op jit(solution)/shard_map/ppermute | solution.py:207
  88.3 1.4 collective-permute-start.14
  90.2 4.5 %collective-permute-done.14 = bf16[64,2048]{1,0:T(8,128)(2,1)S(1)} collective-permute-done((bf16[64,2048]{1,0:T(8,128)(2,1)S(1)}, bf16[64,2048]{1,0:T(8,128)(2,1)S(1)}, u32[]{:S(2)}, u32[]{:S(2)}) %collective-permute-start.14) | collective-permute-done | bytes 262176 | tf_op jit(solution)/shard_map/ppermute | solution.py:204
  94.7 3.2 %collective-permute-done.13 = bf16[64,2048]{1,0:T(8,128)(2,1)S(1)} collective-permute-done((bf16[64,2048]{1,0:T(8,128)(2,1)S(1)}, bf16[64,2048]{1,0:T(8,128)(2,1)S(1)}, u32[]{:S(2)}, u32[]{:S(2)}) %collective-permute-start.13) | collective-permute-done | bytes 262176 | tf_op jit(solution)/shard_map/ppermute | solution.py:207
  99.2 1.8 %collective-permute-done.18 = bf16[64,4096]{1,0:T(8,128)(2,1)S(1)} collective-permute-done((bf16[64,4096]{1,0:T(8,128)(2,1)S(1)}, bf16[64,4096]{1,0:T(8,128)(2,1)S(1)}, u32[]{:S(2)}, u32[]{:S(2)}) %collective-permute-start.18) | collective-permute-done | bytes 524320 | tf_op jit(solution)/shard_map/ppermute | solution.py:228
  101.0 5.1 %fusion.87 = f32[384,1536]{1,0:T(8,128)S(1)} fusion(bf16[384,4096]{1,0:T(8,128)(2,1)S(1)} %constant_dynamic-update-slice_fusion, bf16[4096,1536]{1,0:T(8,128)(2,1)S(1)} %bitcast.162), kind=kOutput, calls=%fused_computation.242 | convolution fusion | flops 4831838208 | bytes 18087936 | tf_op jit(solution)/shard_map/dot_general | solution.py:234
  108.0 1.7 %collective-permute-done.19 = bf16[64,4096]{1,0:T(8,128)(2,1)S(1)} collective-permute-done((bf16[64,4096]{1,0:T(8,128)(2,1)S(1)}, bf16[64,4096]{1,0:T(8,128)(2,1)S(1)}, u32[]{:S(2)}, u32[]{:S(2)}) %collective-permute-start.19) | collective-permute-done | bytes 524320 | tf_op jit(solution)/shard_map/ppermute | solution.py:228
  109.6 6.6 %fusion.32 = f32[128,1536]{1,0:T(8,128)S(1)} fusion(bf16[4096,1536]{1,0:T(8,128)(2,1)} %bitcast.161, bf16[64,4096]{1,0:T(8,128)(2,1)S(1)} %collective-permute-done.19, bf16[64,4096]{1,0:T(8,128)(2,1)S(1)} %fusion.31), kind=kOutput, calls=%fused_computation.57 | convolution fusion | flops 1612709888 | bytes 14417920 | tf_op jit(solution)/shard_map/dot_general | solution.py:234
  120.2 1.2 collective-permute-done.24
  121.4 1.4 collective-permute-start.21
  123.7 6.8 %collective-permute-done.21 = bf16[128,1024]{1,0:T(8,128)(2,1)S(1)} collective-permute-done((bf16[128,1024]{1,0:T(8,128)(2,1)S(1)}, bf16[128,1024]{1,0:T(8,128)(2,1)S(1)}, u32[]{:S(2)}, u32[]{:S(2)}) %collective-permute-start.21) | collective-permute-done | bytes 262176 | tf_op jit(solution)/shard_map/ppermute | solution.py:271
  133.5 1.9 %collective-permute-done.25 = bf16[128,1024]{1,0:T(8,128)(2,1)S(1)} collective-permute-done((bf16[128,1024]{1,0:T(8,128)(2,1)S(1)}, bf16[128,1024]{1,0:T(8,128)(2,1)S(1)}, u32[]{:S(2)}, u32[]{:S(2)}) %collective-permute-start.25) | collective-permute-done | bytes 262176 | tf_op jit(solution)/shard_map/ppermute | solution.py:271
  135.4 2.0 %collective-permute-start.30 = (bf16[128,1024]{1,0:T(8,128)(2,1)S(1)}, bf16[128,1024]{1,0:T(8,128)(2,1)S(1)}, u32[]{:S(2)}, u32[]{:S(2)}) collective-permute-start(bf16[128,1024]{1,0:T(8,128)(2,1)S(1)} %convert_add_fusion.1), channel_id=1, source_target_pairs={{0,3},{1,0},{2,1},{3,2},{4,7},{5,4},{6,5},{7,6},{8,11},{9,8},{10,9... | collective-permute-start | bytes 786440 | tf_op jit(solution)/shard_map/ppermute | solution.py:287
  137.7 1.4 collective-permute-start.26
  140.1 6.8 %collective-permute-done.26 = bf16[128,1024]{1,0:T(8,128)(2,1)S(1)} collective-permute-done((bf16[128,1024]{1,0:T(8,128)(2,1)S(1)}, bf16[128,1024]{1,0:T(8,128)(2,1)S(1)}, u32[]{:S(2)}, u32[]{:S(2)}) %collective-permute-start.26) | collective-permute-done | bytes 262176 | tf_op jit(solution)/shard_map/ppermute | solution.py:271
  147.5 3.8 %collective-permute-done.27 = bf16[128,1024]{1,0:T(8,128)(2,1)S(1)} collective-permute-done((bf16[128,1024]{1,0:T(8,128)(2,1)S(1)}, bf16[128,1024]{1,0:T(8,128)(2,1)S(1)}, u32[]{:S(2)}, u32[]{:S(2)}) %collective-permute-start.27) | collective-permute-done | bytes 262176 | tf_op jit(solution)/shard_map/ppermute | solution.py:271
  151.3 4.0 %collective-permute-done.29 = bf16[128,1024]{1,0:T(8,128)(2,1)S(1)} collective-permute-done((bf16[128,1024]{1,0:T(8,128)(2,1)S(1)}, bf16[128,1024]{1,0:T(8,128)(2,1)S(1)}, u32[]{:S(2)}, u32[]{:S(2)}) %collective-permute-start.29) | collective-permute-done | bytes 262176 | tf_op jit(solution)/shard_map/ppermute | solution.py:287
  (205 shorter events, 38.9 us)
Async XLA Ops:
  3.2 17.5 %all-to-all-start = ((bf16[16,32,256]{2,1,0:T(8,128)(2,1)}), bf16[16,32,256]{2,1,0:T(8,128)(2,1)S(1)}, u32[]{:S(2)}, u32[]{:S(2)}) async-start(bf16[16,32,256]{2,1,0:T(8,128)(2,1)} %broadcast_select_fusion), calls=%async_computation | async-start | bytes 524288 | tf_op jit(solution)/shard_map/all_to_all | solution.py:38
  10.6 27.2 %collective-permute-start.4 = (bf16[1024,1024]{1,0:T(8,128)(2,1)}, bf16[1024,1024]{1,0:T(8,128)(2,1)}, u32[]{:S(2)}, u32[]{:S(2)}) collective-permute-start(bf16[1024,1024]{1,0:T(8,128)(2,1)} %param.22), channel_id=1, source_target_pairs={{0,4},{4,0},{8,12},{12,8},{1,5},{5,1},{9,13},{13,9},{2,6},{6,2},{1... | collective-permute-start | bytes 6291464 | tf_op jit(solution)/shard_map/ppermute | solution.py:143
  25.3 8.1 %collective-permute-start = (bf16[128,1024]{1,0:T(8,128)(2,1)S(1)}, bf16[128,1024]{1,0:T(8,128)(2,1)S(1)}, u32[]{:S(2)}, u32[]{:S(2)}) collective-permute-start(bf16[128,1024]{1,0:T(8,128)(2,1)S(1)} %copy.48), channel_id=1, source_target_pairs={{0,8},{4,12},{8,0},{12,4},{1,9},{5,13},{9,1},{13,5},{2,10},{6,14},... | collective-permute-start | bytes 786440 | tf_op jit(solution)/shard_map/ppermute | solution.py:161
  25.9 6.1 %collective-permute-start.3 = (f32[8,128]{1,0:T(8,128)S(1)}, f32[8,128]{1,0:T(8,128)S(1)}, u32[]{:S(2)}, u32[]{:S(2)}) collective-permute-start(f32[8,128]{1,0:T(8,128)S(1)} %bitcast.178), channel_id=1, source_target_pairs={{0,12},{4,0},{8,4},{12,8},{1,13},{5,1},{9,5},{13,9},{2,14},{6,2},{... | collective-permute-start | bytes 12296 | tf_op jit(solution)/shard_map/ppermute | solution.py:140
  26.4 7.0 %collective-permute-start.2 = (f32[8,128]{1,0:T(8,128)S(1)}, f32[8,128]{1,0:T(8,128)S(1)}, u32[]{:S(2)}, u32[]{:S(2)}) collective-permute-start(f32[8,128]{1,0:T(8,128)S(1)} %bitcast.179), channel_id=1, source_target_pairs={{0,8},{4,12},{8,0},{12,4},{1,9},{5,13},{9,1},{13,5},{2,10},{6,14},... | collective-permute-start | bytes 12296 | tf_op jit(solution)/shard_map/ppermute | solution.py:140
  27.6 5.8 %collective-permute-start.1 = (f32[8,128]{1,0:T(8,128)S(1)}, f32[8,128]{1,0:T(8,128)S(1)}, u32[]{:S(2)}, u32[]{:S(2)}) collective-permute-start(f32[8,128]{1,0:T(8,128)S(1)} %bitcast.180), channel_id=1, source_target_pairs={{0,4},{4,8},{8,12},{12,0},{1,5},{5,9},{9,13},{13,1},{2,6},{6,10},{... | collective-permute-start | bytes 12296 | tf_op jit(solution)/shard_map/ppermute | solution.py:140
  32.1 34.8 %collective-permute-start.5 = (bf16[64,2048]{1,0:T(8,128)(2,1)S(1)}, bf16[64,2048]{1,0:T(8,128)(2,1)S(1)}, u32[]{:S(2)}, u32[]{:S(2)}) collective-permute-start(bf16[64,2048]{1,0:T(8,128)(2,1)S(1)} %dynamic_slice.156), channel_id=1, source_target_pairs={{0,8},{4,12},{8,0},{12,4},{1,9},{5,13},{9,1},{13,5},{2,10},{6,14},... | collective-permute-start | bytes 786440 | tf_op jit(solution)/shard_map/ppermute | solution.py:153
  41.0 19.0 %collective-permute-start.7 = (bf16[64,2048]{1,0:T(8,128)(2,1)}, bf16[64,2048]{1,0:T(8,128)(2,1)S(1)}, u32[]{:S(2)}, u32[]{:S(2)}) collective-permute-start(bf16[64,2048]{1,0:T(8,128)(2,1)} %pad_maximum_fusion.9), channel_id=1, source_target_pairs={{0,3},{1,0},{2,1},{3,2},{4,7},{5,4},{6,5},{7,6},{8,11},{9,8},{10,9... | collective-permute-start | bytes 786440 | tf_op jit(solution)/shard_map/ppermute | solution.py:181
  42.9 17.1 %collective-permute-start.6 = (bf16[64,2048]{1,0:T(8,128)(2,1)}, bf16[64,2048]{1,0:T(8,128)(2,1)S(1)}, u32[]{:S(2)}, u32[]{:S(2)}) collective-permute-start(bf16[64,2048]{1,0:T(8,128)(2,1)} %pad_maximum_fusion.8), channel_id=1, source_target_pairs={{0,1},{1,2},{2,3},{3,0},{4,5},{5,6},{6,7},{7,4},{8,9},{9,10},{10,1... | collective-permute-start | bytes 786440 | tf_op jit(solution)/shard_map/ppermute | solution.py:181
  44.4 22.4 %collective-permute-start.8 = (bf16[64,2048]{1,0:T(8,128)(2,1)}, bf16[64,2048]{1,0:T(8,128)(2,1)S(1)}, u32[]{:S(2)}, u32[]{:S(2)}) collective-permute-start(bf16[64,2048]{1,0:T(8,128)(2,1)} %pad_maximum_fusion.10), channel_id=1, source_target_pairs={{0,2},{1,3},{2,0},{3,1},{4,6},{5,7},{6,4},{7,5},{8,10},{9,11},{10,... | collective-permute-start | bytes 786440 | tf_op jit(solution)/shard_map/ppermute | solution.py:181
  68.1 7.8 %collective-permute-start.10 = (bf16[64,2048]{1,0:T(8,128)(2,1)S(1)}, bf16[64,2048]{1,0:T(8,128)(2,1)S(1)}, u32[]{:S(2)}, u32[]{:S(2)}) collective-permute-start(bf16[64,2048]{1,0:T(8,128)(2,1)S(1)} %fusion.39), channel_id=1, source_target_pairs={{0,8},{4,12},{8,0},{12,4},{1,9},{5,13},{9,1},{13,5},{2,10},{6,14},... | collective-permute-start | bytes 786440 | tf_op jit(solution)/shard_map/ppermute | solution.py:204
  69.1 9.8 %collective-permute-start.9 = (bf16[64,2048]{1,0:T(8,128)(2,1)S(1)}, bf16[64,2048]{1,0:T(8,128)(2,1)S(1)}, u32[]{:S(2)}, u32[]{:S(2)}) collective-permute-start(bf16[64,2048]{1,0:T(8,128)(2,1)S(1)} %fusion.39), channel_id=1, source_target_pairs={{0,1},{1,2},{2,3},{3,0},{4,5},{5,6},{6,7},{7,4},{8,9},{9,10},{10,1... | collective-permute-start | bytes 786440 | tf_op jit(solution)/shard_map/ppermute | solution.py:207
  78.9 7.2 %collective-permute-start.12 = (bf16[64,2048]{1,0:T(8,128)(2,1)S(1)}, bf16[64,2048]{1,0:T(8,128)(2,1)S(1)}, u32[]{:S(2)}, u32[]{:S(2)}) collective-permute-start(bf16[64,2048]{1,0:T(8,128)(2,1)S(1)} %collective-permute-done.9), channel_id=1, source_target_pairs={{0,8},{4,12},{8,0},{12,4},{1,9},{5,13},{9,1},{13,5},{2,10},{6,14},... | collective-permute-start | bytes 786440 | tf_op jit(solution)/shard_map/ppermute | solution.py:204
  79.8 8.5 %collective-permute-start.11 = (bf16[64,2048]{1,0:T(8,128)(2,1)S(1)}, bf16[64,2048]{1,0:T(8,128)(2,1)S(1)}, u32[]{:S(2)}, u32[]{:S(2)}) collective-permute-start(bf16[64,2048]{1,0:T(8,128)(2,1)S(1)} %collective-permute-done.9), channel_id=1, source_target_pairs={{0,1},{1,2},{2,3},{3,0},{4,5},{5,6},{6,7},{7,4},{8,9},{9,10},{10,1... | collective-permute-start | bytes 786440 | tf_op jit(solution)/shard_map/ppermute | solution.py:207
  80.3 17.5 %collective-permute-start.15 = (bf16[64,4096]{1,0:T(8,128)(2,1)S(1)}, bf16[64,4096]{1,0:T(8,128)(2,1)S(1)}, u32[]{:S(2)}, u32[]{:S(2)}) collective-permute-start(bf16[64,4096]{1,0:T(8,128)(2,1)S(1)} %get-tuple-element.245), channel_id=1, source_target_pairs={{0,4},{4,0},{8,12},{12,8},{1,5},{5,1},{9,13},{13,9},{2,6},{6,2},{1... | collective-permute-start | bytes 1572872 | tf_op jit(solution)/shard_map/ppermute | solution.py:228
  88.3 6.4 %collective-permute-start.14 = (bf16[64,2048]{1,0:T(8,128)(2,1)S(1)}, bf16[64,2048]{1,0:T(8,128)(2,1)S(1)}, u32[]{:S(2)}, u32[]{:S(2)}) collective-permute-start(bf16[64,2048]{1,0:T(8,128)(2,1)S(1)} %collective-permute-done.11), channel_id=1, source_target_pairs={{0,8},{4,12},{8,0},{12,4},{1,9},{5,13},{9,1},{13,5},{2,10},{6,14},... | collective-permute-start | bytes 786440 | tf_op jit(solution)/shard_map/ppermute | solution.py:204
  89.6 8.2 %collective-permute-start.13 = (bf16[64,2048]{1,0:T(8,128)(2,1)S(1)}, bf16[64,2048]{1,0:T(8,128)(2,1)S(1)}, u32[]{:S(2)}, u32[]{:S(2)}) collective-permute-start(bf16[64,2048]{1,0:T(8,128)(2,1)S(1)} %collective-permute-done.11), channel_id=1, source_target_pairs={{0,1},{1,2},{2,3},{3,0},{4,5},{5,6},{6,7},{7,4},{8,9},{9,10},{10,1... | collective-permute-start | bytes 786440 | tf_op jit(solution)/shard_map/ppermute | solution.py:207
  90.1 9.0 %collective-permute-start.17 = (bf16[64,4096]{1,0:T(8,128)(2,1)S(1)}, bf16[64,4096]{1,0:T(8,128)(2,1)S(1)}, u32[]{:S(2)}, u32[]{:S(2)}) collective-permute-start(bf16[64,4096]{1,0:T(8,128)(2,1)S(1)} %get-tuple-element.243), channel_id=1, source_target_pairs={{0,4},{4,0},{8,12},{12,8},{1,5},{5,1},{9,13},{13,9},{2,6},{6,2},{1... | collective-permute-start | bytes 1572872 | tf_op jit(solution)/shard_map/ppermute | solution.py:228
  98.1 9.1 %collective-permute-start.16 = (bf16[64,2048]{1,0:T(8,128)(2,1)S(1)}, bf16[64,2048]{1,0:T(8,128)(2,1)S(1)}, u32[]{:S(2)}, u32[]{:S(2)}) collective-permute-start(bf16[64,2048]{1,0:T(8,128)(2,1)S(1)} %collective-permute-done.13), channel_id=1, source_target_pairs={{0,8},{4,12},{8,0},{12,4},{1,9},{5,13},{9,1},{13,5},{2,10},{6,14},... | collective-permute-start | bytes 786440 | tf_op jit(solution)/shard_map/ppermute | solution.py:204
  99.0 2.0 %collective-permute-start.18 = (bf16[64,4096]{1,0:T(8,128)(2,1)S(1)}, bf16[64,4096]{1,0:T(8,128)(2,1)S(1)}, u32[]{:S(2)}, u32[]{:S(2)}) collective-permute-start(bf16[64,4096]{1,0:T(8,128)(2,1)S(1)} %get-tuple-element.241), channel_id=1, source_target_pairs={{0,4},{4,0},{8,12},{12,8},{1,5},{5,1},{9,13},{13,9},{2,6},{6,2},{1... | collective-permute-start | bytes 1572872 | tf_op jit(solution)/shard_map/ppermute | solution.py:228
  107.7 2.0 %collective-permute-start.19 = (bf16[64,4096]{1,0:T(8,128)(2,1)S(1)}, bf16[64,4096]{1,0:T(8,128)(2,1)S(1)}, u32[]{:S(2)}, u32[]{:S(2)}) collective-permute-start(bf16[64,4096]{1,0:T(8,128)(2,1)S(1)} %fusion.31), channel_id=1, source_target_pairs={{0,4},{4,0},{8,12},{12,8},{1,5},{5,1},{9,13},{13,9},{2,6},{6,2},{1... | collective-permute-start | bytes 1572872 | tf_op jit(solution)/shard_map/ppermute | solution.py:228
  117.9 2.0 %collective-permute-start.20 = (bf16[256,1024]{1,0:T(8,128)(2,1)S(1)}, bf16[256,1024]{1,0:T(8,128)(2,1)S(1)}, u32[]{:S(2)}, u32[]{:S(2)}) collective-permute-start(bf16[256,1024]{1,0:T(8,128)(2,1)S(1)} %slice.269), channel_id=1, source_target_pairs={{0,4},{4,0},{8,12},{12,8},{1,5},{5,1},{9,13},{13,9},{2,6},{6,2},{1... | collective-permute-start | bytes 1572872 | tf_op jit(solution)/shard_map/ppermute | solution.py:266
  119.4 2.0 %collective-permute-start.24 = (bf16[256,1024]{1,0:T(8,128)(2,1)S(1)}, bf16[256,1024]{1,0:T(8,128)(2,1)S(1)}, u32[]{:S(2)}, u32[]{:S(2)}) collective-permute-start(bf16[256,1024]{1,0:T(8,128)(2,1)S(1)} %slice.266), channel_id=1, source_target_pairs={{0,4},{4,0},{8,12},{12,8},{1,5},{5,1},{9,13},{13,9},{2,6},{6,2},{1... | collective-permute-start | bytes 1572872 | tf_op jit(solution)/shard_map/ppermute | solution.py:266
  121.4 9.2 %collective-permute-start.21 = (bf16[128,1024]{1,0:T(8,128)(2,1)S(1)}, bf16[128,1024]{1,0:T(8,128)(2,1)S(1)}, u32[]{:S(2)}, u32[]{:S(2)}) collective-permute-start(bf16[128,1024]{1,0:T(8,128)(2,1)S(1)} %slice.273), channel_id=1, source_target_pairs={{0,8},{4,12},{8,0},{12,4},{1,9},{5,13},{9,1},{13,5},{2,10},{6,14},... | collective-permute-start | bytes 786440 | tf_op jit(solution)/shard_map/ppermute | solution.py:271
  122.9 12.4 %collective-permute-start.25 = (bf16[128,1024]{1,0:T(8,128)(2,1)S(1)}, bf16[128,1024]{1,0:T(8,128)(2,1)S(1)}, u32[]{:S(2)}, u32[]{:S(2)}) collective-permute-start(bf16[128,1024]{1,0:T(8,128)(2,1)S(1)} %slice.272), channel_id=1, source_target_pairs={{0,8},{4,12},{8,0},{12,4},{1,9},{5,13},{9,1},{13,5},{2,10},{6,14},... | collective-permute-start | bytes 786440 | tf_op jit(solution)/shard_map/ppermute | solution.py:271
  130.6 9.6 %collective-permute-start.28 = (bf16[128,1024]{1,0:T(8,128)(2,1)S(1)}, bf16[128,1024]{1,0:T(8,128)(2,1)S(1)}, u32[]{:S(2)}, u32[]{:S(2)}) collective-permute-start(bf16[128,1024]{1,0:T(8,128)(2,1)S(1)} %convert_add_fusion.2), channel_id=1, source_target_pairs={{0,1},{1,2},{2,3},{3,0},{4,5},{5,6},{6,7},{7,4},{8,9},{9,10},{10,1... | collective-permute-start | bytes 786440 | tf_op jit(solution)/shard_map/ppermute | solution.py:287
  131.7 5.6 %collective-permute-start.23 = (bf16[256,1024]{1,0:T(8,128)(2,1)S(1)}, bf16[256,1024]{1,0:T(8,128)(2,1)S(1)}, u32[]{:S(2)}, u32[]{:S(2)}) collective-permute-start(bf16[256,1024]{1,0:T(8,128)(2,1)S(1)} %slice.267), channel_id=1, source_target_pairs={{0,4},{4,0},{8,12},{12,8},{1,5},{5,1},{9,13},{13,9},{2,6},{6,2},{1... | collective-permute-start | bytes 1572872 | tf_op jit(solution)/shard_map/ppermute | solution.py:266
  132.9 6.2 %collective-permute-start.22 = (bf16[256,1024]{1,0:T(8,128)(2,1)S(1)}, bf16[256,1024]{1,0:T(8,128)(2,1)S(1)}, u32[]{:S(2)}, u32[]{:S(2)}) collective-permute-start(bf16[256,1024]{1,0:T(8,128)(2,1)S(1)} %slice.268), channel_id=1, source_target_pairs={{0,4},{4,0},{8,12},{12,8},{1,5},{5,1},{9,13},{13,9},{2,6},{6,2},{1... | collective-permute-start | bytes 1572872 | tf_op jit(solution)/shard_map/ppermute | solution.py:266
  135.4 12.1 %collective-permute-start.30 = (bf16[128,1024]{1,0:T(8,128)(2,1)S(1)}, bf16[128,1024]{1,0:T(8,128)(2,1)S(1)}, u32[]{:S(2)}, u32[]{:S(2)}) collective-permute-start(bf16[128,1024]{1,0:T(8,128)(2,1)S(1)} %convert_add_fusion.1), channel_id=1, source_target_pairs={{0,3},{1,0},{2,1},{3,2},{4,7},{5,4},{6,5},{7,6},{8,11},{9,8},{10,9... | collective-permute-start | bytes 786440 | tf_op jit(solution)/shard_map/ppermute | solution.py:287
  137.7 9.3 %collective-permute-start.26 = (bf16[128,1024]{1,0:T(8,128)(2,1)S(1)}, bf16[128,1024]{1,0:T(8,128)(2,1)S(1)}, u32[]{:S(2)}, u32[]{:S(2)}) collective-permute-start(bf16[128,1024]{1,0:T(8,128)(2,1)S(1)} %slice.271), channel_id=1, source_target_pairs={{0,8},{4,12},{8,0},{12,4},{1,9},{5,13},{9,1},{13,5},{2,10},{6,14},... | collective-permute-start | bytes 786440 | tf_op jit(solution)/shard_map/ppermute | solution.py:271
  139.3 12.0 %collective-permute-start.27 = (bf16[128,1024]{1,0:T(8,128)(2,1)S(1)}, bf16[128,1024]{1,0:T(8,128)(2,1)S(1)}, u32[]{:S(2)}, u32[]{:S(2)}) collective-permute-start(bf16[128,1024]{1,0:T(8,128)(2,1)S(1)} %slice.270), channel_id=1, source_target_pairs={{0,8},{4,12},{8,0},{12,4},{1,9},{5,13},{9,1},{13,5},{2,10},{6,14},... | collective-permute-start | bytes 786440 | tf_op jit(solution)/shard_map/ppermute | solution.py:271
  147.0 8.2 %collective-permute-start.29 = (bf16[128,1024]{1,0:T(8,128)(2,1)S(1)}, bf16[128,1024]{1,0:T(8,128)(2,1)S(1)}, u32[]{:S(2)}, u32[]{:S(2)}) collective-permute-start(bf16[128,1024]{1,0:T(8,128)(2,1)S(1)} %add_convert_fusion.1), channel_id=1, source_target_pairs={{0,1},{1,2},{2,3},{3,0},{4,5},{5,6},{6,7},{7,4},{8,9},{9,10},{10,1... | collective-permute-start | bytes 786440 | tf_op jit(solution)/shard_map/ppermute | solution.py:287
  (17 other events, 138.9 us)

commit v8 on v7

--- a/solution.py
+++ b/solution.py
@@ -197,7 +197,7 @@
     gain_f = norm_gain.astype(f32)
     resid_parts = [None] * n_donor
     own_act, other_act = [None] * n_donor, [None] * n_donor
-    batches = [max(1, n_donor - 1), 1]
+    batches = [n_donor // 2, n_donor - n_donor // 2]
     own_rows, other_rows, row_gates = [], [], []
     for slot in range(n_donor):
         part = (z - slot) % n_donor
@@ -273,13 +273,13 @@
         pending.append((block[0], arriving))
     total = resid
     carry = {1: [], -1: []}
-    before = []
+    all_blocks, before = before, []
     for place, step in enumerate(order):
         part_sum, arriving = pending[place]
         part_sum = after(part_sum, *before)
         for got in arriving:
             part_sum = part_sum + got.astype(f32)
-        before = [part_sum]
+        before = [part_sum] + all_blocks
         if step:
             way = 1 if step <= n_donor // 2 else -1
             for got in carry[way]:

time: 157 us -> 153 us (0.975)
  local copies, waits for them, and re-layouts: 24.1 us -> 20.4 us
  other arithmetic: 11.6 us -> 8.41 us
  waiting for transfers between devices: 68.8 us -> 71.9 us
    ppermute x4, waiting for transfers between devices: 19.3 us -> 9.96 us  [shards(): lax.ppermute(block[hop].astype(bf16), 'expert', turn(hop))]
    ppermute x3, waiting for transfers between devices: 4.04 us -> 11.5 us  [shards(): lax.ppermute(part_sum.astype(bf16), 'donor', rotation(n_donor, way))]
    ppermute x3, waiting for transfers between devices: 6.79 us -> 9.42 us  [shards(): lax.ppermute(term(step).astype(bf16), 'donor', rotation(n_donor, step))]
    concatenate x4, local copies, waits for them, and re-layouts: 2.73 us -> 0.32 us  [core_gates(): return jnp.concatenate(rows).reshape(n_donor, part_rows)]
    concatenate x3, other arithmetic: 2.18 us -> 0.06 us  [term(): jnp.concatenate([jnp.where(core == 0, own, other), jnp.where(core == 0, o...]
    dot_general x1, matrix products: 2.3 us -> 0.71 us  [shards(): own_terms = jnp.dot(heads, out_weight, preferred_element_type=f32)]
    unnamed x44 -> x38, local copies, waits for them, and re-layouts: 13.6 us -> 14 us
  transfers between devices with their start and end apart: 32 -> 32, of which waited for: 19 -> 22; matrix products, arithmetic and copies ran while one was open for 29% -> 25% of each run, Pallas kernels for 0% -> 0%
where the time goes in v8:
time: 153 us
  waiting for transfers between devices  71.9 us (47%)
  starting transfers between devices  27.2 us (18%)
  matrix products  22.3 us (15%)
  local copies, waits for them, and re-layouts  20.4 us (13%)
  other arithmetic  8.41 us (5%)
  between operations  2.22 us (1%)
    ppermute x4, waiting for transfers between devices, shards(): lax.ppermute(chunk, 'expert', turn(hop))  16.8 us
    unnamed x38, local copies, waits for them, and re-layouts  14 us
    dot_general x2, matrix products, shards(): gate_up = jnp.dot(rows_in, gate_up_weight, preferred_element_type=f32)  13.1 us
    ppermute x3, waiting for transfers between devices, shards(): lax.ppermute(part_sum.astype(bf16), 'donor', rotation(n_donor, way))  11.5 us
    ppermute x4, waiting for transfers between devices, shards(): lax.ppermute(block[hop].astype(bf16), 'expert', turn(hop))  9.96 us
    ppermute x3, waiting for transfers between devices, shards(): lax.ppermute(term(step).astype(bf16), 'donor', rotation(n_donor, step))  9.42 us
    ppermute x3, waiting for transfers between devices, shards(): chunk = lax.ppermute(chunk, 'donor', rotation(n_donor, 1))  8.42 us
    all_to_all x1, starting transfers between devices, attention(): lax.all_to_all(outgoing, ('expert', 'donor'), split_axis=0, concat_axis=0...  7.39 us
  transfers between devices with their start and end apart: 32, of which 22 were waited for; matrix products, arithmetic and copies ran while one was open for 25% of the time, Pallas kernels for 0%

profile of v8, /device:TPU:0, one launch (start us, length us, event | category | flops | bytes accessed | tf_op | source)
XLA Modules:
  0.0 152.6 jit_solution(6226238771620098209)
XLA Ops:
  3.2 7.4 %all-to-all-start = ((bf16[16,32,256]{2,1,0:T(8,128)(2,1)}), bf16[16,32,256]{2,1,0:T(8,128)(2,1)S(1)}, u32[]{:S(2)}, u32[]{:S(2)}) async-start(bf16[16,32,256]{2,1,0:T(8,128)(2,1)} %broadcast_select_fusion), calls=%async_computation | async-start | bytes 524288 | tf_op jit(solution)/shard_map/all_to_all | solution.py:38
  11.0 1.0 constant_dynamic-slice_fusion.17
  12.1 1.2 dynamic_slice.150
  14.8 5.9 %all-to-all-done = bf16[16,32,256]{2,1,0:T(8,128)(2,1)S(1)} async-done(((bf16[16,32,256]{2,1,0:T(8,128)(2,1)}), bf16[16,32,256]{2,1,0:T(8,128)(2,1)S(1)}, u32[]{:S(2)}, u32[]{:S(2)}) %all-to-all-start) | async-done | bytes 262176 | tf_op jit(solution)/shard_map/all_to_all | solution.py:38
  21.4 1.1 while.22
  22.9 1.8 %while.23 = (s32[]{:T(128)}, f32[128,8]{0,1:T(8,128)S(1)}, f32[128,8,128]{2,0,1:T(8,128)S(1)}, s32[]{:T(128)}, s32[]{:T(128)}, /*index=5*/bf16[128,8,128]{2,0,1:...) while((s32[]{:T(128)}, f32[128,8]{0,1:T(8,128)S(1)}, ...), condition=%wide.region_8.9_spmd, body=%wide.region_6.8_spmd.sunk | while | flops 271188992 | bytes 3691649 | solution.py:94
  26.4 1.2 collective-permute-start.2
  28.0 3.9 %collective-permute-done.3 = f32[8,128]{1,0:T(8,128)S(1)} collective-permute-done((f32[8,128]{1,0:T(8,128)S(1)}, f32[8,128]{1,0:T(8,128)S(1)}, u32[]{:S(2)}, u32[]{:S(2)}) %collective-permute-start.3) | collective-permute-done | bytes 4128 | tf_op jit(solution)/shard_map/ppermute | solution.py:140
  34.2 2.3 %fusion.67 = f32[256,1024]{1,0:T(8,128)S(1)} fusion(bf16[1024,1024]{1,0:T(8,128)(2,1)} %collective-permute-done.4, bf16[64,1024]{1,0:T(8,128)(2,1)S(1)} %get-tuple-element.257, bf16[64,1024]{1,0:T(8,128)(2,1)S(1)} %get-tuple-element.258, bf16[64,1024]{1,0:T(8,128)(2,1)S(1)} %get-tuple-element.259, bf16[64,1024]{1,0:T(8,128)(2,1)S(1)} %get-tuple-element.256), kind=kOutput, calls=%fused_computation.164 | convolution fusion | flops 538968064 | bytes 3670016 | tf_op jit(solution)/shard_map/dot_general | solution.py:167
  36.6 1.3 collective-permute-start.7
  39.8 13.0 %copy.53 = bf16[512,8,2,768]{3,1,2,0:T(8,128)(2,1)} copy(bf16[512,8,2,768]{3,2,1,0:T(2,128)(2,1)} %bitcast.159) | data formatting | bytes 25165824
  52.9 9.4 %collective-permute-done.8 = bf16[64,2048]{1,0:T(8,128)(2,1)S(1)} collective-permute-done((bf16[64,2048]{1,0:T(8,128)(2,1)S(1)}, bf16[64,2048]{1,0:T(8,128)(2,1)S(1)}, u32[]{:S(2)}, u32[]{:S(2)}) %collective-permute-start.8) | collective-permute-done | bytes 262176 | tf_op jit(solution)/shard_map/ppermute | solution.py:181
  62.6 1.0 collective-permute-start.10
  64.4 6.0 %collective-permute-done.10 = bf16[64,2048]{1,0:T(8,128)(2,1)S(1)} collective-permute-done((bf16[64,2048]{1,0:T(8,128)(2,1)S(1)}, bf16[64,2048]{1,0:T(8,128)(2,1)S(1)}, u32[]{:S(2)}, u32[]{:S(2)}) %collective-permute-start.10) | collective-permute-done | bytes 262176 | tf_op jit(solution)/shard_map/ppermute | solution.py:204
  70.4 3.1 %collective-permute-done.9 = bf16[64,2048]{1,0:T(8,128)(2,1)S(1)} collective-permute-done((bf16[64,2048]{1,0:T(8,128)(2,1)S(1)}, bf16[64,2048]{1,0:T(8,128)(2,1)S(1)}, u32[]{:S(2)}, u32[]{:S(2)}) %collective-permute-start.9) | collective-permute-done | bytes 262176 | tf_op jit(solution)/shard_map/ppermute | solution.py:207
  74.2 6.4 %collective-permute-done.12 = bf16[64,2048]{1,0:T(8,128)(2,1)S(1)} collective-permute-done((bf16[64,2048]{1,0:T(8,128)(2,1)S(1)}, bf16[64,2048]{1,0:T(8,128)(2,1)S(1)}, u32[]{:S(2)}, u32[]{:S(2)}) %collective-permute-start.12) | collective-permute-done | bytes 262176 | tf_op jit(solution)/shard_map/ppermute | solution.py:204
  80.6 1.8 %collective-permute-done.11 = bf16[64,2048]{1,0:T(8,128)(2,1)S(1)} collective-permute-done((bf16[64,2048]{1,0:T(8,128)(2,1)S(1)}, bf16[64,2048]{1,0:T(8,128)(2,1)S(1)}, u32[]{:S(2)}, u32[]{:S(2)}) %collective-permute-start.11) | collective-permute-done | bytes 262176 | tf_op jit(solution)/shard_map/ppermute | solution.py:207
  82.4 1.7 %collective-permute-start.14 = (bf16[64,2048]{1,0:T(8,128)(2,1)S(1)}, bf16[64,2048]{1,0:T(8,128)(2,1)S(1)}, u32[]{:S(2)}, u32[]{:S(2)}) collective-permute-start(bf16[64,2048]{1,0:T(8,128)(2,1)S(1)} %collective-permute-done.11), channel_id=1, source_target_pairs={{0,8},{4,12},{8,0},{12,4},{1,9},{5,13},{9,1},{13,5},{2,10},{6,14},... | collective-permute-start | bytes 786440 | tf_op jit(solution)/shard_map/ppermute | solution.py:204
  84.5 4.4 %collective-permute-done.14 = bf16[64,2048]{1,0:T(8,128)(2,1)S(1)} collective-permute-done((bf16[64,2048]{1,0:T(8,128)(2,1)S(1)}, bf16[64,2048]{1,0:T(8,128)(2,1)S(1)}, u32[]{:S(2)}, u32[]{:S(2)}) %collective-permute-start.14) | collective-permute-done | bytes 262176 | tf_op jit(solution)/shard_map/ppermute | solution.py:204
  88.8 3.5 %collective-permute-done.13 = bf16[64,2048]{1,0:T(8,128)(2,1)S(1)} collective-permute-done((bf16[64,2048]{1,0:T(8,128)(2,1)S(1)}, bf16[64,2048]{1,0:T(8,128)(2,1)S(1)}, u32[]{:S(2)}, u32[]{:S(2)}) %collective-permute-start.13) | collective-permute-done | bytes 262176 | tf_op jit(solution)/shard_map/ppermute | solution.py:207
  95.8 6.4 %fusion.4 = f32[256,1536]{1,0:T(8,128)S(1)} fusion(bf16[4096,1536]{1,0:T(8,128)(2,1)} %bitcast.160, bf16[64,4096]{1,0:T(8,128)(2,1)S(1)} %collective-permute-done.17, bf16[64,4096]{1,0:T(8,128)(2,1)S(1)} %collective-permute-done.16, bf16[64,4096]{1,0:T(8,128)(2,1)S(1)} %get-tuple-element.271, bf16[64,4096]{1,0:T(8,128)(2,1)S(1)} %get-tuple-element.272), kind=kOutput, calls=%fused_computation.11 | convolution fusion | flops 3229614080 | bytes 16252928 | tf_op jit(solution)/shard_map/dot_general | solution.py:234
  104.0 1.8 %collective-permute-done.19 = bf16[64,4096]{1,0:T(8,128)(2,1)} collective-permute-done((bf16[64,4096]{1,0:T(8,128)(2,1)S(1)}, bf16[64,4096]{1,0:T(8,128)(2,1)}, u32[]{:S(2)}, u32[]{:S(2)}) %collective-permute-start.19) | collective-permute-done | bytes 524320 | tf_op jit(solution)/shard_map/ppermute | solution.py:228
  105.7 6.7 %fusion.12 = f32[256,1536]{1,0:T(8,128)S(1)} fusion(bf16[4096,1536]{1,0:T(8,128)(2,1)} %bitcast.161, bf16[64,4096]{1,0:T(8,128)(2,1)} %collective-permute-done.19, bf16[64,4096]{1,0:T(8,128)(2,1)} %collective-permute-done.18, bf16[64,4096]{1,0:T(8,128)(2,1)S(1)} %fusion.45, bf16[64,4096]{1,0:T(8,128)(2,1)S(1)} %get-tuple-element.270), kind=kOutput, calls=%fused_computation.19 | convolution fusion | flops 3229614080 | bytes 16252928 | tf_op jit(solution)/shard_map/dot_general | solution.py:234
  117.0 1.2 collective-permute-done.24
  118.8 1.8 %collective-permute-start.25 = (bf16[128,1024]{1,0:T(8,128)(2,1)S(1)}, bf16[128,1024]{1,0:T(8,128)(2,1)S(1)}, u32[]{:S(2)}, u32[]{:S(2)}) collective-permute-start(bf16[128,1024]{1,0:T(8,128)(2,1)S(1)} %slice.270), channel_id=1, source_target_pairs={{0,8},{4,12},{8,0},{12,4},{1,9},{5,13},{9,1},{13,5},{2,10},{6,14},... | collective-permute-start | bytes 786440 | tf_op jit(solution)/shard_map/ppermute | solution.py:271
  120.6 6.8 %collective-permute-done.21 = bf16[128,1024]{1,0:T(8,128)(2,1)S(1)} collective-permute-done((bf16[128,1024]{1,0:T(8,128)(2,1)S(1)}, bf16[128,1024]{1,0:T(8,128)(2,1)S(1)}, u32[]{:S(2)}, u32[]{:S(2)}) %collective-permute-start.21) | collective-permute-done | bytes 262176 | tf_op jit(solution)/shard_map/ppermute | solution.py:271
  132.3 3.2 %collective-permute-start.30 = (bf16[128,1024]{1,0:T(8,128)(2,1)S(1)}, bf16[128,1024]{1,0:T(8,128)(2,1)S(1)}, u32[]{:S(2)}, u32[]{:S(2)}) collective-permute-start(bf16[128,1024]{1,0:T(8,128)(2,1)S(1)} %convert_add_fusion.1), channel_id=1, source_target_pairs={{0,3},{1,0},{2,1},{3,2},{4,7},{5,4},{6,5},{7,6},{8,11},{9,8},{10,9... | collective-permute-start | bytes 786440 | tf_op jit(solution)/shard_map/ppermute | solution.py:287
  135.5 1.4 collective-permute-start.27
  136.9 4.5 %collective-permute-done.28 = bf16[128,1024]{1,0:T(8,128)(2,1)S(1)} collective-permute-done((bf16[128,1024]{1,0:T(8,128)(2,1)S(1)}, bf16[128,1024]{1,0:T(8,128)(2,1)S(1)}, u32[]{:S(2)}, u32[]{:S(2)}) %collective-permute-start.28) | collective-permute-done | bytes 262176 | tf_op jit(solution)/shard_map/ppermute | solution.py:287
  141.8 2.9 %collective-permute-done.27 = bf16[128,1024]{1,0:T(8,128)(2,1)S(1)} collective-permute-done((bf16[128,1024]{1,0:T(8,128)(2,1)S(1)}, bf16[128,1024]{1,0:T(8,128)(2,1)S(1)}, u32[]{:S(2)}, u32[]{:S(2)}) %collective-permute-start.27) | collective-permute-done | bytes 262176 | tf_op jit(solution)/shard_map/ppermute | solution.py:271
  144.7 2.3 %collective-permute-done.30 = bf16[128,1024]{1,0:T(8,128)(2,1)S(1)} collective-permute-done((bf16[128,1024]{1,0:T(8,128)(2,1)S(1)}, bf16[128,1024]{1,0:T(8,128)(2,1)S(1)}, u32[]{:S(2)}, u32[]{:S(2)}) %collective-permute-start.30) | collective-permute-done | bytes 262176 | tf_op jit(solution)/shard_map/ppermute | solution.py:287
  147.0 4.7 %collective-permute-done.29 = bf16[128,1024]{1,0:T(8,128)(2,1)S(1)} collective-permute-done((bf16[128,1024]{1,0:T(8,128)(2,1)S(1)}, bf16[128,1024]{1,0:T(8,128)(2,1)S(1)}, u32[]{:S(2)}, u32[]{:S(2)}) %collective-permute-start.29) | collective-permute-done | bytes 262176 | tf_op jit(solution)/shard_map/ppermute | solution.py:287
  (197 shorter events, 31.9 us)
Async XLA Ops:
  3.2 17.5 %all-to-all-start = ((bf16[16,32,256]{2,1,0:T(8,128)(2,1)}), bf16[16,32,256]{2,1,0:T(8,128)(2,1)S(1)}, u32[]{:S(2)}, u32[]{:S(2)}) async-start(bf16[16,32,256]{2,1,0:T(8,128)(2,1)} %broadcast_select_fusion), calls=%async_computation | async-start | bytes 524288 | tf_op jit(solution)/shard_map/all_to_all | solution.py:38
  10.6 23.5 %collective-permute-start.4 = (bf16[1024,1024]{1,0:T(8,128)(2,1)}, bf16[1024,1024]{1,0:T(8,128)(2,1)}, u32[]{:S(2)}, u32[]{:S(2)}) collective-permute-start(bf16[1024,1024]{1,0:T(8,128)(2,1)} %param.22), channel_id=1, source_target_pairs={{0,4},{4,0},{8,12},{12,8},{1,5},{5,1},{9,13},{13,9},{2,6},{6,2},{1... | collective-permute-start | bytes 6291464 | tf_op jit(solution)/shard_map/ppermute | solution.py:143
  25.2 8.1 %collective-permute-start = (bf16[128,1024]{1,0:T(8,128)(2,1)S(1)}, bf16[128,1024]{1,0:T(8,128)(2,1)S(1)}, u32[]{:S(2)}, u32[]{:S(2)}) collective-permute-start(bf16[128,1024]{1,0:T(8,128)(2,1)S(1)} %copy.48), channel_id=1, source_target_pairs={{0,8},{4,12},{8,0},{12,4},{1,9},{5,13},{9,1},{13,5},{2,10},{6,14},... | collective-permute-start | bytes 786440 | tf_op jit(solution)/shard_map/ppermute | solution.py:161
  25.8 6.2 %collective-permute-start.3 = (f32[8,128]{1,0:T(8,128)S(1)}, f32[8,128]{1,0:T(8,128)S(1)}, u32[]{:S(2)}, u32[]{:S(2)}) collective-permute-start(f32[8,128]{1,0:T(8,128)S(1)} %bitcast.175), channel_id=1, source_target_pairs={{0,12},{4,0},{8,4},{12,8},{1,13},{5,1},{9,5},{13,9},{2,14},{6,2},{... | collective-permute-start | bytes 12296 | tf_op jit(solution)/shard_map/ppermute | solution.py:140
  26.4 7.0 %collective-permute-start.2 = (f32[8,128]{1,0:T(8,128)S(1)}, f32[8,128]{1,0:T(8,128)S(1)}, u32[]{:S(2)}, u32[]{:S(2)}) collective-permute-start(f32[8,128]{1,0:T(8,128)S(1)} %bitcast.176), channel_id=1, source_target_pairs={{0,8},{4,12},{8,0},{12,4},{1,9},{5,13},{9,1},{13,5},{2,10},{6,14},... | collective-permute-start | bytes 12296 | tf_op jit(solution)/shard_map/ppermute | solution.py:140
  27.5 5.8 %collective-permute-start.1 = (f32[8,128]{1,0:T(8,128)S(1)}, f32[8,128]{1,0:T(8,128)S(1)}, u32[]{:S(2)}, u32[]{:S(2)}) collective-permute-start(f32[8,128]{1,0:T(8,128)S(1)} %bitcast.177), channel_id=1, source_target_pairs={{0,4},{4,8},{8,12},{12,0},{1,5},{5,9},{9,13},{13,1},{2,6},{6,10},{... | collective-permute-start | bytes 12296 | tf_op jit(solution)/shard_map/ppermute | solution.py:140
  32.0 30.3 %collective-permute-start.5 = (bf16[64,2048]{1,0:T(8,128)(2,1)S(1)}, bf16[64,2048]{1,0:T(8,128)(2,1)S(1)}, u32[]{:S(2)}, u32[]{:S(2)}) collective-permute-start(bf16[64,2048]{1,0:T(8,128)(2,1)S(1)} %dynamic_slice.156), channel_id=1, source_target_pairs={{0,8},{4,12},{8,0},{12,4},{1,9},{5,13},{9,1},{13,5},{2,10},{6,14},... | collective-permute-start | bytes 786440 | tf_op jit(solution)/shard_map/ppermute | solution.py:153
  36.6 16.3 %collective-permute-start.7 = (bf16[64,2048]{1,0:T(8,128)(2,1)S(1)}, bf16[64,2048]{1,0:T(8,128)(2,1)S(1)}, u32[]{:S(2)}, u32[]{:S(2)}) collective-permute-start(bf16[64,2048]{1,0:T(8,128)(2,1)S(1)} %pad_maximum_fusion.9), channel_id=1, source_target_pairs={{0,3},{1,0},{2,1},{3,2},{4,7},{5,4},{6,5},{7,6},{8,11},{9,8},{10,9... | collective-permute-start | bytes 786440 | tf_op jit(solution)/shard_map/ppermute | solution.py:181
  37.9 15.0 %collective-permute-start.6 = (bf16[64,2048]{1,0:T(8,128)(2,1)S(1)}, bf16[64,2048]{1,0:T(8,128)(2,1)S(1)}, u32[]{:S(2)}, u32[]{:S(2)}) collective-permute-start(bf16[64,2048]{1,0:T(8,128)(2,1)S(1)} %pad_maximum_fusion.8), channel_id=1, source_target_pairs={{0,1},{1,2},{2,3},{3,0},{4,5},{5,6},{6,7},{7,4},{8,9},{9,10},{10,1... | collective-permute-start | bytes 786440 | tf_op jit(solution)/shard_map/ppermute | solution.py:181
  38.8 23.5 %collective-permute-start.8 = (bf16[64,2048]{1,0:T(8,128)(2,1)S(1)}, bf16[64,2048]{1,0:T(8,128)(2,1)S(1)}, u32[]{:S(2)}, u32[]{:S(2)}) collective-permute-start(bf16[64,2048]{1,0:T(8,128)(2,1)S(1)} %pad_maximum_fusion.10), channel_id=1, source_target_pairs={{0,2},{1,3},{2,0},{3,1},{4,6},{5,7},{6,4},{7,5},{8,10},{9,11},{10,... | collective-permute-start | bytes 786440 | tf_op jit(solution)/shard_map/ppermute | solution.py:181
  62.6 7.8 %collective-permute-start.10 = (bf16[64,2048]{1,0:T(8,128)(2,1)S(1)}, bf16[64,2048]{1,0:T(8,128)(2,1)S(1)}, u32[]{:S(2)}, u32[]{:S(2)}) collective-permute-start(bf16[64,2048]{1,0:T(8,128)(2,1)S(1)} %fusion.53), channel_id=1, source_target_pairs={{0,8},{4,12},{8,0},{12,4},{1,9},{5,13},{9,1},{13,5},{2,10},{6,14},... | collective-permute-start | bytes 786440 | tf_op jit(solution)/shard_map/ppermute | solution.py:204
  63.6 9.8 %collective-permute-start.9 = (bf16[64,2048]{1,0:T(8,128)(2,1)S(1)}, bf16[64,2048]{1,0:T(8,128)(2,1)S(1)}, u32[]{:S(2)}, u32[]{:S(2)}) collective-permute-start(bf16[64,2048]{1,0:T(8,128)(2,1)S(1)} %fusion.53), channel_id=1, source_target_pairs={{0,1},{1,2},{2,3},{3,0},{4,5},{5,6},{6,7},{7,4},{8,9},{9,10},{10,1... | collective-permute-start | bytes 786440 | tf_op jit(solution)/shard_map/ppermute | solution.py:207
  73.5 7.2 %collective-permute-start.12 = (bf16[64,2048]{1,0:T(8,128)(2,1)S(1)}, bf16[64,2048]{1,0:T(8,128)(2,1)S(1)}, u32[]{:S(2)}, u32[]{:S(2)}) collective-permute-start(bf16[64,2048]{1,0:T(8,128)(2,1)S(1)} %collective-permute-done.9), channel_id=1, source_target_pairs={{0,8},{4,12},{8,0},{12,4},{1,9},{5,13},{9,1},{13,5},{2,10},{6,14},... | collective-permute-start | bytes 786440 | tf_op jit(solution)/shard_map/ppermute | solution.py:204
  73.9 8.5 %collective-permute-start.11 = (bf16[64,2048]{1,0:T(8,128)(2,1)S(1)}, bf16[64,2048]{1,0:T(8,128)(2,1)S(1)}, u32[]{:S(2)}, u32[]{:S(2)}) collective-permute-start(bf16[64,2048]{1,0:T(8,128)(2,1)S(1)} %collective-permute-done.9), channel_id=1, source_target_pairs={{0,1},{1,2},{2,3},{3,0},{4,5},{5,6},{6,7},{7,4},{8,9},{9,10},{10,1... | collective-permute-start | bytes 786440 | tf_op jit(solution)/shard_map/ppermute | solution.py:207
  82.4 6.4 %collective-permute-start.14 = (bf16[64,2048]{1,0:T(8,128)(2,1)S(1)}, bf16[64,2048]{1,0:T(8,128)(2,1)S(1)}, u32[]{:S(2)}, u32[]{:S(2)}) collective-permute-start(bf16[64,2048]{1,0:T(8,128)(2,1)S(1)} %collective-permute-done.11), channel_id=1, source_target_pairs={{0,8},{4,12},{8,0},{12,4},{1,9},{5,13},{9,1},{13,5},{2,10},{6,14},... | collective-permute-start | bytes 786440 | tf_op jit(solution)/shard_map/ppermute | solution.py:204
  84.2 8.2 %collective-permute-start.13 = (bf16[64,2048]{1,0:T(8,128)(2,1)S(1)}, bf16[64,2048]{1,0:T(8,128)(2,1)S(1)}, u32[]{:S(2)}, u32[]{:S(2)}) collective-permute-start(bf16[64,2048]{1,0:T(8,128)(2,1)S(1)} %collective-permute-done.11), channel_id=1, source_target_pairs={{0,1},{1,2},{2,3},{3,0},{4,5},{5,6},{6,7},{7,4},{8,9},{9,10},{10,1... | collective-permute-start | bytes 786440 | tf_op jit(solution)/shard_map/ppermute | solution.py:207
  93.1 2.0 %collective-permute-start.17 = (bf16[64,4096]{1,0:T(8,128)(2,1)S(1)}, bf16[64,4096]{1,0:T(8,128)(2,1)S(1)}, u32[]{:S(2)}, u32[]{:S(2)}) collective-permute-start(bf16[64,4096]{1,0:T(8,128)(2,1)S(1)} %get-tuple-element.271), channel_id=1, source_target_pairs={{0,4},{4,0},{8,12},{12,8},{1,5},{5,1},{9,13},{13,9},{2,6},{6,2},{1... | collective-permute-start | bytes 1572872 | tf_op jit(solution)/shard_map/ppermute | solution.py:228
  93.2 2.6 %collective-permute-start.16 = (bf16[64,4096]{1,0:T(8,128)(2,1)S(1)}, bf16[64,4096]{1,0:T(8,128)(2,1)S(1)}, u32[]{:S(2)}, u32[]{:S(2)}) collective-permute-start(bf16[64,4096]{1,0:T(8,128)(2,1)S(1)} %get-tuple-element.272), channel_id=1, source_target_pairs={{0,4},{4,0},{8,12},{12,8},{1,5},{5,1},{9,13},{13,9},{2,6},{6,2},{1... | collective-permute-start | bytes 1572872 | tf_op jit(solution)/shard_map/ppermute | solution.py:228
  93.8 9.4 %collective-permute-start.15 = (bf16[64,2048]{1,0:T(8,128)(2,1)S(1)}, bf16[64,2048]{1,0:T(8,128)(2,1)S(1)}, u32[]{:S(2)}, u32[]{:S(2)}) collective-permute-start(bf16[64,2048]{1,0:T(8,128)(2,1)S(1)} %collective-permute-done.13), channel_id=1, source_target_pairs={{0,8},{4,12},{8,0},{12,4},{1,9},{5,13},{9,1},{13,5},{2,10},{6,14},... | collective-permute-start | bytes 786440 | tf_op jit(solution)/shard_map/ppermute | solution.py:204
  94.1 9.9 %collective-permute-start.18 = (bf16[64,4096]{1,0:T(8,128)(2,1)S(1)}, bf16[64,4096]{1,0:T(8,128)(2,1)}, u32[]{:S(2)}, u32[]{:S(2)}) collective-permute-start(bf16[64,4096]{1,0:T(8,128)(2,1)S(1)} %get-tuple-element.270), channel_id=1, source_target_pairs={{0,4},{4,0},{8,12},{12,8},{1,5},{5,1},{9,13},{13,9},{2,6},{6,2},{1... | collective-permute-start | bytes 1572872 | tf_op jit(solution)/shard_map/ppermute | solution.py:228
  103.6 2.1 %collective-permute-start.19 = (bf16[64,4096]{1,0:T(8,128)(2,1)S(1)}, bf16[64,4096]{1,0:T(8,128)(2,1)}, u32[]{:S(2)}, u32[]{:S(2)}) collective-permute-start(bf16[64,4096]{1,0:T(8,128)(2,1)S(1)} %fusion.45), channel_id=1, source_target_pairs={{0,4},{4,0},{8,12},{12,8},{1,5},{5,1},{9,13},{13,9},{2,6},{6,2},{1... | collective-permute-start | bytes 1572872 | tf_op jit(solution)/shard_map/ppermute | solution.py:228
  114.8 2.0 %collective-permute-start.20 = (bf16[256,1024]{1,0:T(8,128)(2,1)S(1)}, bf16[256,1024]{1,0:T(8,128)(2,1)S(1)}, u32[]{:S(2)}, u32[]{:S(2)}) collective-permute-start(bf16[256,1024]{1,0:T(8,128)(2,1)S(1)} %slice.267), channel_id=1, source_target_pairs={{0,4},{4,0},{8,12},{12,8},{1,5},{5,1},{9,13},{13,9},{2,6},{6,2},{1... | collective-permute-start | bytes 1572872 | tf_op jit(solution)/shard_map/ppermute | solution.py:266
  116.3 2.0 %collective-permute-start.24 = (bf16[256,1024]{1,0:T(8,128)(2,1)S(1)}, bf16[256,1024]{1,0:T(8,128)(2,1)S(1)}, u32[]{:S(2)}, u32[]{:S(2)}) collective-permute-start(bf16[256,1024]{1,0:T(8,128)(2,1)S(1)} %slice.264), channel_id=1, source_target_pairs={{0,4},{4,0},{8,12},{12,8},{1,5},{5,1},{9,13},{13,9},{2,6},{6,2},{1... | collective-permute-start | bytes 1572872 | tf_op jit(solution)/shard_map/ppermute | solution.py:266
  118.2 9.1 %collective-permute-start.21 = (bf16[128,1024]{1,0:T(8,128)(2,1)S(1)}, bf16[128,1024]{1,0:T(8,128)(2,1)S(1)}, u32[]{:S(2)}, u32[]{:S(2)}) collective-permute-start(bf16[128,1024]{1,0:T(8,128)(2,1)S(1)} %slice.271), channel_id=1, source_target_pairs={{0,8},{4,12},{8,0},{12,4},{1,9},{5,13},{9,1},{13,5},{2,10},{6,14},... | collective-permute-start | bytes 786440 | tf_op jit(solution)/shard_map/ppermute | solution.py:271
  118.8 13.5 %collective-permute-start.25 = (bf16[128,1024]{1,0:T(8,128)(2,1)S(1)}, bf16[128,1024]{1,0:T(8,128)(2,1)S(1)}, u32[]{:S(2)}, u32[]{:S(2)}) collective-permute-start(bf16[128,1024]{1,0:T(8,128)(2,1)S(1)} %slice.270), channel_id=1, source_target_pairs={{0,8},{4,12},{8,0},{12,4},{1,9},{5,13},{9,1},{13,5},{2,10},{6,14},... | collective-permute-start | bytes 786440 | tf_op jit(solution)/shard_map/ppermute | solution.py:271
  128.5 2.0 %collective-permute-start.23 = (bf16[256,1024]{1,0:T(8,128)(2,1)S(1)}, bf16[256,1024]{1,0:T(8,128)(2,1)S(1)}, u32[]{:S(2)}, u32[]{:S(2)}) collective-permute-start(bf16[256,1024]{1,0:T(8,128)(2,1)S(1)} %slice.265), channel_id=1, source_target_pairs={{0,4},{4,0},{8,12},{12,8},{1,5},{5,1},{9,13},{13,9},{2,6},{6,2},{1... | collective-permute-start | bytes 1572872 | tf_op jit(solution)/shard_map/ppermute | solution.py:266
  129.7 2.1 %collective-permute-start.22 = (bf16[256,1024]{1,0:T(8,128)(2,1)S(1)}, bf16[256,1024]{1,0:T(8,128)(2,1)S(1)}, u32[]{:S(2)}, u32[]{:S(2)}) collective-permute-start(bf16[256,1024]{1,0:T(8,128)(2,1)S(1)} %slice.266), channel_id=1, source_target_pairs={{0,4},{4,0},{8,12},{12,8},{1,5},{5,1},{9,13},{13,9},{2,6},{6,2},{1... | collective-permute-start | bytes 1572872 | tf_op jit(solution)/shard_map/ppermute | solution.py:266
  130.3 11.1 %collective-permute-start.28 = (bf16[128,1024]{1,0:T(8,128)(2,1)S(1)}, bf16[128,1024]{1,0:T(8,128)(2,1)S(1)}, u32[]{:S(2)}, u32[]{:S(2)}) collective-permute-start(bf16[128,1024]{1,0:T(8,128)(2,1)S(1)} %convert_add_fusion.2), channel_id=1, source_target_pairs={{0,1},{1,2},{2,3},{3,0},{4,5},{5,6},{6,7},{7,4},{8,9},{9,10},{10,1... | collective-permute-start | bytes 786440 | tf_op jit(solution)/shard_map/ppermute | solution.py:287
  130.7 10.7 %collective-permute-start.26 = (bf16[128,1024]{1,0:T(8,128)(2,1)S(1)}, bf16[128,1024]{1,0:T(8,128)(2,1)S(1)}, u32[]{:S(2)}, u32[]{:S(2)}) collective-permute-start(bf16[128,1024]{1,0:T(8,128)(2,1)S(1)} %slice.269), channel_id=1, source_target_pairs={{0,8},{4,12},{8,0},{12,4},{1,9},{5,13},{9,1},{13,5},{2,10},{6,14},... | collective-permute-start | bytes 786440 | tf_op jit(solution)/shard_map/ppermute | solution.py:271
  132.3 14.7 %collective-permute-start.30 = (bf16[128,1024]{1,0:T(8,128)(2,1)S(1)}, bf16[128,1024]{1,0:T(8,128)(2,1)S(1)}, u32[]{:S(2)}, u32[]{:S(2)}) collective-permute-start(bf16[128,1024]{1,0:T(8,128)(2,1)S(1)} %convert_add_fusion.1), channel_id=1, source_target_pairs={{0,3},{1,0},{2,1},{3,2},{4,7},{5,4},{6,5},{7,6},{8,11},{9,8},{10,9... | collective-permute-start | bytes 786440 | tf_op jit(solution)/shard_map/ppermute | solution.py:287
  135.5 9.2 %collective-permute-start.27 = (bf16[128,1024]{1,0:T(8,128)(2,1)S(1)}, bf16[128,1024]{1,0:T(8,128)(2,1)S(1)}, u32[]{:S(2)}, u32[]{:S(2)}) collective-permute-start(bf16[128,1024]{1,0:T(8,128)(2,1)S(1)} %slice.268), channel_id=1, source_target_pairs={{0,8},{4,12},{8,0},{12,4},{1,9},{5,13},{9,1},{13,5},{2,10},{6,14},... | collective-permute-start | bytes 786440 | tf_op jit(solution)/shard_map/ppermute | solution.py:271
  141.5 10.2 %collective-permute-start.29 = (bf16[128,1024]{1,0:T(8,128)(2,1)S(1)}, bf16[128,1024]{1,0:T(8,128)(2,1)S(1)}, u32[]{:S(2)}, u32[]{:S(2)}) collective-permute-start(bf16[128,1024]{1,0:T(8,128)(2,1)S(1)} %add_convert_fusion.1), channel_id=1, source_target_pairs={{0,1},{1,2},{2,3},{3,0},{4,5},{5,6},{6,7},{7,4},{8,9},{9,10},{10,1... | collective-permute-start | bytes 786440 | tf_op jit(solution)/shard_map/ppermute | solution.py:287
  (16 other events, 95.2 us)

commit v9 on v8

--- a/solution.py
+++ b/solution.py
@@ -176,13 +176,25 @@
     own_terms, other_terms, w_gate_up = lax.optimization_barrier(
         (own_terms, other_terms, w_gate_up)
     )
-    gate_up_weight = w_gate_up[0].reshape(model_width, 2 * ff_local)
-    gots = [
-        lax.ppermute(term(step).astype(bf16), "donor", rotation(n_donor, step)) for step in steps
+    weights = [
+        w_gate_up[0, row * pair_cols : (row + 1) * pair_cols].reshape(pair_cols, 2 * ff_local)
+        for row in range(n_rows)
     ]
-    gots, gate_up_weight = lax.optimization_barrier((gots, gate_up_weight))
+    early = n_rows // 2
+    carry = {1: [], -1: []}
+    for place, step in enumerate(steps[::-1]):
+        way = 1 if step <= n_donor // 2 else -1
+        part = term(step)
+        for got in carry[way]:
+            part = part + got.astype(f32)
+        got = lax.ppermute(part.astype(bf16), "donor", rotation(n_donor, way))
+        if place == 0:
+            got, weights[:early] = lax.optimization_barrier((got, weights[:early]))
+        if place == n_donor - 2:
+            got, weights[early:] = lax.optimization_barrier((got, weights[early:]))
+        carry[way] = [got]
     total = term(0) + hidden_part.astype(f32)
-    for got in gots:
+    for got in carry[1] + carry[-1]:
         total = total + got.astype(f32)
     chunk = total.astype(bf16)
 
@@ -211,27 +223,36 @@
                 (gots, own_act[:slot], other_act[:slot])
             )
         if n_rows == 2:
-            block = jnp.concatenate(
-                [jnp.where(y == 0, here, gots[0]), jnp.where(y == 0, gots[0], here)], axis=1
-            )
+            pieces = [jnp.where(y == 0, here, gots[0]), jnp.where(y == 0, gots[0], here)]
         else:
-            block = jnp.zeros((part_rows, n_rows, pair_cols), bf16)
-            block = lax.dynamic_update_index_in_dim(block, here, y, 1)
-            for hop, got in enumerate(gots, 1):
-                block = lax.dynamic_update_index_in_dim(block, got, (y - hop) % n_rows, 1)
-            block = block.reshape(part_rows, model_width)
+            stacked = jnp.stack([here] + gots, axis=0)
+            pieces = [pick(stacked, (y - row) % n_rows) for row in range(n_rows)]
+        block = jnp.concatenate(pieces, axis=1)
         resid_parts[slot] = lax.dynamic_slice_in_dim(block, z * columns, columns, 1)
-        block_f = block.astype(f32)
-        inverse = lax.rsqrt(jnp.mean(block_f * block_f, axis=1, keepdims=True) + 1e-06)
-        normed = (block_f * inverse * gain_f[None, :]).astype(bf16)
+        pieces = [piece.astype(f32) for piece in pieces]
+        squares = sum(jnp.sum(piece * piece, axis=1, keepdims=True) for piece in pieces)
+        inverse = lax.rsqrt(squares / model_width + 1e-06)
+        normed = jnp.stack(
+            [
+                (piece * inverse * gain_f[None, row * pair_cols : (row + 1) * pair_cols]).astype(bf16)
+                for row, piece in enumerate(pieces)
+            ],
+            axis=0,
+        )
         own_rows.append(normed)
         other_rows.append(lax.ppermute(normed, "expert", swap))
         row_gates.append((pick(own_gates, part), pick(other_gates, part)))
         if len(row_gates) == batches[0]:
             batch = batches.pop(0)
-            rows_in = jnp.concatenate(own_rows + other_rows, axis=0)
             scale = jnp.concatenate([g[0] for g in row_gates] + [g[1] for g in row_gates])
-            gate_up = jnp.dot(rows_in, gate_up_weight, preferred_element_type=f32)
+            gate_up = sum(
+                jnp.dot(
+                    jnp.concatenate([rows[row] for rows in own_rows + other_rows], axis=0),
+                    weights[row],
+                    preferred_element_type=f32,
+                )
+                for row in range(n_rows)
+            )
             act = jax.nn.silu(gate_up[:, :ff_local]) * gate_up[:, ff_local:]
             act = (act * scale[:, None]).astype(bf16).reshape(2, batch, part_rows, ff_local)
             for i in range(batch):

time: 153 us -> 156 us (1.020)
  local copies, waits for them, and re-layouts: 20.4 us -> 26.9 us
  matrix products: 22.3 us -> 16.3 us
  other arithmetic: 8.41 us -> 11 us
  waiting for transfers between devices: 71.9 us -> 70 us
    ppermute x3, waiting for transfers between devices: 8.42 us -> 23.2 us  [shards(): chunk = lax.ppermute(chunk, 'donor', rotation(n_donor, 1))]
    ppermute x4, waiting for transfers between devices: 16.8 us -> 2.78 us  [shards(): lax.ppermute(chunk, 'expert', turn(hop))]
    slice x0 -> x2, local copies, waits for them, and re-layouts: none -> 11 us  [the longest x1 11 us: shards(): w_gate_up[0, row * pair_cols:(row + 1) * pair_cols]]
    ppermute x1, waiting for transfers between devices: 0.01 us -> 6.85 us  [shards(): got = lax.ppermute(head_out, 'expert', turn(step))]
    dot_general x2 -> x4, matrix products: 13.1 us -> 7.2 us  [shards(): jnp.dot(jnp.concatenate([rows[row] for rows in own_rows + other_rows], ax...]
    ppermute x3, waiting for transfers between devices: 4.41 us -> 0.01 us  [shards(): lax.ppermute(gate_table, 'expert', rotation(n_expert, step))]
    ppermute x3, waiting for transfers between devices: 9.42 us -> 5.18 us  [shards(): got = lax.ppermute(part.astype(bf16), 'donor', rotation(n_donor, way))]
    unnamed x38 -> x37, local copies, waits for them, and re-layouts: 14 us -> 9.91 us
  transfers between devices with their start and end apart: 32 -> 32, of which waited for: 22 -> 18; matrix products, arithmetic and copies ran while one was open for 25% -> 28% of each run, Pallas kernels for 0% -> 0%
where the time goes in v9:
time: 156 us; the launch traced here: 155 us
  waiting for transfers between devices  70 us (45%)
  starting transfers between devices  28.2 us (18%)
  local copies, waits for them, and re-layouts  26.9 us (17%)
  matrix products  16.3 us (10%)
  other arithmetic  11 us (7%)
  between operations  2.85 us (2%)
    ppermute x3, waiting for transfers between devices, shards(): chunk = lax.ppermute(chunk, 'donor', rotation(n_donor, 1))  23.2 us
    ppermute x3, waiting for transfers between devices, shards(): lax.ppermute(part_sum.astype(bf16), 'donor', rotation(n_donor, way))  14.3 us
    slice x1, local copies, waits for them, and re-layouts, shards(): w_gate_up[0, row * pair_cols:(row + 1) * pair_cols]  11 us
    unnamed x37, local copies, waits for them, and re-layouts  9.91 us
    dot_general x4, matrix products, shards(): jnp.dot(jnp.concatenate([rows[row] for rows in own_rows + other_rows], ax...  7.2 us
    ppermute x1, waiting for transfers between devices, shards(): got = lax.ppermute(head_out, 'expert', turn(step))  6.85 us
    ppermute x4, waiting for transfers between devices, shards(): lax.ppermute(block[hop].astype(bf16), 'expert', turn(hop))  6.84 us
    ppermute x3, waiting for transfers between devices, shards(): got = lax.ppermute(part.astype(bf16), 'donor', rotation(n_donor, way))  5.18 us
  transfers between devices with their start and end apart: 32, of which 18 were waited for; matrix products, arithmetic and copies ran while one was open for 28% of the time, Pallas kernels for 0%

profile of v9, /device:TPU:0, one launch (start us, length us, event | category | flops | bytes accessed | tf_op | source)
XLA Modules:
  0.0 155.3 jit_solution(1343575897833371601)
XLA Ops:
  3.3 2.6 %collective-permute-start.2 = (f32[8,128]{1,0:T(8,128)S(1)}, f32[8,128]{1,0:T(8,128)S(1)}, u32[]{:S(2)}, u32[]{:S(2)}) collective-permute-start(f32[8,128]{1,0:T(8,128)S(1)} %bitcast.218), channel_id=1, source_target_pairs={{0,8},{4,12},{8,0},{12,4},{1,9},{5,13},{9,1},{13,5},{2,10},{6,14},... | collective-permute-start | bytes 12296 | tf_op jit(solution)/shard_map/ppermute | solution.py:140
  5.9 1.4 collective-permute-start.3
  9.8 5.0 %all-to-all-start = ((bf16[16,32,256]{2,1,0:T(8,128)(2,1)}), bf16[16,32,256]{2,1,0:T(8,128)(2,1)S(1)}, u32[]{:S(2)}, u32[]{:S(2)}) async-start(bf16[16,32,256]{2,1,0:T(8,128)(2,1)} %broadcast_select_fusion), calls=%async_computation | async-start | bytes 524288 | tf_op jit(solution)/shard_map/all_to_all | solution.py:38
  16.2 1.3 dynamic_slice.150
  19.7 5.1 %all-to-all-done = bf16[16,32,256]{2,1,0:T(8,128)(2,1)S(1)} async-done(((bf16[16,32,256]{2,1,0:T(8,128)(2,1)}), bf16[16,32,256]{2,1,0:T(8,128)(2,1)S(1)}, u32[]{:S(2)}, u32[]{:S(2)}) %all-to-all-start) | async-done | bytes 262176 | tf_op jit(solution)/shard_map/all_to_all | solution.py:38
  25.6 1.2 while.22
  27.1 1.8 %while.23 = (s32[]{:T(128)}, f32[128,8]{0,1:T(8,128)S(1)}, f32[128,8,128]{2,0,1:T(8,128)S(1)}, s32[]{:T(128)}, s32[]{:T(128)}, /*index=5*/bf16[128,8,128]{2,0,1:...) while((s32[]{:T(128)}, f32[128,8]{0,1:T(8,128)S(1)}, ...), condition=%wide.region_8.9_spmd, body=%wide.region_6.8_spmd.sunk | while | flops 271188992 | bytes 3691657 | solution.py:94
  30.3 1.5 collective-permute-start.5
  31.9 6.8 %collective-permute-done = bf16[128,1024]{1,0:T(8,128)(2,1)S(1)} collective-permute-done((bf16[128,1024]{1,0:T(8,128)(2,1)S(1)}, bf16[128,1024]{1,0:T(8,128)(2,1)S(1)}, u32[]{:S(2)}, u32[]{:S(2)}) %collective-permute-start) | collective-permute-done | bytes 262176 | tf_op jit(solution)/shard_map/ppermute | solution.py:161
  39.6 2.3 %fusion.93 = f32[256,1024]{1,0:T(8,128)S(1)} fusion(bf16[1024,1024]{1,0:T(8,128)(2,1)} %collective-permute-done.4, bf16[64,1024]{1,0:T(8,128)(2,1)S(1)} %get-tuple-element.283, bf16[64,1024]{1,0:T(8,128)(2,1)S(1)} %get-tuple-element.284, bf16[64,1024]{1,0:T(8,128)(2,1)S(1)} %get-tuple-element.285, bf16[64,1024]{1,0:T(8,128)(2,1)S(1)} %get-tuple-element.282), kind=kOutput, calls=%fused_computation.208 | convolution fusion | flops 538968064 | bytes 3670016 | tf_op jit(solution)/shard_map/dot_general | solution.py:167
  42.2 11.0 %fusion.123 = (bf16[1,2048,2,768]{3,2,1,0:T(2,128)(2,1)}, bf16[1,2048,2,768]{3,2,1,0:T(2,128)(2,1)S(1)}) fusion(bf16[1,4096,2,768]{3,2,1,0:T(2,128)(2,1)} %param.26), kind=kLoop, calls=%fused_computation.294 | loop fusion | bytes 25165824 | tf_op jit(solution)/shard_map/slice | solution.py:180
  53.3 4.0 %copy.53 = bf16[256,8,2,768]{3,1,2,0:T(8,128)(2,1)} copy(bf16[256,8,2,768]{3,2,1,0:T(2,128)(2,1)S(1)} %bitcast.189) | data formatting | bytes 12582912
  57.3 3.7 %collective-permute-start.8 = (bf16[64,2048]{1,0:T(8,128)(2,1)S(1)}, bf16[64,2048]{1,0:T(8,128)(2,1)S(1)}, u32[]{:S(2)}, u32[]{:S(2)}) collective-permute-start(bf16[64,2048]{1,0:T(8,128)(2,1)S(1)} %pad_maximum_fusion.9), channel_id=1, source_target_pairs={{0,3},{1,0},{2,1},{3,2},{4,7},{5,4},{6,5},{7,6},{8,11},{9,8},{10,9... | collective-permute-start | bytes 786440 | tf_op jit(solution)/shard_map/ppermute | solution.py:190
  61.6 4.1 %copy.54 = bf16[256,8,2,768]{3,1,2,0:T(8,128)(2,1)S(1)} copy(bf16[256,8,2,768]{3,2,1,0:T(2,128)(2,1)} %bitcast.188) | data formatting | bytes 12582912
  65.7 5.2 %collective-permute-done.7 = bf16[64,2048]{1,0:T(8,128)(2,1)S(1)} collective-permute-done((bf16[64,2048]{1,0:T(8,128)(2,1)S(1)}, bf16[64,2048]{1,0:T(8,128)(2,1)S(1)}, u32[]{:S(2)}, u32[]{:S(2)}) %collective-permute-start.7) | collective-permute-done | bytes 262176 | tf_op jit(solution)/shard_map/ppermute | solution.py:190
  71.2 2.1 %collective-permute-start.9 = (bf16[64,2048]{1,0:T(8,128)(2,1)S(1)}, bf16[64,2048]{1,0:T(8,128)(2,1)S(1)}, u32[]{:S(2)}, u32[]{:S(2)}) collective-permute-start(bf16[64,2048]{1,0:T(8,128)(2,1)S(1)} %fusion.78), channel_id=1, source_target_pairs={{0,1},{1,2},{2,3},{3,0},{4,5},{5,6},{6,7},{7,4},{8,9},{9,10},{10,1... | collective-permute-start | bytes 786440 | tf_op jit(solution)/shard_map/ppermute | solution.py:219
  74.2 5.2 %collective-permute-done.9 = bf16[64,2048]{1,0:T(8,128)(2,1)S(1)} collective-permute-done((bf16[64,2048]{1,0:T(8,128)(2,1)S(1)}, bf16[64,2048]{1,0:T(8,128)(2,1)S(1)}, u32[]{:S(2)}, u32[]{:S(2)}) %collective-permute-start.9) | collective-permute-done | bytes 262176 | tf_op jit(solution)/shard_map/ppermute | solution.py:219
  79.4 1.6 %collective-permute-done.10 = bf16[64,2048]{1,0:T(8,128)(2,1)S(1)} collective-permute-done((bf16[64,2048]{1,0:T(8,128)(2,1)S(1)}, bf16[64,2048]{1,0:T(8,128)(2,1)S(1)}, u32[]{:S(2)}, u32[]{:S(2)}) %collective-permute-start.10) | collective-permute-done | bytes 262176 | tf_op jit(solution)/shard_map/ppermute | solution.py:216
  81.5 10.2 %collective-permute-done.11 = bf16[64,2048]{1,0:T(8,128)(2,1)S(1)} collective-permute-done((bf16[64,2048]{1,0:T(8,128)(2,1)S(1)}, bf16[64,2048]{1,0:T(8,128)(2,1)S(1)}, u32[]{:S(2)}, u32[]{:S(2)}) %collective-permute-start.11) | collective-permute-done | bytes 262176 | tf_op jit(solution)/shard_map/ppermute | solution.py:219
  91.9 7.9 %collective-permute-done.13 = bf16[64,2048]{1,0:T(8,128)(2,1)S(1)} collective-permute-done((bf16[64,2048]{1,0:T(8,128)(2,1)S(1)}, bf16[64,2048]{1,0:T(8,128)(2,1)S(1)}, u32[]{:S(2)}, u32[]{:S(2)}) %collective-permute-start.13) | collective-permute-done | bytes 262176 | tf_op jit(solution)/shard_map/ppermute | solution.py:219
  103.5 1.8 %fusion.25 = f32[256,1536]{1,0:T(8,128)S(1)} fusion(bf16[2048,1536]{1,0:T(8,128)(2,1)S(1)} %bitcast.194, bf16[64,2048]{1,0:T(8,128)(2,1)S(1)} %get-tuple-element.277, bf16[64,2048]{1,0:T(8,128)(2,1)S(1)} %get-tuple-element.275, bf16[64,2048]{1,0:T(8,128)(2,1)S(1)} %get-tuple-element.300, bf16[64,2048]{1,0:T(8,128)(2,1)S(1)} %get-tuple-element.301), kind=kOutput, calls=%fused_computation.43 | convolution fusion | flops 1614807040 | bytes 8912896 | tf_op jit(solution)/shard_map/dot_general | solution.py:249
  106.3 1.8 %convolution_add_fusion.2 = f32[256,1536]{1,0:T(8,128)S(1)} fusion(f32[256,1536]{1,0:T(8,128)S(1)} %fusion.25, bf16[2048,1536]{1,0:T(8,128)(2,1)S(1)} %bitcast.192, bf16[64,2048]{1,0:T(8,128)(2,1)S(1)} %get-tuple-element.276, bf16[64,2048]{1,0:T(8,128)(2,1)S(1)} %get-tuple-element.274, bf16[64,2048]{1,0:T(8,128)(2,1)S(1)} %get-tuple-element.313, ...), kind=kOutput, calls=%fused_computation.12 | convolution fusion | flops 1615200256 | bytes 10485760 | tf_op jit(solution)/shard_map/dot_general | solution.py:249
  110.3 1.8 %collective-permute-done.19 = bf16[2,64,2048]{2,1,0:T(8,128)(2,1)S(1)} collective-permute-done((bf16[2,64,2048]{2,1,0:T(8,128)(2,1)S(1)}, bf16[2,64,2048]{2,1,0:T(8,128)(2,1)S(1)}, u32[]{:S(2)}, u32[]{:S(2)}) %collective-permute-start.19) | collective-permute-done | bytes 524320 | tf_op jit(solution)/shard_map/ppermute | solution.py:243
  112.1 1.8 %fusion.40 = f32[256,1536]{1,0:T(8,128)S(1)} fusion(bf16[2048,1536]{1,0:T(8,128)(2,1)S(1)} %bitcast.195, bf16[64,2048]{1,0:T(8,128)(2,1)S(1)} %get-tuple-element.269, bf16[64,2048]{1,0:T(8,128)(2,1)S(1)} %get-tuple-element.267, bf16[64,2048]{1,0:T(8,128)(2,1)S(1)} %get-tuple-element.316, bf16[64,2048]{1,0:T(8,128)(2,1)S(1)} %get-tuple-element.299), kind=kOutput, calls=%fused_computation.58 | convolution fusion | flops 1614807040 | bytes 8912896 | tf_op jit(solution)/shard_map/dot_general | solution.py:249
  113.9 1.8 %convolution_add_fusion.1 = f32[256,1536]{1,0:T(8,128)S(1)} fusion(f32[256,1536]{1,0:T(8,128)S(1)} %fusion.40, bf16[2048,1536]{1,0:T(8,128)(2,1)S(1)} %bitcast.193, bf16[64,2048]{1,0:T(8,128)(2,1)S(1)} %get-tuple-element.268, bf16[64,2048]{1,0:T(8,128)(2,1)S(1)} %get-tuple-element.266, bf16[64,2048]{1,0:T(8,128)(2,1)S(1)} %get-tuple-element.315, ...), kind=kOutput, calls=%fused_computation.11 | convolution fusion | flops 1615200256 | bytes 10485760 | tf_op jit(solution)/shard_map/dot_general | solution.py:249
  121.7 1.7 %collective-permute-start.25 = (bf16[128,1024]{1,0:T(8,128)(2,1)S(1)}, bf16[128,1024]{1,0:T(8,128)(2,1)S(1)}, u32[]{:S(2)}, u32[]{:S(2)}) collective-permute-start(bf16[128,1024]{1,0:T(8,128)(2,1)S(1)} %slice.342), channel_id=1, source_target_pairs={{0,8},{4,12},{8,0},{12,4},{1,9},{5,13},{9,1},{13,5},{2,10},{6,14},... | collective-permute-start | bytes 786440 | tf_op jit(solution)/shard_map/ppermute | solution.py:292
  123.4 6.8 %collective-permute-done.21 = bf16[128,1024]{1,0:T(8,128)(2,1)S(1)} collective-permute-done((bf16[128,1024]{1,0:T(8,128)(2,1)S(1)}, bf16[128,1024]{1,0:T(8,128)(2,1)S(1)}, u32[]{:S(2)}, u32[]{:S(2)}) %collective-permute-start.21) | collective-permute-done | bytes 262176 | tf_op jit(solution)/shard_map/ppermute | solution.py:292
  135.3 3.0 %collective-permute-start.30 = (bf16[128,1024]{1,0:T(8,128)(2,1)S(1)}, bf16[128,1024]{1,0:T(8,128)(2,1)S(1)}, u32[]{:S(2)}, u32[]{:S(2)}) collective-permute-start(bf16[128,1024]{1,0:T(8,128)(2,1)S(1)} %convert_add_fusion.1), channel_id=1, source_target_pairs={{0,3},{1,0},{2,1},{3,2},{4,7},{5,4},{6,5},{7,6},{8,11},{9,8},{10,9... | collective-permute-start | bytes 786440 | tf_op jit(solution)/shard_map/ppermute | solution.py:308
  138.3 1.4 collective-permute-start.27
  139.7 4.4 %collective-permute-done.28 = bf16[128,1024]{1,0:T(8,128)(2,1)S(1)} collective-permute-done((bf16[128,1024]{1,0:T(8,128)(2,1)S(1)}, bf16[128,1024]{1,0:T(8,128)(2,1)S(1)}, u32[]{:S(2)}, u32[]{:S(2)}) %collective-permute-start.28) | collective-permute-done | bytes 262176 | tf_op jit(solution)/shard_map/ppermute | solution.py:308
  144.6 5.2 %collective-permute-done.30 = bf16[128,1024]{1,0:T(8,128)(2,1)S(1)} collective-permute-done((bf16[128,1024]{1,0:T(8,128)(2,1)S(1)}, bf16[128,1024]{1,0:T(8,128)(2,1)S(1)}, u32[]{:S(2)}, u32[]{:S(2)}) %collective-permute-start.30) | collective-permute-done | bytes 262176 | tf_op jit(solution)/shard_map/ppermute | solution.py:308
  149.7 4.7 %collective-permute-done.29 = bf16[128,1024]{1,0:T(8,128)(2,1)S(1)} collective-permute-done((bf16[128,1024]{1,0:T(8,128)(2,1)S(1)}, bf16[128,1024]{1,0:T(8,128)(2,1)S(1)}, u32[]{:S(2)}, u32[]{:S(2)}) %collective-permute-start.29) | collective-permute-done | bytes 262176 | tf_op jit(solution)/shard_map/ppermute | solution.py:308
  (204 shorter events, 35.3 us)
Async XLA Ops:
  2.9 27.5 %collective-permute-start.1 = (f32[8,128]{1,0:T(8,128)S(1)}, f32[8,128]{1,0:T(8,128)S(1)}, u32[]{:S(2)}, u32[]{:S(2)}) collective-permute-start(f32[8,128]{1,0:T(8,128)S(1)} %bitcast.217), channel_id=1, source_target_pairs={{0,4},{4,8},{8,12},{12,0},{1,5},{5,9},{9,13},{13,1},{2,6},{6,10},{... | collective-permute-start | bytes 12296 | tf_op jit(solution)/shard_map/ppermute | solution.py:140
  3.3 28.6 %collective-permute-start.2 = (f32[8,128]{1,0:T(8,128)S(1)}, f32[8,128]{1,0:T(8,128)S(1)}, u32[]{:S(2)}, u32[]{:S(2)}) collective-permute-start(f32[8,128]{1,0:T(8,128)S(1)} %bitcast.218), channel_id=1, source_target_pairs={{0,8},{4,12},{8,0},{12,4},{1,9},{5,13},{9,1},{13,5},{2,10},{6,14},... | collective-permute-start | bytes 12296 | tf_op jit(solution)/shard_map/ppermute | solution.py:140
  5.9 26.0 %collective-permute-start.3 = (f32[8,128]{1,0:T(8,128)S(1)}, f32[8,128]{1,0:T(8,128)S(1)}, u32[]{:S(2)}, u32[]{:S(2)}) collective-permute-start(f32[8,128]{1,0:T(8,128)S(1)} %bitcast.219), channel_id=1, source_target_pairs={{0,12},{4,0},{8,4},{12,8},{1,13},{5,1},{9,5},{13,9},{2,14},{6,2},{... | collective-permute-start | bytes 12296 | tf_op jit(solution)/shard_map/ppermute | solution.py:140
  9.8 15.1 %all-to-all-start = ((bf16[16,32,256]{2,1,0:T(8,128)(2,1)}), bf16[16,32,256]{2,1,0:T(8,128)(2,1)S(1)}, u32[]{:S(2)}, u32[]{:S(2)}) async-start(bf16[16,32,256]{2,1,0:T(8,128)(2,1)} %broadcast_select_fusion), calls=%async_computation | async-start | bytes 524288 | tf_op jit(solution)/shard_map/all_to_all | solution.py:38
  14.8 24.8 %collective-permute-start.4 = (bf16[1024,1024]{1,0:T(8,128)(2,1)}, bf16[1024,1024]{1,0:T(8,128)(2,1)}, u32[]{:S(2)}, u32[]{:S(2)}) collective-permute-start(bf16[1024,1024]{1,0:T(8,128)(2,1)} %param.22), channel_id=1, source_target_pairs={{0,4},{4,0},{8,12},{12,8},{1,5},{5,1},{9,13},{13,9},{2,6},{6,2},{1... | collective-permute-start | bytes 6291464 | tf_op jit(solution)/shard_map/ppermute | solution.py:143
  29.4 9.3 %collective-permute-start = (bf16[128,1024]{1,0:T(8,128)(2,1)S(1)}, bf16[128,1024]{1,0:T(8,128)(2,1)S(1)}, u32[]{:S(2)}, u32[]{:S(2)}) collective-permute-start(bf16[128,1024]{1,0:T(8,128)(2,1)S(1)} %copy.48), channel_id=1, source_target_pairs={{0,8},{4,12},{8,0},{12,4},{1,9},{5,13},{9,1},{13,5},{2,10},{6,14},... | collective-permute-start | bytes 786440 | tf_op jit(solution)/shard_map/ppermute | solution.py:161
  30.3 40.6 %collective-permute-start.5 = (bf16[64,2048]{1,0:T(8,128)(2,1)S(1)}, bf16[64,2048]{1,0:T(8,128)(2,1)S(1)}, u32[]{:S(2)}, u32[]{:S(2)}) collective-permute-start(bf16[64,2048]{1,0:T(8,128)(2,1)S(1)} %dynamic_slice.156), channel_id=1, source_target_pairs={{0,8},{4,12},{8,0},{12,4},{1,9},{5,13},{9,1},{13,5},{2,10},{6,14},... | collective-permute-start | bytes 786440 | tf_op jit(solution)/shard_map/ppermute | solution.py:153
  42.0 19.1 %collective-permute-start.6 = (bf16[64,2048]{1,0:T(8,128)(2,1)S(1)}, bf16[64,2048]{1,0:T(8,128)(2,1)S(1)}, u32[]{:S(2)}, u32[]{:S(2)}) collective-permute-start(bf16[64,2048]{1,0:T(8,128)(2,1)S(1)} %pad_maximum_fusion.8), channel_id=1, source_target_pairs={{0,1},{1,2},{2,3},{3,0},{4,5},{5,6},{6,7},{7,4},{8,9},{9,10},{10,1... | collective-permute-start | bytes 786440 | tf_op jit(solution)/shard_map/ppermute | solution.py:190
  57.3 13.6 %collective-permute-start.8 = (bf16[64,2048]{1,0:T(8,128)(2,1)S(1)}, bf16[64,2048]{1,0:T(8,128)(2,1)S(1)}, u32[]{:S(2)}, u32[]{:S(2)}) collective-permute-start(bf16[64,2048]{1,0:T(8,128)(2,1)S(1)} %pad_maximum_fusion.9), channel_id=1, source_target_pairs={{0,3},{1,0},{2,1},{3,2},{4,7},{5,4},{6,5},{7,6},{8,11},{9,8},{10,9... | collective-permute-start | bytes 786440 | tf_op jit(solution)/shard_map/ppermute | solution.py:190
  61.1 9.8 %collective-permute-start.7 = (bf16[64,2048]{1,0:T(8,128)(2,1)S(1)}, bf16[64,2048]{1,0:T(8,128)(2,1)S(1)}, u32[]{:S(2)}, u32[]{:S(2)}) collective-permute-start(bf16[64,2048]{1,0:T(8,128)(2,1)S(1)} %fusion.79), channel_id=1, source_target_pairs={{0,1},{1,2},{2,3},{3,0},{4,5},{5,6},{6,7},{7,4},{8,9},{9,10},{10,1... | collective-permute-start | bytes 786440 | tf_op jit(solution)/shard_map/ppermute | solution.py:190
  71.2 8.2 %collective-permute-start.9 = (bf16[64,2048]{1,0:T(8,128)(2,1)S(1)}, bf16[64,2048]{1,0:T(8,128)(2,1)S(1)}, u32[]{:S(2)}, u32[]{:S(2)}) collective-permute-start(bf16[64,2048]{1,0:T(8,128)(2,1)S(1)} %fusion.78), channel_id=1, source_target_pairs={{0,1},{1,2},{2,3},{3,0},{4,5},{5,6},{6,7},{7,4},{8,9},{9,10},{10,1... | collective-permute-start | bytes 786440 | tf_op jit(solution)/shard_map/ppermute | solution.py:219
  73.3 7.7 %collective-permute-start.10 = (bf16[64,2048]{1,0:T(8,128)(2,1)S(1)}, bf16[64,2048]{1,0:T(8,128)(2,1)S(1)}, u32[]{:S(2)}, u32[]{:S(2)}) collective-permute-start(bf16[64,2048]{1,0:T(8,128)(2,1)S(1)} %fusion.78), channel_id=1, source_target_pairs={{0,8},{4,12},{8,0},{12,4},{1,9},{5,13},{9,1},{13,5},{2,10},{6,14},... | collective-permute-start | bytes 786440 | tf_op jit(solution)/shard_map/ppermute | solution.py:216
  81.0 10.7 %collective-permute-start.11 = (bf16[64,2048]{1,0:T(8,128)(2,1)S(1)}, bf16[64,2048]{1,0:T(8,128)(2,1)S(1)}, u32[]{:S(2)}, u32[]{:S(2)}) collective-permute-start(bf16[64,2048]{1,0:T(8,128)(2,1)S(1)} %collective-permute-done.9), channel_id=1, source_target_pairs={{0,1},{1,2},{2,3},{3,0},{4,5},{5,6},{6,7},{7,4},{8,9},{9,10},{10,1... | collective-permute-start | bytes 786440 | tf_op jit(solution)/shard_map/ppermute | solution.py:219
  81.2 10.5 %collective-permute-start.12 = (bf16[64,2048]{1,0:T(8,128)(2,1)S(1)}, bf16[64,2048]{1,0:T(8,128)(2,1)S(1)}, u32[]{:S(2)}, u32[]{:S(2)}) collective-permute-start(bf16[64,2048]{1,0:T(8,128)(2,1)S(1)} %collective-permute-done.9), channel_id=1, source_target_pairs={{0,8},{4,12},{8,0},{12,4},{1,9},{5,13},{9,1},{13,5},{2,10},{6,14},... | collective-permute-start | bytes 786440 | tf_op jit(solution)/shard_map/ppermute | solution.py:216
  91.7 8.2 %collective-permute-start.13 = (bf16[64,2048]{1,0:T(8,128)(2,1)S(1)}, bf16[64,2048]{1,0:T(8,128)(2,1)S(1)}, u32[]{:S(2)}, u32[]{:S(2)}) collective-permute-start(bf16[64,2048]{1,0:T(8,128)(2,1)S(1)} %collective-permute-done.11), channel_id=1, source_target_pairs={{0,1},{1,2},{2,3},{3,0},{4,5},{5,6},{6,7},{7,4},{8,9},{9,10},{10,1... | collective-permute-start | bytes 786440 | tf_op jit(solution)/shard_map/ppermute | solution.py:219
  91.7 8.2 %collective-permute-start.14 = (bf16[64,2048]{1,0:T(8,128)(2,1)S(1)}, bf16[64,2048]{1,0:T(8,128)(2,1)S(1)}, u32[]{:S(2)}, u32[]{:S(2)}) collective-permute-start(bf16[64,2048]{1,0:T(8,128)(2,1)S(1)} %collective-permute-done.11), channel_id=1, source_target_pairs={{0,8},{4,12},{8,0},{12,4},{1,9},{5,13},{9,1},{13,5},{2,10},{6,14},... | collective-permute-start | bytes 786440 | tf_op jit(solution)/shard_map/ppermute | solution.py:216
  100.7 2.0 %collective-permute-start.17 = (bf16[2,64,2048]{2,1,0:T(8,128)(2,1)S(1)}, bf16[2,64,2048]{2,1,0:T(8,128)(2,1)S(1)}, u32[]{:S(2)}, u32[]{:S(2)}) collective-permute-start(bf16[2,64,2048]{2,1,0:T(8,128)(2,1)S(1)} %pad_maximum_fusion.2), channel_id=1, source_target_pairs={{0,4},{4,0},{8,12},{12,8},{1,5},{5,1},{9,13},{13,9},{2,6},{6,2},{1... | collective-permute-start | bytes 1572872 | tf_op jit(solution)/shard_map/ppermute | solution.py:243
  100.8 8.7 %collective-permute-start.15 = (bf16[64,2048]{1,0:T(8,128)(2,1)S(1)}, bf16[64,2048]{1,0:T(8,128)(2,1)S(1)}, u32[]{:S(2)}, u32[]{:S(2)}) collective-permute-start(bf16[64,2048]{1,0:T(8,128)(2,1)S(1)} %collective-permute-done.13), channel_id=1, source_target_pairs={{0,8},{4,12},{8,0},{12,4},{1,9},{5,13},{9,1},{13,5},{2,10},{6,14},... | collective-permute-start | bytes 786440 | tf_op jit(solution)/shard_map/ppermute | solution.py:216
  100.9 2.5 %collective-permute-start.16 = (bf16[2,64,2048]{2,1,0:T(8,128)(2,1)S(1)}, bf16[2,64,2048]{2,1,0:T(8,128)(2,1)S(1)}, u32[]{:S(2)}, u32[]{:S(2)}) collective-permute-start(bf16[2,64,2048]{2,1,0:T(8,128)(2,1)S(1)} %pad_maximum_fusion.1), channel_id=1, source_target_pairs={{0,4},{4,0},{8,12},{12,8},{1,5},{5,1},{9,13},{13,9},{2,6},{6,2},{1... | collective-permute-start | bytes 1572872 | tf_op jit(solution)/shard_map/ppermute | solution.py:243
  101.5 8.7 %collective-permute-start.18 = (bf16[2,64,2048]{2,1,0:T(8,128)(2,1)S(1)}, bf16[2,64,2048]{2,1,0:T(8,128)(2,1)S(1)}, u32[]{:S(2)}, u32[]{:S(2)}) collective-permute-start(bf16[2,64,2048]{2,1,0:T(8,128)(2,1)S(1)} %pad_maximum_fusion.4), channel_id=1, source_target_pairs={{0,4},{4,0},{8,12},{12,8},{1,5},{5,1},{9,13},{13,9},{2,6},{6,2},{1... | collective-permute-start | bytes 1572872 | tf_op jit(solution)/shard_map/ppermute | solution.py:243
  110.1 2.0 %collective-permute-start.19 = (bf16[2,64,2048]{2,1,0:T(8,128)(2,1)S(1)}, bf16[2,64,2048]{2,1,0:T(8,128)(2,1)S(1)}, u32[]{:S(2)}, u32[]{:S(2)}) collective-permute-start(bf16[2,64,2048]{2,1,0:T(8,128)(2,1)S(1)} %pad_maximum_fusion.5), channel_id=1, source_target_pairs={{0,4},{4,0},{8,12},{12,8},{1,5},{5,1},{9,13},{13,9},{2,6},{6,2},{1... | collective-permute-start | bytes 1572872 | tf_op jit(solution)/shard_map/ppermute | solution.py:243
  117.8 2.0 %collective-permute-start.20 = (bf16[256,1024]{1,0:T(8,128)(2,1)S(1)}, bf16[256,1024]{1,0:T(8,128)(2,1)S(1)}, u32[]{:S(2)}, u32[]{:S(2)}) collective-permute-start(bf16[256,1024]{1,0:T(8,128)(2,1)S(1)} %slice.339), channel_id=1, source_target_pairs={{0,4},{4,0},{8,12},{12,8},{1,5},{5,1},{9,13},{13,9},{2,6},{6,2},{1... | collective-permute-start | bytes 1572872 | tf_op jit(solution)/shard_map/ppermute | solution.py:287
  119.1 2.0 %collective-permute-start.24 = (bf16[256,1024]{1,0:T(8,128)(2,1)S(1)}, bf16[256,1024]{1,0:T(8,128)(2,1)S(1)}, u32[]{:S(2)}, u32[]{:S(2)}) collective-permute-start(bf16[256,1024]{1,0:T(8,128)(2,1)S(1)} %slice.336), channel_id=1, source_target_pairs={{0,4},{4,0},{8,12},{12,8},{1,5},{5,1},{9,13},{13,9},{2,6},{6,2},{1... | collective-permute-start | bytes 1572872 | tf_op jit(solution)/shard_map/ppermute | solution.py:287
  121.1 9.1 %collective-permute-start.21 = (bf16[128,1024]{1,0:T(8,128)(2,1)S(1)}, bf16[128,1024]{1,0:T(8,128)(2,1)S(1)}, u32[]{:S(2)}, u32[]{:S(2)}) collective-permute-start(bf16[128,1024]{1,0:T(8,128)(2,1)S(1)} %slice.343), channel_id=1, source_target_pairs={{0,8},{4,12},{8,0},{12,4},{1,9},{5,13},{9,1},{13,5},{2,10},{6,14},... | collective-permute-start | bytes 786440 | tf_op jit(solution)/shard_map/ppermute | solution.py:292
  121.7 13.5 %collective-permute-start.25 = (bf16[128,1024]{1,0:T(8,128)(2,1)S(1)}, bf16[128,1024]{1,0:T(8,128)(2,1)S(1)}, u32[]{:S(2)}, u32[]{:S(2)}) collective-permute-start(bf16[128,1024]{1,0:T(8,128)(2,1)S(1)} %slice.342), channel_id=1, source_target_pairs={{0,8},{4,12},{8,0},{12,4},{1,9},{5,13},{9,1},{13,5},{2,10},{6,14},... | collective-permute-start | bytes 786440 | tf_op jit(solution)/shard_map/ppermute | solution.py:292
  131.3 2.0 %collective-permute-start.23 = (bf16[256,1024]{1,0:T(8,128)(2,1)S(1)}, bf16[256,1024]{1,0:T(8,128)(2,1)S(1)}, u32[]{:S(2)}, u32[]{:S(2)}) collective-permute-start(bf16[256,1024]{1,0:T(8,128)(2,1)S(1)} %slice.337), channel_id=1, source_target_pairs={{0,4},{4,0},{8,12},{12,8},{1,5},{5,1},{9,13},{13,9},{2,6},{6,2},{1... | collective-permute-start | bytes 1572872 | tf_op jit(solution)/shard_map/ppermute | solution.py:287
  132.5 2.1 %collective-permute-start.22 = (bf16[256,1024]{1,0:T(8,128)(2,1)S(1)}, bf16[256,1024]{1,0:T(8,128)(2,1)S(1)}, u32[]{:S(2)}, u32[]{:S(2)}) collective-permute-start(bf16[256,1024]{1,0:T(8,128)(2,1)S(1)} %slice.338), channel_id=1, source_target_pairs={{0,4},{4,0},{8,12},{12,8},{1,5},{5,1},{9,13},{13,9},{2,6},{6,2},{1... | collective-permute-start | bytes 1572872 | tf_op jit(solution)/shard_map/ppermute | solution.py:287
  133.1 11.1 %collective-permute-start.28 = (bf16[128,1024]{1,0:T(8,128)(2,1)S(1)}, bf16[128,1024]{1,0:T(8,128)(2,1)S(1)}, u32[]{:S(2)}, u32[]{:S(2)}) collective-permute-start(bf16[128,1024]{1,0:T(8,128)(2,1)S(1)} %convert_add_fusion.2), channel_id=1, source_target_pairs={{0,1},{1,2},{2,3},{3,0},{4,5},{5,6},{6,7},{7,4},{8,9},{9,10},{10,1... | collective-permute-start | bytes 786440 | tf_op jit(solution)/shard_map/ppermute | solution.py:308
  134.5 9.6 %collective-permute-start.26 = (bf16[128,1024]{1,0:T(8,128)(2,1)S(1)}, bf16[128,1024]{1,0:T(8,128)(2,1)S(1)}, u32[]{:S(2)}, u32[]{:S(2)}) collective-permute-start(bf16[128,1024]{1,0:T(8,128)(2,1)S(1)} %slice.341), channel_id=1, source_target_pairs={{0,8},{4,12},{8,0},{12,4},{1,9},{5,13},{9,1},{13,5},{2,10},{6,14},... | collective-permute-start | bytes 786440 | tf_op jit(solution)/shard_map/ppermute | solution.py:292
  135.3 14.4 %collective-permute-start.30 = (bf16[128,1024]{1,0:T(8,128)(2,1)S(1)}, bf16[128,1024]{1,0:T(8,128)(2,1)S(1)}, u32[]{:S(2)}, u32[]{:S(2)}) collective-permute-start(bf16[128,1024]{1,0:T(8,128)(2,1)S(1)} %convert_add_fusion.1), channel_id=1, source_target_pairs={{0,3},{1,0},{2,1},{3,2},{4,7},{5,4},{6,5},{7,6},{8,11},{9,8},{10,9... | collective-permute-start | bytes 786440 | tf_op jit(solution)/shard_map/ppermute | solution.py:308
  138.3 11.4 %collective-permute-start.27 = (bf16[128,1024]{1,0:T(8,128)(2,1)S(1)}, bf16[128,1024]{1,0:T(8,128)(2,1)S(1)}, u32[]{:S(2)}, u32[]{:S(2)}) collective-permute-start(bf16[128,1024]{1,0:T(8,128)(2,1)S(1)} %slice.340), channel_id=1, source_target_pairs={{0,8},{4,12},{8,0},{12,4},{1,9},{5,13},{9,1},{13,5},{2,10},{6,14},... | collective-permute-start | bytes 786440 | tf_op jit(solution)/shard_map/ppermute | solution.py:292
  144.2 10.2 %collective-permute-start.29 = (bf16[128,1024]{1,0:T(8,128)(2,1)S(1)}, bf16[128,1024]{1,0:T(8,128)(2,1)S(1)}, u32[]{:S(2)}, u32[]{:S(2)}) collective-permute-start(bf16[128,1024]{1,0:T(8,128)(2,1)S(1)} %add_convert_fusion.1), channel_id=1, source_target_pairs={{0,1},{1,2},{2,3},{3,0},{4,5},{5,6},{6,7},{7,4},{8,9},{9,10},{10,1... | collective-permute-start | bytes 786440 | tf_op jit(solution)/shard_map/ppermute | solution.py:308
  (15 other events, 100.2 us)

commit v10 on v9

--- a/solution.py
+++ b/solution.py
@@ -176,25 +176,13 @@
     own_terms, other_terms, w_gate_up = lax.optimization_barrier(
         (own_terms, other_terms, w_gate_up)
     )
-    weights = [
-        w_gate_up[0, row * pair_cols : (row + 1) * pair_cols].reshape(pair_cols, 2 * ff_local)
-        for row in range(n_rows)
+    gate_up_weight = w_gate_up[0].reshape(model_width, 2 * ff_local)
+    gots = [
+        lax.ppermute(term(step).astype(bf16), "donor", rotation(n_donor, step)) for step in steps
     ]
-    early = n_rows // 2
-    carry = {1: [], -1: []}
-    for place, step in enumerate(steps[::-1]):
-        way = 1 if step <= n_donor // 2 else -1
-        part = term(step)
-        for got in carry[way]:
-            part = part + got.astype(f32)
-        got = lax.ppermute(part.astype(bf16), "donor", rotation(n_donor, way))
-        if place == 0:
-            got, weights[:early] = lax.optimization_barrier((got, weights[:early]))
-        if place == n_donor - 2:
-            got, weights[early:] = lax.optimization_barrier((got, weights[early:]))
-        carry[way] = [got]
+    gots, gate_up_weight = lax.optimization_barrier((gots, gate_up_weight))
     total = term(0) + hidden_part.astype(f32)
-    for got in carry[1] + carry[-1]:
+    for got in gots:
         total = total + got.astype(f32)
     chunk = total.astype(bf16)
 
@@ -248,7 +236,7 @@
             gate_up = sum(
                 jnp.dot(
                     jnp.concatenate([rows[row] for rows in own_rows + other_rows], axis=0),
-                    weights[row],
+                    gate_up_weight[row * pair_cols : (row + 1) * pair_cols],
                     preferred_element_type=f32,
                 )
                 for row in range(n_rows)

time: 156 us -> 156 us (level)
  local copies, waits for them, and re-layouts: 26.9 us -> 19.8 us
  waiting for transfers between devices: 70 us -> 73.9 us
  other arithmetic: 11 us -> 13.2 us
  matrix products: 16.3 us -> 17.9 us
    ppermute x4, waiting for transfers between devices: 2.78 us -> 17.8 us  [shards(): lax.ppermute(chunk, 'expert', turn(hop))]
    ppermute x3, waiting for transfers between devices: 23.2 us -> 9.45 us  [shards(): chunk = lax.ppermute(chunk, 'donor', rotation(n_donor, 1))]
    slice x1 -> x0, local copies, waits for them, and re-layouts: 11 us -> none  [shards(): w_gate_up[0, row * pair_cols:(row + 1) * pair_cols]]
    ppermute x3, waiting for transfers between devices: 5.18 us -> 9.01 us  [shards(): lax.ppermute(term(step).astype(bf16), 'donor', rotation(n_donor, step))]
    ppermute x4, waiting for transfers between devices: 6.84 us -> 10.2 us  [shards(): lax.ppermute(block[hop].astype(bf16), 'expert', turn(hop))]
    ppermute x3, waiting for transfers between devices: 14.3 us -> 11.4 us  [shards(): lax.ppermute(part_sum.astype(bf16), 'donor', rotation(n_donor, way))]
    concatenate x4, local copies, waits for them, and re-layouts: 0.32 us -> 2.77 us  [core_gates(): return jnp.concatenate(rows).reshape(n_donor, part_rows)]
    ppermute x4, starting transfers between devices: 0.91 us -> 3.13 us  [shards(): lax.ppermute(chunk, 'expert', turn(hop))]
  transfers between devices with their start and end apart: 32 -> 32, of which waited for: 18 -> 23; matrix products, arithmetic and copies ran while one was open for 28% -> 26% of each run, Pallas kernels for 0% -> 0%
where the time goes in v10:
time: 156 us; the launch traced here: 155 us
  waiting for transfers between devices  73.9 us (47%)
  starting transfers between devices  27.2 us (17%)
  local copies, waits for them, and re-layouts  19.8 us (13%)
  matrix products  17.9 us (11%)
  other arithmetic  13.2 us (8%)
  between operations  2.83 us (2%)
    ppermute x4, waiting for transfers between devices, shards(): lax.ppermute(chunk, 'expert', turn(hop))  17.8 us
    ppermute x3, waiting for transfers between devices, shards(): lax.ppermute(part_sum.astype(bf16), 'donor', rotation(n_donor, way))  11.4 us
    ppermute x4, waiting for transfers between devices, shards(): lax.ppermute(block[hop].astype(bf16), 'expert', turn(hop))  10.2 us
    unnamed x34, local copies, waits for them, and re-layouts  9.83 us
    ppermute x3, waiting for transfers between devices, shards(): chunk = lax.ppermute(chunk, 'donor', rotation(n_donor, 1))  9.45 us
    ppermute x3, waiting for transfers between devices, shards(): lax.ppermute(term(step).astype(bf16), 'donor', rotation(n_donor, step))  9.01 us
    dot_general x4, matrix products, shards(): jnp.dot(jnp.concatenate([rows[row] for rows in own_rows + other_rows], ax...  7.23 us
    ppermute x1, waiting for transfers between devices, shards(): got = lax.ppermute(head_out, 'expert', turn(step))  6.86 us
  transfers between devices with their start and end apart: 32, of which 23 were waited for; matrix products, arithmetic and copies ran while one was open for 26% of the time, Pallas kernels for 0%

profile of v10, /device:TPU:0, one launch (start us, length us, event | category | flops | bytes accessed | tf_op | source)
XLA Modules:
  0.0 155.0 jit_solution(3292055785074871852)
XLA Ops:
  2.8 2.4 %collective-permute-start.3 = (f32[8,128]{1,0:T(8,128)S(1)}, f32[8,128]{1,0:T(8,128)S(1)}, u32[]{:S(2)}, u32[]{:S(2)}) collective-permute-start(f32[8,128]{1,0:T(8,128)S(1)} %bitcast.207), channel_id=1, source_target_pairs={{0,12},{4,0},{8,4},{12,8},{1,13},{5,1},{9,5},{13,9},{2,14},{6,2},{... | collective-permute-start | bytes 12296 | tf_op jit(solution)/shard_map/ppermute | solution.py:140
  8.5 6.0 %all-to-all-start = ((bf16[16,32,256]{2,1,0:T(8,128)(2,1)}), bf16[16,32,256]{2,1,0:T(8,128)(2,1)S(1)}, u32[]{:S(2)}, u32[]{:S(2)}) async-start(bf16[16,32,256]{2,1,0:T(8,128)(2,1)} %broadcast_select_fusion), calls=%async_computation | async-start | bytes 524288 | tf_op jit(solution)/shard_map/all_to_all | solution.py:38
  18.5 1.8 %dynamic_slice.156 = bf16[64,2048]{1,0:T(8,128)(2,1)} dynamic-slice(bf16[128,4096]{1,0:T(8,128)(2,1)} %param.16, s32[]{:T(128)S(6)} %select_n.455, s32[]{:T(128)S(6)} %select_n.458), dynamic_slice_sizes={64,2048} | dynamic-slice | bytes 524292 | tf_op jit(solution)/shard_map/dynamic_slice | solution.py:149
  20.5 4.0 %all-to-all-done = bf16[16,32,256]{2,1,0:T(8,128)(2,1)S(1)} async-done(((bf16[16,32,256]{2,1,0:T(8,128)(2,1)}), bf16[16,32,256]{2,1,0:T(8,128)(2,1)S(1)}, u32[]{:S(2)}, u32[]{:S(2)}) %all-to-all-start) | async-done | bytes 262176 | tf_op jit(solution)/shard_map/all_to_all | solution.py:38
  26.9 1.8 %while.23 = (s32[]{:T(128)}, f32[128,8]{0,1:T(8,128)S(1)}, f32[128,8,128]{2,0,1:T(8,128)S(1)}, s32[]{:T(128)}, s32[]{:T(128)}, /*index=5*/bf16[128,8,128]{2,0,1:...) while((s32[]{:T(128)}, f32[128,8]{0,1:T(8,128)S(1)}, ...), condition=%wide.region_8.9_spmd, body=%wide.region_6.8_spmd.sunk | while | flops 271188992 | bytes 3691649 | solution.py:94
  30.0 1.5 collective-permute-start.5
  31.6 6.9 %collective-permute-done = bf16[128,1024]{1,0:T(8,128)(2,1)S(1)} collective-permute-done((bf16[128,1024]{1,0:T(8,128)(2,1)S(1)}, bf16[128,1024]{1,0:T(8,128)(2,1)S(1)}, u32[]{:S(2)}, u32[]{:S(2)}) %collective-permute-start) | collective-permute-done | bytes 262176 | tf_op jit(solution)/shard_map/ppermute | solution.py:161
  40.5 2.3 %fusion.106 = f32[256,1024]{1,0:T(8,128)S(1)} fusion(bf16[1024,1024]{1,0:T(8,128)(2,1)} %param.22, bf16[64,1024]{1,0:T(8,128)(2,1)S(1)} %get-tuple-element.281, bf16[64,1024]{1,0:T(8,128)(2,1)S(1)} %get-tuple-element.282, bf16[64,1024]{1,0:T(8,128)(2,1)S(1)} %get-tuple-element.283, bf16[64,1024]{1,0:T(8,128)(2,1)S(1)} %get-tuple-element.280), kind=kOutput, calls=%fused_computation.215 | convolution fusion | flops 538968064 | bytes 3670016 | tf_op jit(solution)/shard_map/dot_general | solution.py:166
  42.9 2.3 %fusion.105 = f32[256,1024]{1,0:T(8,128)S(1)} fusion(bf16[1024,1024]{1,0:T(8,128)(2,1)} %collective-permute-done.4, bf16[64,1024]{1,0:T(8,128)(2,1)S(1)} %get-tuple-element.281, bf16[64,1024]{1,0:T(8,128)(2,1)S(1)} %get-tuple-element.282, bf16[64,1024]{1,0:T(8,128)(2,1)S(1)} %get-tuple-element.283, bf16[64,1024]{1,0:T(8,128)(2,1)S(1)} %get-tuple-element.280), kind=kOutput, calls=%fused_computation.214 | convolution fusion | flops 538968064 | bytes 3670016 | tf_op jit(solution)/shard_map/dot_general | solution.py:167
  50.6 9.1 %copy.53 = bf16[512,8,2,768]{3,1,2,0:T(8,128)(2,1)S(1)} copy(bf16[512,8,2,768]{3,2,1,0:T(2,128)(2,1)} %bitcast.181) | data formatting | bytes 25165824
  59.9 8.8 %collective-permute-done.8 = bf16[64,2048]{1,0:T(8,128)(2,1)S(1)} collective-permute-done((bf16[64,2048]{1,0:T(8,128)(2,1)}, bf16[64,2048]{1,0:T(8,128)(2,1)S(1)}, u32[]{:S(2)}, u32[]{:S(2)}) %collective-permute-start.8) | collective-permute-done | bytes 262176 | tf_op jit(solution)/shard_map/ppermute | solution.py:181
  71.7 4.8 %collective-permute-done.10 = bf16[64,2048]{1,0:T(8,128)(2,1)S(1)} collective-permute-done((bf16[64,2048]{1,0:T(8,128)(2,1)S(1)}, bf16[64,2048]{1,0:T(8,128)(2,1)S(1)}, u32[]{:S(2)}, u32[]{:S(2)}) %collective-permute-start.10) | collective-permute-done | bytes 262176 | tf_op jit(solution)/shard_map/ppermute | solution.py:204
  76.4 4.1 %collective-permute-done.9 = bf16[64,2048]{1,0:T(8,128)(2,1)S(1)} collective-permute-done((bf16[64,2048]{1,0:T(8,128)(2,1)S(1)}, bf16[64,2048]{1,0:T(8,128)(2,1)S(1)}, u32[]{:S(2)}, u32[]{:S(2)}) %collective-permute-start.9) | collective-permute-done | bytes 262176 | tf_op jit(solution)/shard_map/ppermute | solution.py:207
  81.2 6.5 %collective-permute-done.12 = bf16[64,2048]{1,0:T(8,128)(2,1)S(1)} collective-permute-done((bf16[64,2048]{1,0:T(8,128)(2,1)S(1)}, bf16[64,2048]{1,0:T(8,128)(2,1)S(1)}, u32[]{:S(2)}, u32[]{:S(2)}) %collective-permute-start.12) | collective-permute-done | bytes 262176 | tf_op jit(solution)/shard_map/ppermute | solution.py:204
  87.7 1.8 %collective-permute-done.11 = bf16[64,2048]{1,0:T(8,128)(2,1)S(1)} collective-permute-done((bf16[64,2048]{1,0:T(8,128)(2,1)S(1)}, bf16[64,2048]{1,0:T(8,128)(2,1)S(1)}, u32[]{:S(2)}, u32[]{:S(2)}) %collective-permute-start.11) | collective-permute-done | bytes 262176 | tf_op jit(solution)/shard_map/ppermute | solution.py:207
  89.5 1.7 %collective-permute-start.14 = (bf16[64,2048]{1,0:T(8,128)(2,1)S(1)}, bf16[64,2048]{1,0:T(8,128)(2,1)S(1)}, u32[]{:S(2)}, u32[]{:S(2)}) collective-permute-start(bf16[64,2048]{1,0:T(8,128)(2,1)S(1)} %collective-permute-done.11), channel_id=1, source_target_pairs={{0,8},{4,12},{8,0},{12,4},{1,9},{5,13},{9,1},{13,5},{2,10},{6,14},... | collective-permute-start | bytes 786440 | tf_op jit(solution)/shard_map/ppermute | solution.py:204
  91.5 4.4 %collective-permute-done.14 = bf16[64,2048]{1,0:T(8,128)(2,1)S(1)} collective-permute-done((bf16[64,2048]{1,0:T(8,128)(2,1)S(1)}, bf16[64,2048]{1,0:T(8,128)(2,1)S(1)}, u32[]{:S(2)}, u32[]{:S(2)}) %collective-permute-start.14) | collective-permute-done | bytes 262176 | tf_op jit(solution)/shard_map/ppermute | solution.py:204
  95.9 3.5 %collective-permute-done.13 = bf16[64,2048]{1,0:T(8,128)(2,1)S(1)} collective-permute-done((bf16[64,2048]{1,0:T(8,128)(2,1)S(1)}, bf16[64,2048]{1,0:T(8,128)(2,1)S(1)}, u32[]{:S(2)}, u32[]{:S(2)}) %collective-permute-start.13) | collective-permute-done | bytes 262176 | tf_op jit(solution)/shard_map/ppermute | solution.py:207
  103.0 1.8 %fusion.6 = f32[256,1536]{1,0:T(8,128)S(1)} fusion(bf16[4096,1536]{1,0:T(8,128)(2,1)S(1)} %bitcast.182, bf16[64,2048]{1,0:T(8,128)(2,1)S(1)} %get-tuple-element.275, bf16[64,2048]{1,0:T(8,128)(2,1)S(1)} %get-tuple-element.273, bf16[64,2048]{1,0:T(8,128)(2,1)S(1)} %get-tuple-element.298, bf16[64,2048]{1,0:T(8,128)(2,1)S(1)} %get-tuple-element.299), kind=kOutput, calls=%fused_computation.13 | convolution fusion | flops 1614807040 | bytes 8912896 | tf_op jit(solution)/shard_map/dot_general | solution.py:237
  104.8 1.8 %fusion.12 = f32[256,1536]{1,0:T(8,128)S(1)} fusion(f32[256,1536]{1,0:T(8,128)S(1)} %fusion.6, bf16[4096,1536]{1,0:T(8,128)(2,1)S(1)} %bitcast.183, bf16[64,2048]{1,0:T(8,128)(2,1)S(1)} %get-tuple-element.274, bf16[64,2048]{1,0:T(8,128)(2,1)S(1)} %get-tuple-element.272, bf16[64,2048]{1,0:T(8,128)(2,1)S(1)} %get-tuple-element.311, ...), kind=kOutput, calls=%fused_computation.19 | convolution fusion | flops 1615200256 | bytes 10485760 | tf_op jit(solution)/shard_map/dot_general | solution.py:237
  106.9 2.2 %collective-permute-done.15 = bf16[64,2048]{1,0:T(8,128)(2,1)S(1)} collective-permute-done((bf16[64,2048]{1,0:T(8,128)(2,1)S(1)}, bf16[64,2048]{1,0:T(8,128)(2,1)S(1)}, u32[]{:S(2)}, u32[]{:S(2)}) %collective-permute-start.15) | collective-permute-done | bytes 262176 | tf_op jit(solution)/shard_map/ppermute | solution.py:204
  109.8 1.8 %collective-permute-done.19 = bf16[2,64,2048]{2,1,0:T(8,128)(2,1)S(1)} collective-permute-done((bf16[2,64,2048]{2,1,0:T(8,128)(2,1)S(1)}, bf16[2,64,2048]{2,1,0:T(8,128)(2,1)S(1)}, u32[]{:S(2)}, u32[]{:S(2)}) %collective-permute-start.19) | collective-permute-done | bytes 524320 | tf_op jit(solution)/shard_map/ppermute | solution.py:231
  111.7 1.8 %fusion.4 = f32[256,1536]{1,0:T(8,128)S(1)} fusion(bf16[4096,1536]{1,0:T(8,128)(2,1)S(1)} %bitcast.184, bf16[64,2048]{1,0:T(8,128)(2,1)S(1)} %get-tuple-element.267, bf16[64,2048]{1,0:T(8,128)(2,1)S(1)} %get-tuple-element.265, bf16[64,2048]{1,0:T(8,128)(2,1)S(1)} %get-tuple-element.314, bf16[64,2048]{1,0:T(8,128)(2,1)S(1)} %get-tuple-element.297), kind=kOutput, calls=%fused_computation.11 | convolution fusion | flops 1614807040 | bytes 8912896 | tf_op jit(solution)/shard_map/dot_general | solution.py:237
  113.5 1.8 %fusion.15 = f32[256,1536]{1,0:T(8,128)S(1)} fusion(f32[256,1536]{1,0:T(8,128)S(1)} %fusion.4, bf16[4096,1536]{1,0:T(8,128)(2,1)S(1)} %bitcast.185, bf16[64,2048]{1,0:T(8,128)(2,1)S(1)} %get-tuple-element.266, bf16[64,2048]{1,0:T(8,128)(2,1)S(1)} %get-tuple-element.264, bf16[64,2048]{1,0:T(8,128)(2,1)S(1)} %get-tuple-element.313, ...), kind=kOutput, calls=%fused_computation.20 | convolution fusion | flops 1615200256 | bytes 10485760 | tf_op jit(solution)/shard_map/dot_general | solution.py:237
  121.2 1.8 %collective-permute-start.25 = (bf16[128,1024]{1,0:T(8,128)(2,1)S(1)}, bf16[128,1024]{1,0:T(8,128)(2,1)S(1)}, u32[]{:S(2)}, u32[]{:S(2)}) collective-permute-start(bf16[128,1024]{1,0:T(8,128)(2,1)S(1)} %slice.356), channel_id=1, source_target_pairs={{0,8},{4,12},{8,0},{12,4},{1,9},{5,13},{9,1},{13,5},{2,10},{6,14},... | collective-permute-start | bytes 786440 | tf_op jit(solution)/shard_map/ppermute | solution.py:280
  123.0 6.8 %collective-permute-done.21 = bf16[128,1024]{1,0:T(8,128)(2,1)S(1)} collective-permute-done((bf16[128,1024]{1,0:T(8,128)(2,1)S(1)}, bf16[128,1024]{1,0:T(8,128)(2,1)S(1)}, u32[]{:S(2)}, u32[]{:S(2)}) %collective-permute-start.21) | collective-permute-done | bytes 262176 | tf_op jit(solution)/shard_map/ppermute | solution.py:280
  134.9 3.0 %collective-permute-start.30 = (bf16[128,1024]{1,0:T(8,128)(2,1)S(1)}, bf16[128,1024]{1,0:T(8,128)(2,1)S(1)}, u32[]{:S(2)}, u32[]{:S(2)}) collective-permute-start(bf16[128,1024]{1,0:T(8,128)(2,1)S(1)} %convert_add_fusion.1), channel_id=1, source_target_pairs={{0,3},{1,0},{2,1},{3,2},{4,7},{5,4},{6,5},{7,6},{8,11},{9,8},{10,9... | collective-permute-start | bytes 786440 | tf_op jit(solution)/shard_map/ppermute | solution.py:296
  137.9 1.4 collective-permute-start.27
  139.3 4.5 %collective-permute-done.28 = bf16[128,1024]{1,0:T(8,128)(2,1)S(1)} collective-permute-done((bf16[128,1024]{1,0:T(8,128)(2,1)S(1)}, bf16[128,1024]{1,0:T(8,128)(2,1)S(1)}, u32[]{:S(2)}, u32[]{:S(2)}) %collective-permute-start.28) | collective-permute-done | bytes 262176 | tf_op jit(solution)/shard_map/ppermute | solution.py:296
  144.2 2.9 %collective-permute-done.27 = bf16[128,1024]{1,0:T(8,128)(2,1)S(1)} collective-permute-done((bf16[128,1024]{1,0:T(8,128)(2,1)S(1)}, bf16[128,1024]{1,0:T(8,128)(2,1)S(1)}, u32[]{:S(2)}, u32[]{:S(2)}) %collective-permute-start.27) | collective-permute-done | bytes 262176 | tf_op jit(solution)/shard_map/ppermute | solution.py:280
  147.1 2.3 %collective-permute-done.30 = bf16[128,1024]{1,0:T(8,128)(2,1)S(1)} collective-permute-done((bf16[128,1024]{1,0:T(8,128)(2,1)S(1)}, bf16[128,1024]{1,0:T(8,128)(2,1)S(1)}, u32[]{:S(2)}, u32[]{:S(2)}) %collective-permute-start.30) | collective-permute-done | bytes 262176 | tf_op jit(solution)/shard_map/ppermute | solution.py:296
  149.4 4.7 %collective-permute-done.29 = bf16[128,1024]{1,0:T(8,128)(2,1)S(1)} collective-permute-done((bf16[128,1024]{1,0:T(8,128)(2,1)S(1)}, bf16[128,1024]{1,0:T(8,128)(2,1)S(1)}, u32[]{:S(2)}, u32[]{:S(2)}) %collective-permute-start.29) | collective-permute-done | bytes 262176 | tf_op jit(solution)/shard_map/ppermute | solution.py:296
  (199 shorter events, 42.8 us)
Async XLA Ops:
  2.8 27.2 %collective-permute-start.3 = (f32[8,128]{1,0:T(8,128)S(1)}, f32[8,128]{1,0:T(8,128)S(1)}, u32[]{:S(2)}, u32[]{:S(2)}) collective-permute-start(f32[8,128]{1,0:T(8,128)S(1)} %bitcast.207), channel_id=1, source_target_pairs={{0,12},{4,0},{8,4},{12,8},{1,13},{5,1},{9,5},{13,9},{2,14},{6,2},{... | collective-permute-start | bytes 12296 | tf_op jit(solution)/shard_map/ppermute | solution.py:140
  5.2 26.4 %collective-permute-start.2 = (f32[8,128]{1,0:T(8,128)S(1)}, f32[8,128]{1,0:T(8,128)S(1)}, u32[]{:S(2)}, u32[]{:S(2)}) collective-permute-start(f32[8,128]{1,0:T(8,128)S(1)} %bitcast.208), channel_id=1, source_target_pairs={{0,8},{4,12},{8,0},{12,4},{1,9},{5,13},{9,1},{13,5},{2,10},{6,14},... | collective-permute-start | bytes 12296 | tf_op jit(solution)/shard_map/ppermute | solution.py:140
  5.8 25.7 %collective-permute-start.1 = (f32[8,128]{1,0:T(8,128)S(1)}, f32[8,128]{1,0:T(8,128)S(1)}, u32[]{:S(2)}, u32[]{:S(2)}) collective-permute-start(f32[8,128]{1,0:T(8,128)S(1)} %bitcast.209), channel_id=1, source_target_pairs={{0,4},{4,8},{8,12},{12,0},{1,5},{5,9},{9,13},{13,1},{2,6},{6,10},{... | collective-permute-start | bytes 12296 | tf_op jit(solution)/shard_map/ppermute | solution.py:140
  8.5 16.1 %all-to-all-start = ((bf16[16,32,256]{2,1,0:T(8,128)(2,1)}), bf16[16,32,256]{2,1,0:T(8,128)(2,1)S(1)}, u32[]{:S(2)}, u32[]{:S(2)}) async-start(bf16[16,32,256]{2,1,0:T(8,128)(2,1)} %broadcast_select_fusion), calls=%async_computation | async-start | bytes 524288 | tf_op jit(solution)/shard_map/all_to_all | solution.py:38
  14.5 28.3 %collective-permute-start.4 = (bf16[1024,1024]{1,0:T(8,128)(2,1)}, bf16[1024,1024]{1,0:T(8,128)(2,1)}, u32[]{:S(2)}, u32[]{:S(2)}) collective-permute-start(bf16[1024,1024]{1,0:T(8,128)(2,1)} %param.22), channel_id=1, source_target_pairs={{0,4},{4,0},{8,12},{12,8},{1,5},{5,1},{9,13},{13,9},{2,6},{6,2},{1... | collective-permute-start | bytes 6291464 | tf_op jit(solution)/shard_map/ppermute | solution.py:143
  29.2 9.3 %collective-permute-start = (bf16[128,1024]{1,0:T(8,128)(2,1)S(1)}, bf16[128,1024]{1,0:T(8,128)(2,1)S(1)}, u32[]{:S(2)}, u32[]{:S(2)}) collective-permute-start(bf16[128,1024]{1,0:T(8,128)(2,1)S(1)} %copy.48), channel_id=1, source_target_pairs={{0,8},{4,12},{8,0},{12,4},{1,9},{5,13},{9,1},{13,5},{2,10},{6,14},... | collective-permute-start | bytes 786440 | tf_op jit(solution)/shard_map/ppermute | solution.py:161
  30.0 38.7 %collective-permute-start.5 = (bf16[64,2048]{1,0:T(8,128)(2,1)}, bf16[64,2048]{1,0:T(8,128)(2,1)S(1)}, u32[]{:S(2)}, u32[]{:S(2)}) collective-permute-start(bf16[64,2048]{1,0:T(8,128)(2,1)} %dynamic_slice.156), channel_id=1, source_target_pairs={{0,8},{4,12},{8,0},{12,4},{1,9},{5,13},{9,1},{13,5},{2,10},{6,14},... | collective-permute-start | bytes 786440 | tf_op jit(solution)/shard_map/ppermute | solution.py:153
  45.3 14.5 %collective-permute-start.7 = (bf16[64,2048]{1,0:T(8,128)(2,1)S(1)}, bf16[64,2048]{1,0:T(8,128)(2,1)S(1)}, u32[]{:S(2)}, u32[]{:S(2)}) collective-permute-start(bf16[64,2048]{1,0:T(8,128)(2,1)S(1)} %pad_maximum_fusion.9), channel_id=1, source_target_pairs={{0,3},{1,0},{2,1},{3,2},{4,7},{5,4},{6,5},{7,6},{8,11},{9,8},{10,9... | collective-permute-start | bytes 786440 | tf_op jit(solution)/shard_map/ppermute | solution.py:181
  46.9 13.0 %collective-permute-start.6 = (bf16[64,2048]{1,0:T(8,128)(2,1)}, bf16[64,2048]{1,0:T(8,128)(2,1)S(1)}, u32[]{:S(2)}, u32[]{:S(2)}) collective-permute-start(bf16[64,2048]{1,0:T(8,128)(2,1)} %pad_maximum_fusion.8), channel_id=1, source_target_pairs={{0,1},{1,2},{2,3},{3,0},{4,5},{5,6},{6,7},{7,4},{8,9},{9,10},{10,1... | collective-permute-start | bytes 786440 | tf_op jit(solution)/shard_map/ppermute | solution.py:181
  48.8 19.9 %collective-permute-start.8 = (bf16[64,2048]{1,0:T(8,128)(2,1)}, bf16[64,2048]{1,0:T(8,128)(2,1)S(1)}, u32[]{:S(2)}, u32[]{:S(2)}) collective-permute-start(bf16[64,2048]{1,0:T(8,128)(2,1)} %pad_maximum_fusion.10), channel_id=1, source_target_pairs={{0,2},{1,3},{2,0},{3,1},{4,6},{5,7},{6,4},{7,5},{8,10},{9,11},{10,... | collective-permute-start | bytes 786440 | tf_op jit(solution)/shard_map/ppermute | solution.py:181
  70.0 6.4 %collective-permute-start.10 = (bf16[64,2048]{1,0:T(8,128)(2,1)S(1)}, bf16[64,2048]{1,0:T(8,128)(2,1)S(1)}, u32[]{:S(2)}, u32[]{:S(2)}) collective-permute-start(bf16[64,2048]{1,0:T(8,128)(2,1)S(1)} %fusion.91), channel_id=1, source_target_pairs={{0,8},{4,12},{8,0},{12,4},{1,9},{5,13},{9,1},{13,5},{2,10},{6,14},... | collective-permute-start | bytes 786440 | tf_op jit(solution)/shard_map/ppermute | solution.py:204
  70.8 9.8 %collective-permute-start.9 = (bf16[64,2048]{1,0:T(8,128)(2,1)S(1)}, bf16[64,2048]{1,0:T(8,128)(2,1)S(1)}, u32[]{:S(2)}, u32[]{:S(2)}) collective-permute-start(bf16[64,2048]{1,0:T(8,128)(2,1)S(1)} %fusion.91), channel_id=1, source_target_pairs={{0,1},{1,2},{2,3},{3,0},{4,5},{5,6},{6,7},{7,4},{8,9},{9,10},{10,1... | collective-permute-start | bytes 786440 | tf_op jit(solution)/shard_map/ppermute | solution.py:207
  80.6 7.1 %collective-permute-start.12 = (bf16[64,2048]{1,0:T(8,128)(2,1)S(1)}, bf16[64,2048]{1,0:T(8,128)(2,1)S(1)}, u32[]{:S(2)}, u32[]{:S(2)}) collective-permute-start(bf16[64,2048]{1,0:T(8,128)(2,1)S(1)} %collective-permute-done.9), channel_id=1, source_target_pairs={{0,8},{4,12},{8,0},{12,4},{1,9},{5,13},{9,1},{13,5},{2,10},{6,14},... | collective-permute-start | bytes 786440 | tf_op jit(solution)/shard_map/ppermute | solution.py:204
  80.9 8.6 %collective-permute-start.11 = (bf16[64,2048]{1,0:T(8,128)(2,1)S(1)}, bf16[64,2048]{1,0:T(8,128)(2,1)S(1)}, u32[]{:S(2)}, u32[]{:S(2)}) collective-permute-start(bf16[64,2048]{1,0:T(8,128)(2,1)S(1)} %collective-permute-done.9), channel_id=1, source_target_pairs={{0,1},{1,2},{2,3},{3,0},{4,5},{5,6},{6,7},{7,4},{8,9},{9,10},{10,1... | collective-permute-start | bytes 786440 | tf_op jit(solution)/shard_map/ppermute | solution.py:207
  89.5 6.4 %collective-permute-start.14 = (bf16[64,2048]{1,0:T(8,128)(2,1)S(1)}, bf16[64,2048]{1,0:T(8,128)(2,1)S(1)}, u32[]{:S(2)}, u32[]{:S(2)}) collective-permute-start(bf16[64,2048]{1,0:T(8,128)(2,1)S(1)} %collective-permute-done.11), channel_id=1, source_target_pairs={{0,8},{4,12},{8,0},{12,4},{1,9},{5,13},{9,1},{13,5},{2,10},{6,14},... | collective-permute-start | bytes 786440 | tf_op jit(solution)/shard_map/ppermute | solution.py:204
  91.2 8.2 %collective-permute-start.13 = (bf16[64,2048]{1,0:T(8,128)(2,1)S(1)}, bf16[64,2048]{1,0:T(8,128)(2,1)S(1)}, u32[]{:S(2)}, u32[]{:S(2)}) collective-permute-start(bf16[64,2048]{1,0:T(8,128)(2,1)S(1)} %collective-permute-done.11), channel_id=1, source_target_pairs={{0,1},{1,2},{2,3},{3,0},{4,5},{5,6},{6,7},{7,4},{8,9},{9,10},{10,1... | collective-permute-start | bytes 786440 | tf_op jit(solution)/shard_map/ppermute | solution.py:207
  100.2 2.0 %collective-permute-start.16 = (bf16[2,64,2048]{2,1,0:T(8,128)(2,1)S(1)}, bf16[2,64,2048]{2,1,0:T(8,128)(2,1)S(1)}, u32[]{:S(2)}, u32[]{:S(2)}) collective-permute-start(bf16[2,64,2048]{2,1,0:T(8,128)(2,1)S(1)} %pad_maximum_fusion.1), channel_id=1, source_target_pairs={{0,4},{4,0},{8,12},{12,8},{1,5},{5,1},{9,13},{13,9},{2,6},{6,2},{1... | collective-permute-start | bytes 1572872 | tf_op jit(solution)/shard_map/ppermute | solution.py:231
  100.4 8.7 %collective-permute-start.15 = (bf16[64,2048]{1,0:T(8,128)(2,1)S(1)}, bf16[64,2048]{1,0:T(8,128)(2,1)S(1)}, u32[]{:S(2)}, u32[]{:S(2)}) collective-permute-start(bf16[64,2048]{1,0:T(8,128)(2,1)S(1)} %collective-permute-done.13), channel_id=1, source_target_pairs={{0,8},{4,12},{8,0},{12,4},{1,9},{5,13},{9,1},{13,5},{2,10},{6,14},... | collective-permute-start | bytes 786440 | tf_op jit(solution)/shard_map/ppermute | solution.py:204
  100.7 2.2 %collective-permute-start.17 = (bf16[2,64,2048]{2,1,0:T(8,128)(2,1)S(1)}, bf16[2,64,2048]{2,1,0:T(8,128)(2,1)S(1)}, u32[]{:S(2)}, u32[]{:S(2)}) collective-permute-start(bf16[2,64,2048]{2,1,0:T(8,128)(2,1)S(1)} %pad_maximum_fusion.2), channel_id=1, source_target_pairs={{0,4},{4,0},{8,12},{12,8},{1,5},{5,1},{9,13},{13,9},{2,6},{6,2},{1... | collective-permute-start | bytes 1572872 | tf_op jit(solution)/shard_map/ppermute | solution.py:231
  101.1 8.7 %collective-permute-start.18 = (bf16[2,64,2048]{2,1,0:T(8,128)(2,1)S(1)}, bf16[2,64,2048]{2,1,0:T(8,128)(2,1)S(1)}, u32[]{:S(2)}, u32[]{:S(2)}) collective-permute-start(bf16[2,64,2048]{2,1,0:T(8,128)(2,1)S(1)} %pad_maximum_fusion.4), channel_id=1, source_target_pairs={{0,4},{4,0},{8,12},{12,8},{1,5},{5,1},{9,13},{13,9},{2,6},{6,2},{1... | collective-permute-start | bytes 1572872 | tf_op jit(solution)/shard_map/ppermute | solution.py:231
  109.6 2.0 %collective-permute-start.19 = (bf16[2,64,2048]{2,1,0:T(8,128)(2,1)S(1)}, bf16[2,64,2048]{2,1,0:T(8,128)(2,1)S(1)}, u32[]{:S(2)}, u32[]{:S(2)}) collective-permute-start(bf16[2,64,2048]{2,1,0:T(8,128)(2,1)S(1)} %pad_maximum_fusion.5), channel_id=1, source_target_pairs={{0,4},{4,0},{8,12},{12,8},{1,5},{5,1},{9,13},{13,9},{2,6},{6,2},{1... | collective-permute-start | bytes 1572872 | tf_op jit(solution)/shard_map/ppermute | solution.py:231
  117.4 2.0 %collective-permute-start.20 = (bf16[256,1024]{1,0:T(8,128)(2,1)S(1)}, bf16[256,1024]{1,0:T(8,128)(2,1)S(1)}, u32[]{:S(2)}, u32[]{:S(2)}) collective-permute-start(bf16[256,1024]{1,0:T(8,128)(2,1)S(1)} %slice.353), channel_id=1, source_target_pairs={{0,4},{4,0},{8,12},{12,8},{1,5},{5,1},{9,13},{13,9},{2,6},{6,2},{1... | collective-permute-start | bytes 1572872 | tf_op jit(solution)/shard_map/ppermute | solution.py:275
  118.7 2.0 %collective-permute-start.24 = (bf16[256,1024]{1,0:T(8,128)(2,1)S(1)}, bf16[256,1024]{1,0:T(8,128)(2,1)S(1)}, u32[]{:S(2)}, u32[]{:S(2)}) collective-permute-start(bf16[256,1024]{1,0:T(8,128)(2,1)S(1)} %slice.350), channel_id=1, source_target_pairs={{0,4},{4,0},{8,12},{12,8},{1,5},{5,1},{9,13},{13,9},{2,6},{6,2},{1... | collective-permute-start | bytes 1572872 | tf_op jit(solution)/shard_map/ppermute | solution.py:275
  120.7 9.1 %collective-permute-start.21 = (bf16[128,1024]{1,0:T(8,128)(2,1)S(1)}, bf16[128,1024]{1,0:T(8,128)(2,1)S(1)}, u32[]{:S(2)}, u32[]{:S(2)}) collective-permute-start(bf16[128,1024]{1,0:T(8,128)(2,1)S(1)} %slice.357), channel_id=1, source_target_pairs={{0,8},{4,12},{8,0},{12,4},{1,9},{5,13},{9,1},{13,5},{2,10},{6,14},... | collective-permute-start | bytes 786440 | tf_op jit(solution)/shard_map/ppermute | solution.py:280
  121.2 13.7 %collective-permute-start.25 = (bf16[128,1024]{1,0:T(8,128)(2,1)S(1)}, bf16[128,1024]{1,0:T(8,128)(2,1)S(1)}, u32[]{:S(2)}, u32[]{:S(2)}) collective-permute-start(bf16[128,1024]{1,0:T(8,128)(2,1)S(1)} %slice.356), channel_id=1, source_target_pairs={{0,8},{4,12},{8,0},{12,4},{1,9},{5,13},{9,1},{13,5},{2,10},{6,14},... | collective-permute-start | bytes 786440 | tf_op jit(solution)/shard_map/ppermute | solution.py:280
  130.9 2.0 %collective-permute-start.23 = (bf16[256,1024]{1,0:T(8,128)(2,1)S(1)}, bf16[256,1024]{1,0:T(8,128)(2,1)S(1)}, u32[]{:S(2)}, u32[]{:S(2)}) collective-permute-start(bf16[256,1024]{1,0:T(8,128)(2,1)S(1)} %slice.351), channel_id=1, source_target_pairs={{0,4},{4,0},{8,12},{12,8},{1,5},{5,1},{9,13},{13,9},{2,6},{6,2},{1... | collective-permute-start | bytes 1572872 | tf_op jit(solution)/shard_map/ppermute | solution.py:275
  132.0 2.1 %collective-permute-start.22 = (bf16[256,1024]{1,0:T(8,128)(2,1)S(1)}, bf16[256,1024]{1,0:T(8,128)(2,1)S(1)}, u32[]{:S(2)}, u32[]{:S(2)}) collective-permute-start(bf16[256,1024]{1,0:T(8,128)(2,1)S(1)} %slice.352), channel_id=1, source_target_pairs={{0,4},{4,0},{8,12},{12,8},{1,5},{5,1},{9,13},{13,9},{2,6},{6,2},{1... | collective-permute-start | bytes 1572872 | tf_op jit(solution)/shard_map/ppermute | solution.py:275
  132.6 11.1 %collective-permute-start.28 = (bf16[128,1024]{1,0:T(8,128)(2,1)S(1)}, bf16[128,1024]{1,0:T(8,128)(2,1)S(1)}, u32[]{:S(2)}, u32[]{:S(2)}) collective-permute-start(bf16[128,1024]{1,0:T(8,128)(2,1)S(1)} %convert_add_fusion.2), channel_id=1, source_target_pairs={{0,1},{1,2},{2,3},{3,0},{4,5},{5,6},{6,7},{7,4},{8,9},{9,10},{10,1... | collective-permute-start | bytes 786440 | tf_op jit(solution)/shard_map/ppermute | solution.py:296
  133.1 10.7 %collective-permute-start.26 = (bf16[128,1024]{1,0:T(8,128)(2,1)S(1)}, bf16[128,1024]{1,0:T(8,128)(2,1)S(1)}, u32[]{:S(2)}, u32[]{:S(2)}) collective-permute-start(bf16[128,1024]{1,0:T(8,128)(2,1)S(1)} %slice.355), channel_id=1, source_target_pairs={{0,8},{4,12},{8,0},{12,4},{1,9},{5,13},{9,1},{13,5},{2,10},{6,14},... | collective-permute-start | bytes 786440 | tf_op jit(solution)/shard_map/ppermute | solution.py:280
  134.9 14.5 %collective-permute-start.30 = (bf16[128,1024]{1,0:T(8,128)(2,1)S(1)}, bf16[128,1024]{1,0:T(8,128)(2,1)S(1)}, u32[]{:S(2)}, u32[]{:S(2)}) collective-permute-start(bf16[128,1024]{1,0:T(8,128)(2,1)S(1)} %convert_add_fusion.1), channel_id=1, source_target_pairs={{0,3},{1,0},{2,1},{3,2},{4,7},{5,4},{6,5},{7,6},{8,11},{9,8},{10,9... | collective-permute-start | bytes 786440 | tf_op jit(solution)/shard_map/ppermute | solution.py:296
  137.9 9.2 %collective-permute-start.27 = (bf16[128,1024]{1,0:T(8,128)(2,1)S(1)}, bf16[128,1024]{1,0:T(8,128)(2,1)S(1)}, u32[]{:S(2)}, u32[]{:S(2)}) collective-permute-start(bf16[128,1024]{1,0:T(8,128)(2,1)S(1)} %slice.354), channel_id=1, source_target_pairs={{0,8},{4,12},{8,0},{12,4},{1,9},{5,13},{9,1},{13,5},{2,10},{6,14},... | collective-permute-start | bytes 786440 | tf_op jit(solution)/shard_map/ppermute | solution.py:280
  143.9 10.2 %collective-permute-start.29 = (bf16[128,1024]{1,0:T(8,128)(2,1)S(1)}, bf16[128,1024]{1,0:T(8,128)(2,1)S(1)}, u32[]{:S(2)}, u32[]{:S(2)}) collective-permute-start(bf16[128,1024]{1,0:T(8,128)(2,1)S(1)} %add_convert_fusion.1), channel_id=1, source_target_pairs={{0,1},{1,2},{2,3},{3,0},{4,5},{5,6},{6,7},{7,4},{8,9},{9,10},{10,1... | collective-permute-start | bytes 786440 | tf_op jit(solution)/shard_map/ppermute | solution.py:296
  (14 other events, 93.3 us)

commit v11 on v10

--- a/solution.py
+++ b/solution.py
@@ -136,9 +136,6 @@
     gates = route_probs / jnp.sum(route_probs, axis=1, keepdims=True)
     hits = expert_ids[:, :, None] == jnp.arange(experts_all, dtype=jnp.int32)
     gate_table = jnp.sum(jnp.where(hits, gates[:, :, None], 0.0), axis=1).T
-    tables = [gate_table] + [
-        lax.ppermute(gate_table, "expert", rotation(n_expert, step)) for step in range(1, n_expert)
-    ]
 
     other_weight = lax.ppermute(out_weight, "expert", swap)
 
@@ -154,6 +151,10 @@
         hidden_part = jnp.where((y - step) % n_rows == part_owner, got, hidden_part)
 
     head_out = attention(queries, suffix_kv, kv_pool, page_table, prefix_len)
+    gate_table = after(gate_table, head_out)
+    tables = [gate_table] + [
+        lax.ppermute(gate_table, "expert", rotation(n_expert, step)) for step in range(1, n_expert)
+    ]
 
     heads = jnp.zeros((n_rows, suffix_len, head_out.shape[1]), bf16)
     heads = lax.dynamic_update_index_in_dim(heads, head_out, y, 0)

time: 156 us -> 153 us (0.981)
  other arithmetic: 13.2 us -> 11.2 us
    ppermute x1, waiting for transfers between devices: 6.86 us -> 0.01 us  [shards(): got = lax.ppermute(head_out, 'expert', turn(step))]
    ppermute x3, waiting for transfers between devices: 0.01 us -> 2.8 us  [shards(): lax.ppermute(gate_table, 'expert', rotation(n_expert, step))]
    all_to_all x1, waiting for transfers between devices: 4.01 us -> 5.8 us  [attention(): lax.all_to_all(outgoing, ('expert', 'donor'), split_axis=0, concat_axis=0...]
    ppermute x3, waiting for transfers between devices: 9.01 us -> 10.7 us  [shards(): lax.ppermute(term(step).astype(bf16), 'donor', rotation(n_donor, step))]
    unnamed x34 -> x36, local copies, waits for them, and re-layouts: 9.83 us -> 9.84 us
  transfers between devices with their start and end apart: 32 -> 32, of which waited for: 23 -> 24; matrix products, arithmetic and copies ran while one was open for 26% -> 25% of each run, Pallas kernels for 0% -> 0%
where the time goes in v11:
time: 153 us
  waiting for transfers between devices  72.9 us (48%)
  starting transfers between devices  27.8 us (18%)
  local copies, waits for them, and re-layouts  20.5 us (13%)
  matrix products  17.9 us (12%)
  other arithmetic  11.2 us (7%)
  between operations  2.26 us (1%)
    ppermute x4, waiting for transfers between devices, shards(): lax.ppermute(chunk, 'expert', turn(hop))  19 us
    ppermute x3, waiting for transfers between devices, shards(): lax.ppermute(part_sum.astype(bf16), 'donor', rotation(n_donor, way))  11.4 us
    ppermute x3, waiting for transfers between devices, shards(): lax.ppermute(term(step).astype(bf16), 'donor', rotation(n_donor, step))  10.7 us
    ppermute x4, waiting for transfers between devices, shards(): lax.ppermute(block[hop].astype(bf16), 'expert', turn(hop))  10.2 us
    unnamed x36, local copies, waits for them, and re-layouts  9.84 us
    ppermute x3, waiting for transfers between devices, shards(): chunk = lax.ppermute(chunk, 'donor', rotation(n_donor, 1))  8.4 us
    all_to_all x1, starting transfers between devices, attention(): lax.all_to_all(outgoing, ('expert', 'donor'), split_axis=0, concat_axis=0...  7.39 us
    dot_general x4, matrix products, shards(): jnp.dot(jnp.concatenate([rows[row] for rows in own_rows + other_rows], ax...  7.23 us
  transfers between devices with their start and end apart: 32, of which 24 were waited for; matrix products, arithmetic and copies ran while one was open for 25% of the time, Pallas kernels for 0%

profile of v11, /device:TPU:0, one launch (start us, length us, event | category | flops | bytes accessed | tf_op | source)
XLA Modules:
  0.0 152.6 jit_solution(2755669320416618652)
XLA Ops:
  3.2 7.4 %all-to-all-start = ((bf16[16,32,256]{2,1,0:T(8,128)(2,1)}), bf16[16,32,256]{2,1,0:T(8,128)(2,1)S(1)}, u32[]{:S(2)}, u32[]{:S(2)}) async-start(bf16[16,32,256]{2,1,0:T(8,128)(2,1)} %broadcast_select_fusion), calls=%async_computation | async-start | bytes 524288 | tf_op jit(solution)/shard_map/all_to_all | solution.py:38
  12.1 1.3 dynamic_slice.150
  14.9 5.8 %all-to-all-done = bf16[16,32,256]{2,1,0:T(8,128)(2,1)S(1)} async-done(((bf16[16,32,256]{2,1,0:T(8,128)(2,1)}), bf16[16,32,256]{2,1,0:T(8,128)(2,1)S(1)}, u32[]{:S(2)}, u32[]{:S(2)}) %all-to-all-start) | async-done | bytes 262176 | tf_op jit(solution)/shard_map/all_to_all | solution.py:38
  23.0 1.8 %while.23 = (s32[]{:T(128)}, f32[128,8]{0,1:T(8,128)S(1)}, f32[128,8,128]{2,0,1:T(8,128)S(1)}, s32[]{:T(128)}, s32[]{:T(128)}, /*index=5*/bf16[128,8,128]{2,0,1:...) while((s32[]{:T(128)}, f32[128,8]{0,1:T(8,128)S(1)}, ...), condition=%wide.region_8.9_spmd, body=%wide.region_6.8_spmd.sunk | while | flops 271188992 | bytes 3691649 | solution.py:94
  25.9 1.8 %dynamic_slice.156 = bf16[64,2048]{1,0:T(8,128)(2,1)} dynamic-slice(bf16[128,4096]{1,0:T(8,128)(2,1)} %param.16, s32[]{:T(128)S(6)} %select_n.455, s32[]{:T(128)S(6)} %select_n.458), dynamic_slice_sizes={64,2048} | dynamic-slice | bytes 524292 | tf_op jit(solution)/shard_map/dynamic_slice | solution.py:146
  29.8 2.3 %collective-permute-done.3 = f32[8,128]{1,0:T(8,128)S(1)} collective-permute-done((f32[8,128]{1,0:T(8,128)S(1)}, f32[8,128]{1,0:T(8,128)S(1)}, u32[]{:S(2)}, u32[]{:S(2)}) %collective-permute-start.3) | collective-permute-done | bytes 4128 | tf_op jit(solution)/shard_map/ppermute | solution.py:156
  35.5 2.3 %fusion.106 = f32[256,1024]{1,0:T(8,128)S(1)} fusion(bf16[1024,1024]{1,0:T(8,128)(2,1)} %param.22, bf16[64,1024]{1,0:T(8,128)(2,1)S(1)} %get-tuple-element.283, bf16[64,1024]{1,0:T(8,128)(2,1)S(1)} %get-tuple-element.284, bf16[64,1024]{1,0:T(8,128)(2,1)S(1)} %get-tuple-element.285, bf16[64,1024]{1,0:T(8,128)(2,1)S(1)} %get-tuple-element.282), kind=kOutput, calls=%fused_computation.215 | convolution fusion | flops 538968064 | bytes 3670016 | tf_op jit(solution)/shard_map/dot_general | solution.py:167
  37.8 2.3 %fusion.105 = f32[256,1024]{1,0:T(8,128)S(1)} fusion(bf16[1024,1024]{1,0:T(8,128)(2,1)} %collective-permute-done.4, bf16[64,1024]{1,0:T(8,128)(2,1)S(1)} %get-tuple-element.283, bf16[64,1024]{1,0:T(8,128)(2,1)S(1)} %get-tuple-element.284, bf16[64,1024]{1,0:T(8,128)(2,1)S(1)} %get-tuple-element.285, bf16[64,1024]{1,0:T(8,128)(2,1)S(1)} %get-tuple-element.282), kind=kOutput, calls=%fused_computation.214 | convolution fusion | flops 538968064 | bytes 3670016 | tf_op jit(solution)/shard_map/dot_general | solution.py:168
  40.3 1.3 collective-permute-start.7
  46.2 9.1 %copy.53 = bf16[512,8,2,768]{3,1,2,0:T(8,128)(2,1)S(1)} copy(bf16[512,8,2,768]{3,2,1,0:T(2,128)(2,1)} %bitcast.181) | data formatting | bytes 25165824
  55.6 10.4 %collective-permute-done.8 = bf16[64,2048]{1,0:T(8,128)(2,1)S(1)} collective-permute-done((bf16[64,2048]{1,0:T(8,128)(2,1)}, bf16[64,2048]{1,0:T(8,128)(2,1)S(1)}, u32[]{:S(2)}, u32[]{:S(2)}) %collective-permute-start.8) | collective-permute-done | bytes 262176 | tf_op jit(solution)/shard_map/ppermute | solution.py:182
  68.9 6.2 %collective-permute-done.10 = bf16[64,2048]{1,0:T(8,128)(2,1)S(1)} collective-permute-done((bf16[64,2048]{1,0:T(8,128)(2,1)S(1)}, bf16[64,2048]{1,0:T(8,128)(2,1)S(1)}, u32[]{:S(2)}, u32[]{:S(2)}) %collective-permute-start.10) | collective-permute-done | bytes 262176 | tf_op jit(solution)/shard_map/ppermute | solution.py:205
  75.1 3.1 %collective-permute-done.9 = bf16[64,2048]{1,0:T(8,128)(2,1)S(1)} collective-permute-done((bf16[64,2048]{1,0:T(8,128)(2,1)S(1)}, bf16[64,2048]{1,0:T(8,128)(2,1)S(1)}, u32[]{:S(2)}, u32[]{:S(2)}) %collective-permute-start.9) | collective-permute-done | bytes 262176 | tf_op jit(solution)/shard_map/ppermute | solution.py:208
  79.3 6.0 %collective-permute-done.12 = bf16[64,2048]{1,0:T(8,128)(2,1)S(1)} collective-permute-done((bf16[64,2048]{1,0:T(8,128)(2,1)S(1)}, bf16[64,2048]{1,0:T(8,128)(2,1)S(1)}, u32[]{:S(2)}, u32[]{:S(2)}) %collective-permute-start.12) | collective-permute-done | bytes 262176 | tf_op jit(solution)/shard_map/ppermute | solution.py:205
  85.3 2.1 %collective-permute-done.11 = bf16[64,2048]{1,0:T(8,128)(2,1)S(1)} collective-permute-done((bf16[64,2048]{1,0:T(8,128)(2,1)S(1)}, bf16[64,2048]{1,0:T(8,128)(2,1)S(1)}, u32[]{:S(2)}, u32[]{:S(2)}) %collective-permute-start.11) | collective-permute-done | bytes 262176 | tf_op jit(solution)/shard_map/ppermute | solution.py:208
  87.5 1.4 collective-permute-start.14
  89.1 4.7 %collective-permute-done.14 = bf16[64,2048]{1,0:T(8,128)(2,1)S(1)} collective-permute-done((bf16[64,2048]{1,0:T(8,128)(2,1)S(1)}, bf16[64,2048]{1,0:T(8,128)(2,1)S(1)}, u32[]{:S(2)}, u32[]{:S(2)}) %collective-permute-start.14) | collective-permute-done | bytes 262176 | tf_op jit(solution)/shard_map/ppermute | solution.py:205
  93.8 3.2 %collective-permute-done.13 = bf16[64,2048]{1,0:T(8,128)(2,1)S(1)} collective-permute-done((bf16[64,2048]{1,0:T(8,128)(2,1)S(1)}, bf16[64,2048]{1,0:T(8,128)(2,1)S(1)}, u32[]{:S(2)}, u32[]{:S(2)}) %collective-permute-start.13) | collective-permute-done | bytes 262176 | tf_op jit(solution)/shard_map/ppermute | solution.py:208
  100.7 1.8 %fusion.6 = f32[256,1536]{1,0:T(8,128)S(1)} fusion(bf16[4096,1536]{1,0:T(8,128)(2,1)S(1)} %bitcast.182, bf16[64,2048]{1,0:T(8,128)(2,1)S(1)} %get-tuple-element.277, bf16[64,2048]{1,0:T(8,128)(2,1)S(1)} %get-tuple-element.275, bf16[64,2048]{1,0:T(8,128)(2,1)S(1)} %get-tuple-element.300, bf16[64,2048]{1,0:T(8,128)(2,1)S(1)} %get-tuple-element.301), kind=kOutput, calls=%fused_computation.13 | convolution fusion | flops 1614807040 | bytes 8912896 | tf_op jit(solution)/shard_map/dot_general | solution.py:238
  102.5 1.8 %fusion.12 = f32[256,1536]{1,0:T(8,128)S(1)} fusion(f32[256,1536]{1,0:T(8,128)S(1)} %fusion.6, bf16[4096,1536]{1,0:T(8,128)(2,1)S(1)} %bitcast.183, bf16[64,2048]{1,0:T(8,128)(2,1)S(1)} %get-tuple-element.276, bf16[64,2048]{1,0:T(8,128)(2,1)S(1)} %get-tuple-element.274, bf16[64,2048]{1,0:T(8,128)(2,1)S(1)} %get-tuple-element.313, ...), kind=kOutput, calls=%fused_computation.19 | convolution fusion | flops 1615200256 | bytes 10485760 | tf_op jit(solution)/shard_map/dot_general | solution.py:238
  104.6 2.1 %collective-permute-done.15 = bf16[64,2048]{1,0:T(8,128)(2,1)S(1)} collective-permute-done((bf16[64,2048]{1,0:T(8,128)(2,1)S(1)}, bf16[64,2048]{1,0:T(8,128)(2,1)S(1)}, u32[]{:S(2)}, u32[]{:S(2)}) %collective-permute-start.15) | collective-permute-done | bytes 262176 | tf_op jit(solution)/shard_map/ppermute | solution.py:205
  107.5 1.8 %collective-permute-done.19 = bf16[2,64,2048]{2,1,0:T(8,128)(2,1)S(1)} collective-permute-done((bf16[2,64,2048]{2,1,0:T(8,128)(2,1)S(1)}, bf16[2,64,2048]{2,1,0:T(8,128)(2,1)S(1)}, u32[]{:S(2)}, u32[]{:S(2)}) %collective-permute-start.19) | collective-permute-done | bytes 524320 | tf_op jit(solution)/shard_map/ppermute | solution.py:232
  109.3 1.8 %fusion.4 = f32[256,1536]{1,0:T(8,128)S(1)} fusion(bf16[4096,1536]{1,0:T(8,128)(2,1)S(1)} %bitcast.184, bf16[64,2048]{1,0:T(8,128)(2,1)S(1)} %get-tuple-element.269, bf16[64,2048]{1,0:T(8,128)(2,1)S(1)} %get-tuple-element.267, bf16[64,2048]{1,0:T(8,128)(2,1)S(1)} %get-tuple-element.316, bf16[64,2048]{1,0:T(8,128)(2,1)S(1)} %get-tuple-element.299), kind=kOutput, calls=%fused_computation.11 | convolution fusion | flops 1614807040 | bytes 8912896 | tf_op jit(solution)/shard_map/dot_general | solution.py:238
  111.1 1.8 %fusion.15 = f32[256,1536]{1,0:T(8,128)S(1)} fusion(f32[256,1536]{1,0:T(8,128)S(1)} %fusion.4, bf16[4096,1536]{1,0:T(8,128)(2,1)S(1)} %bitcast.185, bf16[64,2048]{1,0:T(8,128)(2,1)S(1)} %get-tuple-element.268, bf16[64,2048]{1,0:T(8,128)(2,1)S(1)} %get-tuple-element.266, bf16[64,2048]{1,0:T(8,128)(2,1)S(1)} %get-tuple-element.315, ...), kind=kOutput, calls=%fused_computation.20 | convolution fusion | flops 1615200256 | bytes 10485760 | tf_op jit(solution)/shard_map/dot_general | solution.py:238
  119.2 1.5 collective-permute-start.25
  120.6 6.8 %collective-permute-done.21 = bf16[128,1024]{1,0:T(8,128)(2,1)S(1)} collective-permute-done((bf16[128,1024]{1,0:T(8,128)(2,1)S(1)}, bf16[128,1024]{1,0:T(8,128)(2,1)S(1)}, u32[]{:S(2)}, u32[]{:S(2)}) %collective-permute-start.21) | collective-permute-done | bytes 262176 | tf_op jit(solution)/shard_map/ppermute | solution.py:281
  132.5 3.0 %collective-permute-start.30 = (bf16[128,1024]{1,0:T(8,128)(2,1)S(1)}, bf16[128,1024]{1,0:T(8,128)(2,1)S(1)}, u32[]{:S(2)}, u32[]{:S(2)}) collective-permute-start(bf16[128,1024]{1,0:T(8,128)(2,1)S(1)} %convert_add_fusion.1), channel_id=1, source_target_pairs={{0,3},{1,0},{2,1},{3,2},{4,7},{5,4},{6,5},{7,6},{8,11},{9,8},{10,9... | collective-permute-start | bytes 786440 | tf_op jit(solution)/shard_map/ppermute | solution.py:297
  135.5 1.4 collective-permute-start.27
  136.9 4.5 %collective-permute-done.28 = bf16[128,1024]{1,0:T(8,128)(2,1)S(1)} collective-permute-done((bf16[128,1024]{1,0:T(8,128)(2,1)S(1)}, bf16[128,1024]{1,0:T(8,128)(2,1)S(1)}, u32[]{:S(2)}, u32[]{:S(2)}) %collective-permute-start.28) | collective-permute-done | bytes 262176 | tf_op jit(solution)/shard_map/ppermute | solution.py:297
  141.8 2.9 %collective-permute-done.27 = bf16[128,1024]{1,0:T(8,128)(2,1)S(1)} collective-permute-done((bf16[128,1024]{1,0:T(8,128)(2,1)S(1)}, bf16[128,1024]{1,0:T(8,128)(2,1)S(1)}, u32[]{:S(2)}, u32[]{:S(2)}) %collective-permute-start.27) | collective-permute-done | bytes 262176 | tf_op jit(solution)/shard_map/ppermute | solution.py:281
  144.7 2.3 %collective-permute-done.30 = bf16[128,1024]{1,0:T(8,128)(2,1)S(1)} collective-permute-done((bf16[128,1024]{1,0:T(8,128)(2,1)S(1)}, bf16[128,1024]{1,0:T(8,128)(2,1)S(1)}, u32[]{:S(2)}, u32[]{:S(2)}) %collective-permute-start.30) | collective-permute-done | bytes 262176 | tf_op jit(solution)/shard_map/ppermute | solution.py:297
  147.0 4.7 %collective-permute-done.29 = bf16[128,1024]{1,0:T(8,128)(2,1)S(1)} collective-permute-done((bf16[128,1024]{1,0:T(8,128)(2,1)S(1)}, bf16[128,1024]{1,0:T(8,128)(2,1)S(1)}, u32[]{:S(2)}, u32[]{:S(2)}) %collective-permute-start.29) | collective-permute-done | bytes 262176 | tf_op jit(solution)/shard_map/ppermute | solution.py:297
  (201 shorter events, 42.7 us)
Async XLA Ops:
  3.2 17.5 %all-to-all-start = ((bf16[16,32,256]{2,1,0:T(8,128)(2,1)}), bf16[16,32,256]{2,1,0:T(8,128)(2,1)S(1)}, u32[]{:S(2)}, u32[]{:S(2)}) async-start(bf16[16,32,256]{2,1,0:T(8,128)(2,1)} %broadcast_select_fusion), calls=%async_computation | async-start | bytes 524288 | tf_op jit(solution)/shard_map/all_to_all | solution.py:38
  10.6 27.2 %collective-permute-start.4 = (bf16[1024,1024]{1,0:T(8,128)(2,1)}, bf16[1024,1024]{1,0:T(8,128)(2,1)}, u32[]{:S(2)}, u32[]{:S(2)}) collective-permute-start(bf16[1024,1024]{1,0:T(8,128)(2,1)} %param.22), channel_id=1, source_target_pairs={{0,4},{4,0},{8,12},{12,8},{1,5},{5,1},{9,13},{13,9},{2,6},{6,2},{1... | collective-permute-start | bytes 6291464 | tf_op jit(solution)/shard_map/ppermute | solution.py:140
  25.3 8.1 %collective-permute-start = (bf16[128,1024]{1,0:T(8,128)(2,1)S(1)}, bf16[128,1024]{1,0:T(8,128)(2,1)S(1)}, u32[]{:S(2)}, u32[]{:S(2)}) collective-permute-start(bf16[128,1024]{1,0:T(8,128)(2,1)S(1)} %copy.48), channel_id=1, source_target_pairs={{0,8},{4,12},{8,0},{12,4},{1,9},{5,13},{9,1},{13,5},{2,10},{6,14},... | collective-permute-start | bytes 786440 | tf_op jit(solution)/shard_map/ppermute | solution.py:162
  27.8 4.3 %collective-permute-start.3 = (f32[8,128]{1,0:T(8,128)S(1)}, f32[8,128]{1,0:T(8,128)S(1)}, u32[]{:S(2)}, u32[]{:S(2)}) collective-permute-start(f32[8,128]{1,0:T(8,128)S(1)} %bitcast.207), channel_id=1, source_target_pairs={{0,12},{4,0},{8,4},{12,8},{1,13},{5,1},{9,5},{13,9},{2,14},{6,2},{... | collective-permute-start | bytes 12296 | tf_op jit(solution)/shard_map/ppermute | solution.py:156
  28.3 5.1 %collective-permute-start.2 = (f32[8,128]{1,0:T(8,128)S(1)}, f32[8,128]{1,0:T(8,128)S(1)}, u32[]{:S(2)}, u32[]{:S(2)}) collective-permute-start(f32[8,128]{1,0:T(8,128)S(1)} %bitcast.208), channel_id=1, source_target_pairs={{0,8},{4,12},{8,0},{12,4},{1,9},{5,13},{9,1},{13,5},{2,10},{6,14},... | collective-permute-start | bytes 12296 | tf_op jit(solution)/shard_map/ppermute | solution.py:156
  29.4 4.0 %collective-permute-start.1 = (f32[8,128]{1,0:T(8,128)S(1)}, f32[8,128]{1,0:T(8,128)S(1)}, u32[]{:S(2)}, u32[]{:S(2)}) collective-permute-start(f32[8,128]{1,0:T(8,128)S(1)} %bitcast.209), channel_id=1, source_target_pairs={{0,4},{4,8},{8,12},{12,0},{1,5},{5,9},{9,13},{13,1},{2,6},{6,10},{... | collective-permute-start | bytes 12296 | tf_op jit(solution)/shard_map/ppermute | solution.py:156
  32.1 34.0 %collective-permute-start.5 = (bf16[64,2048]{1,0:T(8,128)(2,1)}, bf16[64,2048]{1,0:T(8,128)(2,1)S(1)}, u32[]{:S(2)}, u32[]{:S(2)}) collective-permute-start(bf16[64,2048]{1,0:T(8,128)(2,1)} %dynamic_slice.156), channel_id=1, source_target_pairs={{0,8},{4,12},{8,0},{12,4},{1,9},{5,13},{9,1},{13,5},{2,10},{6,14},... | collective-permute-start | bytes 786440 | tf_op jit(solution)/shard_map/ppermute | solution.py:150
  40.3 15.3 %collective-permute-start.7 = (bf16[64,2048]{1,0:T(8,128)(2,1)S(1)}, bf16[64,2048]{1,0:T(8,128)(2,1)S(1)}, u32[]{:S(2)}, u32[]{:S(2)}) collective-permute-start(bf16[64,2048]{1,0:T(8,128)(2,1)S(1)} %pad_maximum_fusion.9), channel_id=1, source_target_pairs={{0,3},{1,0},{2,1},{3,2},{4,7},{5,4},{6,5},{7,6},{8,11},{9,8},{10,9... | collective-permute-start | bytes 786440 | tf_op jit(solution)/shard_map/ppermute | solution.py:182
  42.3 13.3 %collective-permute-start.6 = (bf16[64,2048]{1,0:T(8,128)(2,1)}, bf16[64,2048]{1,0:T(8,128)(2,1)S(1)}, u32[]{:S(2)}, u32[]{:S(2)}) collective-permute-start(bf16[64,2048]{1,0:T(8,128)(2,1)} %pad_maximum_fusion.8), channel_id=1, source_target_pairs={{0,1},{1,2},{2,3},{3,0},{4,5},{5,6},{6,7},{7,4},{8,9},{9,10},{10,1... | collective-permute-start | bytes 786440 | tf_op jit(solution)/shard_map/ppermute | solution.py:182
  43.8 22.2 %collective-permute-start.8 = (bf16[64,2048]{1,0:T(8,128)(2,1)}, bf16[64,2048]{1,0:T(8,128)(2,1)S(1)}, u32[]{:S(2)}, u32[]{:S(2)}) collective-permute-start(bf16[64,2048]{1,0:T(8,128)(2,1)} %pad_maximum_fusion.10), channel_id=1, source_target_pairs={{0,2},{1,3},{2,0},{3,1},{4,6},{5,7},{6,4},{7,5},{8,10},{9,11},{10,... | collective-permute-start | bytes 786440 | tf_op jit(solution)/shard_map/ppermute | solution.py:182
  67.3 7.8 %collective-permute-start.10 = (bf16[64,2048]{1,0:T(8,128)(2,1)S(1)}, bf16[64,2048]{1,0:T(8,128)(2,1)S(1)}, u32[]{:S(2)}, u32[]{:S(2)}) collective-permute-start(bf16[64,2048]{1,0:T(8,128)(2,1)S(1)} %fusion.91), channel_id=1, source_target_pairs={{0,8},{4,12},{8,0},{12,4},{1,9},{5,13},{9,1},{13,5},{2,10},{6,14},... | collective-permute-start | bytes 786440 | tf_op jit(solution)/shard_map/ppermute | solution.py:205
  68.3 9.8 %collective-permute-start.9 = (bf16[64,2048]{1,0:T(8,128)(2,1)S(1)}, bf16[64,2048]{1,0:T(8,128)(2,1)S(1)}, u32[]{:S(2)}, u32[]{:S(2)}) collective-permute-start(bf16[64,2048]{1,0:T(8,128)(2,1)S(1)} %fusion.91), channel_id=1, source_target_pairs={{0,1},{1,2},{2,3},{3,0},{4,5},{5,6},{6,7},{7,4},{8,9},{9,10},{10,1... | collective-permute-start | bytes 786440 | tf_op jit(solution)/shard_map/ppermute | solution.py:208
  78.1 7.2 %collective-permute-start.12 = (bf16[64,2048]{1,0:T(8,128)(2,1)S(1)}, bf16[64,2048]{1,0:T(8,128)(2,1)S(1)}, u32[]{:S(2)}, u32[]{:S(2)}) collective-permute-start(bf16[64,2048]{1,0:T(8,128)(2,1)S(1)} %collective-permute-done.9), channel_id=1, source_target_pairs={{0,8},{4,12},{8,0},{12,4},{1,9},{5,13},{9,1},{13,5},{2,10},{6,14},... | collective-permute-start | bytes 786440 | tf_op jit(solution)/shard_map/ppermute | solution.py:205
  79.0 8.5 %collective-permute-start.11 = (bf16[64,2048]{1,0:T(8,128)(2,1)S(1)}, bf16[64,2048]{1,0:T(8,128)(2,1)S(1)}, u32[]{:S(2)}, u32[]{:S(2)}) collective-permute-start(bf16[64,2048]{1,0:T(8,128)(2,1)S(1)} %collective-permute-done.9), channel_id=1, source_target_pairs={{0,1},{1,2},{2,3},{3,0},{4,5},{5,6},{6,7},{7,4},{8,9},{9,10},{10,1... | collective-permute-start | bytes 786440 | tf_op jit(solution)/shard_map/ppermute | solution.py:208
  87.5 6.4 %collective-permute-start.14 = (bf16[64,2048]{1,0:T(8,128)(2,1)S(1)}, bf16[64,2048]{1,0:T(8,128)(2,1)S(1)}, u32[]{:S(2)}, u32[]{:S(2)}) collective-permute-start(bf16[64,2048]{1,0:T(8,128)(2,1)S(1)} %collective-permute-done.11), channel_id=1, source_target_pairs={{0,8},{4,12},{8,0},{12,4},{1,9},{5,13},{9,1},{13,5},{2,10},{6,14},... | collective-permute-start | bytes 786440 | tf_op jit(solution)/shard_map/ppermute | solution.py:205
  88.9 8.2 %collective-permute-start.13 = (bf16[64,2048]{1,0:T(8,128)(2,1)S(1)}, bf16[64,2048]{1,0:T(8,128)(2,1)S(1)}, u32[]{:S(2)}, u32[]{:S(2)}) collective-permute-start(bf16[64,2048]{1,0:T(8,128)(2,1)S(1)} %collective-permute-done.11), channel_id=1, source_target_pairs={{0,1},{1,2},{2,3},{3,0},{4,5},{5,6},{6,7},{7,4},{8,9},{9,10},{10,1... | collective-permute-start | bytes 786440 | tf_op jit(solution)/shard_map/ppermute | solution.py:208
  97.9 2.0 %collective-permute-start.16 = (bf16[2,64,2048]{2,1,0:T(8,128)(2,1)S(1)}, bf16[2,64,2048]{2,1,0:T(8,128)(2,1)S(1)}, u32[]{:S(2)}, u32[]{:S(2)}) collective-permute-start(bf16[2,64,2048]{2,1,0:T(8,128)(2,1)S(1)} %pad_maximum_fusion.1), channel_id=1, source_target_pairs={{0,4},{4,0},{8,12},{12,8},{1,5},{5,1},{9,13},{13,9},{2,6},{6,2},{1... | collective-permute-start | bytes 1572872 | tf_op jit(solution)/shard_map/ppermute | solution.py:232
  98.0 8.7 %collective-permute-start.15 = (bf16[64,2048]{1,0:T(8,128)(2,1)S(1)}, bf16[64,2048]{1,0:T(8,128)(2,1)S(1)}, u32[]{:S(2)}, u32[]{:S(2)}) collective-permute-start(bf16[64,2048]{1,0:T(8,128)(2,1)S(1)} %collective-permute-done.13), channel_id=1, source_target_pairs={{0,8},{4,12},{8,0},{12,4},{1,9},{5,13},{9,1},{13,5},{2,10},{6,14},... | collective-permute-start | bytes 786440 | tf_op jit(solution)/shard_map/ppermute | solution.py:205
  98.7 2.0 %collective-permute-start.17 = (bf16[2,64,2048]{2,1,0:T(8,128)(2,1)S(1)}, bf16[2,64,2048]{2,1,0:T(8,128)(2,1)S(1)}, u32[]{:S(2)}, u32[]{:S(2)}) collective-permute-start(bf16[2,64,2048]{2,1,0:T(8,128)(2,1)S(1)} %pad_maximum_fusion.2), channel_id=1, source_target_pairs={{0,4},{4,0},{8,12},{12,8},{1,5},{5,1},{9,13},{13,9},{2,6},{6,2},{1... | collective-permute-start | bytes 1572872 | tf_op jit(solution)/shard_map/ppermute | solution.py:232
  99.0 8.4 %collective-permute-start.18 = (bf16[2,64,2048]{2,1,0:T(8,128)(2,1)S(1)}, bf16[2,64,2048]{2,1,0:T(8,128)(2,1)S(1)}, u32[]{:S(2)}, u32[]{:S(2)}) collective-permute-start(bf16[2,64,2048]{2,1,0:T(8,128)(2,1)S(1)} %pad_maximum_fusion.4), channel_id=1, source_target_pairs={{0,4},{4,0},{8,12},{12,8},{1,5},{5,1},{9,13},{13,9},{2,6},{6,2},{1... | collective-permute-start | bytes 1572872 | tf_op jit(solution)/shard_map/ppermute | solution.py:232
  107.3 2.0 %collective-permute-start.19 = (bf16[2,64,2048]{2,1,0:T(8,128)(2,1)S(1)}, bf16[2,64,2048]{2,1,0:T(8,128)(2,1)S(1)}, u32[]{:S(2)}, u32[]{:S(2)}) collective-permute-start(bf16[2,64,2048]{2,1,0:T(8,128)(2,1)S(1)} %pad_maximum_fusion.5), channel_id=1, source_target_pairs={{0,4},{4,0},{8,12},{12,8},{1,5},{5,1},{9,13},{13,9},{2,6},{6,2},{1... | collective-permute-start | bytes 1572872 | tf_op jit(solution)/shard_map/ppermute | solution.py:232
  115.0 2.0 %collective-permute-start.20 = (bf16[256,1024]{1,0:T(8,128)(2,1)S(1)}, bf16[256,1024]{1,0:T(8,128)(2,1)S(1)}, u32[]{:S(2)}, u32[]{:S(2)}) collective-permute-start(bf16[256,1024]{1,0:T(8,128)(2,1)S(1)} %slice.353), channel_id=1, source_target_pairs={{0,4},{4,0},{8,12},{12,8},{1,5},{5,1},{9,13},{13,9},{2,6},{6,2},{1... | collective-permute-start | bytes 1572872 | tf_op jit(solution)/shard_map/ppermute | solution.py:276
  116.3 2.0 %collective-permute-start.24 = (bf16[256,1024]{1,0:T(8,128)(2,1)S(1)}, bf16[256,1024]{1,0:T(8,128)(2,1)S(1)}, u32[]{:S(2)}, u32[]{:S(2)}) collective-permute-start(bf16[256,1024]{1,0:T(8,128)(2,1)S(1)} %slice.350), channel_id=1, source_target_pairs={{0,4},{4,0},{8,12},{12,8},{1,5},{5,1},{9,13},{13,9},{2,6},{6,2},{1... | collective-permute-start | bytes 1572872 | tf_op jit(solution)/shard_map/ppermute | solution.py:276
  118.3 9.1 %collective-permute-start.21 = (bf16[128,1024]{1,0:T(8,128)(2,1)S(1)}, bf16[128,1024]{1,0:T(8,128)(2,1)S(1)}, u32[]{:S(2)}, u32[]{:S(2)}) collective-permute-start(bf16[128,1024]{1,0:T(8,128)(2,1)S(1)} %slice.357), channel_id=1, source_target_pairs={{0,8},{4,12},{8,0},{12,4},{1,9},{5,13},{9,1},{13,5},{2,10},{6,14},... | collective-permute-start | bytes 786440 | tf_op jit(solution)/shard_map/ppermute | solution.py:281
  119.2 13.3 %collective-permute-start.25 = (bf16[128,1024]{1,0:T(8,128)(2,1)S(1)}, bf16[128,1024]{1,0:T(8,128)(2,1)S(1)}, u32[]{:S(2)}, u32[]{:S(2)}) collective-permute-start(bf16[128,1024]{1,0:T(8,128)(2,1)S(1)} %slice.356), channel_id=1, source_target_pairs={{0,8},{4,12},{8,0},{12,4},{1,9},{5,13},{9,1},{13,5},{2,10},{6,14},... | collective-permute-start | bytes 786440 | tf_op jit(solution)/shard_map/ppermute | solution.py:281
  128.5 2.0 %collective-permute-start.23 = (bf16[256,1024]{1,0:T(8,128)(2,1)S(1)}, bf16[256,1024]{1,0:T(8,128)(2,1)S(1)}, u32[]{:S(2)}, u32[]{:S(2)}) collective-permute-start(bf16[256,1024]{1,0:T(8,128)(2,1)S(1)} %slice.351), channel_id=1, source_target_pairs={{0,4},{4,0},{8,12},{12,8},{1,5},{5,1},{9,13},{13,9},{2,6},{6,2},{1... | collective-permute-start | bytes 1572872 | tf_op jit(solution)/shard_map/ppermute | solution.py:276
  129.7 2.1 %collective-permute-start.22 = (bf16[256,1024]{1,0:T(8,128)(2,1)S(1)}, bf16[256,1024]{1,0:T(8,128)(2,1)S(1)}, u32[]{:S(2)}, u32[]{:S(2)}) collective-permute-start(bf16[256,1024]{1,0:T(8,128)(2,1)S(1)} %slice.352), channel_id=1, source_target_pairs={{0,4},{4,0},{8,12},{12,8},{1,5},{5,1},{9,13},{13,9},{2,6},{6,2},{1... | collective-permute-start | bytes 1572872 | tf_op jit(solution)/shard_map/ppermute | solution.py:276
  130.3 11.1 %collective-permute-start.28 = (bf16[128,1024]{1,0:T(8,128)(2,1)S(1)}, bf16[128,1024]{1,0:T(8,128)(2,1)S(1)}, u32[]{:S(2)}, u32[]{:S(2)}) collective-permute-start(bf16[128,1024]{1,0:T(8,128)(2,1)S(1)} %convert_add_fusion.2), channel_id=1, source_target_pairs={{0,1},{1,2},{2,3},{3,0},{4,5},{5,6},{6,7},{7,4},{8,9},{9,10},{10,1... | collective-permute-start | bytes 786440 | tf_op jit(solution)/shard_map/ppermute | solution.py:297
  130.7 10.7 %collective-permute-start.26 = (bf16[128,1024]{1,0:T(8,128)(2,1)S(1)}, bf16[128,1024]{1,0:T(8,128)(2,1)S(1)}, u32[]{:S(2)}, u32[]{:S(2)}) collective-permute-start(bf16[128,1024]{1,0:T(8,128)(2,1)S(1)} %slice.355), channel_id=1, source_target_pairs={{0,8},{4,12},{8,0},{12,4},{1,9},{5,13},{9,1},{13,5},{2,10},{6,14},... | collective-permute-start | bytes 786440 | tf_op jit(solution)/shard_map/ppermute | solution.py:281
  132.5 14.5 %collective-permute-start.30 = (bf16[128,1024]{1,0:T(8,128)(2,1)S(1)}, bf16[128,1024]{1,0:T(8,128)(2,1)S(1)}, u32[]{:S(2)}, u32[]{:S(2)}) collective-permute-start(bf16[128,1024]{1,0:T(8,128)(2,1)S(1)} %convert_add_fusion.1), channel_id=1, source_target_pairs={{0,3},{1,0},{2,1},{3,2},{4,7},{5,4},{6,5},{7,6},{8,11},{9,8},{10,9... | collective-permute-start | bytes 786440 | tf_op jit(solution)/shard_map/ppermute | solution.py:297
  135.5 9.2 %collective-permute-start.27 = (bf16[128,1024]{1,0:T(8,128)(2,1)S(1)}, bf16[128,1024]{1,0:T(8,128)(2,1)S(1)}, u32[]{:S(2)}, u32[]{:S(2)}) collective-permute-start(bf16[128,1024]{1,0:T(8,128)(2,1)S(1)} %slice.354), channel_id=1, source_target_pairs={{0,8},{4,12},{8,0},{12,4},{1,9},{5,13},{9,1},{13,5},{2,10},{6,14},... | collective-permute-start | bytes 786440 | tf_op jit(solution)/shard_map/ppermute | solution.py:281
  141.5 10.2 %collective-permute-start.29 = (bf16[128,1024]{1,0:T(8,128)(2,1)S(1)}, bf16[128,1024]{1,0:T(8,128)(2,1)S(1)}, u32[]{:S(2)}, u32[]{:S(2)}) collective-permute-start(bf16[128,1024]{1,0:T(8,128)(2,1)S(1)} %add_convert_fusion.1), channel_id=1, source_target_pairs={{0,1},{1,2},{2,3},{3,0},{4,5},{5,6},{6,7},{7,4},{8,9},{9,10},{10,1... | collective-permute-start | bytes 786440 | tf_op jit(solution)/shard_map/ppermute | solution.py:297
  (15 other events, 96.1 us)

commit v12 on v11

--- a/solution.py
+++ b/solution.py
@@ -174,9 +174,7 @@
             [jnp.where(core == 0, own, other), jnp.where(core == 0, other, own)], axis=1
         )
 
-    own_terms, other_terms, w_gate_up = lax.optimization_barrier(
-        (own_terms, other_terms, w_gate_up)
-    )
+    w_gate_up = after(w_gate_up, own_terms[:1, :1], other_terms[:1, :1])
     gate_up_weight = w_gate_up[0].reshape(model_width, 2 * ff_local)
     gots = [
         lax.ppermute(term(step).astype(bf16), "donor", rotation(n_donor, step)) for step in steps

time: 153 us -> 165 us (1.078)
  local copies, waits for them, and re-layouts: 20.5 us -> 24.5 us
  waiting for transfers between devices: 72.9 us -> 76.9 us
  matrix products: 17.9 us -> 20.8 us
    ppermute x3, waiting for transfers between devices: 10.7 us -> 18.9 us  [shards(): lax.ppermute(term(step).astype(bf16), 'donor', rotation(n_donor, step))]
    unnamed x36 -> x42, local copies, waits for them, and re-layouts: 9.84 us -> 14 us
    ppermute x4, waiting for transfers between devices: 19 us -> 15.8 us  [shards(): lax.ppermute(chunk, 'expert', turn(hop))]
    dot_general x4, matrix products: 7.23 us -> 10.1 us  [shards(): jnp.dot(jnp.concatenate([rows[row] for rows in own_rows + other_rows], ax...]
  transfers between devices with their start and end apart: 32 -> 32, of which waited for: 24 -> 23; matrix products, arithmetic and copies ran while one was open for 25% -> 28% of each run, Pallas kernels for 0% -> 0%
where the time goes in v12:
time: 165 us; the launch traced here: 164 us
  waiting for transfers between devices  76.9 us (47%)
  starting transfers between devices  28.5 us (17%)
  local copies, waits for them, and re-layouts  24.5 us (15%)
  matrix products  20.8 us (13%)
  other arithmetic  11.3 us (7%)
  between operations  2.37 us (1%)
    ppermute x3, waiting for transfers between devices, shards(): lax.ppermute(term(step).astype(bf16), 'donor', rotation(n_donor, step))  18.9 us
    ppermute x4, waiting for transfers between devices, shards(): lax.ppermute(chunk, 'expert', turn(hop))  15.8 us
    unnamed x42, local copies, waits for them, and re-layouts  14 us
    ppermute x3, waiting for transfers between devices, shards(): lax.ppermute(part_sum.astype(bf16), 'donor', rotation(n_donor, way))  11.4 us
    dot_general x4, matrix products, shards(): jnp.dot(jnp.concatenate([rows[row] for rows in own_rows + other_rows], ax...  10.1 us
    ppermute x4, waiting for transfers between devices, shards(): lax.ppermute(block[hop].astype(bf16), 'expert', turn(hop))  10.1 us
    ppermute x3, waiting for transfers between devices, shards(): chunk = lax.ppermute(chunk, 'donor', rotation(n_donor, 1))  9.21 us
    all_to_all x1, starting transfers between devices, attention(): lax.all_to_all(outgoing, ('expert', 'donor'), split_axis=0, concat_axis=0...  7.39 us
  transfers between devices with their start and end apart: 32, of which 23 were waited for; matrix products, arithmetic and copies ran while one was open for 28% of the time, Pallas kernels for 0%

profile of v12, /device:TPU:0, one launch (start us, length us, event | category | flops | bytes accessed | tf_op | source)
XLA Modules:
  0.0 164.4 jit_solution(12963627082355399352)
XLA Ops:
  3.2 7.4 %all-to-all-start = ((bf16[16,32,256]{2,1,0:T(8,128)(2,1)}), bf16[16,32,256]{2,1,0:T(8,128)(2,1)S(1)}, u32[]{:S(2)}, u32[]{:S(2)}) async-start(bf16[16,32,256]{2,1,0:T(8,128)(2,1)} %broadcast_select_fusion), calls=%async_computation | async-start | bytes 524288 | tf_op jit(solution)/shard_map/all_to_all | solution.py:38
  12.1 1.3 dynamic_slice.150
  15.0 5.7 %all-to-all-done = bf16[16,32,256]{2,1,0:T(8,128)(2,1)S(1)} async-done(((bf16[16,32,256]{2,1,0:T(8,128)(2,1)}), bf16[16,32,256]{2,1,0:T(8,128)(2,1)S(1)}, u32[]{:S(2)}, u32[]{:S(2)}) %all-to-all-start) | async-done | bytes 262176 | tf_op jit(solution)/shard_map/all_to_all | solution.py:38
  21.4 1.2 while.22
  23.1 1.9 %while.23 = (s32[]{:T(128)}, f32[128,8]{0,1:T(8,128)S(1)}, f32[128,8,128]{2,0,1:T(8,128)S(1)}, s32[]{:T(128)}, s32[]{:T(128)}, /*index=5*/bf16[128,8,128]{2,0,1:...) while((s32[]{:T(128)}, f32[128,8]{0,1:T(8,128)S(1)}, ...), condition=%wide.region_8.9_spmd, body=%wide.region_6.8_spmd.sunk | while | flops 271188992 | bytes 3691649 | solution.py:94
  26.0 13.2 %copy.53 = bf16[512,8,2,768]{3,1,2,0:T(8,128)(2,1)} copy(bf16[512,8,2,768]{3,2,1,0:T(2,128)(2,1)} %bitcast.181) | data formatting | bytes 25165824
  39.2 1.8 %dynamic_slice.156 = bf16[64,2048]{1,0:T(8,128)(2,1)} dynamic-slice(bf16[128,4096]{1,0:T(8,128)(2,1)} %param.16, s32[]{:T(128)S(6)} %select_n.455, s32[]{:T(128)S(6)} %select_n.458), dynamic_slice_sizes={64,2048} | dynamic-slice | bytes 524292 | tf_op jit(solution)/shard_map/dynamic_slice | solution.py:146
  47.7 2.3 %fusion.106 = f32[256,1024]{1,0:T(8,128)S(1)} fusion(bf16[1024,1024]{1,0:T(8,128)(2,1)} %param.22, bf16[64,1024]{1,0:T(8,128)(2,1)S(1)} %get-tuple-element.277, bf16[64,1024]{1,0:T(8,128)(2,1)S(1)} %get-tuple-element.278, bf16[64,1024]{1,0:T(8,128)(2,1)S(1)} %get-tuple-element.279, bf16[64,1024]{1,0:T(8,128)(2,1)S(1)} %get-tuple-element.276), kind=kOutput, calls=%fused_computation.215 | convolution fusion | flops 538968064 | bytes 3670016 | tf_op jit(solution)/shard_map/dot_general | solution.py:167
  50.1 2.3 %fusion.105 = f32[256,1024]{1,0:T(8,128)S(1)} fusion(bf16[1024,1024]{1,0:T(8,128)(2,1)} %collective-permute-done.4, bf16[64,1024]{1,0:T(8,128)(2,1)S(1)} %get-tuple-element.277, bf16[64,1024]{1,0:T(8,128)(2,1)S(1)} %get-tuple-element.278, bf16[64,1024]{1,0:T(8,128)(2,1)S(1)} %get-tuple-element.279, bf16[64,1024]{1,0:T(8,128)(2,1)S(1)} %get-tuple-element.276), kind=kOutput, calls=%fused_computation.214 | convolution fusion | flops 538968064 | bytes 3670016 | tf_op jit(solution)/shard_map/dot_general | solution.py:168
  52.5 1.8 %collective-permute-start.7 = (bf16[64,2048]{1,0:T(8,128)(2,1)S(1)}, bf16[64,2048]{1,0:T(8,128)(2,1)S(1)}, u32[]{:S(2)}, u32[]{:S(2)}) collective-permute-start(bf16[64,2048]{1,0:T(8,128)(2,1)S(1)} %pad_maximum_fusion.9), channel_id=1, source_target_pairs={{0,3},{1,0},{2,1},{3,2},{4,7},{5,4},{6,5},{7,6},{8,11},{9,8},{10,9... | collective-permute-start | bytes 786440 | tf_op jit(solution)/shard_map/ppermute | solution.py:180
  58.0 7.6 %collective-permute-done.7 = bf16[64,2048]{1,0:T(8,128)(2,1)S(1)} collective-permute-done((bf16[64,2048]{1,0:T(8,128)(2,1)S(1)}, bf16[64,2048]{1,0:T(8,128)(2,1)S(1)}, u32[]{:S(2)}, u32[]{:S(2)}) %collective-permute-start.7) | collective-permute-done | bytes 262176 | tf_op jit(solution)/shard_map/ppermute | solution.py:180
  65.5 1.8 %collective-permute-done.6 = bf16[64,2048]{1,0:T(8,128)(2,1)S(1)} collective-permute-done((bf16[64,2048]{1,0:T(8,128)(2,1)}, bf16[64,2048]{1,0:T(8,128)(2,1)S(1)}, u32[]{:S(2)}, u32[]{:S(2)}) %collective-permute-start.6) | collective-permute-done | bytes 262176 | tf_op jit(solution)/shard_map/ppermute | solution.py:180
  67.3 9.6 %collective-permute-done.8 = bf16[64,2048]{1,0:T(8,128)(2,1)S(1)} collective-permute-done((bf16[64,2048]{1,0:T(8,128)(2,1)}, bf16[64,2048]{1,0:T(8,128)(2,1)S(1)}, u32[]{:S(2)}, u32[]{:S(2)}) %collective-permute-start.8) | collective-permute-done | bytes 262176 | tf_op jit(solution)/shard_map/ppermute | solution.py:180
  76.9 1.2 fusion.91
  79.9 5.0 %collective-permute-done.10 = bf16[64,2048]{1,0:T(8,128)(2,1)S(1)} collective-permute-done((bf16[64,2048]{1,0:T(8,128)(2,1)S(1)}, bf16[64,2048]{1,0:T(8,128)(2,1)S(1)}, u32[]{:S(2)}, u32[]{:S(2)}) %collective-permute-start.10) | collective-permute-done | bytes 262176 | tf_op jit(solution)/shard_map/ppermute | solution.py:203
  84.9 3.9 %collective-permute-done.9 = bf16[64,2048]{1,0:T(8,128)(2,1)S(1)} collective-permute-done((bf16[64,2048]{1,0:T(8,128)(2,1)S(1)}, bf16[64,2048]{1,0:T(8,128)(2,1)S(1)}, u32[]{:S(2)}, u32[]{:S(2)}) %collective-permute-start.9) | collective-permute-done | bytes 262176 | tf_op jit(solution)/shard_map/ppermute | solution.py:206
  90.1 5.6 %collective-permute-done.12 = bf16[64,2048]{1,0:T(8,128)(2,1)S(1)} collective-permute-done((bf16[64,2048]{1,0:T(8,128)(2,1)S(1)}, bf16[64,2048]{1,0:T(8,128)(2,1)S(1)}, u32[]{:S(2)}, u32[]{:S(2)}) %collective-permute-start.12) | collective-permute-done | bytes 262176 | tf_op jit(solution)/shard_map/ppermute | solution.py:203
  95.7 2.6 %collective-permute-done.11 = bf16[64,2048]{1,0:T(8,128)(2,1)S(1)} collective-permute-done((bf16[64,2048]{1,0:T(8,128)(2,1)S(1)}, bf16[64,2048]{1,0:T(8,128)(2,1)S(1)}, u32[]{:S(2)}, u32[]{:S(2)}) %collective-permute-start.11) | collective-permute-done | bytes 262176 | tf_op jit(solution)/shard_map/ppermute | solution.py:206
  99.5 5.2 %collective-permute-done.14 = bf16[64,2048]{1,0:T(8,128)(2,1)S(1)} collective-permute-done((bf16[64,2048]{1,0:T(8,128)(2,1)S(1)}, bf16[64,2048]{1,0:T(8,128)(2,1)S(1)}, u32[]{:S(2)}, u32[]{:S(2)}) %collective-permute-start.14) | collective-permute-done | bytes 262176 | tf_op jit(solution)/shard_map/ppermute | solution.py:203
  104.7 2.7 %collective-permute-done.13 = bf16[64,2048]{1,0:T(8,128)(2,1)S(1)} collective-permute-done((bf16[64,2048]{1,0:T(8,128)(2,1)S(1)}, bf16[64,2048]{1,0:T(8,128)(2,1)S(1)}, u32[]{:S(2)}, u32[]{:S(2)}) %collective-permute-start.13) | collective-permute-done | bytes 262176 | tf_op jit(solution)/shard_map/ppermute | solution.py:206
  110.3 1.2 collective-permute-done.17
  111.6 4.7 %fusion.6 = f32[256,1536]{1,0:T(8,128)S(1)} fusion(bf16[4096,1536]{1,0:T(8,128)(2,1)} %bitcast.182, bf16[64,2048]{1,0:T(8,128)(2,1)S(1)} %get-tuple-element.271, bf16[64,2048]{1,0:T(8,128)(2,1)S(1)} %get-tuple-element.269, bf16[64,2048]{1,0:T(8,128)(2,1)S(1)} %get-tuple-element.294, bf16[64,2048]{1,0:T(8,128)(2,1)S(1)} %get-tuple-element.295), kind=kOutput, calls=%fused_computation.13 | convolution fusion | flops 1614807040 | bytes 8912896 | tf_op jit(solution)/shard_map/dot_general | solution.py:236
  116.4 1.8 %fusion.12 = f32[256,1536]{1,0:T(8,128)S(1)} fusion(f32[256,1536]{1,0:T(8,128)S(1)} %fusion.6, bf16[4096,1536]{1,0:T(8,128)(2,1)S(1)} %bitcast.185, bf16[64,2048]{1,0:T(8,128)(2,1)S(1)} %get-tuple-element.270, bf16[64,2048]{1,0:T(8,128)(2,1)S(1)} %get-tuple-element.268, bf16[64,2048]{1,0:T(8,128)(2,1)S(1)} %get-tuple-element.307, ...), kind=kOutput, calls=%fused_computation.19 | convolution fusion | flops 1615200256 | bytes 10485760 | tf_op jit(solution)/shard_map/dot_general | solution.py:236
  119.4 1.6 collective-permute-done.19
  121.1 1.8 %fusion.4 = f32[256,1536]{1,0:T(8,128)S(1)} fusion(bf16[4096,1536]{1,0:T(8,128)(2,1)S(1)} %bitcast.186, bf16[64,2048]{1,0:T(8,128)(2,1)S(1)} %get-tuple-element.263, bf16[64,2048]{1,0:T(8,128)(2,1)S(1)} %get-tuple-element.261, bf16[64,2048]{1,0:T(8,128)(2,1)S(1)} %get-tuple-element.310, bf16[64,2048]{1,0:T(8,128)(2,1)S(1)} %get-tuple-element.293), kind=kOutput, calls=%fused_computation.11 | convolution fusion | flops 1614807040 | bytes 8912896 | tf_op jit(solution)/shard_map/dot_general | solution.py:236
  122.9 1.8 %fusion.15 = f32[256,1536]{1,0:T(8,128)S(1)} fusion(f32[256,1536]{1,0:T(8,128)S(1)} %fusion.4, bf16[4096,1536]{1,0:T(8,128)(2,1)S(1)} %bitcast.187, bf16[64,2048]{1,0:T(8,128)(2,1)S(1)} %get-tuple-element.262, bf16[64,2048]{1,0:T(8,128)(2,1)S(1)} %get-tuple-element.260, bf16[64,2048]{1,0:T(8,128)(2,1)S(1)} %get-tuple-element.309, ...), kind=kOutput, calls=%fused_computation.20 | convolution fusion | flops 1615200256 | bytes 10485760 | tf_op jit(solution)/shard_map/dot_general | solution.py:236
  132.5 6.8 %collective-permute-done.21 = bf16[128,1024]{1,0:T(8,128)(2,1)S(1)} collective-permute-done((bf16[128,1024]{1,0:T(8,128)(2,1)S(1)}, bf16[128,1024]{1,0:T(8,128)(2,1)S(1)}, u32[]{:S(2)}, u32[]{:S(2)}) %collective-permute-start.21) | collective-permute-done | bytes 262176 | tf_op jit(solution)/shard_map/ppermute | solution.py:279
  144.3 3.3 %collective-permute-start.30 = (bf16[128,1024]{1,0:T(8,128)(2,1)S(1)}, bf16[128,1024]{1,0:T(8,128)(2,1)S(1)}, u32[]{:S(2)}, u32[]{:S(2)}) collective-permute-start(bf16[128,1024]{1,0:T(8,128)(2,1)S(1)} %convert_add_fusion.1), channel_id=1, source_target_pairs={{0,3},{1,0},{2,1},{3,2},{4,7},{5,4},{6,5},{7,6},{8,11},{9,8},{10,9... | collective-permute-start | bytes 786440 | tf_op jit(solution)/shard_map/ppermute | solution.py:295
  148.7 4.5 %collective-permute-done.28 = bf16[128,1024]{1,0:T(8,128)(2,1)S(1)} collective-permute-done((bf16[128,1024]{1,0:T(8,128)(2,1)S(1)}, bf16[128,1024]{1,0:T(8,128)(2,1)S(1)}, u32[]{:S(2)}, u32[]{:S(2)}) %collective-permute-start.28) | collective-permute-done | bytes 262176 | tf_op jit(solution)/shard_map/ppermute | solution.py:295
  153.7 2.9 %collective-permute-done.27 = bf16[128,1024]{1,0:T(8,128)(2,1)S(1)} collective-permute-done((bf16[128,1024]{1,0:T(8,128)(2,1)S(1)}, bf16[128,1024]{1,0:T(8,128)(2,1)S(1)}, u32[]{:S(2)}, u32[]{:S(2)}) %collective-permute-start.27) | collective-permute-done | bytes 262176 | tf_op jit(solution)/shard_map/ppermute | solution.py:279
  156.6 2.3 %collective-permute-done.30 = bf16[128,1024]{1,0:T(8,128)(2,1)S(1)} collective-permute-done((bf16[128,1024]{1,0:T(8,128)(2,1)S(1)}, bf16[128,1024]{1,0:T(8,128)(2,1)S(1)}, u32[]{:S(2)}, u32[]{:S(2)}) %collective-permute-start.30) | collective-permute-done | bytes 262176 | tf_op jit(solution)/shard_map/ppermute | solution.py:295
  158.9 4.7 %collective-permute-done.29 = bf16[128,1024]{1,0:T(8,128)(2,1)S(1)} collective-permute-done((bf16[128,1024]{1,0:T(8,128)(2,1)S(1)}, bf16[128,1024]{1,0:T(8,128)(2,1)S(1)}, u32[]{:S(2)}, u32[]{:S(2)}) %collective-permute-start.29) | collective-permute-done | bytes 262176 | tf_op jit(solution)/shard_map/ppermute | solution.py:295
  (208 shorter events, 43.8 us)
Async XLA Ops:
  3.2 17.5 %all-to-all-start = ((bf16[16,32,256]{2,1,0:T(8,128)(2,1)}), bf16[16,32,256]{2,1,0:T(8,128)(2,1)S(1)}, u32[]{:S(2)}, u32[]{:S(2)}) async-start(bf16[16,32,256]{2,1,0:T(8,128)(2,1)} %broadcast_select_fusion), calls=%async_computation | async-start | bytes 524288 | tf_op jit(solution)/shard_map/all_to_all | solution.py:38
  10.6 39.4 %collective-permute-start.4 = (bf16[1024,1024]{1,0:T(8,128)(2,1)}, bf16[1024,1024]{1,0:T(8,128)(2,1)}, u32[]{:S(2)}, u32[]{:S(2)}) collective-permute-start(bf16[1024,1024]{1,0:T(8,128)(2,1)} %param.22), channel_id=1, source_target_pairs={{0,4},{4,0},{8,12},{12,8},{1,5},{5,1},{9,13},{13,9},{2,6},{6,2},{1... | collective-permute-start | bytes 6291464 | tf_op jit(solution)/shard_map/ppermute | solution.py:140
  25.4 20.4 %collective-permute-start = (bf16[128,1024]{1,0:T(8,128)(2,1)S(1)}, bf16[128,1024]{1,0:T(8,128)(2,1)S(1)}, u32[]{:S(2)}, u32[]{:S(2)}) collective-permute-start(bf16[128,1024]{1,0:T(8,128)(2,1)S(1)} %copy.48), channel_id=1, source_target_pairs={{0,8},{4,12},{8,0},{12,4},{1,9},{5,13},{9,1},{13,5},{2,10},{6,14},... | collective-permute-start | bytes 786440 | tf_op jit(solution)/shard_map/ppermute | solution.py:162
  41.0 2.0 %collective-permute-start.3 = (f32[8,128]{1,0:T(8,128)S(1)}, f32[8,128]{1,0:T(8,128)S(1)}, u32[]{:S(2)}, u32[]{:S(2)}) collective-permute-start(f32[8,128]{1,0:T(8,128)S(1)} %bitcast.209), channel_id=1, source_target_pairs={{0,12},{4,0},{8,4},{12,8},{1,13},{5,1},{9,5},{13,9},{2,14},{6,2},{... | collective-permute-start | bytes 12296 | tf_op jit(solution)/shard_map/ppermute | solution.py:156
  41.6 3.6 %collective-permute-start.2 = (f32[8,128]{1,0:T(8,128)S(1)}, f32[8,128]{1,0:T(8,128)S(1)}, u32[]{:S(2)}, u32[]{:S(2)}) collective-permute-start(f32[8,128]{1,0:T(8,128)S(1)} %bitcast.210), channel_id=1, source_target_pairs={{0,8},{4,12},{8,0},{12,4},{1,9},{5,13},{9,1},{13,5},{2,10},{6,14},... | collective-permute-start | bytes 12296 | tf_op jit(solution)/shard_map/ppermute | solution.py:156
  42.7 3.0 %collective-permute-start.1 = (f32[8,128]{1,0:T(8,128)S(1)}, f32[8,128]{1,0:T(8,128)S(1)}, u32[]{:S(2)}, u32[]{:S(2)}) collective-permute-start(f32[8,128]{1,0:T(8,128)S(1)} %bitcast.211), channel_id=1, source_target_pairs={{0,4},{4,8},{8,12},{12,0},{1,5},{5,9},{9,13},{13,1},{2,6},{6,10},{... | collective-permute-start | bytes 12296 | tf_op jit(solution)/shard_map/ppermute | solution.py:156
  43.0 33.8 %collective-permute-start.5 = (bf16[64,2048]{1,0:T(8,128)(2,1)}, bf16[64,2048]{1,0:T(8,128)(2,1)S(1)}, u32[]{:S(2)}, u32[]{:S(2)}) collective-permute-start(bf16[64,2048]{1,0:T(8,128)(2,1)} %dynamic_slice.156), channel_id=1, source_target_pairs={{0,8},{4,12},{8,0},{12,4},{1,9},{5,13},{9,1},{13,5},{2,10},{6,14},... | collective-permute-start | bytes 786440 | tf_op jit(solution)/shard_map/ppermute | solution.py:150
  52.5 13.0 %collective-permute-start.7 = (bf16[64,2048]{1,0:T(8,128)(2,1)S(1)}, bf16[64,2048]{1,0:T(8,128)(2,1)S(1)}, u32[]{:S(2)}, u32[]{:S(2)}) collective-permute-start(bf16[64,2048]{1,0:T(8,128)(2,1)S(1)} %pad_maximum_fusion.9), channel_id=1, source_target_pairs={{0,3},{1,0},{2,1},{3,2},{4,7},{5,4},{6,5},{7,6},{8,11},{9,8},{10,9... | collective-permute-start | bytes 786440 | tf_op jit(solution)/shard_map/ppermute | solution.py:180
  55.0 12.3 %collective-permute-start.6 = (bf16[64,2048]{1,0:T(8,128)(2,1)}, bf16[64,2048]{1,0:T(8,128)(2,1)S(1)}, u32[]{:S(2)}, u32[]{:S(2)}) collective-permute-start(bf16[64,2048]{1,0:T(8,128)(2,1)} %pad_maximum_fusion.8), channel_id=1, source_target_pairs={{0,1},{1,2},{2,3},{3,0},{4,5},{5,6},{6,7},{7,4},{8,9},{9,10},{10,1... | collective-permute-start | bytes 786440 | tf_op jit(solution)/shard_map/ppermute | solution.py:180
  56.0 20.8 %collective-permute-start.8 = (bf16[64,2048]{1,0:T(8,128)(2,1)}, bf16[64,2048]{1,0:T(8,128)(2,1)S(1)}, u32[]{:S(2)}, u32[]{:S(2)}) collective-permute-start(bf16[64,2048]{1,0:T(8,128)(2,1)} %pad_maximum_fusion.10), channel_id=1, source_target_pairs={{0,2},{1,3},{2,0},{3,1},{4,6},{5,7},{6,4},{7,5},{8,10},{9,11},{10,... | collective-permute-start | bytes 786440 | tf_op jit(solution)/shard_map/ppermute | solution.py:180
  78.1 6.8 %collective-permute-start.10 = (bf16[64,2048]{1,0:T(8,128)(2,1)S(1)}, bf16[64,2048]{1,0:T(8,128)(2,1)S(1)}, u32[]{:S(2)}, u32[]{:S(2)}) collective-permute-start(bf16[64,2048]{1,0:T(8,128)(2,1)S(1)} %fusion.91), channel_id=1, source_target_pairs={{0,8},{4,12},{8,0},{12,4},{1,9},{5,13},{9,1},{13,5},{2,10},{6,14},... | collective-permute-start | bytes 786440 | tf_op jit(solution)/shard_map/ppermute | solution.py:203
  79.2 9.6 %collective-permute-start.9 = (bf16[64,2048]{1,0:T(8,128)(2,1)S(1)}, bf16[64,2048]{1,0:T(8,128)(2,1)S(1)}, u32[]{:S(2)}, u32[]{:S(2)}) collective-permute-start(bf16[64,2048]{1,0:T(8,128)(2,1)S(1)} %fusion.91), channel_id=1, source_target_pairs={{0,1},{1,2},{2,3},{3,0},{4,5},{5,6},{6,7},{7,4},{8,9},{9,10},{10,1... | collective-permute-start | bytes 786440 | tf_op jit(solution)/shard_map/ppermute | solution.py:206
  88.8 6.9 %collective-permute-start.12 = (bf16[64,2048]{1,0:T(8,128)(2,1)S(1)}, bf16[64,2048]{1,0:T(8,128)(2,1)S(1)}, u32[]{:S(2)}, u32[]{:S(2)}) collective-permute-start(bf16[64,2048]{1,0:T(8,128)(2,1)S(1)} %collective-permute-done.9), channel_id=1, source_target_pairs={{0,8},{4,12},{8,0},{12,4},{1,9},{5,13},{9,1},{13,5},{2,10},{6,14},... | collective-permute-start | bytes 786440 | tf_op jit(solution)/shard_map/ppermute | solution.py:203
  89.9 8.5 %collective-permute-start.11 = (bf16[64,2048]{1,0:T(8,128)(2,1)S(1)}, bf16[64,2048]{1,0:T(8,128)(2,1)S(1)}, u32[]{:S(2)}, u32[]{:S(2)}) collective-permute-start(bf16[64,2048]{1,0:T(8,128)(2,1)S(1)} %collective-permute-done.9), channel_id=1, source_target_pairs={{0,1},{1,2},{2,3},{3,0},{4,5},{5,6},{6,7},{7,4},{8,9},{9,10},{10,1... | collective-permute-start | bytes 786440 | tf_op jit(solution)/shard_map/ppermute | solution.py:206
  98.3 6.4 %collective-permute-start.14 = (bf16[64,2048]{1,0:T(8,128)(2,1)S(1)}, bf16[64,2048]{1,0:T(8,128)(2,1)S(1)}, u32[]{:S(2)}, u32[]{:S(2)}) collective-permute-start(bf16[64,2048]{1,0:T(8,128)(2,1)S(1)} %collective-permute-done.11), channel_id=1, source_target_pairs={{0,8},{4,12},{8,0},{12,4},{1,9},{5,13},{9,1},{13,5},{2,10},{6,14},... | collective-permute-start | bytes 786440 | tf_op jit(solution)/shard_map/ppermute | solution.py:203
  99.2 8.2 %collective-permute-start.13 = (bf16[64,2048]{1,0:T(8,128)(2,1)S(1)}, bf16[64,2048]{1,0:T(8,128)(2,1)S(1)}, u32[]{:S(2)}, u32[]{:S(2)}) collective-permute-start(bf16[64,2048]{1,0:T(8,128)(2,1)S(1)} %collective-permute-done.11), channel_id=1, source_target_pairs={{0,1},{1,2},{2,3},{3,0},{4,5},{5,6},{6,7},{7,4},{8,9},{9,10},{10,1... | collective-permute-start | bytes 786440 | tf_op jit(solution)/shard_map/ppermute | solution.py:206
  108.2 2.0 %collective-permute-start.16 = (bf16[2,64,2048]{2,1,0:T(8,128)(2,1)S(1)}, bf16[2,64,2048]{2,1,0:T(8,128)(2,1)S(1)}, u32[]{:S(2)}, u32[]{:S(2)}) collective-permute-start(bf16[2,64,2048]{2,1,0:T(8,128)(2,1)S(1)} %pad_maximum_fusion.1), channel_id=1, source_target_pairs={{0,4},{4,0},{8,12},{12,8},{1,5},{5,1},{9,13},{13,9},{2,6},{6,2},{1... | collective-permute-start | bytes 1572872 | tf_op jit(solution)/shard_map/ppermute | solution.py:230
  108.4 10.1 %collective-permute-start.15 = (bf16[64,2048]{1,0:T(8,128)(2,1)S(1)}, bf16[64,2048]{1,0:T(8,128)(2,1)S(1)}, u32[]{:S(2)}, u32[]{:S(2)}) collective-permute-start(bf16[64,2048]{1,0:T(8,128)(2,1)S(1)} %collective-permute-done.13), channel_id=1, source_target_pairs={{0,8},{4,12},{8,0},{12,4},{1,9},{5,13},{9,1},{13,5},{2,10},{6,14},... | collective-permute-start | bytes 786440 | tf_op jit(solution)/shard_map/ppermute | solution.py:203
  109.6 2.0 %collective-permute-start.17 = (bf16[2,64,2048]{2,1,0:T(8,128)(2,1)S(1)}, bf16[2,64,2048]{2,1,0:T(8,128)(2,1)S(1)}, u32[]{:S(2)}, u32[]{:S(2)}) collective-permute-start(bf16[2,64,2048]{2,1,0:T(8,128)(2,1)S(1)} %pad_maximum_fusion.2), channel_id=1, source_target_pairs={{0,4},{4,0},{8,12},{12,8},{1,5},{5,1},{9,13},{13,9},{2,6},{6,2},{1... | collective-permute-start | bytes 1572872 | tf_op jit(solution)/shard_map/ppermute | solution.py:230
  109.9 9.5 %collective-permute-start.18 = (bf16[2,64,2048]{2,1,0:T(8,128)(2,1)S(1)}, bf16[2,64,2048]{2,1,0:T(8,128)(2,1)S(1)}, u32[]{:S(2)}, u32[]{:S(2)}) collective-permute-start(bf16[2,64,2048]{2,1,0:T(8,128)(2,1)S(1)} %pad_maximum_fusion.4), channel_id=1, source_target_pairs={{0,4},{4,0},{8,12},{12,8},{1,5},{5,1},{9,13},{13,9},{2,6},{6,2},{1... | collective-permute-start | bytes 1572872 | tf_op jit(solution)/shard_map/ppermute | solution.py:230
  119.0 2.0 %collective-permute-start.19 = (bf16[2,64,2048]{2,1,0:T(8,128)(2,1)S(1)}, bf16[2,64,2048]{2,1,0:T(8,128)(2,1)S(1)}, u32[]{:S(2)}, u32[]{:S(2)}) collective-permute-start(bf16[2,64,2048]{2,1,0:T(8,128)(2,1)S(1)} %pad_maximum_fusion.5), channel_id=1, source_target_pairs={{0,4},{4,0},{8,12},{12,8},{1,5},{5,1},{9,13},{13,9},{2,6},{6,2},{1... | collective-permute-start | bytes 1572872 | tf_op jit(solution)/shard_map/ppermute | solution.py:230
  126.8 2.0 %collective-permute-start.20 = (bf16[256,1024]{1,0:T(8,128)(2,1)S(1)}, bf16[256,1024]{1,0:T(8,128)(2,1)S(1)}, u32[]{:S(2)}, u32[]{:S(2)}) collective-permute-start(bf16[256,1024]{1,0:T(8,128)(2,1)S(1)} %slice.363), channel_id=1, source_target_pairs={{0,4},{4,0},{8,12},{12,8},{1,5},{5,1},{9,13},{13,9},{2,6},{6,2},{1... | collective-permute-start | bytes 1572872 | tf_op jit(solution)/shard_map/ppermute | solution.py:274
  128.2 2.0 %collective-permute-start.24 = (bf16[256,1024]{1,0:T(8,128)(2,1)S(1)}, bf16[256,1024]{1,0:T(8,128)(2,1)S(1)}, u32[]{:S(2)}, u32[]{:S(2)}) collective-permute-start(bf16[256,1024]{1,0:T(8,128)(2,1)S(1)} %slice.360), channel_id=1, source_target_pairs={{0,4},{4,0},{8,12},{12,8},{1,5},{5,1},{9,13},{13,9},{2,6},{6,2},{1... | collective-permute-start | bytes 1572872 | tf_op jit(solution)/shard_map/ppermute | solution.py:274
  130.1 9.1 %collective-permute-start.21 = (bf16[128,1024]{1,0:T(8,128)(2,1)S(1)}, bf16[128,1024]{1,0:T(8,128)(2,1)S(1)}, u32[]{:S(2)}, u32[]{:S(2)}) collective-permute-start(bf16[128,1024]{1,0:T(8,128)(2,1)S(1)} %slice.367), channel_id=1, source_target_pairs={{0,8},{4,12},{8,0},{12,4},{1,9},{5,13},{9,1},{13,5},{2,10},{6,14},... | collective-permute-start | bytes 786440 | tf_op jit(solution)/shard_map/ppermute | solution.py:279
  131.3 13.0 %collective-permute-start.25 = (bf16[128,1024]{1,0:T(8,128)(2,1)S(1)}, bf16[128,1024]{1,0:T(8,128)(2,1)S(1)}, u32[]{:S(2)}, u32[]{:S(2)}) collective-permute-start(bf16[128,1024]{1,0:T(8,128)(2,1)S(1)} %slice.366), channel_id=1, source_target_pairs={{0,8},{4,12},{8,0},{12,4},{1,9},{5,13},{9,1},{13,5},{2,10},{6,14},... | collective-permute-start | bytes 786440 | tf_op jit(solution)/shard_map/ppermute | solution.py:279
  140.3 2.0 %collective-permute-start.23 = (bf16[256,1024]{1,0:T(8,128)(2,1)S(1)}, bf16[256,1024]{1,0:T(8,128)(2,1)S(1)}, u32[]{:S(2)}, u32[]{:S(2)}) collective-permute-start(bf16[256,1024]{1,0:T(8,128)(2,1)S(1)} %slice.361), channel_id=1, source_target_pairs={{0,4},{4,0},{8,12},{12,8},{1,5},{5,1},{9,13},{13,9},{2,6},{6,2},{1... | collective-permute-start | bytes 1572872 | tf_op jit(solution)/shard_map/ppermute | solution.py:274
  141.5 2.1 %collective-permute-start.22 = (bf16[256,1024]{1,0:T(8,128)(2,1)S(1)}, bf16[256,1024]{1,0:T(8,128)(2,1)S(1)}, u32[]{:S(2)}, u32[]{:S(2)}) collective-permute-start(bf16[256,1024]{1,0:T(8,128)(2,1)S(1)} %slice.362), channel_id=1, source_target_pairs={{0,4},{4,0},{8,12},{12,8},{1,5},{5,1},{9,13},{13,9},{2,6},{6,2},{1... | collective-permute-start | bytes 1572872 | tf_op jit(solution)/shard_map/ppermute | solution.py:274
  142.1 11.1 %collective-permute-start.28 = (bf16[128,1024]{1,0:T(8,128)(2,1)S(1)}, bf16[128,1024]{1,0:T(8,128)(2,1)S(1)}, u32[]{:S(2)}, u32[]{:S(2)}) collective-permute-start(bf16[128,1024]{1,0:T(8,128)(2,1)S(1)} %convert_add_fusion.2), channel_id=1, source_target_pairs={{0,1},{1,2},{2,3},{3,0},{4,5},{5,6},{6,7},{7,4},{8,9},{9,10},{10,1... | collective-permute-start | bytes 786440 | tf_op jit(solution)/shard_map/ppermute | solution.py:295
  142.6 10.7 %collective-permute-start.26 = (bf16[128,1024]{1,0:T(8,128)(2,1)S(1)}, bf16[128,1024]{1,0:T(8,128)(2,1)S(1)}, u32[]{:S(2)}, u32[]{:S(2)}) collective-permute-start(bf16[128,1024]{1,0:T(8,128)(2,1)S(1)} %slice.365), channel_id=1, source_target_pairs={{0,8},{4,12},{8,0},{12,4},{1,9},{5,13},{9,1},{13,5},{2,10},{6,14},... | collective-permute-start | bytes 786440 | tf_op jit(solution)/shard_map/ppermute | solution.py:279
  144.3 14.5 %collective-permute-start.30 = (bf16[128,1024]{1,0:T(8,128)(2,1)S(1)}, bf16[128,1024]{1,0:T(8,128)(2,1)S(1)}, u32[]{:S(2)}, u32[]{:S(2)}) collective-permute-start(bf16[128,1024]{1,0:T(8,128)(2,1)S(1)} %convert_add_fusion.1), channel_id=1, source_target_pairs={{0,3},{1,0},{2,1},{3,2},{4,7},{5,4},{6,5},{7,6},{8,11},{9,8},{10,9... | collective-permute-start | bytes 786440 | tf_op jit(solution)/shard_map/ppermute | solution.py:295
  147.6 9.0 %collective-permute-start.27 = (bf16[128,1024]{1,0:T(8,128)(2,1)S(1)}, bf16[128,1024]{1,0:T(8,128)(2,1)S(1)}, u32[]{:S(2)}, u32[]{:S(2)}) collective-permute-start(bf16[128,1024]{1,0:T(8,128)(2,1)S(1)} %slice.364), channel_id=1, source_target_pairs={{0,8},{4,12},{8,0},{12,4},{1,9},{5,13},{9,1},{13,5},{2,10},{6,14},... | collective-permute-start | bytes 786440 | tf_op jit(solution)/shard_map/ppermute | solution.py:279
  153.3 10.2 %collective-permute-start.29 = (bf16[128,1024]{1,0:T(8,128)(2,1)S(1)}, bf16[128,1024]{1,0:T(8,128)(2,1)S(1)}, u32[]{:S(2)}, u32[]{:S(2)}) collective-permute-start(bf16[128,1024]{1,0:T(8,128)(2,1)S(1)} %add_convert_fusion.1), channel_id=1, source_target_pairs={{0,1},{1,2},{2,3},{3,0},{4,5},{5,6},{6,7},{7,4},{8,9},{9,10},{10,1... | collective-permute-start | bytes 786440 | tf_op jit(solution)/shard_map/ppermute | solution.py:295
  (18 other events, 130.7 us)

commit v13 on v11

--- a/solution.py
+++ b/solution.py
@@ -198,7 +198,7 @@
     gain_f = norm_gain.astype(f32)
     resid_parts = [None] * n_donor
     own_act, other_act = [None] * n_donor, [None] * n_donor
-    batches = [n_donor // 2, n_donor - n_donor // 2]
+    batches = [max(1, n_donor - 1), 1]
     own_rows, other_rows, row_gates = [], [], []
     for slot in range(n_donor):
         part = (z - slot) % n_donor

time: 153 us -> 157 us (1.026)
  waiting for transfers between devices: 72.9 us -> 63.7 us
  matrix products: 17.9 us -> 23.7 us
  local copies, waits for them, and re-layouts: 20.5 us -> 24.4 us
  other arithmetic: 11.2 us -> 13.4 us
    ppermute x4, waiting for transfers between devices: 19 us -> 0.01 us  [shards(): lax.ppermute(chunk, 'expert', turn(hop))]
    ppermute x3, waiting for transfers between devices: 8.4 us -> 23.9 us  [shards(): chunk = lax.ppermute(chunk, 'donor', rotation(n_donor, 1))]
    dot_general x4, matrix products: 7.23 us -> 13 us  [shards(): jnp.dot(jnp.concatenate([rows[row] for rows in own_rows + other_rows], ax...]
    ppermute x3, waiting for transfers between devices: 10.7 us -> 6.55 us  [shards(): lax.ppermute(term(step).astype(bf16), 'donor', rotation(n_donor, step))]
    unnamed x36 -> x46, local copies, waits for them, and re-layouts: 9.84 us -> 13.8 us
    ppermute x4, waiting for transfers between devices: 10.2 us -> 6.77 us  [shards(): lax.ppermute(block[hop].astype(bf16), 'expert', turn(hop))]
    ppermute x4, starting transfers between devices: 3.92 us -> 1.68 us  [shards(): lax.ppermute(chunk, 'expert', turn(hop))]
    ppermute x3, waiting for transfers between devices: 11.4 us -> 13.2 us  [shards(): lax.ppermute(part_sum.astype(bf16), 'donor', rotation(n_donor, way))]
  transfers between devices with their start and end apart: 32 -> 32, of which waited for: 24 -> 16; matrix products, arithmetic and copies ran while one was open for 25% -> 29% of each run, Pallas kernels for 0% -> 0%
where the time goes in v13:
time: 157 us
  waiting for transfers between devices  63.7 us (41%)
  starting transfers between devices  29.1 us (19%)
  local copies, waits for them, and re-layouts  24.4 us (16%)
  matrix products  23.7 us (15%)
  other arithmetic  13.4 us (9%)
  between operations  2.44 us (2%)
    ppermute x3, waiting for transfers between devices, shards(): chunk = lax.ppermute(chunk, 'donor', rotation(n_donor, 1))  23.9 us
    unnamed x46, local copies, waits for them, and re-layouts  13.8 us
    ppermute x3, waiting for transfers between devices, shards(): lax.ppermute(part_sum.astype(bf16), 'donor', rotation(n_donor, way))  13.2 us
    dot_general x4, matrix products, shards(): jnp.dot(jnp.concatenate([rows[row] for rows in own_rows + other_rows], ax...  13 us
    all_to_all x1, starting transfers between devices, attention(): lax.all_to_all(outgoing, ('expert', 'donor'), split_axis=0, concat_axis=0...  7.39 us
    ppermute x4, waiting for transfers between devices, shards(): lax.ppermute(block[hop].astype(bf16), 'expert', turn(hop))  6.77 us
    ppermute x3, waiting for transfers between devices, shards(): lax.ppermute(term(step).astype(bf16), 'donor', rotation(n_donor, step))  6.55 us
    all_to_all x1, waiting for transfers between devices, attention(): lax.all_to_all(outgoing, ('expert', 'donor'), split_axis=0, concat_axis=0...  5.67 us
  transfers between devices with their start and end apart: 32, of which 16 were waited for; matrix products, arithmetic and copies ran while one was open for 29% of the time, Pallas kernels for 0%

profile of v13, /device:TPU:0, one launch (start us, length us, event | category | flops | bytes accessed | tf_op | source)
XLA Modules:
  0.0 156.9 jit_solution(5383691067882469939)
XLA Ops:
  3.2 7.4 %all-to-all-start = ((bf16[16,32,256]{2,1,0:T(8,128)(2,1)}), bf16[16,32,256]{2,1,0:T(8,128)(2,1)S(1)}, u32[]{:S(2)}, u32[]{:S(2)}) async-start(bf16[16,32,256]{2,1,0:T(8,128)(2,1)} %broadcast_select_fusion), calls=%async_computation | async-start | bytes 524288 | tf_op jit(solution)/shard_map/all_to_all | solution.py:38
  11.1 1.0 constant_dynamic-slice_fusion.17
  12.2 1.3 dynamic_slice.150
  15.0 5.7 %all-to-all-done = bf16[16,32,256]{2,1,0:T(8,128)(2,1)S(1)} async-done(((bf16[16,32,256]{2,1,0:T(8,128)(2,1)}), bf16[16,32,256]{2,1,0:T(8,128)(2,1)S(1)}, u32[]{:S(2)}, u32[]{:S(2)}) %all-to-all-start) | async-done | bytes 262176 | tf_op jit(solution)/shard_map/all_to_all | solution.py:38
  21.4 1.2 while.22
  23.1 1.9 %while.23 = (s32[]{:T(128)}, f32[128,8]{0,1:T(8,128)S(1)}, f32[128,8,128]{2,0,1:T(8,128)S(1)}, s32[]{:T(128)}, s32[]{:T(128)}, /*index=5*/bf16[128,8,128]{2,0,1:...) while((s32[]{:T(128)}, f32[128,8]{0,1:T(8,128)S(1)}, ...), condition=%wide.region_8.9_spmd, body=%wide.region_6.8_spmd.sunk | while | flops 271188992 | bytes 3691657 | solution.py:94
  26.0 1.1 dynamic_slice.156
  27.3 1.5 collective-permute-start.2
  28.8 1.4 collective-permute-start.3
  30.4 1.8 %collective-permute-done.1 = f32[8,128]{1,0:T(8,128)S(1)} collective-permute-done((f32[8,128]{1,0:T(8,128)S(1)}, f32[8,128]{1,0:T(8,128)S(1)}, u32[]{:S(2)}, u32[]{:S(2)}) %collective-permute-start.1) | collective-permute-done | bytes 4128 | tf_op jit(solution)/shard_map/ppermute | solution.py:156
  32.2 1.9 %collective-permute-start.5 = (bf16[64,2048]{1,0:T(8,128)(2,1)S(1)}, bf16[64,2048]{1,0:T(8,128)(2,1)S(1)}, u32[]{:S(2)}, u32[]{:S(2)}) collective-permute-start(bf16[64,2048]{1,0:T(8,128)(2,1)S(1)} %dynamic_slice.156), channel_id=1, source_target_pairs={{0,8},{4,12},{8,0},{12,4},{1,9},{5,13},{9,1},{13,5},{2,10},{6,14},... | collective-permute-start | bytes 786440 | tf_op jit(solution)/shard_map/ppermute | solution.py:150
  36.1 2.3 %fusion.88 = f32[256,1024]{1,0:T(8,128)S(1)} fusion(bf16[1024,1024]{1,0:T(8,128)(2,1)} %param.22, bf16[64,1024]{1,0:T(8,128)(2,1)S(1)} %get-tuple-element.295, bf16[64,1024]{1,0:T(8,128)(2,1)S(1)} %get-tuple-element.296, bf16[64,1024]{1,0:T(8,128)(2,1)S(1)} %get-tuple-element.297, bf16[64,1024]{1,0:T(8,128)(2,1)S(1)} %get-tuple-element.294), kind=kOutput, calls=%fused_computation.197 | convolution fusion | flops 538968064 | bytes 3670016 | tf_op jit(solution)/shard_map/dot_general | solution.py:167
  38.5 2.3 %fusion.87 = f32[256,1024]{1,0:T(8,128)S(1)} fusion(bf16[1024,1024]{1,0:T(8,128)(2,1)} %collective-permute-done.4, bf16[64,1024]{1,0:T(8,128)(2,1)S(1)} %get-tuple-element.295, bf16[64,1024]{1,0:T(8,128)(2,1)S(1)} %get-tuple-element.296, bf16[64,1024]{1,0:T(8,128)(2,1)S(1)} %get-tuple-element.297, bf16[64,1024]{1,0:T(8,128)(2,1)S(1)} %get-tuple-element.294), kind=kOutput, calls=%fused_computation.196 | convolution fusion | flops 538968064 | bytes 3670016 | tf_op jit(solution)/shard_map/dot_general | solution.py:168
  42.8 3.4 %collective-permute-start.7 = (bf16[64,2048]{1,0:T(8,128)(2,1)}, bf16[64,2048]{1,0:T(8,128)(2,1)S(1)}, u32[]{:S(2)}, u32[]{:S(2)}) collective-permute-start(bf16[64,2048]{1,0:T(8,128)(2,1)} %pad_maximum_fusion.9), channel_id=1, source_target_pairs={{0,3},{1,0},{2,1},{3,2},{4,7},{5,4},{6,5},{7,6},{8,11},{9,8},{10,9... | collective-permute-start | bytes 786440 | tf_op jit(solution)/shard_map/ppermute | solution.py:182
  48.4 13.1 %copy.53 = bf16[512,8,2,768]{3,1,2,0:T(8,128)(2,1)} copy(bf16[512,8,2,768]{3,2,1,0:T(2,128)(2,1)} %bitcast.198) | data formatting | bytes 25165824
  61.5 6.5 %collective-permute-done.8 = bf16[64,2048]{1,0:T(8,128)(2,1)S(1)} collective-permute-done((bf16[64,2048]{1,0:T(8,128)(2,1)}, bf16[64,2048]{1,0:T(8,128)(2,1)S(1)}, u32[]{:S(2)}, u32[]{:S(2)}) %collective-permute-start.8) | collective-permute-done | bytes 262176 | tf_op jit(solution)/shard_map/ppermute | solution.py:182
  68.1 1.2 fusion.61
  70.5 8.7 %collective-permute-done.9 = bf16[64,2048]{1,0:T(8,128)(2,1)S(1)} collective-permute-done((bf16[64,2048]{1,0:T(8,128)(2,1)S(1)}, bf16[64,2048]{1,0:T(8,128)(2,1)S(1)}, u32[]{:S(2)}, u32[]{:S(2)}) %collective-permute-start.9) | collective-permute-done | bytes 262176 | tf_op jit(solution)/shard_map/ppermute | solution.py:208
  80.5 7.6 %collective-permute-done.11 = bf16[64,2048]{1,0:T(8,128)(2,1)S(1)} collective-permute-done((bf16[64,2048]{1,0:T(8,128)(2,1)S(1)}, bf16[64,2048]{1,0:T(8,128)(2,1)S(1)}, u32[]{:S(2)}, u32[]{:S(2)}) %collective-permute-start.11) | collective-permute-done | bytes 262176 | tf_op jit(solution)/shard_map/ppermute | solution.py:208
  88.7 7.6 %collective-permute-done.13 = bf16[64,2048]{1,0:T(8,128)(2,1)S(1)} collective-permute-done((bf16[64,2048]{1,0:T(8,128)(2,1)S(1)}, bf16[64,2048]{1,0:T(8,128)(2,1)S(1)}, u32[]{:S(2)}, u32[]{:S(2)}) %collective-permute-start.13) | collective-permute-done | bytes 262176 | tf_op jit(solution)/shard_map/ppermute | solution.py:208
  99.8 2.6 %fusion.6 = f32[384,1536]{1,0:T(8,128)S(1)} fusion(bf16[384,2048]{1,0:T(8,128)(2,1)S(1)} %get-tuple-element.283, bf16[4096,1536]{1,0:T(8,128)(2,1)S(1)} %bitcast.201), kind=kOutput, calls=%fused_computation.13 | convolution fusion | flops 2415919104 | bytes 10223616 | tf_op jit(solution)/shard_map/dot_general | solution.py:238
  102.5 2.6 %fusion.12 = f32[384,1536]{1,0:T(8,128)S(1)} fusion(f32[384,1536]{1,0:T(8,128)S(1)} %fusion.6, bf16[384,2048]{1,0:T(8,128)(2,1)S(1)} %get-tuple-element.282, bf16[4096,1536]{1,0:T(8,128)(2,1)S(1)} %bitcast.202), kind=kOutput, calls=%fused_computation.19 | convolution fusion | flops 2416508928 | bytes 12582912 | tf_op jit(solution)/shard_map/dot_general | solution.py:238
  107.8 1.9 %collective-permute-done.19 = bf16[2,64,2048]{2,1,0:T(8,128)(2,1)S(1)} collective-permute-done((bf16[2,64,2048]{2,1,0:T(8,128)(2,1)}, bf16[2,64,2048]{2,1,0:T(8,128)(2,1)S(1)}, u32[]{:S(2)}, u32[]{:S(2)}) %collective-permute-start.19) | collective-permute-done | bytes 524320 | tf_op jit(solution)/shard_map/ppermute | solution.py:232
  109.7 3.8 %fusion.4 = f32[128,1536]{1,0:T(8,128)S(1)} fusion(bf16[4096,1536]{1,0:T(8,128)(2,1)} %bitcast.199, bf16[64,2048]{1,0:T(8,128)(2,1)S(1)} %get-tuple-element.279, bf16[64,2048]{1,0:T(8,128)(2,1)S(1)} %get-tuple-element.319), kind=kOutput, calls=%fused_computation.11 | convolution fusion | flops 806354944 | bytes 7602176 | tf_op jit(solution)/shard_map/dot_general | solution.py:238
  113.6 4.0 %fusion.15 = f32[128,1536]{1,0:T(8,128)S(1)} fusion(f32[128,1536]{1,0:T(8,128)S(1)} %fusion.4, bf16[4096,1536]{1,0:T(8,128)(2,1)} %bitcast.200, bf16[64,2048]{1,0:T(8,128)(2,1)S(1)} %get-tuple-element.278, bf16[64,2048]{1,0:T(8,128)(2,1)S(1)} %get-tuple-element.318), kind=kOutput, calls=%fused_computation.20 | convolution fusion | flops 806551552 | bytes 8388608 | tf_op jit(solution)/shard_map/dot_general | solution.py:238
  122.7 1.9 %collective-permute-start.21 = (bf16[128,1024]{1,0:T(8,128)(2,1)S(1)}, bf16[128,1024]{1,0:T(8,128)(2,1)S(1)}, u32[]{:S(2)}, u32[]{:S(2)}) collective-permute-start(bf16[128,1024]{1,0:T(8,128)(2,1)S(1)} %slice.365), channel_id=1, source_target_pairs={{0,8},{4,12},{8,0},{12,4},{1,9},{5,13},{9,1},{13,5},{2,10},{6,14},... | collective-permute-start | bytes 786440 | tf_op jit(solution)/shard_map/ppermute | solution.py:281
  125.0 6.8 %collective-permute-done.21 = bf16[128,1024]{1,0:T(8,128)(2,1)S(1)} collective-permute-done((bf16[128,1024]{1,0:T(8,128)(2,1)S(1)}, bf16[128,1024]{1,0:T(8,128)(2,1)S(1)}, u32[]{:S(2)}, u32[]{:S(2)}) %collective-permute-start.21) | collective-permute-done | bytes 262176 | tf_op jit(solution)/shard_map/ppermute | solution.py:281
  136.1 2.0 %collective-permute-start.26 = (bf16[128,1024]{1,0:T(8,128)(2,1)S(1)}, bf16[128,1024]{1,0:T(8,128)(2,1)S(1)}, u32[]{:S(2)}, u32[]{:S(2)}) collective-permute-start(bf16[128,1024]{1,0:T(8,128)(2,1)S(1)} %slice.363), channel_id=1, source_target_pairs={{0,8},{4,12},{8,0},{12,4},{1,9},{5,13},{9,1},{13,5},{2,10},{6,14},... | collective-permute-start | bytes 786440 | tf_op jit(solution)/shard_map/ppermute | solution.py:281
  138.4 2.8 %collective-permute-start.30 = (bf16[128,1024]{1,0:T(8,128)(2,1)S(1)}, bf16[128,1024]{1,0:T(8,128)(2,1)S(1)}, u32[]{:S(2)}, u32[]{:S(2)}) collective-permute-start(bf16[128,1024]{1,0:T(8,128)(2,1)S(1)} %convert_add_fusion.1), channel_id=1, source_target_pairs={{0,3},{1,0},{2,1},{3,2},{4,7},{5,4},{6,5},{7,6},{8,11},{9,8},{10,9... | collective-permute-start | bytes 786440 | tf_op jit(solution)/shard_map/ppermute | solution.py:297
  141.9 3.8 %collective-permute-done.28 = bf16[128,1024]{1,0:T(8,128)(2,1)S(1)} collective-permute-done((bf16[128,1024]{1,0:T(8,128)(2,1)S(1)}, bf16[128,1024]{1,0:T(8,128)(2,1)S(1)}, u32[]{:S(2)}, u32[]{:S(2)}) %collective-permute-start.28) | collective-permute-done | bytes 262176 | tf_op jit(solution)/shard_map/ppermute | solution.py:297
  146.6 4.7 %collective-permute-done.30 = bf16[128,1024]{1,0:T(8,128)(2,1)S(1)} collective-permute-done((bf16[128,1024]{1,0:T(8,128)(2,1)S(1)}, bf16[128,1024]{1,0:T(8,128)(2,1)S(1)}, u32[]{:S(2)}, u32[]{:S(2)}) %collective-permute-start.30) | collective-permute-done | bytes 262176 | tf_op jit(solution)/shard_map/ppermute | solution.py:297
  151.3 4.7 %collective-permute-done.29 = bf16[128,1024]{1,0:T(8,128)(2,1)S(1)} collective-permute-done((bf16[128,1024]{1,0:T(8,128)(2,1)S(1)}, bf16[128,1024]{1,0:T(8,128)(2,1)S(1)}, u32[]{:S(2)}, u32[]{:S(2)}) %collective-permute-start.29) | collective-permute-done | bytes 262176 | tf_op jit(solution)/shard_map/ppermute | solution.py:297
  (213 shorter events, 37.0 us)
Async XLA Ops:
  3.2 17.5 %all-to-all-start = ((bf16[16,32,256]{2,1,0:T(8,128)(2,1)}), bf16[16,32,256]{2,1,0:T(8,128)(2,1)S(1)}, u32[]{:S(2)}, u32[]{:S(2)}) async-start(bf16[16,32,256]{2,1,0:T(8,128)(2,1)} %broadcast_select_fusion), calls=%async_computation | async-start | bytes 524288 | tf_op jit(solution)/shard_map/all_to_all | solution.py:38
  10.6 27.8 %collective-permute-start.4 = (bf16[1024,1024]{1,0:T(8,128)(2,1)}, bf16[1024,1024]{1,0:T(8,128)(2,1)}, u32[]{:S(2)}, u32[]{:S(2)}) collective-permute-start(bf16[1024,1024]{1,0:T(8,128)(2,1)} %param.22), channel_id=1, source_target_pairs={{0,4},{4,0},{8,12},{12,8},{1,5},{5,1},{9,13},{13,9},{2,6},{6,2},{1... | collective-permute-start | bytes 6291464 | tf_op jit(solution)/shard_map/ppermute | solution.py:140
  25.4 8.6 %collective-permute-start = (bf16[128,1024]{1,0:T(8,128)(2,1)S(1)}, bf16[128,1024]{1,0:T(8,128)(2,1)S(1)}, u32[]{:S(2)}, u32[]{:S(2)}) collective-permute-start(bf16[128,1024]{1,0:T(8,128)(2,1)S(1)} %copy.48), channel_id=1, source_target_pairs={{0,8},{4,12},{8,0},{12,4},{1,9},{5,13},{9,1},{13,5},{2,10},{6,14},... | collective-permute-start | bytes 786440 | tf_op jit(solution)/shard_map/ppermute | solution.py:162
  27.2 5.0 %collective-permute-start.1 = (f32[8,128]{1,0:T(8,128)S(1)}, f32[8,128]{1,0:T(8,128)S(1)}, u32[]{:S(2)}, u32[]{:S(2)}) collective-permute-start(f32[8,128]{1,0:T(8,128)S(1)} %bitcast.219), channel_id=1, source_target_pairs={{0,4},{4,8},{8,12},{12,0},{1,5},{5,9},{9,13},{13,1},{2,6},{6,10},{... | collective-permute-start | bytes 12296 | tf_op jit(solution)/shard_map/ppermute | solution.py:156
  27.3 6.8 %collective-permute-start.2 = (f32[8,128]{1,0:T(8,128)S(1)}, f32[8,128]{1,0:T(8,128)S(1)}, u32[]{:S(2)}, u32[]{:S(2)}) collective-permute-start(f32[8,128]{1,0:T(8,128)S(1)} %bitcast.220), channel_id=1, source_target_pairs={{0,8},{4,12},{8,0},{12,4},{1,9},{5,13},{9,1},{13,5},{2,10},{6,14},... | collective-permute-start | bytes 12296 | tf_op jit(solution)/shard_map/ppermute | solution.py:156
  28.8 5.3 %collective-permute-start.3 = (f32[8,128]{1,0:T(8,128)S(1)}, f32[8,128]{1,0:T(8,128)S(1)}, u32[]{:S(2)}, u32[]{:S(2)}) collective-permute-start(f32[8,128]{1,0:T(8,128)S(1)} %bitcast.221), channel_id=1, source_target_pairs={{0,12},{4,0},{8,4},{12,8},{1,13},{5,1},{9,5},{13,9},{2,14},{6,2},{... | collective-permute-start | bytes 12296 | tf_op jit(solution)/shard_map/ppermute | solution.py:156
  32.2 35.9 %collective-permute-start.5 = (bf16[64,2048]{1,0:T(8,128)(2,1)S(1)}, bf16[64,2048]{1,0:T(8,128)(2,1)S(1)}, u32[]{:S(2)}, u32[]{:S(2)}) collective-permute-start(bf16[64,2048]{1,0:T(8,128)(2,1)S(1)} %dynamic_slice.156), channel_id=1, source_target_pairs={{0,8},{4,12},{8,0},{12,4},{1,9},{5,13},{9,1},{13,5},{2,10},{6,14},... | collective-permute-start | bytes 786440 | tf_op jit(solution)/shard_map/ppermute | solution.py:150
  41.6 19.9 %collective-permute-start.6 = (bf16[64,2048]{1,0:T(8,128)(2,1)}, bf16[64,2048]{1,0:T(8,128)(2,1)S(1)}, u32[]{:S(2)}, u32[]{:S(2)}) collective-permute-start(bf16[64,2048]{1,0:T(8,128)(2,1)} %pad_maximum_fusion.8), channel_id=1, source_target_pairs={{0,1},{1,2},{2,3},{3,0},{4,5},{5,6},{6,7},{7,4},{8,9},{9,10},{10,1... | collective-permute-start | bytes 786440 | tf_op jit(solution)/shard_map/ppermute | solution.py:182
  42.8 18.7 %collective-permute-start.7 = (bf16[64,2048]{1,0:T(8,128)(2,1)}, bf16[64,2048]{1,0:T(8,128)(2,1)S(1)}, u32[]{:S(2)}, u32[]{:S(2)}) collective-permute-start(bf16[64,2048]{1,0:T(8,128)(2,1)} %pad_maximum_fusion.9), channel_id=1, source_target_pairs={{0,3},{1,0},{2,1},{3,2},{4,7},{5,4},{6,5},{7,6},{8,11},{9,8},{10,9... | collective-permute-start | bytes 786440 | tf_op jit(solution)/shard_map/ppermute | solution.py:182
  46.9 21.2 %collective-permute-start.8 = (bf16[64,2048]{1,0:T(8,128)(2,1)}, bf16[64,2048]{1,0:T(8,128)(2,1)S(1)}, u32[]{:S(2)}, u32[]{:S(2)}) collective-permute-start(bf16[64,2048]{1,0:T(8,128)(2,1)} %pad_maximum_fusion.10), channel_id=1, source_target_pairs={{0,2},{1,3},{2,0},{3,1},{4,6},{5,7},{6,4},{7,5},{8,10},{9,11},{10,... | collective-permute-start | bytes 786440 | tf_op jit(solution)/shard_map/ppermute | solution.py:182
  69.3 9.9 %collective-permute-start.9 = (bf16[64,2048]{1,0:T(8,128)(2,1)S(1)}, bf16[64,2048]{1,0:T(8,128)(2,1)S(1)}, u32[]{:S(2)}, u32[]{:S(2)}) collective-permute-start(bf16[64,2048]{1,0:T(8,128)(2,1)S(1)} %fusion.61), channel_id=1, source_target_pairs={{0,1},{1,2},{2,3},{3,0},{4,5},{5,6},{6,7},{7,4},{8,9},{9,10},{10,1... | collective-permute-start | bytes 786440 | tf_op jit(solution)/shard_map/ppermute | solution.py:208
  69.4 9.8 %collective-permute-start.10 = (bf16[64,2048]{1,0:T(8,128)(2,1)S(1)}, bf16[64,2048]{1,0:T(8,128)(2,1)S(1)}, u32[]{:S(2)}, u32[]{:S(2)}) collective-permute-start(bf16[64,2048]{1,0:T(8,128)(2,1)S(1)} %fusion.61), channel_id=1, source_target_pairs={{0,8},{4,12},{8,0},{12,4},{1,9},{5,13},{9,1},{13,5},{2,10},{6,14},... | collective-permute-start | bytes 786440 | tf_op jit(solution)/shard_map/ppermute | solution.py:205
  79.2 8.9 %collective-permute-start.11 = (bf16[64,2048]{1,0:T(8,128)(2,1)S(1)}, bf16[64,2048]{1,0:T(8,128)(2,1)S(1)}, u32[]{:S(2)}, u32[]{:S(2)}) collective-permute-start(bf16[64,2048]{1,0:T(8,128)(2,1)S(1)} %collective-permute-done.9), channel_id=1, source_target_pairs={{0,1},{1,2},{2,3},{3,0},{4,5},{5,6},{6,7},{7,4},{8,9},{9,10},{10,1... | collective-permute-start | bytes 786440 | tf_op jit(solution)/shard_map/ppermute | solution.py:208
  79.2 8.9 %collective-permute-start.12 = (bf16[64,2048]{1,0:T(8,128)(2,1)S(1)}, bf16[64,2048]{1,0:T(8,128)(2,1)S(1)}, u32[]{:S(2)}, u32[]{:S(2)}) collective-permute-start(bf16[64,2048]{1,0:T(8,128)(2,1)S(1)} %collective-permute-done.9), channel_id=1, source_target_pairs={{0,8},{4,12},{8,0},{12,4},{1,9},{5,13},{9,1},{13,5},{2,10},{6,14},... | collective-permute-start | bytes 786440 | tf_op jit(solution)/shard_map/ppermute | solution.py:205
  80.2 16.1 %collective-permute-start.15 = (bf16[2,64,2048]{2,1,0:T(8,128)(2,1)S(1)}, bf16[2,64,2048]{2,1,0:T(8,128)(2,1)S(1)}, u32[]{:S(2)}, u32[]{:S(2)}) collective-permute-start(bf16[2,64,2048]{2,1,0:T(8,128)(2,1)S(1)} %pad_maximum_fusion.1), channel_id=1, source_target_pairs={{0,4},{4,0},{8,12},{12,8},{1,5},{5,1},{9,13},{13,9},{2,6},{6,2},{1... | collective-permute-start | bytes 1572872 | tf_op jit(solution)/shard_map/ppermute | solution.py:232
  88.1 8.2 %collective-permute-start.13 = (bf16[64,2048]{1,0:T(8,128)(2,1)S(1)}, bf16[64,2048]{1,0:T(8,128)(2,1)S(1)}, u32[]{:S(2)}, u32[]{:S(2)}) collective-permute-start(bf16[64,2048]{1,0:T(8,128)(2,1)S(1)} %collective-permute-done.11), channel_id=1, source_target_pairs={{0,1},{1,2},{2,3},{3,0},{4,5},{5,6},{6,7},{7,4},{8,9},{9,10},{10,1... | collective-permute-start | bytes 786440 | tf_op jit(solution)/shard_map/ppermute | solution.py:208
  88.1 8.2 %collective-permute-start.14 = (bf16[64,2048]{1,0:T(8,128)(2,1)S(1)}, bf16[64,2048]{1,0:T(8,128)(2,1)S(1)}, u32[]{:S(2)}, u32[]{:S(2)}) collective-permute-start(bf16[64,2048]{1,0:T(8,128)(2,1)S(1)} %collective-permute-done.11), channel_id=1, source_target_pairs={{0,8},{4,12},{8,0},{12,4},{1,9},{5,13},{9,1},{13,5},{2,10},{6,14},... | collective-permute-start | bytes 786440 | tf_op jit(solution)/shard_map/ppermute | solution.py:205
  96.3 9.9 %collective-permute-start.16 = (bf16[64,2048]{1,0:T(8,128)(2,1)S(1)}, bf16[64,2048]{1,0:T(8,128)(2,1)S(1)}, u32[]{:S(2)}, u32[]{:S(2)}) collective-permute-start(bf16[64,2048]{1,0:T(8,128)(2,1)S(1)} %collective-permute-done.13), channel_id=1, source_target_pairs={{0,8},{4,12},{8,0},{12,4},{1,9},{5,13},{9,1},{13,5},{2,10},{6,14},... | collective-permute-start | bytes 786440 | tf_op jit(solution)/shard_map/ppermute | solution.py:205
  97.1 2.0 %collective-permute-start.17 = (bf16[2,64,2048]{2,1,0:T(8,128)(2,1)S(1)}, bf16[2,64,2048]{2,1,0:T(8,128)(2,1)S(1)}, u32[]{:S(2)}, u32[]{:S(2)}) collective-permute-start(bf16[2,64,2048]{2,1,0:T(8,128)(2,1)S(1)} %pad_maximum_fusion.2), channel_id=1, source_target_pairs={{0,4},{4,0},{8,12},{12,8},{1,5},{5,1},{9,13},{13,9},{2,6},{6,2},{1... | collective-permute-start | bytes 1572872 | tf_op jit(solution)/shard_map/ppermute | solution.py:232
  97.2 2.6 %collective-permute-start.18 = (bf16[2,64,2048]{2,1,0:T(8,128)(2,1)S(1)}, bf16[2,64,2048]{2,1,0:T(8,128)(2,1)S(1)}, u32[]{:S(2)}, u32[]{:S(2)}) collective-permute-start(bf16[2,64,2048]{2,1,0:T(8,128)(2,1)S(1)} %pad_maximum_fusion.3), channel_id=1, source_target_pairs={{0,4},{4,0},{8,12},{12,8},{1,5},{5,1},{9,13},{13,9},{2,6},{6,2},{1... | collective-permute-start | bytes 1572872 | tf_op jit(solution)/shard_map/ppermute | solution.py:232
  107.6 2.1 %collective-permute-start.19 = (bf16[2,64,2048]{2,1,0:T(8,128)(2,1)}, bf16[2,64,2048]{2,1,0:T(8,128)(2,1)S(1)}, u32[]{:S(2)}, u32[]{:S(2)}) collective-permute-start(bf16[2,64,2048]{2,1,0:T(8,128)(2,1)} %pad_maximum_fusion.5), channel_id=1, source_target_pairs={{0,4},{4,0},{8,12},{12,8},{1,5},{5,1},{9,13},{13,9},{2,6},{6,2},{1... | collective-permute-start | bytes 1572872 | tf_op jit(solution)/shard_map/ppermute | solution.py:232
  119.4 2.0 %collective-permute-start.20 = (bf16[256,1024]{1,0:T(8,128)(2,1)S(1)}, bf16[256,1024]{1,0:T(8,128)(2,1)S(1)}, u32[]{:S(2)}, u32[]{:S(2)}) collective-permute-start(bf16[256,1024]{1,0:T(8,128)(2,1)S(1)} %slice.361), channel_id=1, source_target_pairs={{0,4},{4,0},{8,12},{12,8},{1,5},{5,1},{9,13},{13,9},{2,6},{6,2},{1... | collective-permute-start | bytes 1572872 | tf_op jit(solution)/shard_map/ppermute | solution.py:276
  120.7 2.0 %collective-permute-start.24 = (bf16[256,1024]{1,0:T(8,128)(2,1)S(1)}, bf16[256,1024]{1,0:T(8,128)(2,1)S(1)}, u32[]{:S(2)}, u32[]{:S(2)}) collective-permute-start(bf16[256,1024]{1,0:T(8,128)(2,1)S(1)} %slice.358), channel_id=1, source_target_pairs={{0,4},{4,0},{8,12},{12,8},{1,5},{5,1},{9,13},{13,9},{2,6},{6,2},{1... | collective-permute-start | bytes 1572872 | tf_op jit(solution)/shard_map/ppermute | solution.py:276
  122.7 9.1 %collective-permute-start.21 = (bf16[128,1024]{1,0:T(8,128)(2,1)S(1)}, bf16[128,1024]{1,0:T(8,128)(2,1)S(1)}, u32[]{:S(2)}, u32[]{:S(2)}) collective-permute-start(bf16[128,1024]{1,0:T(8,128)(2,1)S(1)} %slice.365), channel_id=1, source_target_pairs={{0,8},{4,12},{8,0},{12,4},{1,9},{5,13},{9,1},{13,5},{2,10},{6,14},... | collective-permute-start | bytes 786440 | tf_op jit(solution)/shard_map/ppermute | solution.py:281
  124.8 13.5 %collective-permute-start.25 = (bf16[128,1024]{1,0:T(8,128)(2,1)S(1)}, bf16[128,1024]{1,0:T(8,128)(2,1)S(1)}, u32[]{:S(2)}, u32[]{:S(2)}) collective-permute-start(bf16[128,1024]{1,0:T(8,128)(2,1)S(1)} %slice.364), channel_id=1, source_target_pairs={{0,8},{4,12},{8,0},{12,4},{1,9},{5,13},{9,1},{13,5},{2,10},{6,14},... | collective-permute-start | bytes 786440 | tf_op jit(solution)/shard_map/ppermute | solution.py:281
  132.9 2.0 %collective-permute-start.23 = (bf16[256,1024]{1,0:T(8,128)(2,1)S(1)}, bf16[256,1024]{1,0:T(8,128)(2,1)S(1)}, u32[]{:S(2)}, u32[]{:S(2)}) collective-permute-start(bf16[256,1024]{1,0:T(8,128)(2,1)S(1)} %slice.359), channel_id=1, source_target_pairs={{0,4},{4,0},{8,12},{12,8},{1,5},{5,1},{9,13},{13,9},{2,6},{6,2},{1... | collective-permute-start | bytes 1572872 | tf_op jit(solution)/shard_map/ppermute | solution.py:276
  134.0 2.1 %collective-permute-start.22 = (bf16[256,1024]{1,0:T(8,128)(2,1)S(1)}, bf16[256,1024]{1,0:T(8,128)(2,1)S(1)}, u32[]{:S(2)}, u32[]{:S(2)}) collective-permute-start(bf16[256,1024]{1,0:T(8,128)(2,1)S(1)} %slice.360), channel_id=1, source_target_pairs={{0,4},{4,0},{8,12},{12,8},{1,5},{5,1},{9,13},{13,9},{2,6},{6,2},{1... | collective-permute-start | bytes 1572872 | tf_op jit(solution)/shard_map/ppermute | solution.py:276
  134.6 11.1 %collective-permute-start.28 = (bf16[128,1024]{1,0:T(8,128)(2,1)S(1)}, bf16[128,1024]{1,0:T(8,128)(2,1)S(1)}, u32[]{:S(2)}, u32[]{:S(2)}) collective-permute-start(bf16[128,1024]{1,0:T(8,128)(2,1)S(1)} %convert_add_fusion.2), channel_id=1, source_target_pairs={{0,1},{1,2},{2,3},{3,0},{4,5},{5,6},{6,7},{7,4},{8,9},{9,10},{10,1... | collective-permute-start | bytes 786440 | tf_op jit(solution)/shard_map/ppermute | solution.py:297
  136.1 9.6 %collective-permute-start.26 = (bf16[128,1024]{1,0:T(8,128)(2,1)S(1)}, bf16[128,1024]{1,0:T(8,128)(2,1)S(1)}, u32[]{:S(2)}, u32[]{:S(2)}) collective-permute-start(bf16[128,1024]{1,0:T(8,128)(2,1)S(1)} %slice.363), channel_id=1, source_target_pairs={{0,8},{4,12},{8,0},{12,4},{1,9},{5,13},{9,1},{13,5},{2,10},{6,14},... | collective-permute-start | bytes 786440 | tf_op jit(solution)/shard_map/ppermute | solution.py:281
  138.4 12.9 %collective-permute-start.30 = (bf16[128,1024]{1,0:T(8,128)(2,1)S(1)}, bf16[128,1024]{1,0:T(8,128)(2,1)S(1)}, u32[]{:S(2)}, u32[]{:S(2)}) collective-permute-start(bf16[128,1024]{1,0:T(8,128)(2,1)S(1)} %convert_add_fusion.1), channel_id=1, source_target_pairs={{0,3},{1,0},{2,1},{3,2},{4,7},{5,4},{6,5},{7,6},{8,11},{9,8},{10,9... | collective-permute-start | bytes 786440 | tf_op jit(solution)/shard_map/ppermute | solution.py:297
  141.2 10.1 %collective-permute-start.27 = (bf16[128,1024]{1,0:T(8,128)(2,1)S(1)}, bf16[128,1024]{1,0:T(8,128)(2,1)S(1)}, u32[]{:S(2)}, u32[]{:S(2)}) collective-permute-start(bf16[128,1024]{1,0:T(8,128)(2,1)S(1)} %slice.362), channel_id=1, source_target_pairs={{0,8},{4,12},{8,0},{12,4},{1,9},{5,13},{9,1},{13,5},{2,10},{6,14},... | collective-permute-start | bytes 786440 | tf_op jit(solution)/shard_map/ppermute | solution.py:281
  145.8 10.2 %collective-permute-start.29 = (bf16[128,1024]{1,0:T(8,128)(2,1)S(1)}, bf16[128,1024]{1,0:T(8,128)(2,1)S(1)}, u32[]{:S(2)}, u32[]{:S(2)}) collective-permute-start(bf16[128,1024]{1,0:T(8,128)(2,1)S(1)} %add_convert_fusion.1), channel_id=1, source_target_pairs={{0,1},{1,2},{2,3},{3,0},{4,5},{5,6},{6,7},{7,4},{8,9},{9,10},{10,1... | collective-permute-start | bytes 786440 | tf_op jit(solution)/shard_map/ppermute | solution.py:297
  (19 other events, 136.3 us)
